TPU v7x, 32 devices: a whole 2x2x4 slice. The times are simulated.
32 devices in a mesh: ctx: 16 (over z, x, core), ch: 2 (over y).
Axes of the slice: x: 2, y: 2, z: 4, core: 2. Of those that a mesh axis runs over, the one named last changes fastest.
Arguments:
- q_in: bfloat16 [2048, 8192], P('ctx', 'ch'), may hold values from -6 to 6
- k_in: bfloat16 [2048, 8192], P('ctx', 'ch'), may hold values from -6 to 6
- v_in: bfloat16 [2048, 8192], P('ctx', 'ch'), may hold values from -6 to 6
- stretch_of_slot: int32 [32], replicated, may hold values from 0 to 31, each once
- short_weight: float32 [3, 7, 8192], P(None, None, 'ch'), may hold values from -2 to 2
- rates: float32 [16, 8192], P(None, 'ch'), may hold values from 4.8828124e-06 to 0.03
- residues: float32 [16, 8192], P(None, 'ch'), may hold values from -12 to 12
- skip: float32 [8192], P('ch'), may hold values from -4 to 4
- gain: float32 [8192], P('ch'), may hold values from 0.5 to 1.5
Outputs:
- operator_out: bfloat16 [2048, 8192], P('ctx', 'ch')
Inputs may be any that keep to these rules, and one draw needn't show every extreme that they name: stretch_of_slot names every sequence stretch exactly once.
All inputs are finite; a program needn't handle non-finite values.
Results may differ from a plain program's by a relative error of at most 0.001.
Values may be sent and summed in bfloat16 or wider, within the bound.
No kernel may reach another device: no remote copies, remote signals or barrier semaphores. Data moves between devices by JAX's collectives and lax.ppermute only.
A program may use at most 64 MiB of HBM per device.

v0:
```python
import jax
import jax.numpy as jnp
from jax import lax
from jax.sharding import PartitionSpec as P

D = 8192


def decay_combine(earlier, later):
    return (earlier[0] * later[0], earlier[1] * later[0] + later[1])


def on_device(q_in, k_in, v_in, stretch_of_slot, short_weight, rates, residues, skip, gain):
    tokens, width = q_in.shape
    stretch = tokens // 2
    reach = short_weight.shape[1] - 1
    order = rates.shape[0]
    span = float(stretch)
    my_index = lax.axis_index("ctx")
    own_stretches = lax.dynamic_slice_in_dim(stretch_of_slot, 2 * my_index, 2)
    stacked = jnp.stack([q_in, k_in, v_in]).reshape(3, 2, stretch, width)
    tail_rows = (
        stacked[:, :, stretch - reach :, :].transpose(1, 0, 2, 3).reshape(2, 3 * reach, width)
    )
    stretch_ids = stretch_of_slot
    select = (stretch_ids[None, :] == own_stretches[:, None] - 1).astype(jnp.bfloat16)
    previous = jnp.einsum(
        "mn,nxw->mxw",
        select,
        lax.all_gather(tail_rows, "ctx", axis=0, tiled=True),
        preferred_element_type=jnp.float32,
    )
    previous = previous.reshape(2, 3, reach, width).transpose(1, 0, 2, 3)
    extended = jnp.concatenate([previous, stacked.astype(jnp.float32)], axis=2)
    features = jnp.zeros((3, 2, stretch, width), jnp.float32)
    for shift_by in range(reach + 1):
        features = (
            features
            + short_weight[:, shift_by][:, None, None, :]
            * extended[:, :, reach - shift_by : reach - shift_by + stretch, :]
        )
    query = features[0]
    mixed_in = features[1] * features[2]
    positions = jnp.arange(stretch, dtype=jnp.float32)
    scaled = residues * jnp.sqrt(-jnp.expm1(-2.0 * rates))

    def mode_pass(mode, state):
        local_conv, ends = state
        rate = lax.dynamic_index_in_dim(rates, mode, 0, keepdims=False)
        amount = lax.dynamic_index_in_dim(scaled, mode, 0, keepdims=False)
        factors = jnp.broadcast_to(jnp.exp(-rate)[None, None, :], mixed_in.shape)
        running = lax.associative_scan(decay_combine, (factors, mixed_in), axis=1)[1]
        local_conv = local_conv + amount[None, None, :] * running
        ends = lax.dynamic_update_index_in_dim(ends, running[:, stretch - 1 : stretch, :], mode, 1)
        return (local_conv, ends)

    local_conv, ends = lax.fori_loop(
        0,
        order,
        mode_pass,
        (jnp.zeros((2, stretch, width), jnp.float32), jnp.zeros((2, order, width), jnp.float32)),
    )
    pieces = lax.all_gather(ends, "ctx", axis=0, tiled=True)
    stretch_ids = stretch_of_slot

    def one_target(target):
        gaps = target - 1 - stretch_ids
        before = gaps >= 0
        steps_back = jnp.maximum(gaps, 0).astype(jnp.float32)
        weights = jnp.where(
            before[:, None, None], jnp.exp(-rates[None] * (span * steps_back[:, None, None])), 0.0
        )
        return jnp.sum(weights * pieces, axis=0)

    starts = lax.map(one_target, own_stretches)

    def carry_pass(mode, total):
        rate = lax.dynamic_index_in_dim(rates, mode, 0, keepdims=False)
        amount = lax.dynamic_index_in_dim(scaled, mode, 0, keepdims=False)
        lifted = jnp.exp(-rate[None, :] * (positions[:, None] + 1.0))
        begin = lax.dynamic_index_in_dim(starts, mode, 1, keepdims=False)
        return total + (amount[None, :] * lifted)[None] * begin[:, None, :]

    carried = lax.fori_loop(0, order, carry_pass, jnp.zeros((2, stretch, width), jnp.float32))
    output = local_conv + carried + skip[None, None, :] * mixed_in
    zvalues = query * output
    squares = lax.psum(jnp.sum(zvalues * zvalues, axis=-1), "ch")
    scale = lax.rsqrt(squares / D + 1e-05)
    normed = (zvalues * scale[:, :, None] * gain[None, None, :]).astype(jnp.bfloat16)
    return normed.reshape(tokens, width)


def solution(mesh):
    in_specs = (
        P("ctx", "ch"),
        P("ctx", "ch"),
        P("ctx", "ch"),
        P(),
        P(None, None, "ch"),
        P(None, "ch"),
        P(None, "ch"),
        P("ch"),
        P("ch"),
    )
    out_specs = P("ctx", "ch")
    return jax.shard_map(
        on_device, mesh=mesh, in_specs=in_specs, out_specs=out_specs, check_vma=False
    )
```

profile of v0, /device:TPU:0, one launch (start us, length us, event | category | flops | bytes accessed | tf_op | source)
XLA Modules:
  0.0 781.2 jit_solution(13600498471908510249)
XLA Ops:
  6.5 4.3 pad_maximum_fusion.6
  15.4 61.5 %all-gather.3.cloned.1.call-done = bf16[32,18,4096]{2,1,0:T(8,128)(2,1)} async-done(((bf16[2,18,4096]{2,1,0:T(8,128)(2,1)}), bf16[32,18,4096]{2,1,0:T(8,128)(2,1)}) %all-gather.3.cloned.1.call-update) | async-done | bytes 4718608 | tf_op jit(solution)/shard_map/all_gather | solution.py:30
  76.9 8.1 %fusion.25 = f32[2,18,4096]{2,0,1:T(2,128)S(1)} fusion(bf16[32,18,4096]{2,1,0:T(8,128)(2,1)} %all-gather.3.cloned.1.call-done, s32[32]{0:T(128)S(1)} %copy-done.7, s32[2]{0:T(128)S(1)} %get-tuple-element.404), kind=kOutput, calls=%fused_computation.72 | convolution fusion | flops 9437248 | bytes 5308552 | tf_op jit(solution)/shard_map/mn,nxw->mxw/dot_general | solution.py:27
  85.3 6.6 fusion.11
  97.1 529.3 %while.43 = (s32[]{:T(128)}, f32[2,64,4096]{2,1,0:T(8,128)}, f32[2,16,4096]{2,1,0:T(8,128)}, f32[16,4096]{1,0:T(8,128)}, f32[2,64,4096]{2,1,0:T(8,128)}, /*index...) while((s32[]{:T(128)}, f32[2,64,4096]{2,1,0:T(8,128)}, f32[2,16,4096]{2,1,0:T(8,128)}, ...), condition=%wide.region_1.2_spmd.clone, body=%wide.region_0.1_spmd.clone.sunk | while | flops 5578755 | bytes 65405104 | solution.py:57
  114.4 4.2 slice.590
  146.9 4.2 slice.590
  180.0 4.2 slice.590
  213.2 4.2 slice.590
  246.3 4.2 slice.590
  279.4 4.2 slice.590
  312.5 4.2 slice.590
  345.7 4.2 slice.590
  378.8 4.2 slice.590
  411.9 4.2 slice.590
  445.0 4.2 slice.590
  544.4 4.2 slice.590
  626.4 73.6 %all-gather.5.cloned.1.call-done = f32[32,16,4096]{2,1,0:T(8,128)} async-done(((f32[2,16,4096]{2,1,0:T(8,128)}), f32[32,16,4096]{2,1,0:T(8,128)}) %all-gather.5.cloned.1.call-update) | async-done | bytes 8388624 | tf_op jit(solution)/shard_map/all_gather | solution.py:63
  700.9 13.0 %while.42 = (s32[]{:T(128)}, f32[2,16,4096]{2,1,0:T(8,128)}, s32[2]{0:T(128)S(1)}, s32[32]{0:T(128)S(1)}, f32[1,16,4096]{2,1,0:T(8,128)S(1)}, /*index=5*/f32[32,16,4096]{2,1,0:T(8,128)}, s32[]{:T(128)}, s32[1]{0:T(128)}) while((s32[]{:T(128)}, f32[2,16,4096]{2,1,0:T(8,128)}, s32[2]{0:T(128)S(1)}, s32[32]{0:T(128)S(1)}, ...), condition=%wide.region_4.5_spmd, body=%wide.region_2.4_spmd.sunk | while | flops 8323267 | bytes 9438389 | solution.py:75
  702.3 4.4 multiply_reduce_fusion.3
  708.8 4.4 multiply_reduce_fusion.3
  713.9 47.3 %while.44 = (s32[]{:T(128)}, f32[2,64,4096]{2,1,0:T(8,128)S(1)}, f32[16,4096]{1,0:T(8,128)}, f32[16,4096]{1,0:T(8,128)}, f32[2,16,4096]{2,1,0:T(8,128)}, /*index=5*/s32[]{:T(128)}, s32[]{:T(128)}) while((s32[]{:T(128)}, f32[2,64,4096]{2,1,0:T(8,128)S(1)}, f32[16,4096]{1,0:T(8,128)}, f32[16,4096]{1,0:T(8,128)}, ...), condition=%wide.region_6.7_spmd.clone, body=%wide.region_5.6_spmd.clone.sunk | while | flops 2101315 | bytes 6554207 | solution.py:84
  761.2 5.3 multiply_reduce_fusion.1
  766.6 4.9 psum.7
  (1024 shorter events, 535.6 us)
Async XLA Ops:
  6.5 70.4 %all-gather.3.cloned.1.call-start = ((), (), s32[]{:S(2)}) async-start(), calls=%async_computation | async-start | bytes 6684672 | tf_op jit(solution)/shard_map/all_gather | solution.py:30
  6.5 5.8 copy-start.3
  6.5 6.7 copy-start.7
  6.5 7.0 copy-start.4
  12.2 687.9 %all-gather.5.cloned.1.call-start = ((), (), s32[]{:S(2)}) async-start(), calls=%async_computation.1 | async-start | bytes 8912896 | tf_op jit(solution)/shard_map/all_gather | solution.py:63
  76.9 8.4 %copy-start.2 = (f32[3,2,64,4096]{3,2,1,0:T(8,128)S(1)}, f32[3,2,64,4096]{3,2,1,0:T(8,128)}, u32[]{:S(2)}) copy-start(f32[3,2,64,4096]{3,2,1,0:T(8,128)} %get-tuple-element.420) | copy-start | bytes 18874372
  118.8 4.6 copy-start
  151.3 4.6 copy-start
  184.4 4.6 copy-start
  217.6 4.6 copy-start
  250.7 4.6 copy-start
  283.8 4.6 copy-start
  316.9 4.6 copy-start
  350.1 4.6 copy-start
  383.2 4.6 copy-start
  416.3 4.6 copy-start
  449.4 4.6 copy-start
  482.5 4.6 copy-start
  515.7 4.6 copy-start
  548.8 4.6 copy-start
  581.9 4.6 copy-start
  615.0 4.6 copy-start
  713.9 47.3 %copy-start.5 = (f32[4096]{0:T(1024)S(1)}, f32[4096]{0:T(1024)}, u32[]{:S(2)}) copy-start(f32[4096]{0:T(1024)} %param.22) | copy-start | bytes 49156
  761.2 10.2 %copy-start.6 = (f32[4096]{0:T(1024)S(1)}, f32[4096]{0:T(1024)}, u32[]{:S(2)}) copy-start(f32[4096]{0:T(1024)} %param.23) | copy-start | bytes 49156
  (1 other events, 2.7 us)
Sparse Core Ops, SparseCore 0:
  12.3 64.5 all-gather.2
  626.6 73.4 all-gather.4
where the time goes:
time: 788 us; the launch traced here: 781 us
  local copies, waits for them, and re-layouts  431 us (55%)
  other arithmetic  180 us (23%)
  waiting for transfers between devices  135 us (17%)
  between operations  13.5 us (2%)
  loops' own time  8.14 us (1%)
  matrix products  8.06 us (1%)
    slice x288, local copies, waits for them, and re-layouts, mode_pass(): lax.associative_scan(decay_combine, (factors, mixed_in), axis=1)[1]  250 us
    pad x160, local copies, waits for them, and re-layouts, mode_pass(): lax.associative_scan(decay_combine, (factors, mixed_in), axis=1)[1]  127 us
    all_gather x1, waiting for transfers between devices, on_device(): pieces = lax.all_gather(ends, 'ctx', axis=0, tiled=True)  73.6 us
    add x16, other arithmetic, mode_pass(): local_conv = local_conv + amount[None, None, :] * running  63.1 us
    all_gather x1, waiting for transfers between devices, on_device(): lax.all_gather(tail_rows, 'ctx', axis=0, tiled=True)  61.5 us
    dynamic_update_slice x16, local copies, waits for them, and re-layouts, mode_pass(): lax.dynamic_update_index_in_dim(ends, running[:, stretch - 1:stretch, :],...  28.2 us
    add x96, other arithmetic, mode_pass(): lax.associative_scan(decay_combine, (factors, mixed_in), axis=1)[1]  20.6 us
    dynamic_slice x32, local copies, waits for them, and re-layouts, carry_pass(): begin = lax.dynamic_index_in_dim(starts, mode, 1, keepdims=False)  16.2 us
  transfers between devices with their start and end apart: 2, of which 2 were waited for; matrix products, arithmetic and copies ran while one was open for 0% of the time, Pallas kernels for 0%

commit v1 on v0

v1 whole, which is shorter than its diff:
```python
from decimal import Decimal, getcontext

import jax
import jax.numpy as jnp
import ml_dtypes
import numpy as np
from jax import lax
from jax.experimental import pallas as pl
from jax.experimental.pallas import tpu as pltpu
from jax.sharding import PartitionSpec as P

F32, BF16 = jnp.float32, jnp.bfloat16
LANES = 128
STRETCH = 64
REACH = 6
INNER = STRETCH - REACH
NODES = (1, 8, 21, 36, 49, 56)
ANCHORS = ("0.000511", "0.004393", "0.011118", "0.018882", "0.025607", "0.029489")
RANK = len(NODES)
PIECE = 6 * REACH + 2 * RANK
BACK = 2 * REACH + 2 * RANK


def cardinal_table():
    getcontext().prec = 50
    anchors = [Decimal(a) for a in ANCHORS]
    table = [[(-a * n).exp() for n in NODES] for a in anchors]
    right = [[(-a * d).exp() for d in range(INNER)] for a in anchors]
    for col in range(RANK):
        pivot = max(range(col, RANK), key=lambda row: abs(table[row][col]))
        table[col], table[pivot] = table[pivot], table[col]
        right[col], right[pivot] = right[pivot], right[col]
        for row in range(RANK):
            if row != col:
                factor = table[row][col] / table[col][col]
                table[row] = [x - factor * y for x, y in zip(table[row], table[col])]
                right[row] = [x - factor * y for x, y in zip(right[row], right[col])]
    return np.array([[float(x / table[j][j]) for x in right[j]] for j in range(RANK)], np.float32)


def halves(values):
    high = values.astype(ml_dtypes.bfloat16)
    low = (values - high.astype(np.float32)).astype(ml_dtypes.bfloat16)
    return high, low


def constant_matrices():
    cardinal = cardinal_table()
    ends = np.zeros((16, STRETCH), np.float32)
    local = np.zeros((RANK, STRETCH, STRETCH), np.float32)
    lift = np.zeros((2, 2 * STRETCH, 2 * BACK), np.float32)
    high, low = (h.astype(np.float32) for h in halves(cardinal))
    for j in range(RANK):
        for s in range(REACH, STRETCH):
            ends[j, s] = cardinal[j, STRETCH - 1 - s]
            local[j, s:, s] = cardinal[j, : STRETCH - s]
        for half in range(2):
            rows = slice(half * STRETCH + REACH, (half + 1) * STRETCH)
            at = half * BACK + 2 * REACH
            lift[0, rows, at + j] = high[j]
            lift[0, rows, at + RANK + j] = high[j]
            lift[1, rows, at + j] = low[j]
    for half in range(2):
        for t in range(REACH):
            lift[0, half * STRETCH + t, half * BACK + t] = 1.0
            lift[0, half * STRETCH + t, half * BACK + REACH + t] = 1.0
    local = local.reshape(RANK * STRETCH, STRETCH)

    def triple(m):
        h, l = halves(m)
        return np.concatenate([h, h, l], axis=1)

    lifted = np.concatenate([lift[0], lift[1]], axis=1).astype(ml_dtypes.bfloat16)
    return triple(ends), triple(local), lifted


def split(values):
    high = values.astype(BF16)
    return high, (values - high.astype(F32)).astype(BF16)


def amplitude(rate, residue):
    x = 2.0 * rate
    series = 1.0 - x * (0.5 - x * (1 / 6 - x * (1 / 24 - x * (1 / 120 - x * (1 / 720)))))
    return residue * jnp.sqrt(x * series)


def gather_kernel(q_ref, k_ref, v_ref, taps_ref, ends_ref, pay_ref, u_ref, xs, pay):
    tile = k_ref.shape[1]
    for g in range(tile // LANES):
        cols = slice(g * LANES, (g + 1) * LANES)
        for i in range(2):
            rows = slice(i * STRETCH, (i + 1) * STRETCH)
            for a, ref in enumerate((q_ref, k_ref, v_ref)):
                base = i * (STRETCH + 8) + 8
                if a == 0:
                    xs[a, g, base : base + 16, :] = ref[i * STRETCH : i * STRETCH + 16, cols].astype(F32)
                    xs[a, g, base + STRETCH - 16 : base + STRETCH, :] = ref[
                        (i + 1) * STRETCH - 16 : (i + 1) * STRETCH, cols
                    ].astype(F32)
                else:
                    xs[a, g, base - 8 : base, :] = jnp.zeros((8, LANES), F32)
                    xs[a, g, base : base + STRETCH, :] = ref[rows, cols].astype(F32)
                pay[g, i * PIECE + a * REACH : i * PIECE + (a + 1) * REACH, :] = xs[
                    a, g, base + STRETCH - REACH : base + STRETCH, :
                ]
                pay[g, i * PIECE + (3 + a) * REACH : i * PIECE + (4 + a) * REACH, :] = xs[
                    a, g, base : base + REACH, :
                ]
        taps = [[taps_ref[a, j : j + 1, cols] for j in range(REACH + 1)] for a in (1, 2)]
        for i in range(2):
            for b in range(STRETCH // 16):
                base = i * (STRETCH + 8) + 8 + 16 * b
                both = []
                for a in range(2):
                    total = taps[a][0] * xs[1 + a, g, base : base + 16, :]
                    for j in range(1, REACH + 1):
                        total = total + taps[a][j] * xs[1 + a, g, base - j : base - j + 16, :]
                    both.append(total)
                mixed = both[0] * both[1]
                if b == 0:
                    row = lax.broadcasted_iota(jnp.int32, (16, LANES), 0)
                    mixed = jnp.where(row >= REACH, mixed, 0.0)
                high, low = split(mixed)
                rows = slice(i * STRETCH + 16 * b, i * STRETCH + 16 * b + 16)
                u_ref[0, rows, cols] = high
                u_ref[1, rows, cols] = low
    for i in range(2):
        rows = slice(i * STRETCH, (i + 1) * STRETCH)
        high, low = u_ref[0, rows, :], u_ref[1, rows, :]
        moments = jnp.dot(
            ends_ref[...], jnp.concatenate([high, low, high], axis=0), preferred_element_type=F32
        )
        top, rest = split(moments)
        for g in range(tile // LANES):
            cols = slice(g * LANES, (g + 1) * LANES)
            at = i * PIECE + 6 * REACH
            pay[g, at : at + RANK, :] = top.astype(F32)[:RANK, cols]
            pay[g, at + RANK : at + 2 * RANK, :] = rest.astype(F32)[:RANK, cols]
    for g in range(tile // LANES):
        cols = slice(g * LANES, (g + 1) * LANES)
        pay_ref[:, cols] = pay[g].astype(BF16)


def local_kernel(q_ref, u_ref, taps_ref, rates_ref, res_ref, skip_ref, local_ref, qc_ref, y_ref, xs):
    tile = q_ref.shape[1]
    for g in range(tile // LANES):
        cols = slice(g * LANES, (g + 1) * LANES)
        taps = [taps_ref[0, j : j + 1, cols] for j in range(REACH + 1)]
        for i in range(2):
            base = i * (STRETCH + 8) + 8
            xs[g, base - 8 : base, :] = jnp.zeros((8, LANES), F32)
            xs[g, base : base + STRETCH, :] = q_ref[i * STRETCH : (i + 1) * STRETCH, cols].astype(F32)
            for b in range(STRETCH // 8):
                at = base + 8 * b
                total = taps[0] * xs[g, at : at + 8, :]
                for j in range(1, REACH + 1):
                    total = total + taps[j] * xs[g, at - j : at - j + 8, :]
                if b == 0:
                    row = lax.broadcasted_iota(jnp.int32, (8, LANES), 0)
                    total = jnp.where(row >= REACH, total, 1.0)
                qc_ref[i * STRETCH + 8 * b : i * STRETCH + 8 * b + 8, cols] = total
    rate = rates_ref[...]
    amount = amplitude(rate, res_ref[...])
    weights = [jnp.sum(amount * jnp.exp(-rate * float(n)), axis=0, keepdims=True) for n in NODES]
    for i in range(2):
        rows = slice(i * STRETCH, (i + 1) * STRETCH)
        high, low = u_ref[0, rows, :], u_ref[1, rows, :]
        parts = jnp.dot(
            local_ref[...], jnp.concatenate([high, low, high], axis=0), preferred_element_type=F32
        )
        total = skip_ref[...] * (high.astype(F32) + low.astype(F32))
        for j in range(RANK):
            total = total + weights[j] * parts[j * STRETCH : (j + 1) * STRETCH, :]
        y_ref[rows, :] = total


def middle_kernel(
    me_ref, perm_ref, x_ref, taps_ref, rates_ref, res_ref, skip_ref, out_ref,
    raw, ext, moments, heads, inject, states, mids, carried, result,
):
    slots = perm_ref.shape[0]
    width = x_ref.shape[2]
    groups = width // LANES

    ext[:, :, 0, :, :] = jnp.zeros((3, groups, 16, LANES), F32)
    ext[:, :, :, 8:16, :] = jnp.zeros((3, groups, slots + 1, 8, LANES), F32)
    heads[:, :, 0:8, :] = jnp.zeros((groups, slots, 8, LANES), F32)

    def unpack(src, carry):
        for g in range(groups):
            raw[g] = x_ref[src, :, g * LANES : (g + 1) * LANES].astype(F32)
        for i in range(2):
            n = perm_ref[2 * src + i]
            for g in range(groups):
                for a in range(3):
                    at = i * PIECE + a * REACH
                    ext[a, g, n + 1, 0:REACH, :] = raw[g, at : at + REACH, :]
                    at = i * PIECE + (3 + a) * REACH
                    ext[a, g, n, REACH : 2 * REACH, :] = raw[g, at : at + REACH, :]
                at = i * PIECE + 6 * REACH
                moments[g, n, 0:RANK, :] = raw[g, at : at + RANK, :] + raw[g, at + RANK : at + 2 * RANK, :]
        return carry

    lax.fori_loop(0, slots // 2, unpack, 0)

    row = lax.broadcasted_iota(jnp.int32, (8, LANES), 0)
    rate = [rates_ref[:, g * LANES : (g + 1) * LANES] for g in range(groups)]
    amount = [amplitude(rate[g], res_ref[:, g * LANES : (g + 1) * LANES]) for g in range(groups)]

    for g in range(groups):
        cols = slice(g * LANES, (g + 1) * LANES)
        enter = [jnp.exp(-rate[g] * float(REACH - 1 - s)) for s in range(REACH)]
        gather = [jnp.exp(-rate[g] * float(n)) for n in NODES]
        taps = [[taps_ref[a, j : j + 1, cols] for j in range(REACH + 1)] for a in range(3)]

        def head_pass(n, carry, g=g, taps=taps, enter=enter, gather=gather):
            feats = []
            for a in range(3):
                total = taps[a][0] * ext[a, g, n, REACH : REACH + 8, :]
                for j in range(1, REACH + 1):
                    total = total + taps[a][j] * ext[a, g, n, REACH - j : REACH - j + 8, :]
                feats.append(jnp.where(row < REACH, total, 0.0))
            mixed = feats[1] * feats[2]
            heads[g, n, 8:16, :] = mixed
            carried[g, n, 0:8, :] = feats[0]
            first = enter[0] * mixed[0:1, :]
            for s in range(1, REACH):
                first = first + enter[s] * mixed[s : s + 1, :]
            second = gather[0] * moments[g, n, 0:1, :]
            for j in range(1, RANK):
                second = second + gather[j] * moments[g, n, j : j + 1, :]
            inject[g, n, 0:16, :] = first
            inject[g, n, 16:32, :] = second
            return carry

        lax.fori_loop(0, slots, head_pass, 0, unroll=2)

    fade_head = [jnp.exp(-rate[g] * float(REACH)) for g in range(groups)]
    fade_rest = [jnp.exp(-rate[g] * float(INNER)) for g in range(groups)]

    def scan_pass(n, state):
        after = []
        for g in range(groups):
            states[g, n] = state[g]
            mid = fade_head[g] * state[g] + inject[g, n, 0:16, :]
            mids[g, n] = mid
            after.append(fade_rest[g] * mid + inject[g, n, 16:32, :])
        return tuple(after)

    lax.fori_loop(0, slots, scan_pass, tuple(jnp.zeros((16, LANES), F32) for _ in range(groups)), unroll=4)

    for g in range(groups):
        cols = slice(g * LANES, (g + 1) * LANES)
        taps = [jnp.sum(amount[g] * jnp.exp(-rate[g] * float(d)), axis=0, keepdims=True) for d in range(REACH)]
        taps[0] = taps[0] + skip_ref[:, cols]
        lifts = [amount[g] * jnp.exp(-rate[g] * float(t + 1)) for t in range(REACH)]
        spread = [amount[g] * jnp.exp(-rate[g] * float(n + 1)) for n in NODES]

        def out_pass(n, carry, g=g, taps=taps, lifts=lifts, spread=spread):
            state, mid = states[g, n], mids[g, n]
            total = taps[0] * heads[g, n, 8:16, :]
            for d in range(1, REACH):
                total = total + taps[d] * heads[g, n, 8 - d : 16 - d, :]
            for t in range(REACH):
                carried[g, n, 8 + t : 9 + t, :] = jnp.sum(lifts[t] * state, axis=0, keepdims=True)
                carried[g, n, 16 + t : 17 + t, :] = jnp.sum(spread[t] * mid, axis=0, keepdims=True)
            z = carried[g, n, 0:8, :] * (total + carried[g, n, 8:16, :])
            high, low = split(z)
            result[g, n, 0:REACH, :] = high.astype(F32)[:REACH]
            result[g, n, REACH : 2 * REACH, :] = low.astype(F32)[:REACH]
            high, low = split(carried[g, n, 16:24, :])
            result[g, n, 2 * REACH : 2 * REACH + RANK, :] = high.astype(F32)[:RANK]
            result[g, n, 2 * REACH + RANK : BACK, :] = low.astype(F32)[:RANK]
            return carry

        lax.fori_loop(0, slots, out_pass, 0, unroll=2)

    def pack(src, carry):
        for g in range(groups):
            both = [result[g, perm_ref[2 * src + i], :, :] for i in range(2)]
            out_ref[src, :, g * LANES : (g + 1) * LANES] = jnp.concatenate(both, axis=0).astype(BF16)
        return carry

    lax.fori_loop(0, slots // 2, pack, 0)


def join_kernel(back_ref, lift_ref, qc_ref, y_ref, z_ref, sq_ref, total):
    step = pl.program_id(0)
    back = back_ref[...]
    carry = jnp.dot(lift_ref[...], jnp.concatenate([back, back], axis=0), preferred_element_type=F32)
    z = qc_ref[...] * (y_ref[...] + carry)
    z_ref[...] = z
    squares = z * z
    part = squares[:, :LANES]
    for g in range(1, z.shape[1] // LANES):
        part = part + squares[:, g * LANES : (g + 1) * LANES]

    @pl.when(step == 0)
    def _():
        total[...] = part

    @pl.when(step > 0)
    def _():
        total[...] += part

    @pl.when(step == pl.num_programs(0) - 1)
    def _():
        sq_ref[...] = jnp.sum(total[...], axis=1, keepdims=True)


PARAMS = pltpu.CompilerParams(vmem_limit_bytes=48 * 1024 * 1024)


def on_device(sizes, q_in, k_in, v_in, stretch_of_slot, short_weight, rates, residues, skip, gain):
    n_ctx, n_ch = sizes
    tokens, width = q_in.shape
    slots = stretch_of_slot.shape[0]
    order = rates.shape[0]
    share = width // n_ctx
    direct = share % LANES == 0
    tile = share if direct else 2 * LANES
    steps = width // tile
    ends_np, local_np, lift_np = constant_matrices()
    ends, local, lift = jnp.asarray(ends_np), jnp.asarray(local_np), jnp.asarray(lift_np)
    skip, gain = skip.reshape(1, width), gain.reshape(1, width)
    me = lax.axis_index("ctx").astype(jnp.int32).reshape(1)

    def whole(array):
        return pl.BlockSpec(array.shape, lambda c: (0,) * array.ndim)

    def columns(*lead):
        return pl.BlockSpec((*lead, tile), lambda c: (0,) * len(lead) + (c,))

    def payload(rows):
        if direct:
            return (
                jax.ShapeDtypeStruct((n_ctx, rows, share), BF16),
                pl.BlockSpec((None, rows, share), lambda c: (c, 0, 0)),
            )
        return jax.ShapeDtypeStruct((rows, width), BF16), columns(rows)

    groups = tile // LANES
    pay_shape, pay_spec = payload(2 * PIECE)
    pay, mixed = pl.pallas_call(
        gather_kernel,
        grid=(steps,),
        in_specs=[columns(tokens)] * 3 + [columns(3, REACH + 1), whole(ends)],
        out_specs=[pay_spec, columns(2, tokens)],
        out_shape=[pay_shape, jax.ShapeDtypeStruct((2, tokens, width), BF16)],
        scratch_shapes=[
            pltpu.VMEM((3, groups, 2 * (STRETCH + 8), LANES), F32),
            pltpu.VMEM((groups, 2 * PIECE, LANES), F32),
        ],
        compiler_params=PARAMS,
        name="gather_pieces",
    )(q_in, k_in, v_in, short_weight, ends)
    if not direct:
        pay = pay.reshape(2 * PIECE, n_ctx, share).transpose(1, 0, 2)
    arrived = lax.all_to_all(pay, "ctx", 0, 0, tiled=True)

    query, inner = pl.pallas_call(
        local_kernel,
        grid=(steps,),
        in_specs=[
            columns(tokens),
            columns(2, tokens),
            columns(3, REACH + 1),
            columns(order),
            columns(order),
            columns(1),
            whole(local),
        ],
        out_specs=[columns(tokens)] * 2,
        out_shape=[jax.ShapeDtypeStruct((tokens, width), F32)] * 2,
        scratch_shapes=[pltpu.VMEM((groups, 2 * (STRETCH + 8), LANES), F32)],
        compiler_params=PARAMS,
        name="local_filter",
        cost_estimate=pl.CostEstimate(flops=10**10, bytes_accessed=8 * 10**6, transcendentals=0),
    )(q_in, mixed, short_weight, rates, residues, skip, local)

    if direct:
        mine = (short_weight, rates, residues, skip)
        lanes = share

        def own(*lead):
            return pl.BlockSpec((*lead, share), lambda c, me_ref, perm_ref: (0,) * len(lead) + (me_ref[0],))

    else:
        lanes = -(-share // LANES) * LANES

        def widen(array, fill=0.0):
            pad = [(0, 0)] * (array.ndim - 1) + [(0, lanes - share)]
            return jnp.pad(array, pad, constant_values=fill)

        def cut(array, fill=0.0):
            return widen(
                lax.dynamic_slice_in_dim(array, lax.axis_index("ctx") * share, share, array.ndim - 1), fill
            )

        mine = (cut(short_weight), cut(rates, 0.01), cut(residues), cut(skip))
        arrived = widen(arrived)

        def own(*lead):
            return pl.BlockSpec((*lead, lanes), lambda c, me_ref, perm_ref: (0,) * (len(lead) + 1))

    groups = lanes // LANES
    back = pl.pallas_call(
        middle_kernel,
        grid_spec=pltpu.PrefetchScalarGridSpec(
            num_scalar_prefetch=2,
            grid=(1,),
            in_specs=[
                pl.BlockSpec((n_ctx, 2 * PIECE, lanes), lambda c, me_ref, perm_ref: (0, 0, 0)),
                own(3, REACH + 1),
                own(order),
                own(order),
                own(1),
            ],
            out_specs=pl.BlockSpec((n_ctx, 2 * BACK, lanes), lambda c, me_ref, perm_ref: (0, 0, 0)),
            scratch_shapes=[
                pltpu.VMEM((groups, 2 * PIECE, LANES), F32),
                pltpu.VMEM((3, groups, slots + 1, 16, LANES), F32),
                pltpu.VMEM((groups, slots, 8, LANES), F32),
                pltpu.VMEM((groups, slots, 16, LANES), F32),
                pltpu.VMEM((groups, slots, 2 * order, LANES), F32),
                pltpu.VMEM((groups, slots, order, LANES), F32),
                pltpu.VMEM((groups, slots, order, LANES), F32),
                pltpu.VMEM((groups, slots, 24, LANES), F32),
                pltpu.VMEM((groups, slots, BACK, LANES), F32),
            ],
        ),
        out_shape=jax.ShapeDtypeStruct((n_ctx, 2 * BACK, lanes), BF16),
        compiler_params=PARAMS,
        name="carry_states",
    )(me, stretch_of_slot, arrived, *mine)
    if not direct:
        back = back[:, :, :share]
    back = lax.all_to_all(back, "ctx", 0, 0, tiled=True)
    if not direct:
        back = back.transpose(1, 0, 2).reshape(2 * BACK, width)

    _, back_spec = payload(2 * BACK)
    zvalues, squares = pl.pallas_call(
        join_kernel,
        grid=(steps,),
        in_specs=[back_spec, whole(lift), columns(tokens), columns(tokens)],
        out_specs=[columns(tokens), pl.BlockSpec((tokens, 1), lambda c: (0, 0))],
        out_shape=[
            jax.ShapeDtypeStruct((tokens, width), F32),
            jax.ShapeDtypeStruct((tokens, 1), F32),
        ],
        scratch_shapes=[pltpu.VMEM((tokens, LANES), F32)],
        compiler_params=PARAMS,
        name="join_carry",
    )(back, lift, query, inner)
    total = squares
    for shift in range(1, n_ch):
        total = total + lax.ppermute(squares, "ch", [(i, (i + shift) % n_ch) for i in range(n_ch)])
    scale = lax.rsqrt(total / (width * n_ch) + 1e-05)
    return (zvalues * scale * gain).astype(BF16)


def solution(mesh):
    sizes = (mesh.shape["ctx"], mesh.shape["ch"])
    in_specs = (
        P("ctx", "ch"),
        P("ctx", "ch"),
        P("ctx", "ch"),
        P(),
        P(None, None, "ch"),
        P(None, "ch"),
        P(None, "ch"),
        P("ch"),
        P("ch"),
    )

    def run(*arrays):
        return on_device(sizes, *arrays)

    return jax.shard_map(run, mesh=mesh, in_specs=in_specs, out_specs=P("ctx", "ch"), check_vma=False)
```

time: 788 us -> 80.3 us (0.10)
  local copies, waits for them, and re-layouts: 431 us -> 7.54 us
  other arithmetic: 180 us -> 1.36 us
  waiting for transfers between devices: 135 us -> 21.6 us
  Pallas kernels: 0 us -> 34.3 us
  starting transfers between devices: 0.04 us -> 14.4 us
  between operations: 13.5 us -> 0.1 us
  loops' own time: 8.14 us -> 0 us
  matrix products: 8.06 us -> 0 us
    slice x289 -> x0, local copies, waits for them, and re-layouts: 250 us -> none  [the longest x288 250 us: mode_pass(): lax.associative_scan(decay_combine, (factors, mixed_in), axis=1)[1]]
    all_gather x2 -> x0, waiting for transfers between devices: 135 us -> none  [the longest x1 73.6 us: on_device(): pieces = lax.all_gather(ends, 'ctx', axis=0, tiled=True)]
    pad x160 -> x0, local copies, waits for them, and re-layouts: 127 us -> none  [mode_pass(): lax.associative_scan(decay_combine, (factors, mixed_in), axis=1)[1]]
    add x289 -> x0, other arithmetic: 112 us -> none  [the longest x16 63.1 us: mode_pass(): local_conv = local_conv + amount[None, None, :] * running]
    pallas_call x0 -> x4, Pallas kernels: none -> 34.3 us  [the longest x1 11.7 us: on_device(): pl.pallas_call(local_kernel, grid=(steps,), in_specs=[columns(tokens), co...]
    dynamic_update_slice x18 -> x0, local copies, waits for them, and re-layouts: 29.7 us -> none  [the longest x16 28.2 us: mode_pass(): lax.dynamic_update_index_in_dim(ends, running[:, stretch - 1:stretch, :],...]
    all_to_all x0 -> x2, waiting for transfers between devices: none -> 18.7 us  [the longest x1 18.7 us: on_device(): arrived = lax.all_to_all(pay, 'ctx', 0, 0, tiled=True)]
    neg x17 -> x0, other arithmetic: 17.8 us -> none  [the longest x16 16 us: carry_pass(): lifted = jnp.exp(-rate[None, :] * (positions[:, None] + 1.0))]
  transfers between devices with their start and end apart: 2 -> 3, of which waited for: 2 -> 2; matrix products, arithmetic and copies ran while one was open for 0% -> 0% of each run, Pallas kernels for 0% -> 15%
where the time goes in v1:
time: 80.3 us; the launch traced here: 79.3 us
  Pallas kernels  34.3 us (43%)
  waiting for transfers between devices  21.6 us (27%)
  starting transfers between devices  14.4 us (18%)
  local copies, waits for them, and re-layouts  7.54 us (9%)
  other arithmetic  1.36 us (2%)
    all_to_all x1, waiting for transfers between devices, on_device(): arrived = lax.all_to_all(pay, 'ctx', 0, 0, tiled=True)  18.7 us
    pallas_call x1, Pallas kernels, on_device(): pl.pallas_call(local_kernel, grid=(steps,), in_specs=[columns(tokens), co...  11.7 us
    pallas_call x1, Pallas kernels, on_device(): pl.pallas_call(join_kernel, grid=(steps,), in_specs=[back_spec, whole(lif...  9.18 us
    pallas_call x1, Pallas kernels, on_device(): pl.pallas_call(gather_kernel, grid=(steps,), in_specs=[columns(tokens)] *...  8.4 us
    unnamed x28, local copies, waits for them, and re-layouts  7.54 us
    all_to_all x1, starting transfers between devices, on_device(): arrived = lax.all_to_all(pay, 'ctx', 0, 0, tiled=True)  7.36 us
    all_to_all x1, starting transfers between devices, on_device(): back = lax.all_to_all(back, 'ctx', 0, 0, tiled=True)  5.47 us
    pallas_call x1, Pallas kernels, on_device(): pl.pallas_call(middle_kernel, grid_spec=pltpu.PrefetchScalarGridSpec(num_...  5 us
  transfers between devices with their start and end apart: 3, of which 2 were waited for; matrix products, arithmetic and copies ran while one was open for 0% of the time, Pallas kernels for 15%

profile of v1, /device:TPU:0, one launch (start us, length us, event | category | flops | bytes accessed | tf_op | source)
XLA Modules:
  0.0 79.3 jit_solution(3376265926162930298)
XLA Ops:
  0.0 1.0 %copy-done = f32[3,7,4096]{2,1,0:T(8,128)S(1)} copy-done((f32[3,7,4096]{2,1,0:T(8,128)S(1)}, f32[3,7,4096]{2,1,0:T(8,128)}, u32[]{:S(2)}) %copy-start) | copy-done | bytes 344088
  1.0 1.2 %copy-done.2 = bf16[128,4096]{1,0:T(8,128)(2,1)S(1)} copy-done((bf16[128,4096]{1,0:T(8,128)(2,1)S(1)}, bf16[128,4096]{1,0:T(8,128)(2,1)}, u32[]{:S(2)}) %copy-start.2) | copy-done | bytes 1048600
  2.2 1.2 %copy-done.3 = bf16[128,4096]{1,0:T(8,128)(2,1)S(1)} copy-done((bf16[128,4096]{1,0:T(8,128)(2,1)S(1)}, bf16[128,4096]{1,0:T(8,128)(2,1)}, u32[]{:S(2)}) %copy-start.3) | copy-done | bytes 1048600
  3.4 1.2 %copy-done.4 = bf16[128,4096]{1,0:T(8,128)(2,1)S(1)} copy-done((bf16[128,4096]{1,0:T(8,128)(2,1)S(1)}, bf16[128,4096]{1,0:T(8,128)(2,1)}, u32[]{:S(2)}) %copy-start.4) | copy-done | bytes 1048600
  4.7 0.7 copy-done.10
  5.4 0.0 copy-start.11
  5.4 8.4 %gather_pieces.1 = (bf16[16,96,256]{2,1,0:T(8,128)(2,1)}, bf16[2,128,4096]{2,1,0:T(8,128)(2,1)}) custom-call(bf16[128,4096]{1,0:T(8,128)(2,1)S(1)} %copy-done.4, bf16[128,4096]{1,0:T(8,128)(2,1)S(1)} %copy-done.2, bf16[128,4096]{1,0:T(8,128)(2,1)S(1)} %copy-done.3, f32[3,7,4096]{2,1,0:T(8,128)S(1)} %copy-done, bf16[16,192]{1,0:T(8,128)(2,1)S(1)} %copy-done.10), custom_call_target="tpu_custom_call" | custom-call | tf_op jit(solution)/shard_map/gather_pieces/pallas_call | solution.py:345
  13.8 7.4 %all-to-all-start = ((bf16[16,96,256]{2,1,0:T(8,128)(2,1)}), bf16[16,96,256]{2,1,0:T(8,128)(2,1)S(1)}, u32[]{:S(2)}, u32[]{:S(2)}) async-start(bf16[16,96,256]{2,1,0:T(8,128)(2,1)} %get-tuple-element.11), calls=%async_computation | async-start | bytes 1572864 | tf_op jit(solution)/shard_map/all_to_all | solution.py:360
  21.2 18.7 %all-to-all-done.x_ref = bf16[16,96,256]{2,1,0:T(8,128)(2,1)S(1)} async-done(((bf16[16,96,256]{2,1,0:T(8,128)(2,1)}), bf16[16,96,256]{2,1,0:T(8,128)(2,1)S(1)}, u32[]{:S(2)}, u32[]{:S(2)}) %all-to-all-start) | async-done | bytes 786464 | tf_op jit(solution)/shard_map/all_to_all | solution.py:360
  39.9 0.0 copy-done.9
  39.9 0.0 copy-done.11
  39.9 5.0 %carry_states.1 = bf16[16,48,256]{2,1,0:T(8,128)(2,1)} custom-call(s32[1]{0:T(128)} %bitcast.me_ref, s32[32]{0:T(128)S(1)} %copy-done.11, bf16[16,96,256]{2,1,0:T(8,128)(2,1)S(1)} %all-to-all-done.x_ref, f32[3,7,4096]{2,1,0:T(8,128)S(1)} %copy-done.1, f32[16,4096]{1,0:T(8,128)S(1)} %copy-done.6, f32[16,4096]{1,0:T(8,128)S(1)} %copy-done.7, f32[1,4096]{1,0:T(1,128)S(1)} %bitcast.2), custom_call_target="tpu_custom_call" | custom-call | tf_op jit(solution)/shard_map/carry_states/pallas_call | solution.py:408
  44.9 5.5 %all-to-all-start.1 = ((bf16[16,48,256]{2,1,0:T(8,128)(2,1)}), bf16[16,48,256]{2,1,0:T(8,128)(2,1)S(1)}, u32[]{:S(2)}, u32[]{:S(2)}) async-start(bf16[16,48,256]{2,1,0:T(8,128)(2,1)} %carry_states.1), calls=%async_computation.1 | async-start | bytes 786432 | tf_op jit(solution)/shard_map/all_to_all | solution.py:439
  50.4 0.0 copy-start.5
  50.4 1.2 %copy-done.5 = bf16[128,4096]{1,0:T(8,128)(2,1)S(1)} copy-done((bf16[128,4096]{1,0:T(8,128)(2,1)S(1)}, bf16[128,4096]{1,0:T(8,128)(2,1)}, u32[]{:S(2)}) %copy-start.5) | copy-done | bytes 1048600
  51.6 0.9 %copy-done.12 = bf16[384,192]{1,0:T(8,128)(2,1)S(1)} copy-done((bf16[384,192]{1,0:T(8,128)(2,1)S(1)}, bf16[384,192]{1,0:T(8,128)(2,1)}, u32[]{:S(2)}) %copy-start.12) | copy-done | bytes 147480
  52.5 11.7 %local_filter.1 = (f32[128,4096]{1,0:T(8,128)S(1)}, f32[128,4096]{1,0:T(8,128)}) custom-call(bf16[128,4096]{1,0:T(8,128)(2,1)S(1)} %copy-done.5, bf16[2,128,4096]{2,1,0:T(8,128)(2,1)} %get-tuple-element.12.u_ref, f32[3,7,4096]{2,1,0:T(8,128)S(1)} %copy-done.1, f32[16,4096]{1,0:T(8,128)S(1)} %copy-done.6, f32[16,4096]{1,0:T(8,128)S(1)} %copy-done.7, ...), custom_call_target="tpu_custom_call" | custom-call | flops 10000000000 | bytes 8000000 | tf_op jit(solution)/shard_map/local_filter/pallas_call | solution.py:362
  64.3 0.0 all-to-all-done.1.back_ref
  64.3 0.0 copy-done.8
  64.3 9.2 %join_carry.1 = (f32[128,4096]{1,0:T(8,128)S(1)}, f32[128,1]{1,0:T(8,128)S(1)}) custom-call(bf16[16,48,256]{2,1,0:T(8,128)(2,1)S(1)} %all-to-all-done.1.back_ref, bf16[128,96]{1,0:T(8,128)(2,1)S(1)} %copy-done.8, f32[128,4096]{1,0:T(8,128)S(1)} %get-tuple-element.13.qc_ref, f32[128,4096]{1,0:T(8,128)} %get-tuple-element.14.y_ref), custom_call_target="tpu_custom_call" | custom-call | tf_op jit(solution)/shard_map/join_carry/pallas_call | solution.py:444
  73.5 1.6 %collective-permute-start = (f32[128,1]{1,0:T(8,128)S(1)}, f32[128,1]{1,0:T(8,128)S(1)}, u32[]{:S(2)}, u32[]{:S(2)}) collective-permute-start(f32[128,1]{1,0:T(8,128)S(1)} %get-tuple-element.16), channel_id=1, source_target_pairs={{0,1},{1,0},{2,3},{3,2},{4,5},{5,4},{6,7},{7,6},{8,9},{9,8},{10,11... | collective-permute-start | bytes 1544 | tf_op jit(solution)/shard_map/ppermute | solution.py:459
  75.0 2.9 %collective-permute-done = f32[128,1]{1,0:T(8,128)S(1)} collective-permute-done((f32[128,1]{1,0:T(8,128)S(1)}, f32[128,1]{1,0:T(8,128)S(1)}, u32[]{:S(2)}, u32[]{:S(2)}) %collective-permute-start) | collective-permute-done | bytes 544 | tf_op jit(solution)/shard_map/ppermute | solution.py:459
  78.0 0.1 rsqrt_reduce_fusion
  78.1 1.3 %multiply_convert_fusion = bf16[128,4096]{1,0:T(8,128)(2,1)} fusion(f32[128,4096]{1,0:T(8,128)S(1)} %get-tuple-element.15, f32[4096]{0:T(1024)S(1)} %copy-done.13, f32[128]{0:T(128)S(1)} %rsqrt_reduce_fusion), kind=kLoop, calls=%fused_computation | loop fusion | flops 1572864 | bytes 3162624 | tf_op jit(solution)/shard_map/convert_element_type | solution.py:461
  (16 shorter events, 0.0 us)
Async XLA Ops:
  0.0 1.0 %copy-start = (f32[3,7,4096]{2,1,0:T(8,128)S(1)}, f32[3,7,4096]{2,1,0:T(8,128)}, u32[]{:S(2)}) copy-start(f32[3,7,4096]{2,1,0:T(8,128)} %taps_ref.5) | copy-start | bytes 1032196
  1.0 1.2 %copy-start.2 = (bf16[128,4096]{1,0:T(8,128)(2,1)S(1)}, bf16[128,4096]{1,0:T(8,128)(2,1)}, u32[]{:S(2)}) copy-start(bf16[128,4096]{1,0:T(8,128)(2,1)} %k_ref.1) | copy-start | bytes 3145732
  2.2 1.2 %copy-start.3 = (bf16[128,4096]{1,0:T(8,128)(2,1)S(1)}, bf16[128,4096]{1,0:T(8,128)(2,1)}, u32[]{:S(2)}) copy-start(bf16[128,4096]{1,0:T(8,128)(2,1)} %v_ref.1) | copy-start | bytes 3145732
  3.4 1.2 %copy-start.4 = (bf16[128,4096]{1,0:T(8,128)(2,1)S(1)}, bf16[128,4096]{1,0:T(8,128)(2,1)}, u32[]{:S(2)}) copy-start(bf16[128,4096]{1,0:T(8,128)(2,1)} %q_ref.3) | copy-start | bytes 3145732
  4.7 0.7 copy-start.10
  5.4 34.5 %copy-start.1 = (f32[3,7,4096]{2,1,0:T(8,128)S(1)}, f32[3,7,4096]{2,1,0:T(8,128)}, u32[]{:S(2)}) copy-start(f32[3,7,4096]{2,1,0:T(8,128)} %taps_ref.5) | copy-start | bytes 1032196
  5.4 34.5 %copy-start.6 = (f32[16,4096]{1,0:T(8,128)S(1)}, f32[16,4096]{1,0:T(8,128)}, u32[]{:S(2)}) copy-start(f32[16,4096]{1,0:T(8,128)} %rates_ref.3) | copy-start | bytes 786436
  5.4 34.5 %copy-start.7 = (f32[16,4096]{1,0:T(8,128)S(1)}, f32[16,4096]{1,0:T(8,128)}, u32[]{:S(2)}) copy-start(f32[16,4096]{1,0:T(8,128)} %res_ref.3) | copy-start | bytes 786436
  5.4 34.5 %copy-start.9 = (f32[4096]{0:T(1024)S(1)}, f32[4096]{0:T(1024)}, u32[]{:S(2)}) copy-start(f32[4096]{0:T(1024)} %param.19) | copy-start | bytes 49156
  5.4 34.5 %copy-start.11 = (s32[32]{0:T(128)S(1)}, s32[32]{0:T(128)}, u32[]{:S(2)}) copy-start(s32[32]{0:T(128)} %perm_ref.1) | copy-start | bytes 388
  13.8 26.1 %all-to-all-start = ((bf16[16,96,256]{2,1,0:T(8,128)(2,1)}), bf16[16,96,256]{2,1,0:T(8,128)(2,1)S(1)}, u32[]{:S(2)}, u32[]{:S(2)}) async-start(bf16[16,96,256]{2,1,0:T(8,128)(2,1)} %get-tuple-element.11), calls=%async_computation | async-start | bytes 1572864 | tf_op jit(solution)/shard_map/all_to_all | solution.py:360
  44.9 19.4 %all-to-all-start.1 = ((bf16[16,48,256]{2,1,0:T(8,128)(2,1)}), bf16[16,48,256]{2,1,0:T(8,128)(2,1)S(1)}, u32[]{:S(2)}, u32[]{:S(2)}) async-start(bf16[16,48,256]{2,1,0:T(8,128)(2,1)} %carry_states.1), calls=%async_computation.1 | async-start | bytes 786432 | tf_op jit(solution)/shard_map/all_to_all | solution.py:439
  50.4 1.2 %copy-start.5 = (bf16[128,4096]{1,0:T(8,128)(2,1)S(1)}, bf16[128,4096]{1,0:T(8,128)(2,1)}, u32[]{:S(2)}) copy-start(bf16[128,4096]{1,0:T(8,128)(2,1)} %q_ref.3) | copy-start | bytes 3145732
  51.6 0.9 %copy-start.12 = (bf16[384,192]{1,0:T(8,128)(2,1)S(1)}, bf16[384,192]{1,0:T(8,128)(2,1)}, u32[]{:S(2)}) copy-start(bf16[384,192]{1,0:T(8,128)(2,1)} %constant.18.clone.local_ref) | copy-start | bytes 442372
  52.5 11.7 %copy-start.8 = (bf16[128,96]{1,0:T(8,128)(2,1)S(1)}, bf16[128,96]{1,0:T(8,128)(2,1)}, u32[]{:S(2)}) copy-start(bf16[128,96]{1,0:T(8,128)(2,1)} %constant.19.clone.lift_ref) | copy-start | bytes 73732
  64.3 13.8 %copy-start.13 = (f32[4096]{0:T(1024)S(1)}, f32[4096]{0:T(1024)}, u32[]{:S(2)}) copy-start(f32[4096]{0:T(1024)} %param.20) | copy-start | bytes 49156
  73.5 4.5 %collective-permute-start = (f32[128,1]{1,0:T(8,128)S(1)}, f32[128,1]{1,0:T(8,128)S(1)}, u32[]{:S(2)}, u32[]{:S(2)}) collective-permute-start(f32[128,1]{1,0:T(8,128)S(1)} %get-tuple-element.16), channel_id=1, source_target_pairs={{0,1},{1,0},{2,3},{3,2},{4,5},{5,4},{6,7},{7,6},{8,9},{9,8},{10,11... | collective-permute-start | bytes 1544 | tf_op jit(solution)/shard_map/ppermute | solution.py:459

commit v2 on v1

v2 whole, which is shorter than its diff:
```python
from decimal import Decimal, getcontext

import jax
import jax.numpy as jnp
import ml_dtypes
import numpy as np
from jax import lax
from jax.experimental import pallas as pl
from jax.experimental.pallas import tpu as pltpu
from jax.sharding import PartitionSpec as P

F32, BF16 = jnp.float32, jnp.bfloat16
LANES = 128
STRETCH = 64
REACH = 6
INNER = STRETCH - REACH
NODES = (1, 8, 21, 36, 49, 56)
ANCHORS = ("0.000511", "0.004393", "0.011118", "0.018882", "0.025607", "0.029489")
RANK = len(NODES)
RAW = 6 * REACH
BACK = 2 * REACH + 2 * RANK


def cardinal_table():
    getcontext().prec = 50
    anchors = [Decimal(a) for a in ANCHORS]
    table = [[(-a * n).exp() for n in NODES] for a in anchors]
    right = [[(-a * d).exp() for d in range(INNER)] for a in anchors]
    for col in range(RANK):
        pivot = max(range(col, RANK), key=lambda row: abs(table[row][col]))
        table[col], table[pivot] = table[pivot], table[col]
        right[col], right[pivot] = right[pivot], right[col]
        for row in range(RANK):
            if row != col:
                factor = table[row][col] / table[col][col]
                table[row] = [x - factor * y for x, y in zip(table[row], table[col])]
                right[row] = [x - factor * y for x, y in zip(right[row], right[col])]
    return np.array([[float(x / table[j][j]) for x in right[j]] for j in range(RANK)], np.float32)


def halves(values):
    high = values.astype(ml_dtypes.bfloat16)
    low = (values - high.astype(np.float32)).astype(ml_dtypes.bfloat16)
    return high, low


def constant_matrices():
    cardinal = cardinal_table()
    ends = np.zeros((16, STRETCH), np.float32)
    local = np.zeros((RANK, STRETCH, STRETCH), np.float32)
    lift = np.zeros((2, 2 * STRETCH, 2 * BACK), np.float32)
    high, low = (h.astype(np.float32) for h in halves(cardinal))
    for j in range(RANK):
        for s in range(REACH, STRETCH):
            ends[j, s] = cardinal[j, STRETCH - 1 - s]
            local[j, s:, s] = cardinal[j, : STRETCH - s]
        for half in range(2):
            rows = slice(half * STRETCH + REACH, (half + 1) * STRETCH)
            at = half * BACK + 2 * REACH
            lift[0, rows, at + j] = high[j]
            lift[0, rows, at + RANK + j] = high[j]
            lift[1, rows, at + j] = low[j]
    for half in range(2):
        for t in range(REACH):
            lift[0, half * STRETCH + t, half * BACK + t] = 1.0
            lift[0, half * STRETCH + t, half * BACK + REACH + t] = 1.0
    local = local.reshape(RANK * STRETCH, STRETCH)

    def triple(m):
        h, l = halves(m)
        return np.concatenate([h, h, l], axis=1)

    lifted = np.concatenate([lift[0], lift[1]], axis=1).astype(ml_dtypes.bfloat16)
    return triple(ends), triple(local), lifted


def split(values):
    high = values.astype(BF16)
    return high, (values - high.astype(F32)).astype(BF16)


def amplitude(rate, residue):
    x = 2.0 * rate
    series = 1.0 - x * (0.5 - x * (1 / 6 - x * (1 / 24 - x * (1 / 120 - x * (1 / 720)))))
    return residue * jnp.sqrt(x * series)


def put(ref, group, values):
    if len(ref.shape) == 3:
        share = ref.shape[2]
        dest, at = divmod(group * LANES, share)
        ref[dest, :, at : at + LANES] = values
    else:
        ref[:, group * LANES : (group + 1) * LANES] = values


def raw_kernel(*refs):
    ins, out_ref, rows, pay = refs[:12], refs[12], refs[13], refs[14]
    for g in range(ins[0].shape[1] // LANES):
        cols = slice(g * LANES, (g + 1) * LANES)
        for a in range(3):
            for i in range(2):
                first, last = ins[4 * a + 2 * i], ins[4 * a + 2 * i + 1]
                rows[g, 2 * a + i, 0:16, :] = first[:, cols].astype(F32)
                rows[g, 2 * a + i, 16:32, :] = last[:, cols].astype(F32)
                at = i * RAW + a * REACH
                pay[g, at : at + REACH, :] = rows[g, 2 * a + i, 32 - REACH : 32, :]
                at = at + 3 * REACH
                pay[g, at : at + REACH, :] = rows[g, 2 * a + i, 0:REACH, :]
        put(out_ref, g, pay[g].astype(BF16))


def gather_kernel(k_ref, v_ref, taps_ref, ends_ref, pay_ref, u_ref, xs, pay):
    tile = k_ref.shape[1]
    groups = tile // LANES
    for g in range(groups):
        cols = slice(g * LANES, (g + 1) * LANES)
        for i in range(2):
            rows = slice(i * STRETCH, (i + 1) * STRETCH)
            for a, ref in enumerate((k_ref, v_ref)):
                base = i * (STRETCH + 8) + 8
                xs[a, g, base - 8 : base, :] = jnp.zeros((8, LANES), F32)
                xs[a, g, base : base + STRETCH, :] = ref[rows, cols].astype(F32)
        taps = [[taps_ref[a, j : j + 1, cols] for j in range(REACH + 1)] for a in (1, 2)]
        for i in range(2):
            for b in range(STRETCH // 16):
                base = i * (STRETCH + 8) + 8 + 16 * b
                both = []
                for a in range(2):
                    total = taps[a][0] * xs[a, g, base : base + 16, :]
                    for j in range(1, REACH + 1):
                        total = total + taps[a][j] * xs[a, g, base - j : base - j + 16, :]
                    both.append(total)
                mixed = both[0] * both[1]
                if b == 0:
                    row = lax.broadcasted_iota(jnp.int32, (16, LANES), 0)
                    mixed = jnp.where(row >= REACH, mixed, 0.0)
                high, low = split(mixed)
                rows = slice(i * STRETCH + 16 * b, i * STRETCH + 16 * b + 16)
                u_ref[0, rows, cols] = high
                u_ref[1, rows, cols] = low
    span = min(tile, 2 * LANES)
    for c in range(tile // span):
        cols = slice(c * span, (c + 1) * span)
        for i in range(2):
            rows = slice(i * STRETCH, (i + 1) * STRETCH)
            high, low = u_ref[0, rows, cols], u_ref[1, rows, cols]
            moments = jnp.dot(
                ends_ref[...], jnp.concatenate([high, low, high], axis=0), preferred_element_type=F32
            )
            top, rest = split(moments)
            for h in range(span // LANES):
                g = c * (span // LANES) + h
                lanes = slice(h * LANES, (h + 1) * LANES)
                at = 2 * RANK * i
                pay[g, at : at + RANK, :] = top.astype(F32)[:RANK, lanes]
                pay[g, at + RANK : at + 2 * RANK, :] = rest.astype(F32)[:RANK, lanes]
    for g in range(groups):
        put(pay_ref, g, pay[g].astype(BF16))


def local_kernel(q_ref, u_ref, taps_ref, rates_ref, res_ref, skip_ref, local_ref, qc_ref, y_ref, xs):
    tile = q_ref.shape[1]
    for g in range(tile // LANES):
        cols = slice(g * LANES, (g + 1) * LANES)
        taps = [taps_ref[0, j : j + 1, cols] for j in range(REACH + 1)]
        for i in range(2):
            base = i * (STRETCH + 8) + 8
            xs[g, base - 8 : base, :] = jnp.zeros((8, LANES), F32)
            xs[g, base : base + STRETCH, :] = q_ref[i * STRETCH : (i + 1) * STRETCH, cols].astype(F32)
            for b in range(STRETCH // 8):
                at = base + 8 * b
                total = taps[0] * xs[g, at : at + 8, :]
                for j in range(1, REACH + 1):
                    total = total + taps[j] * xs[g, at - j : at - j + 8, :]
                if b == 0:
                    row = lax.broadcasted_iota(jnp.int32, (8, LANES), 0)
                    total = jnp.where(row >= REACH, total, 1.0)
                qc_ref[i * STRETCH + 8 * b : i * STRETCH + 8 * b + 8, cols] = total
    span = min(tile, 2 * LANES)
    for c in range(tile // span):
        cols = slice(c * span, (c + 1) * span)
        rate = rates_ref[:, cols]
        amount = amplitude(rate, res_ref[:, cols])
        weights = [jnp.sum(amount * jnp.exp(-rate * float(n)), axis=0, keepdims=True) for n in NODES]
        for i in range(2):
            rows = slice(i * STRETCH, (i + 1) * STRETCH)
            high, low = u_ref[0, rows, cols], u_ref[1, rows, cols]
            parts = jnp.dot(
                local_ref[...], jnp.concatenate([high, low, high], axis=0), preferred_element_type=F32
            )
            total = skip_ref[:, cols] * (high.astype(F32) + low.astype(F32))
            for j in range(RANK):
                total = total + weights[j] * parts[j * STRETCH : (j + 1) * STRETCH, :]
            y_ref[rows, cols] = total


def heads_kernel(
    me_ref, perm_ref, x_ref, taps_ref, rates_ref, res_ref, skip_ref, heads_ref, first_ref, raw, ext, past
):
    slots = perm_ref.shape[0]
    groups = x_ref.shape[2] // LANES
    ext[:, :, 0, :, :] = jnp.zeros((3, groups, 16, LANES), F32)
    ext[:, :, :, 8:16, :] = jnp.zeros((3, groups, slots + 1, 8, LANES), F32)
    past[:, :, 0:8, :] = jnp.zeros((groups, slots, 8, LANES), F32)

    def unpack(src, carry):
        for g in range(groups):
            raw[g] = x_ref[src, :, g * LANES : (g + 1) * LANES].astype(F32)
        for i in range(2):
            n = perm_ref[2 * src + i]
            for g in range(groups):
                for a in range(3):
                    at = i * RAW + a * REACH
                    ext[a, g, n + 1, 0:REACH, :] = raw[g, at : at + REACH, :]
                    at = at + 3 * REACH
                    ext[a, g, n, REACH : 2 * REACH, :] = raw[g, at : at + REACH, :]
        return carry

    lax.fori_loop(0, slots // 2, unpack, 0)
    row = lax.broadcasted_iota(jnp.int32, (8, LANES), 0)

    for g in range(groups):
        cols = slice(g * LANES, (g + 1) * LANES)
        rate = rates_ref[:, cols]
        amount = amplitude(rate, res_ref[:, cols])
        enter = [jnp.exp(-rate * float(REACH - 1 - s)) for s in range(REACH)]
        taps = [[taps_ref[a, j : j + 1, cols] for j in range(REACH + 1)] for a in range(3)]
        near = [jnp.sum(amount * jnp.exp(-rate * float(d)), axis=0, keepdims=True) for d in range(REACH)]
        near[0] = near[0] + skip_ref[:, cols]

        def head_pass(n, carry, g=g, taps=taps, enter=enter, near=near):
            feats = []
            for a in range(3):
                total = taps[a][0] * ext[a, g, n, REACH : REACH + 8, :]
                for j in range(1, REACH + 1):
                    total = total + taps[a][j] * ext[a, g, n, REACH - j : REACH - j + 8, :]
                feats.append(jnp.where(row < REACH, total, 0.0))
            mixed = feats[1] * feats[2]
            past[g, n, 8:16, :] = mixed
            total = near[0] * mixed
            for d in range(1, REACH):
                total = total + near[d] * past[g, n, 8 - d : 16 - d, :]
            heads_ref[g, n, 0:8, :] = feats[0]
            heads_ref[g, n, 8:16, :] = total
            first = enter[0] * mixed[0:1, :]
            for s in range(1, REACH):
                first = first + enter[s] * mixed[s : s + 1, :]
            first_ref[g, n] = first
            return carry

        lax.fori_loop(0, slots, head_pass, 0, unroll=2)


def states_kernel(
    me_ref, perm_ref, x_ref, heads_ref, first_ref, rates_ref, res_ref, out_ref,
    raw, moments, second, states, mids, carried, result,
):
    slots = perm_ref.shape[0]
    groups = x_ref.shape[2] // LANES

    def unpack(src, carry):
        for g in range(groups):
            raw[g] = x_ref[src, :, g * LANES : (g + 1) * LANES].astype(F32)
        for i in range(2):
            n = perm_ref[2 * src + i]
            for g in range(groups):
                at = 2 * RANK * i
                moments[g, n, 0:RANK, :] = raw[g, at : at + RANK, :] + raw[g, at + RANK : at + 2 * RANK, :]
        return carry

    lax.fori_loop(0, slots // 2, unpack, 0)

    rate = [rates_ref[:, g * LANES : (g + 1) * LANES] for g in range(groups)]
    amount = [amplitude(rate[g], res_ref[:, g * LANES : (g + 1) * LANES]) for g in range(groups)]
    for g in range(groups):
        gather = [jnp.exp(-rate[g] * float(n)) for n in NODES]

        def rest_pass(n, carry, g=g, gather=gather):
            total = gather[0] * moments[g, n, 0:1, :]
            for j in range(1, RANK):
                total = total + gather[j] * moments[g, n, j : j + 1, :]
            second[g, n] = total
            return carry

        lax.fori_loop(0, slots, rest_pass, 0, unroll=4)

    fade_head = [jnp.exp(-rate[g] * float(REACH)) for g in range(groups)]
    fade_rest = [jnp.exp(-rate[g] * float(INNER)) for g in range(groups)]

    def scan_pass(n, state):
        after = []
        for g in range(groups):
            states[g, n] = state[g]
            mid = fade_head[g] * state[g] + first_ref[g, n]
            mids[g, n] = mid
            after.append(fade_rest[g] * mid + second[g, n])
        return tuple(after)

    lax.fori_loop(0, slots, scan_pass, tuple(jnp.zeros((16, LANES), F32) for _ in range(groups)), unroll=4)

    for g in range(groups):
        lifts = [amount[g] * jnp.exp(-rate[g] * float(t + 1)) for t in range(REACH)]
        spread = [amount[g] * jnp.exp(-rate[g] * float(n + 1)) for n in NODES]

        def out_pass(n, carry, g=g, lifts=lifts, spread=spread):
            state, mid = states[g, n], mids[g, n]
            for t in range(REACH):
                carried[g, n, t : 1 + t, :] = jnp.sum(lifts[t] * state, axis=0, keepdims=True)
                carried[g, n, 8 + t : 9 + t, :] = jnp.sum(spread[t] * mid, axis=0, keepdims=True)
            z = heads_ref[g, n, 0:8, :] * (heads_ref[g, n, 8:16, :] + carried[g, n, 0:8, :])
            high, low = split(z)
            result[g, n, 0:REACH, :] = high.astype(F32)[:REACH]
            result[g, n, REACH : 2 * REACH, :] = low.astype(F32)[:REACH]
            high, low = split(carried[g, n, 8:16, :])
            result[g, n, 2 * REACH : 2 * REACH + RANK, :] = high.astype(F32)[:RANK]
            result[g, n, 2 * REACH + RANK : BACK, :] = low.astype(F32)[:RANK]
            return carry

        lax.fori_loop(0, slots, out_pass, 0, unroll=2)

    def pack(src, carry):
        for g in range(groups):
            both = [result[g, perm_ref[2 * src + i], :, :] for i in range(2)]
            out_ref[src, :, g * LANES : (g + 1) * LANES] = jnp.concatenate(both, axis=0).astype(BF16)
        return carry

    lax.fori_loop(0, slots // 2, pack, 0)


def join_kernel(back_ref, lift_ref, qc_ref, y_ref, z_ref, sq_ref, total):
    step = pl.program_id(0)
    part = jnp.zeros(total.shape, F32)
    by_dest = len(back_ref.shape) == 3
    span = back_ref.shape[-1] if by_dest else 2 * LANES
    for c in range(qc_ref.shape[1] // span):
        cols = slice(c * span, (c + 1) * span)
        back = back_ref[c] if by_dest else back_ref[:, cols]
        carry = jnp.dot(lift_ref[...], jnp.concatenate([back, back], axis=0), preferred_element_type=F32)
        z = qc_ref[:, cols] * (y_ref[:, cols] + carry)
        z_ref[:, cols] = z
        squares = z * z
        for g in range(span // LANES):
            part = part + squares[:, g * LANES : (g + 1) * LANES]

    @pl.when(step == 0)
    def _():
        total[...] = part

    @pl.when(step > 0)
    def _():
        total[...] += part

    @pl.when(step == pl.num_programs(0) - 1)
    def _():
        sq_ref[...] = jnp.sum(total[...].T, axis=0, keepdims=True)


def limit(mib):
    return pltpu.CompilerParams(vmem_limit_bytes=mib * 1024 * 1024)


def on_device(sizes, q_in, k_in, v_in, stretch_of_slot, short_weight, rates, residues, skip, gain):
    n_ctx, n_ch = sizes
    tokens, width = q_in.shape
    slots = stretch_of_slot.shape[0]
    order = rates.shape[0]
    share = width // n_ctx
    direct = share % LANES == 0
    tile = min(width, 1024)
    steps = width // tile
    groups = tile // LANES
    ends_np, local_np, lift_np = constant_matrices()
    ends, local, lift = jnp.asarray(ends_np), jnp.asarray(local_np), jnp.asarray(lift_np)
    skip, gain = skip.reshape(1, width), gain.reshape(1, width)
    me = lax.axis_index("ctx").astype(jnp.int32).reshape(1)

    def whole(array):
        return pl.BlockSpec(array.shape, lambda c: (0,) * array.ndim)

    def columns(*lead):
        return pl.BlockSpec((*lead, tile), lambda c: (0,) * len(lead) + (c,))

    def payload(rows):
        if direct:
            return (
                jax.ShapeDtypeStruct((n_ctx, rows, share), BF16),
                pl.BlockSpec((tile // share, rows, share), lambda c: (c, 0, 0)),
            )
        return jax.ShapeDtypeStruct((rows, width), BF16), columns(rows)

    def exchange(array):
        if direct:
            return lax.all_to_all(array, "ctx", 0, 0, tiled=True)
        array = array.reshape(array.shape[0], n_ctx, share).transpose(1, 0, 2)
        return widen(lax.all_to_all(array, "ctx", 0, 0, tiled=True))

    lanes = -(-share // LANES) * LANES

    def widen(array, fill=0.0):
        pad = [(0, 0)] * (array.ndim - 1) + [(0, lanes - share)]
        return jnp.pad(array, pad, constant_values=fill)

    if direct:
        mine = (short_weight, rates, residues, skip)

        def own(*lead):
            return pl.BlockSpec((*lead, share), lambda c, me_ref, perm_ref: (0,) * len(lead) + (me_ref[0],))

    else:

        def cut(array, fill=0.0):
            return widen(
                lax.dynamic_slice_in_dim(array, lax.axis_index("ctx") * share, share, array.ndim - 1), fill
            )

        mine = (cut(short_weight), cut(rates, 0.01), cut(residues), cut(skip))

        def own(*lead):
            return pl.BlockSpec((*lead, lanes), lambda c, me_ref, perm_ref: (0,) * (len(lead) + 1))

    def full(*shape):
        return pl.BlockSpec(shape, lambda c, me_ref, perm_ref: (0,) * len(shape))

    raw_shape, raw_spec = payload(2 * RAW)
    edges = [0, STRETCH // 16 - 1, STRETCH // 16, 2 * STRETCH // 16 - 1]
    raw = pl.pallas_call(
        raw_kernel,
        grid=(steps,),
        in_specs=[pl.BlockSpec((16, tile), lambda c, r=r: (r, c)) for _ in range(3) for r in edges],
        out_specs=raw_spec,
        out_shape=raw_shape,
        scratch_shapes=[pltpu.VMEM((groups, 6, 32, LANES), F32), pltpu.VMEM((groups, 2 * RAW, LANES), F32)],
        compiler_params=limit(60),
        name="edge_rows",
    )(*[array for array in (q_in, k_in, v_in) for _ in edges])
    raw = exchange(raw)

    pay_shape, pay_spec = payload(4 * RANK)
    pay, mixed = pl.pallas_call(
        gather_kernel,
        grid=(steps,),
        in_specs=[columns(tokens)] * 2 + [columns(3, REACH + 1), whole(ends)],
        out_specs=[pay_spec, columns(2, tokens)],
        out_shape=[pay_shape, jax.ShapeDtypeStruct((2, tokens, width), BF16)],
        scratch_shapes=[
            pltpu.VMEM((2, groups, 2 * (STRETCH + 8), LANES), F32),
            pltpu.VMEM((groups, 4 * RANK, LANES), F32),
        ],
        compiler_params=limit(60),
        name="gather_moments",
        cost_estimate=pl.CostEstimate(flops=10**9, bytes_accessed=10 * 10**6, transcendentals=0),
    )(k_in, v_in, short_weight, ends)
    pay = exchange(pay)

    query, inner = pl.pallas_call(
        local_kernel,
        grid=(steps,),
        in_specs=[
            columns(tokens),
            columns(2, tokens),
            columns(3, REACH + 1),
            columns(order),
            columns(order),
            columns(1),
            whole(local),
        ],
        out_specs=[columns(tokens)] * 2,
        out_shape=[jax.ShapeDtypeStruct((tokens, width), F32)] * 2,
        scratch_shapes=[pltpu.VMEM((groups, 2 * (STRETCH + 8), LANES), F32)],
        compiler_params=limit(40),
        name="local_filter",
        cost_estimate=pl.CostEstimate(flops=10**9, bytes_accessed=20 * 10**6, transcendentals=0),
    )(q_in, mixed, short_weight, rates, residues, skip, local)
    raw, query, inner = lax.optimization_barrier((raw, query, inner))

    groups = lanes // LANES
    heads, first = pl.pallas_call(
        heads_kernel,
        grid_spec=pltpu.PrefetchScalarGridSpec(
            num_scalar_prefetch=2,
            grid=(1,),
            in_specs=[full(n_ctx, 2 * RAW, lanes), own(3, REACH + 1), own(order), own(order), own(1)],
            out_specs=[full(groups, slots, 16, LANES), full(groups, slots, order, LANES)],
            scratch_shapes=[
                pltpu.VMEM((groups, 2 * RAW, LANES), F32),
                pltpu.VMEM((3, groups, slots + 1, 16, LANES), F32),
                pltpu.VMEM((groups, slots, 16, LANES), F32),
            ],
        ),
        out_shape=[
            jax.ShapeDtypeStruct((groups, slots, 16, LANES), F32),
            jax.ShapeDtypeStruct((groups, slots, order, LANES), F32),
        ],
        compiler_params=limit(32),
        name="head_tokens",
    )(me, stretch_of_slot, raw, *mine)

    back = pl.pallas_call(
        states_kernel,
        grid_spec=pltpu.PrefetchScalarGridSpec(
            num_scalar_prefetch=2,
            grid=(1,),
            in_specs=[
                full(n_ctx, 4 * RANK, lanes),
                full(groups, slots, 16, LANES),
                full(groups, slots, order, LANES),
                own(order),
                own(order),
            ],
            out_specs=full(n_ctx, 2 * BACK, lanes),
            scratch_shapes=[
                pltpu.VMEM((groups, 4 * RANK, LANES), F32),
                pltpu.VMEM((groups, slots, 8, LANES), F32),
                pltpu.VMEM((groups, slots, order, LANES), F32),
                pltpu.VMEM((groups, slots, order, LANES), F32),
                pltpu.VMEM((groups, slots, order, LANES), F32),
                pltpu.VMEM((groups, slots, 16, LANES), F32),
                pltpu.VMEM((groups, slots, BACK, LANES), F32),
            ],
        ),
        out_shape=jax.ShapeDtypeStruct((n_ctx, 2 * BACK, lanes), BF16),
        compiler_params=limit(32),
        name="carry_states",
    )(me, stretch_of_slot, pay, heads, first, mine[1], mine[2])
    if not direct:
        back = back[:, :, :share]
    back = lax.all_to_all(back, "ctx", 0, 0, tiled=True)
    if not direct:
        back = back.transpose(1, 0, 2).reshape(2 * BACK, width)

    _, back_spec = payload(2 * BACK)
    zvalues, squares = pl.pallas_call(
        join_kernel,
        grid=(steps,),
        in_specs=[back_spec, whole(lift), columns(tokens), columns(tokens)],
        out_specs=[columns(tokens), pl.BlockSpec((1, tokens), lambda c: (0, 0))],
        out_shape=[
            jax.ShapeDtypeStruct((tokens, width), F32),
            jax.ShapeDtypeStruct((1, tokens), F32),
        ],
        scratch_shapes=[pltpu.VMEM((tokens, LANES), F32)],
        compiler_params=limit(32),
        name="join_carry",
    )(back, lift, query, inner)
    total = squares
    for shift in range(1, n_ch):
        total = total + lax.ppermute(squares, "ch", [(i, (i + shift) % n_ch) for i in range(n_ch)])
    scale = lax.rsqrt(total / (width * n_ch) + 1e-05)
    return (zvalues * scale.reshape(tokens, 1) * gain).astype(BF16)


def solution(mesh):
    sizes = (mesh.shape["ctx"], mesh.shape["ch"])
    in_specs = (
        P("ctx", "ch"),
        P("ctx", "ch"),
        P("ctx", "ch"),
        P(),
        P(None, None, "ch"),
        P(None, "ch"),
        P(None, "ch"),
        P("ch"),
        P("ch"),
    )

    def run(*arrays):
        return on_device(sizes, *arrays)

    return jax.shard_map(run, mesh=mesh, in_specs=in_specs, out_specs=P("ctx", "ch"), check_vma=False)
```

time: 80.3 us -> 72.7 us (0.905)
  blocking collectives: 0 us -> 18 us
  Pallas kernels: 34.3 us -> 20 us
  waiting for transfers between devices: 21.6 us -> 11.7 us
  starting transfers between devices: 14.4 us -> 13.4 us
    all_to_all x0 -> x1, blocking collectives: none -> 18 us  [on_device(): back = lax.all_to_all(back, 'ctx', 0, 0, tiled=True)]
    all_to_all x2, waiting for transfers between devices: 18.7 us -> 9.65 us  [exchange(): return lax.all_to_all(array, 'ctx', 0, 0, tiled=True)]
    pallas_call x1, Pallas kernels: 11.7 us -> 3.98 us  [on_device(): pl.pallas_call(local_kernel, grid=(steps,), in_specs=[columns(tokens), co...]
    pallas_call x1, Pallas kernels: 9.18 us -> 1.53 us  [on_device(): pl.pallas_call(join_kernel, grid=(steps,), in_specs=[back_spec, whole(lif...]
    pallas_call x1 -> x3, Pallas kernels: 5 us -> 8.67 us  [the longest x1 3.44 us: on_device(): pl.pallas_call(raw_kernel, grid=(steps,), in_specs=[pl.BlockSpec((16, til...]
    pallas_call x1, Pallas kernels: 8.4 us -> 5.82 us  [on_device(): pl.pallas_call(gather_kernel, grid=(steps,), in_specs=[columns(tokens)] *...]
    all_to_all x2, starting transfers between devices: 12.8 us -> 11.8 us  [exchange(): return lax.all_to_all(array, 'ctx', 0, 0, tiled=True)]
    ppermute x1, waiting for transfers between devices: 2.92 us -> 2.02 us  [on_device(): lax.ppermute(squares, 'ch', [(i, (i + shift) % n_ch) for i in range(n_ch)])]
  transfers between devices with their start and end apart: 3 -> 3, of which waited for: 2 -> 2; matrix products, arithmetic and copies ran while one was open for 0% -> 0% of each run, Pallas kernels for 15% -> 17%
where the time goes in v2:
time: 72.7 us; the launch traced here: 71.9 us
  Pallas kernels  20 us (28%)
  blocking collectives  18 us (25%)
  starting transfers between devices  13.4 us (18%)
  waiting for transfers between devices  11.7 us (16%)
  local copies, waits for them, and re-layouts  7.44 us (10%)
  other arithmetic  1.27 us (2%)
    all_to_all x1, blocking collectives, on_device(): back = lax.all_to_all(back, 'ctx', 0, 0, tiled=True)  18 us
    all_to_all x2, starting transfers between devices, exchange(): return lax.all_to_all(array, 'ctx', 0, 0, tiled=True)  11.8 us
    all_to_all x2, waiting for transfers between devices, exchange(): return lax.all_to_all(array, 'ctx', 0, 0, tiled=True)  9.65 us
    unnamed x28, local copies, waits for them, and re-layouts  7.44 us
    pallas_call x1, Pallas kernels, on_device(): pl.pallas_call(gather_kernel, grid=(steps,), in_specs=[columns(tokens)] *...  5.82 us
    pallas_call x1, Pallas kernels, on_device(): pl.pallas_call(local_kernel, grid=(steps,), in_specs=[columns(tokens), co...  3.98 us
    pallas_call x1, Pallas kernels, on_device(): pl.pallas_call(raw_kernel, grid=(steps,), in_specs=[pl.BlockSpec((16, til...  3.44 us
    pallas_call x1, Pallas kernels, on_device(): pl.pallas_call(states_kernel, grid_spec=pltpu.PrefetchScalarGridSpec(num_...  2.99 us
  transfers between devices with their start and end apart: 3, of which 2 were waited for; matrix products, arithmetic and copies ran while one was open for 0% of the time, Pallas kernels for 17%

profile of v2, /device:TPU:0, one launch (start us, length us, event | category | flops | bytes accessed | tf_op | source)
XLA Modules:
  0.0 71.9 jit_solution(8001392783690237192)
XLA Ops:
  0.0 3.4 %edge_rows.1 = bf16[16,72,256]{2,1,0:T(8,128)(2,1)} custom-call(bf16[128,4096]{1,0:T(8,128)(2,1)} %q_ref.1, bf16[128,4096]{1,0:T(8,128)(2,1)} %q_ref.1, bf16[128,4096]{1,0:T(8,128)(2,1)} %q_ref.1, bf16[128,4096]{1,0:T(8,128)(2,1)} %q_ref.1, bf16[128,4096]{1,0:T(8,128)(2,1)} %refs_7_.1, bf16[128,4096]{1,0:T(8,128)(2,1)} %refs_7_.1, ...), custom_call_target="tpu_custom_call" | custom-call | tf_op jit(solution)/shard_map/edge_rows/pallas_call | solution.py:427
  3.4 7.4 %all-to-all-start.1 = ((bf16[16,72,256]{2,1,0:T(8,128)(2,1)}), bf16[16,72,256]{2,1,0:T(8,128)(2,1)S(1)}, u32[]{:S(2)}, u32[]{:S(2)}) async-start(bf16[16,72,256]{2,1,0:T(8,128)(2,1)} %edge_rows.1), calls=%async_computation.1 | async-start | bytes 1179648 | tf_op jit(solution)/shard_map/all_to_all | solution.py:394
  10.8 0.0 copy-start
  10.8 0.0 copy-start.1
  10.8 0.0 copy-start.2
  10.8 0.0 copy-start.8
  10.9 0.0 copy-start.9
  10.9 0.0 copy-start.10
  10.9 5.8 %gather_moments.1 = (bf16[16,24,256]{2,1,0:T(8,128)(2,1)}, bf16[2,128,4096]{2,1,0:T(8,128)(2,1)}) custom-call(bf16[128,4096]{1,0:T(8,128)(2,1)} %refs_7_.1, bf16[128,4096]{1,0:T(8,128)(2,1)} %refs_11_.1, f32[3,7,4096]{2,1,0:T(8,128)} %taps_ref.5, bf16[16,192]{1,0:T(8,128)(2,1)} %constant.17.clone.ends_ref), custom_call_target="tpu_custom_call" | custom-call | flops 1000000000 | bytes 10000000 | tf_op jit(solution)/shard_map/gather_moments/pallas_call | solution.py:440
  16.7 9.7 %all-to-all-done.1.x_ref = bf16[16,72,256]{2,1,0:T(8,128)(2,1)S(1)} async-done(((bf16[16,72,256]{2,1,0:T(8,128)(2,1)}), bf16[16,72,256]{2,1,0:T(8,128)(2,1)S(1)}, u32[]{:S(2)}, u32[]{:S(2)}) %all-to-all-start.1) | async-done | bytes 589856 | tf_op jit(solution)/shard_map/all_to_all | solution.py:394
  26.4 4.4 %all-to-all-start = ((bf16[16,24,256]{2,1,0:T(8,128)(2,1)}), bf16[16,24,256]{2,1,0:T(8,128)(2,1)S(1)}, u32[]{:S(2)}, u32[]{:S(2)}) async-start(bf16[16,24,256]{2,1,0:T(8,128)(2,1)} %get-tuple-element.16), calls=%async_computation | async-start | bytes 393216 | tf_op jit(solution)/shard_map/all_to_all | solution.py:394
  30.9 1.6 %copy-done.3 = bf16[2,128,4096]{2,1,0:T(8,128)(2,1)S(1)} copy-done((bf16[2,128,4096]{2,1,0:T(8,128)(2,1)S(1)}, bf16[2,128,4096]{2,1,0:T(8,128)(2,1)}, u32[]{:S(2)}) %copy-start.3) | copy-done | bytes 2097176
  32.4 4.0 %local_filter.1 = (f32[128,4096]{1,0:T(8,128)S(1)}, f32[128,4096]{1,0:T(8,128)S(1)}) custom-call(bf16[128,4096]{1,0:T(8,128)(2,1)S(1)} %copy-done, bf16[2,128,4096]{2,1,0:T(8,128)(2,1)S(1)} %copy-done.3, f32[3,7,4096]{2,1,0:T(8,128)S(1)} %copy-done.8, f32[16,4096]{1,0:T(8,128)S(1)} %copy-done.1, f32[16,4096]{1,0:T(8,128)S(1)} %copy-done.2, ...), custom_call_target="tpu_custom_call" | custom-call | flops 1000000000 | bytes 20000000 | tf_op jit(solution)/shard_map/local_filter/pallas_call | solution.py:456
  36.4 1.3 %copy-done.4 = f32[128,4096]{1,0:T(8,128)} copy-done((f32[128,4096]{1,0:T(8,128)}, f32[128,4096]{1,0:T(8,128)S(1)}, u32[]{:S(2)}) %copy-start.4) | copy-done | bytes 2097176
  37.8 1.3 %copy-done.6 = f32[128,4096]{1,0:T(8,128)} copy-done((f32[128,4096]{1,0:T(8,128)}, f32[128,4096]{1,0:T(8,128)S(1)}, u32[]{:S(2)}) %copy-start.6) | copy-done | bytes 2097176
  39.1 2.2 %head_tokens.1 = (f32[2,32,16,128]{3,2,1,0:T(8,128)S(1)}, f32[2,32,16,128]{3,2,1,0:T(8,128)S(1)}) custom-call(s32[1]{0:T(128)} %bitcast.me_ref, s32[32]{0:T(128)S(1)} %copy-done.12, bf16[16,72,256]{2,1,0:T(8,128)(2,1)S(1)} %all-to-all-done.1.x_ref, f32[3,7,4096]{2,1,0:T(8,128)S(1)} %copy-done.8, f32[16,4096]{1,0:T(8,128)S(1)} %copy-done.1, ...), custom_call_target="tpu_custom_call" | custom-call | tf_op jit(solution)/shard_map/head_tokens/pallas_call | solution.py:478
  41.3 3.0 %carry_states.1 = bf16[16,48,256]{2,1,0:T(8,128)(2,1)S(1)} custom-call(s32[1]{0:T(128)} %bitcast.me_ref, s32[32]{0:T(128)S(1)} %copy-done.12, bf16[16,24,256]{2,1,0:T(8,128)(2,1)S(1)} %all-to-all-done.x_ref, f32[2,32,16,128]{3,2,1,0:T(8,128)S(1)} %get-tuple-element.21.heads_ref, f32[2,32,16,128]{3,2,1,0:T(8,128)S(1)} %get-tuple-element.22.first_ref, ...), custom_call_target="tpu_custom_call" | custom-call | tf_op jit(solution)/shard_map/carry_states/pallas_call | solution.py:499
  44.3 18.0 %all_to_all.15.back_ref = bf16[16,48,256]{2,1,0:T(8,128)(2,1)S(1)} all-to-all(bf16[16,48,256]{2,1,0:T(8,128)(2,1)S(1)} %carry_states.1), channel_id=1, replica_groups=mesh['ctx'=16,'ch'=2] {'ctx'}, dimensions={0} | all-to-all | bytes 786432 | tf_op jit(solution)/shard_map/all_to_all | solution.py:528
  62.3 1.6 %copy-done.5 = f32[128,4096]{1,0:T(8,128)S(1)} copy-done((f32[128,4096]{1,0:T(8,128)S(1)}, f32[128,4096]{1,0:T(8,128)}, u32[]{:S(2)}) %copy-start.5) | copy-done | bytes 2097176
  63.9 1.6 %copy-done.7 = f32[128,4096]{1,0:T(8,128)S(1)} copy-done((f32[128,4096]{1,0:T(8,128)S(1)}, f32[128,4096]{1,0:T(8,128)}, u32[]{:S(2)}) %copy-start.7) | copy-done | bytes 2097176
  65.5 1.5 %join_carry.1 = (f32[128,4096]{1,0:T(8,128)S(1)}, f32[1,128]{1,0:T(1,128)S(1)}) custom-call(bf16[16,48,256]{2,1,0:T(8,128)(2,1)S(1)} %all_to_all.15.back_ref, bf16[128,96]{1,0:T(8,128)(2,1)S(1)} %copy-done.11, f32[128,4096]{1,0:T(8,128)S(1)} %copy-done.5, f32[128,4096]{1,0:T(8,128)S(1)} %copy-done.7), custom_call_target="tpu_custom_call" | custom-call | tf_op jit(solution)/shard_map/join_carry/pallas_call | solution.py:533
  67.1 1.6 %collective-permute-start = (f32[1,128]{1,0:T(1,128)S(1)}, f32[1,128]{1,0:T(1,128)S(1)}, u32[]{:S(2)}, u32[]{:S(2)}) collective-permute-start(f32[1,128]{1,0:T(1,128)S(1)} %get-tuple-element.26), channel_id=1, source_target_pairs={{0,1},{1,0},{2,3},{3,2},{4,5},{5,4},{6,7},{7,6},{8,9},{9,8},{10,11... | collective-permute-start | bytes 1544 | tf_op jit(solution)/shard_map/ppermute | solution.py:548
  68.6 2.0 %collective-permute-done = f32[1,128]{1,0:T(1,128)S(1)} collective-permute-done((f32[1,128]{1,0:T(1,128)S(1)}, f32[1,128]{1,0:T(1,128)S(1)}, u32[]{:S(2)}, u32[]{:S(2)}) %collective-permute-start) | collective-permute-done | bytes 544 | tf_op jit(solution)/shard_map/ppermute | solution.py:548
  70.7 1.3 %multiply_convert_fusion = bf16[128,4096]{1,0:T(8,128)(2,1)} fusion(f32[128,4096]{1,0:T(8,128)S(1)} %get-tuple-element.25, f32[4096]{0:T(1024)S(1)} %copy-done.13, f32[128]{0:T(128)S(1)} %rsqrt_bitcast_fusion), kind=kLoop, calls=%fused_computation | loop fusion | flops 1572864 | bytes 3162624 | tf_op jit(solution)/shard_map/convert_element_type | solution.py:550
  (19 shorter events, 0.0 us)
Async XLA Ops:
  3.4 22.9 %all-to-all-start.1 = ((bf16[16,72,256]{2,1,0:T(8,128)(2,1)}), bf16[16,72,256]{2,1,0:T(8,128)(2,1)S(1)}, u32[]{:S(2)}, u32[]{:S(2)}) async-start(bf16[16,72,256]{2,1,0:T(8,128)(2,1)} %edge_rows.1), calls=%async_computation.1 | async-start | bytes 1179648 | tf_op jit(solution)/shard_map/all_to_all | solution.py:394
  10.8 20.0 %copy-start = (bf16[128,4096]{1,0:T(8,128)(2,1)S(1)}, bf16[128,4096]{1,0:T(8,128)(2,1)}, u32[]{:S(2)}) copy-start(bf16[128,4096]{1,0:T(8,128)(2,1)} %q_ref.1) | copy-start | bytes 3145732
  10.8 20.0 %copy-start.1 = (f32[16,4096]{1,0:T(8,128)S(1)}, f32[16,4096]{1,0:T(8,128)}, u32[]{:S(2)}) copy-start(f32[16,4096]{1,0:T(8,128)} %rates_ref.5) | copy-start | bytes 786436
  10.8 20.0 %copy-start.2 = (f32[16,4096]{1,0:T(8,128)S(1)}, f32[16,4096]{1,0:T(8,128)}, u32[]{:S(2)}) copy-start(f32[16,4096]{1,0:T(8,128)} %res_ref.5) | copy-start | bytes 786436
  10.8 20.0 %copy-start.8 = (f32[3,7,4096]{2,1,0:T(8,128)S(1)}, f32[3,7,4096]{2,1,0:T(8,128)}, u32[]{:S(2)}) copy-start(f32[3,7,4096]{2,1,0:T(8,128)} %taps_ref.5) | copy-start | bytes 1032196
  10.9 20.0 %copy-start.9 = (bf16[384,192]{1,0:T(8,128)(2,1)S(1)}, bf16[384,192]{1,0:T(8,128)(2,1)}, u32[]{:S(2)}) copy-start(bf16[384,192]{1,0:T(8,128)(2,1)} %constant.18.clone.local_ref) | copy-start | bytes 442372
  10.9 20.0 %copy-start.10 = (f32[4096]{0:T(1024)S(1)}, f32[4096]{0:T(1024)}, u32[]{:S(2)}) copy-start(f32[4096]{0:T(1024)} %param.19) | copy-start | bytes 49156
  26.4 15.0 %all-to-all-start = ((bf16[16,24,256]{2,1,0:T(8,128)(2,1)}), bf16[16,24,256]{2,1,0:T(8,128)(2,1)S(1)}, u32[]{:S(2)}, u32[]{:S(2)}) async-start(bf16[16,24,256]{2,1,0:T(8,128)(2,1)} %get-tuple-element.16), calls=%async_computation | async-start | bytes 393216 | tf_op jit(solution)/shard_map/all_to_all | solution.py:394
  30.9 1.6 %copy-start.3 = (bf16[2,128,4096]{2,1,0:T(8,128)(2,1)S(1)}, bf16[2,128,4096]{2,1,0:T(8,128)(2,1)}, u32[]{:S(2)}) copy-start(bf16[2,128,4096]{2,1,0:T(8,128)(2,1)} %get-tuple-element.17.u_ref) | copy-start | bytes 6291460
  32.4 6.6 %copy-start.12 = (s32[32]{0:T(128)S(1)}, s32[32]{0:T(128)}, u32[]{:S(2)}) copy-start(s32[32]{0:T(128)} %perm_ref.3) | copy-start | bytes 388
  36.4 1.3 %copy-start.4 = (f32[128,4096]{1,0:T(8,128)}, f32[128,4096]{1,0:T(8,128)S(1)}, u32[]{:S(2)}) copy-start(f32[128,4096]{1,0:T(8,128)S(1)} %get-tuple-element.23.qc_ref) | copy-start | bytes 6291460
  37.8 1.3 %copy-start.6 = (f32[128,4096]{1,0:T(8,128)}, f32[128,4096]{1,0:T(8,128)S(1)}, u32[]{:S(2)}) copy-start(f32[128,4096]{1,0:T(8,128)S(1)} %get-tuple-element.24.y_ref) | copy-start | bytes 6291460
  39.1 23.3 %copy-start.11 = (bf16[128,96]{1,0:T(8,128)(2,1)S(1)}, bf16[128,96]{1,0:T(8,128)(2,1)}, u32[]{:S(2)}) copy-start(bf16[128,96]{1,0:T(8,128)(2,1)} %constant.19.clone.lift_ref) | copy-start | bytes 73732
  62.3 1.6 %copy-start.5 = (f32[128,4096]{1,0:T(8,128)S(1)}, f32[128,4096]{1,0:T(8,128)}, u32[]{:S(2)}) copy-start(f32[128,4096]{1,0:T(8,128)} %copy-done.4) | copy-start | bytes 6291460
  63.9 1.6 %copy-start.7 = (f32[128,4096]{1,0:T(8,128)S(1)}, f32[128,4096]{1,0:T(8,128)}, u32[]{:S(2)}) copy-start(f32[128,4096]{1,0:T(8,128)} %copy-done.6) | copy-start | bytes 6291460
  65.5 5.2 %copy-start.13 = (f32[4096]{0:T(1024)S(1)}, f32[4096]{0:T(1024)}, u32[]{:S(2)}) copy-start(f32[4096]{0:T(1024)} %param.20) | copy-start | bytes 49156
  67.1 3.6 %collective-permute-start = (f32[1,128]{1,0:T(1,128)S(1)}, f32[1,128]{1,0:T(1,128)S(1)}, u32[]{:S(2)}, u32[]{:S(2)}) collective-permute-start(f32[1,128]{1,0:T(1,128)S(1)} %get-tuple-element.26), channel_id=1, source_target_pairs={{0,1},{1,0},{2,3},{3,2},{4,5},{5,4},{6,7},{7,6},{8,9},{9,8},{10,11... | collective-permute-start | bytes 1544 | tf_op jit(solution)/shard_map/ppermute | solution.py:548

commit v3 on v2

--- a/solution.py
+++ b/solution.py
@@ -1,3 +1,4 @@
+import functools
 from decimal import Decimal, getcontext
 
 import jax
@@ -94,53 +95,114 @@
         ref[:, group * LANES : (group + 1) * LANES] = values
 
 
-def raw_kernel(*refs):
-    ins, out_ref, rows, pay = refs[:12], refs[12], refs[13], refs[14]
-    for g in range(ins[0].shape[1] // LANES):
-        cols = slice(g * LANES, (g + 1) * LANES)
-        for a in range(3):
+EDGES = (0, STRETCH - 16, STRETCH, 2 * STRETCH - 16)
+
+
+def raw_kernel(q_ref, k_ref, v_ref, out_ref, held, rows, pay, sems):
+    chunks = sems.shape[0]
+    wide = q_ref.shape[1] // chunks
+
+    def copies(c):
+        cols = pl.ds(c * wide, wide)
+        return [
+            pltpu.make_async_copy(ref.at[pl.ds(at, 16), cols], held.at[4 * a + e, :, cols], sems.at[c, 4 * a + e])
+            for a, ref in enumerate((q_ref, k_ref, v_ref))
+            for e, at in enumerate(EDGES)
+        ]
+
+    for c in range(chunks):
+        for copy in copies(c):
+            copy.start()
+    for c in range(chunks):
+        for copy in copies(c):
+            copy.wait()
+        for g in range(c * wide // LANES, (c + 1) * wide // LANES):
+            cols = slice(g * LANES, (g + 1) * LANES)
+            for a in range(3):
+                for i in range(2):
+                    for e in range(2):
+                        rows[g, 2 * a + i, 16 * e : 16 * e + 16, :] = held[4 * a + 2 * i + e, :, cols].astype(F32)
+                    at = i * RAW + a * REACH
+                    pay[g, at : at + REACH, :] = rows[g, 2 * a + i, 32 - REACH : 32, :]
+                    at = at + 3 * REACH
+                    pay[g, at : at + REACH, :] = rows[g, 2 * a + i, 0:REACH, :]
+            put(out_ref, g, pay[g].astype(BF16))
+
+
+def gather_kernel(*refs, pieces, direct):
+    me_ref, k_ref, v_ref, taps_ref, ends_ref = refs[:5]
+    refs = refs[5:]
+    weights, refs = (refs[:4], refs[4:]) if direct else ((), refs)
+    u_ref, pay_refs, refs = refs[0], refs[1 : 1 + pieces], refs[1 + pieces :]
+    kept, refs = (refs[:4], refs[4:]) if direct else ((), refs)
+    held, taps_vm, xs, pay, sems, tap_sem, own_sems = refs
+    width = k_ref.shape[1]
+    span = 2 * LANES
+    blocks = width // span
+
+    def copies(c):
+        cols = pl.ds(pl.multiple_of(c * span, span), span)
+        return [
+            pltpu.make_async_copy(ref.at[:, cols], held.at[a, :, cols], sems.at[a, c])
+            for a, ref in enumerate((k_ref, v_ref))
+        ]
+
+    def own_copies():
+        share = kept[0].shape[-1]
+        cols = pl.ds(pl.multiple_of(me_ref[0] * share, share), share)
+        views = (weights[0].at[:, :, cols], weights[1].at[:, cols], weights[2].at[:, cols], weights[3].at[:, cols])
+        return [pltpu.make_async_copy(view, ref, own_sems.at[n]) for n, (view, ref) in enumerate(zip(views, kept))]
+
+    tap_copy = pltpu.make_async_copy(taps_ref, taps_vm, tap_sem.at[0])
+    tap_copy.start()
+
+    def begin(c, carry):
+        for copy in copies(c):
+            copy.start()
+        return carry
+
+    lax.fori_loop(0, blocks, begin, 0)
+    if direct:
+        for copy in own_copies():
+            copy.start()
+    for a in range(2):
+        for h in range(2):
             for i in range(2):
-                first, last = ins[4 * a + 2 * i], ins[4 * a + 2 * i + 1]
-                rows[g, 2 * a + i, 0:16, :] = first[:, cols].astype(F32)
-                rows[g, 2 * a + i, 16:32, :] = last[:, cols].astype(F32)
-                at = i * RAW + a * REACH
-                pay[g, at : at + REACH, :] = rows[g, 2 * a + i, 32 - REACH : 32, :]
-                at = at + 3 * REACH
-                pay[g, at : at + REACH, :] = rows[g, 2 * a + i, 0:REACH, :]
-        put(out_ref, g, pay[g].astype(BF16))
-
-
-def gather_kernel(k_ref, v_ref, taps_ref, ends_ref, pay_ref, u_ref, xs, pay):
-    tile = k_ref.shape[1]
-    groups = tile // LANES
-    for g in range(groups):
-        cols = slice(g * LANES, (g + 1) * LANES)
-        for i in range(2):
-            rows = slice(i * STRETCH, (i + 1) * STRETCH)
-            for a, ref in enumerate((k_ref, v_ref)):
-                base = i * (STRETCH + 8) + 8
-                xs[a, g, base - 8 : base, :] = jnp.zeros((8, LANES), F32)
-                xs[a, g, base : base + STRETCH, :] = ref[rows, cols].astype(F32)
-        taps = [[taps_ref[a, j : j + 1, cols] for j in range(REACH + 1)] for a in (1, 2)]
-        for i in range(2):
-            for b in range(STRETCH // 16):
-                base = i * (STRETCH + 8) + 8 + 16 * b
-                both = []
-                for a in range(2):
-                    total = taps[a][0] * xs[a, g, base : base + 16, :]
-                    for j in range(1, REACH + 1):
-                        total = total + taps[a][j] * xs[a, g, base - j : base - j + 16, :]
-                    both.append(total)
-                mixed = both[0] * both[1]
-                if b == 0:
-                    row = lax.broadcasted_iota(jnp.int32, (16, LANES), 0)
-                    mixed = jnp.where(row >= REACH, mixed, 0.0)
-                high, low = split(mixed)
-                rows = slice(i * STRETCH + 16 * b, i * STRETCH + 16 * b + 16)
-                u_ref[0, rows, cols] = high
-                u_ref[1, rows, cols] = low
-    span = min(tile, 2 * LANES)
-    for c in range(tile // span):
+                at = i * (STRETCH + 8)
+                xs[a, h, at : at + 8, :] = jnp.zeros((8, LANES), F32)
+    tap_copy.wait()
+
+    def features(c, carry):
+        for copy in copies(c):
+            copy.wait()
+        for h in range(2):
+            cols = pl.ds(pl.multiple_of(c * span + h * LANES, LANES), LANES)
+            for a in range(2):
+                for i in range(2):
+                    base = i * (STRETCH + 8) + 8
+                    xs[a, h, base : base + STRETCH, :] = held[a, i * STRETCH : (i + 1) * STRETCH, cols].astype(F32)
+            taps = [[taps_vm[a, j : j + 1, cols] for j in range(REACH + 1)] for a in (1, 2)]
+            for i in range(2):
+                for b in range(STRETCH // 16):
+                    base = i * (STRETCH + 8) + 8 + 16 * b
+                    both = []
+                    for a in range(2):
+                        total = taps[a][0] * xs[a, h, base : base + 16, :]
+                        for j in range(1, REACH + 1):
+                            total = total + taps[a][j] * xs[a, h, base - j : base - j + 16, :]
+                        both.append(total)
+                    mixed = both[0] * both[1]
+                    if b == 0:
+                        row = lax.broadcasted_iota(jnp.int32, (16, LANES), 0)
+                        mixed = jnp.where(row >= REACH, mixed, 0.0)
+                    high, low = split(mixed)
+                    rows = slice(i * STRETCH + 16 * b, i * STRETCH + 16 * b + 16)
+                    u_ref[0, rows, cols] = high
+                    u_ref[1, rows, cols] = low
+        return carry
+
+    lax.fori_loop(0, blocks, features, 0)
+    for c in range(blocks):
         cols = slice(c * span, (c + 1) * span)
         for i in range(2):
             rows = slice(i * STRETCH, (i + 1) * STRETCH)
@@ -149,14 +211,23 @@
                 ends_ref[...], jnp.concatenate([high, low, high], axis=0), preferred_element_type=F32
             )
             top, rest = split(moments)
-            for h in range(span // LANES):
-                g = c * (span // LANES) + h
+            at = 2 * RANK * i
+            for h in range(2):
                 lanes = slice(h * LANES, (h + 1) * LANES)
-                at = 2 * RANK * i
-                pay[g, at : at + RANK, :] = top.astype(F32)[:RANK, lanes]
-                pay[g, at + RANK : at + 2 * RANK, :] = rest.astype(F32)[:RANK, lanes]
-    for g in range(groups):
-        put(pay_ref, g, pay[g].astype(BF16))
+                pay[2 * c + h, at : at + RANK, :] = top.astype(F32)[:RANK, lanes]
+                pay[2 * c + h, at + RANK : at + 2 * RANK, :] = rest.astype(F32)[:RANK, lanes]
+    if direct:
+        share = kept[0].shape[-1]
+        per = share // LANES
+        for s in range(pieces):
+            dest = lax.rem(me_ref[0] + s, pieces)
+            for h in range(per):
+                pay_refs[s][:, h * LANES : (h + 1) * LANES] = pay[per * dest + h].astype(BF16)
+        for copy in own_copies():
+            copy.wait()
+    else:
+        for g in range(width // LANES):
+            pay_refs[0][:, g * LANES : (g + 1) * LANES] = pay[g].astype(BF16)
 
 
 def local_kernel(q_ref, u_ref, taps_ref, rates_ref, res_ref, skip_ref, local_ref, qc_ref, y_ref, xs):
@@ -196,7 +267,7 @@
 
 
 def heads_kernel(
-    me_ref, perm_ref, x_ref, taps_ref, rates_ref, res_ref, skip_ref, heads_ref, first_ref, raw, ext, past
+    perm_ref, x_ref, taps_ref, rates_ref, res_ref, skip_ref, heads_ref, first_ref, raw, ext, past
 ):
     slots = perm_ref.shape[0]
     groups = x_ref.shape[2] // LANES
@@ -252,24 +323,33 @@
         lax.fori_loop(0, slots, head_pass, 0, unroll=2)
 
 
-def states_kernel(
-    me_ref, perm_ref, x_ref, heads_ref, first_ref, rates_ref, res_ref, out_ref,
-    raw, moments, second, states, mids, carried, result,
-):
+def states_kernel(me_ref, perm_ref, *refs, pieces):
+    xs, refs = refs[:pieces], refs[pieces:]
+    heads_ref, first_ref, rates_ref, res_ref, out_ref = refs[:5]
+    raw, moments, second, states, mids, carried, result = refs[5:]
     slots = perm_ref.shape[0]
-    groups = x_ref.shape[2] // LANES
-
-    def unpack(src, carry):
+    groups = rates_ref.shape[1] // LANES
+
+    def place(src, values):
         for g in range(groups):
-            raw[g] = x_ref[src, :, g * LANES : (g + 1) * LANES].astype(F32)
+            raw[g] = values(g).astype(F32)
         for i in range(2):
             n = perm_ref[2 * src + i]
             for g in range(groups):
                 at = 2 * RANK * i
                 moments[g, n, 0:RANK, :] = raw[g, at : at + RANK, :] + raw[g, at + RANK : at + 2 * RANK, :]
-        return carry
-
-    lax.fori_loop(0, slots // 2, unpack, 0)
+
+    if pieces > 1:
+        for s in range(pieces):
+            src = lax.rem(me_ref[0] + (pieces - s), pieces)
+            place(src, lambda g, s=s: xs[s][:, g * LANES : (g + 1) * LANES])
+    else:
+
+        def unpack(src, carry):
+            place(src, lambda g: xs[0][src, :, g * LANES : (g + 1) * LANES])
+            return carry
+
+        lax.fori_loop(0, slots // 2, unpack, 0)
 
     rate = [rates_ref[:, g * LANES : (g + 1) * LANES] for g in range(groups)]
     amount = [amplitude(rate[g], res_ref[:, g * LANES : (g + 1) * LANES]) for g in range(groups)]
@@ -401,57 +481,67 @@
         pad = [(0, 0)] * (array.ndim - 1) + [(0, lanes - share)]
         return jnp.pad(array, pad, constant_values=fill)
 
-    if direct:
-        mine = (short_weight, rates, residues, skip)
-
-        def own(*lead):
-            return pl.BlockSpec((*lead, share), lambda c, me_ref, perm_ref: (0,) * len(lead) + (me_ref[0],))
-
-    else:
-
-        def cut(array, fill=0.0):
-            return widen(
-                lax.dynamic_slice_in_dim(array, lax.axis_index("ctx") * share, share, array.ndim - 1), fill
-            )
-
-        mine = (cut(short_weight), cut(rates, 0.01), cut(residues), cut(skip))
-
-        def own(*lead):
-            return pl.BlockSpec((*lead, lanes), lambda c, me_ref, perm_ref: (0,) * (len(lead) + 1))
-
-    def full(*shape):
-        return pl.BlockSpec(shape, lambda c, me_ref, perm_ref: (0,) * len(shape))
-
-    raw_shape, raw_spec = payload(2 * RAW)
-    edges = [0, STRETCH // 16 - 1, STRETCH // 16, 2 * STRETCH // 16 - 1]
+    def cut(array, fill=0.0):
+        return widen(lax.dynamic_slice_in_dim(array, lax.axis_index("ctx") * share, share, array.ndim - 1), fill)
+
+    smem = pl.BlockSpec(memory_space=pltpu.SMEM)
+    vmem = pl.BlockSpec(memory_space=pltpu.VMEM)
+    hbm = pl.BlockSpec(memory_space=pltpu.HBM)
+    f32 = lambda *shape: jax.ShapeDtypeStruct(shape, F32)
+
+    pin = lambda array: pltpu.with_memory_space_constraint(array, pltpu.HBM)
+    raw_shape, _ = payload(2 * RAW)
+    all_groups = width // LANES
+    chunks = 2
     raw = pl.pallas_call(
         raw_kernel,
-        grid=(steps,),
-        in_specs=[pl.BlockSpec((16, tile), lambda c, r=r: (r, c)) for _ in range(3) for r in edges],
-        out_specs=raw_spec,
+        in_specs=[hbm] * 3,
+        out_specs=vmem,
         out_shape=raw_shape,
-        scratch_shapes=[pltpu.VMEM((groups, 6, 32, LANES), F32), pltpu.VMEM((groups, 2 * RAW, LANES), F32)],
-        compiler_params=limit(60),
+        scratch_shapes=[
+            pltpu.VMEM((12, 16, width), BF16),
+            pltpu.VMEM((all_groups, 6, 32, LANES), F32),
+            pltpu.VMEM((all_groups, 2 * RAW, LANES), F32),
+            pltpu.SemaphoreType.DMA((chunks, 12)),
+        ],
+        compiler_params=limit(24),
         name="edge_rows",
-    )(*[array for array in (q_in, k_in, v_in) for _ in edges])
+    )(pin(q_in), pin(k_in), pin(v_in))
+    raw, after_raw = lax.optimization_barrier((raw, me))
     raw = exchange(raw)
 
-    pay_shape, pay_spec = payload(4 * RANK)
-    pay, mixed = pl.pallas_call(
-        gather_kernel,
-        grid=(steps,),
-        in_specs=[columns(tokens)] * 2 + [columns(3, REACH + 1), whole(ends)],
-        out_specs=[pay_spec, columns(2, tokens)],
-        out_shape=[pay_shape, jax.ShapeDtypeStruct((2, tokens, width), BF16)],
+    pieces = n_ctx if direct else 1
+    pay_shape = jax.ShapeDtypeStruct((4 * RANK, share if direct else width), BF16)
+    weights = (short_weight, rates, residues, skip)
+    own = [f32(*w.shape[:-1], share) for w in weights] if direct else []
+    blocks = width // (2 * LANES)
+    outs = pl.pallas_call(
+        functools.partial(gather_kernel, pieces=pieces, direct=direct),
+        in_specs=[smem] + [hbm] * 3 + [vmem] + [hbm] * len(own),
+        out_specs=[vmem] * (1 + pieces + len(own)),
+        out_shape=[jax.ShapeDtypeStruct((2, tokens, width), BF16)] + [pay_shape] * pieces + own,
         scratch_shapes=[
-            pltpu.VMEM((2, groups, 2 * (STRETCH + 8), LANES), F32),
-            pltpu.VMEM((groups, 4 * RANK, LANES), F32),
+            pltpu.VMEM((2, tokens, width), BF16),
+            pltpu.VMEM(short_weight.shape, F32),
+            pltpu.VMEM((2, 2, 2 * (STRETCH + 8), LANES), F32),
+            pltpu.VMEM((all_groups, 4 * RANK, LANES), F32),
+            pltpu.SemaphoreType.DMA((2, blocks)),
+            pltpu.SemaphoreType.DMA((1,)),
+            pltpu.SemaphoreType.DMA((4,)),
         ],
-        compiler_params=limit(60),
+        compiler_params=limit(24),
         name="gather_moments",
         cost_estimate=pl.CostEstimate(flops=10**9, bytes_accessed=10 * 10**6, transcendentals=0),
-    )(k_in, v_in, short_weight, ends)
-    pay = exchange(pay)
+    )(after_raw, pin(k_in), pin(v_in), pin(short_weight), ends, *(map(pin, weights) if direct else ()))
+    mixed = outs[0]
+    if direct:
+        mine = outs[1 + pieces :]
+        pays = [outs[1]]
+        for shift in range(1, n_ctx):
+            pays.append(lax.ppermute(outs[1 + shift], "ctx", [(i, (i + shift) % n_ctx) for i in range(n_ctx)]))
+    else:
+        mine = (cut(short_weight), cut(rates, 0.01), cut(residues), cut(skip))
+        pays = [exchange(outs[1])]
 
     query, inner = pl.pallas_call(
         local_kernel,
@@ -466,63 +556,45 @@
             whole(local),
         ],
         out_specs=[columns(tokens)] * 2,
-        out_shape=[jax.ShapeDtypeStruct((tokens, width), F32)] * 2,
+        out_shape=[f32(tokens, width)] * 2,
         scratch_shapes=[pltpu.VMEM((groups, 2 * (STRETCH + 8), LANES), F32)],
-        compiler_params=limit(40),
+        compiler_params=limit(24),
         name="local_filter",
         cost_estimate=pl.CostEstimate(flops=10**9, bytes_accessed=20 * 10**6, transcendentals=0),
     )(q_in, mixed, short_weight, rates, residues, skip, local)
-    raw, query, inner = lax.optimization_barrier((raw, query, inner))
 
     groups = lanes // LANES
     heads, first = pl.pallas_call(
         heads_kernel,
-        grid_spec=pltpu.PrefetchScalarGridSpec(
-            num_scalar_prefetch=2,
-            grid=(1,),
-            in_specs=[full(n_ctx, 2 * RAW, lanes), own(3, REACH + 1), own(order), own(order), own(1)],
-            out_specs=[full(groups, slots, 16, LANES), full(groups, slots, order, LANES)],
-            scratch_shapes=[
-                pltpu.VMEM((groups, 2 * RAW, LANES), F32),
-                pltpu.VMEM((3, groups, slots + 1, 16, LANES), F32),
-                pltpu.VMEM((groups, slots, 16, LANES), F32),
-            ],
-        ),
-        out_shape=[
-            jax.ShapeDtypeStruct((groups, slots, 16, LANES), F32),
-            jax.ShapeDtypeStruct((groups, slots, order, LANES), F32),
+        in_specs=[smem] + [vmem] * 5,
+        out_specs=[vmem] * 2,
+        scratch_shapes=[
+            pltpu.VMEM((groups, 2 * RAW, LANES), F32),
+            pltpu.VMEM((3, groups, slots + 1, 16, LANES), F32),
+            pltpu.VMEM((groups, slots, 16, LANES), F32),
         ],
-        compiler_params=limit(32),
+        out_shape=[f32(groups, slots, 16, LANES), f32(groups, slots, order, LANES)],
+        compiler_params=limit(24),
         name="head_tokens",
-    )(me, stretch_of_slot, raw, *mine)
+    )(stretch_of_slot, raw, *mine)
 
     back = pl.pallas_call(
-        states_kernel,
-        grid_spec=pltpu.PrefetchScalarGridSpec(
-            num_scalar_prefetch=2,
-            grid=(1,),
-            in_specs=[
-                full(n_ctx, 4 * RANK, lanes),
-                full(groups, slots, 16, LANES),
-                full(groups, slots, order, LANES),
-                own(order),
-                own(order),
-            ],
-            out_specs=full(n_ctx, 2 * BACK, lanes),
-            scratch_shapes=[
-                pltpu.VMEM((groups, 4 * RANK, LANES), F32),
-                pltpu.VMEM((groups, slots, 8, LANES), F32),
-                pltpu.VMEM((groups, slots, order, LANES), F32),
-                pltpu.VMEM((groups, slots, order, LANES), F32),
-                pltpu.VMEM((groups, slots, order, LANES), F32),
-                pltpu.VMEM((groups, slots, 16, LANES), F32),
-                pltpu.VMEM((groups, slots, BACK, LANES), F32),
-            ],
-        ),
+        functools.partial(states_kernel, pieces=pieces),
+        in_specs=[smem] * 2 + [vmem] * (pieces + 4),
+        out_specs=vmem,
+        scratch_shapes=[
+            pltpu.VMEM((groups, 4 * RANK, LANES), F32),
+            pltpu.VMEM((groups, slots, 8, LANES), F32),
+            pltpu.VMEM((groups, slots, order, LANES), F32),
+            pltpu.VMEM((groups, slots, order, LANES), F32),
+            pltpu.VMEM((groups, slots, order, LANES), F32),
+            pltpu.VMEM((groups, slots, 16, LANES), F32),
+            pltpu.VMEM((groups, slots, BACK, LANES), F32),
+        ],
         out_shape=jax.ShapeDtypeStruct((n_ctx, 2 * BACK, lanes), BF16),
-        compiler_params=limit(32),
+        compiler_params=limit(24),
         name="carry_states",
-    )(me, stretch_of_slot, pay, heads, first, mine[1], mine[2])
+    )(me, stretch_of_slot, *pays, heads, first, mine[1], mine[2])
     if not direct:
         back = back[:, :, :share]
     back = lax.all_to_all(back, "ctx", 0, 0, tiled=True)
@@ -540,7 +612,7 @@
             jax.ShapeDtypeStruct((1, tokens), F32),
         ],
         scratch_shapes=[pltpu.VMEM((tokens, LANES), F32)],
-        compiler_params=limit(32),
+        compiler_params=limit(24),
         name="join_carry",
     )(back, lift, query, inner)
     total = squares

time: 72.7 us -> 73.4 us (level)
  starting transfers between devices: 13.4 us -> 32.7 us
  blocking collectives: 18 us -> 0 us
  local copies, waits for them, and re-layouts: 7.44 us -> 12.6 us
  waiting for transfers between devices: 11.7 us -> 7.63 us
  Pallas kernels: 20 us -> 18.3 us
    ppermute x0 -> x15, starting transfers between devices: none -> 18.9 us  [on_device(): lax.ppermute(outs[1 + shift], 'ctx', [(i, (i + shift) % n_ctx) for i in r...]
    all_to_all x1 -> x0, blocking collectives: 18 us -> none  [on_device(): back = lax.all_to_all(back, 'ctx', 0, 0, tiled=True)]
    all_to_all x2 -> x1, waiting for transfers between devices: 9.65 us -> 0.01 us  [exchange(): return lax.all_to_all(array, 'ctx', 0, 0, tiled=True)]
    unnamed x28 -> x34, local copies, waits for them, and re-layouts: 7.44 us -> 12.6 us
    all_to_all x0 -> x1, starting transfers between devices: none -> 4.85 us  [on_device(): back = lax.all_to_all(back, 'ctx', 0, 0, tiled=True)]
    all_to_all x2 -> x1, starting transfers between devices: 11.8 us -> 7.37 us  [exchange(): return lax.all_to_all(array, 'ctx', 0, 0, tiled=True)]
    ppermute x0 -> x15, waiting for transfers between devices: none -> 3.95 us  [on_device(): lax.ppermute(outs[1 + shift], 'ctx', [(i, (i + shift) % n_ctx) for i in r...]
    pallas_call x4, Pallas kernels: 14.5 us -> 12.8 us  [the longest x1 4.97 us: on_device(): pl.pallas_call(functools.partial(gather_kernel, pieces=pieces, direct=dir...]
  transfers between devices with their start and end apart: 3 -> 18, of which waited for: 2 -> 4; matrix products, arithmetic and copies ran while one was open for 0% -> 0% of each run, Pallas kernels for 17% -> 15%
where the time goes in v3:
time: 73.4 us; the launch traced here: 72.7 us
  starting transfers between devices  32.7 us (45%)
  Pallas kernels  18.3 us (25%)
  local copies, waits for them, and re-layouts  12.6 us (17%)
  waiting for transfers between devices  7.63 us (10%)
  other arithmetic  1.27 us (2%)
    ppermute x15, starting transfers between devices, on_device(): lax.ppermute(outs[1 + shift], 'ctx', [(i, (i + shift) % n_ctx) for i in r...  18.9 us
    unnamed x34, local copies, waits for them, and re-layouts  12.6 us
    all_to_all x1, starting transfers between devices, exchange(): return lax.all_to_all(array, 'ctx', 0, 0, tiled=True)  7.37 us
    pallas_call x1, Pallas kernels, on_device(): pl.pallas_call(functools.partial(gather_kernel, pieces=pieces, direct=dir...  4.97 us
    all_to_all x1, starting transfers between devices, on_device(): back = lax.all_to_all(back, 'ctx', 0, 0, tiled=True)  4.85 us
    pallas_call x1, Pallas kernels, on_device(): pl.pallas_call(local_kernel, grid=(steps,), in_specs=[columns(tokens), co...  3.98 us
    ppermute x15, waiting for transfers between devices, on_device(): lax.ppermute(outs[1 + shift], 'ctx', [(i, (i + shift) % n_ctx) for i in r...  3.95 us
    pallas_call x1, Pallas kernels, on_device(): pl.pallas_call(functools.partial(states_kernel, pieces=pieces), in_specs=...  2.93 us
  transfers between devices with their start and end apart: 18, of which 4 were waited for; matrix products, arithmetic and copies ran while one was open for 0% of the time, Pallas kernels for 15%

profile of v3, /device:TPU:0, one launch (start us, length us, event | category | flops | bytes accessed | tf_op | source)
XLA Modules:
  0.0 72.7 jit_solution(5651420186103754584)
XLA Ops:
  0.0 2.6 %edge_rows.1 = bf16[16,72,256]{2,1,0:T(8,128)(2,1)} custom-call(bf16[128,4096]{1,0:T(8,128)(2,1)} %q_ref.3, bf16[128,4096]{1,0:T(8,128)(2,1)} %refs_1_.1, bf16[128,4096]{1,0:T(8,128)(2,1)} %refs_2_.1), custom_call_target="tpu_custom_call" | custom-call | tf_op jit(solution)/shard_map/edge_rows/pallas_call | solution.py:496
  2.6 7.4 %all-to-all-start = ((bf16[16,72,256]{2,1,0:T(8,128)(2,1)}), bf16[16,72,256]{2,1,0:T(8,128)(2,1)S(1)}, u32[]{:S(2)}, u32[]{:S(2)}) async-start(bf16[16,72,256]{2,1,0:T(8,128)(2,1)} %edge_rows.1), calls=%async_computation | async-start | bytes 1179648 | tf_op jit(solution)/shard_map/all_to_all | solution.py:474
  10.0 5.0 %gather_moments.1 = (bf16[2,128,4096]{2,1,0:T(8,128)(2,1)S(1)}, bf16[24,256]{1,0:T(8,128)(2,1)S(1)}, bf16[24,256]{1,0:T(8,128)(2,1)S(1)}, bf16[24,256]{1,0:T(8,1...) custom-call(s32[1]{0:T(128)} %bitcast.refs_0_.me_ref, ...), custom_call_target="tpu_custom_call" | custom-call | flops 1000000000 | bytes 10000000 | tf_op jit(solution)/shard_map/gather_moments/pallas_call | solution.py:518
  15.0 1.3 %copy-done.1 = bf16[2,128,4096]{2,1,0:T(8,128)(2,1)} copy-done((bf16[2,128,4096]{2,1,0:T(8,128)(2,1)}, bf16[2,128,4096]{2,1,0:T(8,128)(2,1)S(1)}, u32[]{:S(2)}) %copy-start.1) | copy-done | bytes 2097176
  16.8 1.7 %collective-permute-start.1 = (bf16[24,256]{1,0:T(8,128)(2,1)S(1)}, bf16[24,256]{1,0:T(8,128)(2,1)S(1)}, u32[]{:S(2)}, u32[]{:S(2)}) collective-permute-start(bf16[24,256]{1,0:T(8,128)(2,1)S(1)} %get-tuple-element.37), channel_id=1, source_target_pairs={{0,4},{2,6},{4,8},{6,10},{8,12},{10,14},{12,16},{14,18},{16,20},{1... | collective-permute-start | bytes 36872 | tf_op jit(solution)/shard_map/ppermute | solution.py:541
  18.5 2.2 %collective-permute-start.2 = (bf16[24,256]{1,0:T(8,128)(2,1)S(1)}, bf16[24,256]{1,0:T(8,128)(2,1)S(1)}, u32[]{:S(2)}, u32[]{:S(2)}) collective-permute-start(bf16[24,256]{1,0:T(8,128)(2,1)S(1)} %get-tuple-element.38), channel_id=1, source_target_pairs={{0,6},{2,8},{4,10},{6,12},{8,14},{10,16},{12,18},{14,20},{16,22},{... | collective-permute-start | bytes 36872 | tf_op jit(solution)/shard_map/ppermute | solution.py:541
  20.7 1.5 %collective-permute-start.3 = (bf16[24,256]{1,0:T(8,128)(2,1)S(1)}, bf16[24,256]{1,0:T(8,128)(2,1)S(1)}, u32[]{:S(2)}, u32[]{:S(2)}) collective-permute-start(bf16[24,256]{1,0:T(8,128)(2,1)S(1)} %get-tuple-element.39), channel_id=1, source_target_pairs={{0,8},{2,10},{4,12},{6,14},{8,16},{10,18},{12,20},{14,22},{16,24},... | collective-permute-start | bytes 36872 | tf_op jit(solution)/shard_map/ppermute | solution.py:541
  22.3 3.1 %collective-permute-done.refs_1_ = bf16[24,256]{1,0:T(8,128)(2,1)S(1)} collective-permute-done((bf16[24,256]{1,0:T(8,128)(2,1)S(1)}, bf16[24,256]{1,0:T(8,128)(2,1)S(1)}, u32[]{:S(2)}, u32[]{:S(2)}) %collective-permute-start) | collective-permute-done | bytes 12320 | tf_op jit(solution)/shard_map/ppermute | solution.py:541
  26.2 1.6 %collective-permute-start.6 = (bf16[24,256]{1,0:T(8,128)(2,1)S(1)}, bf16[24,256]{1,0:T(8,128)(2,1)S(1)}, u32[]{:S(2)}, u32[]{:S(2)}) collective-permute-start(bf16[24,256]{1,0:T(8,128)(2,1)S(1)} %get-tuple-element.42), channel_id=1, source_target_pairs={{0,14},{2,16},{4,18},{6,20},{8,22},{10,24},{12,26},{14,28},{16,30}... | collective-permute-start | bytes 36872 | tf_op jit(solution)/shard_map/ppermute | solution.py:541
  29.0 2.3 %collective-permute-start.8 = (bf16[24,256]{1,0:T(8,128)(2,1)S(1)}, bf16[24,256]{1,0:T(8,128)(2,1)S(1)}, u32[]{:S(2)}, u32[]{:S(2)}) collective-permute-start(bf16[24,256]{1,0:T(8,128)(2,1)S(1)} %get-tuple-element.44), channel_id=1, source_target_pairs={{0,18},{2,20},{4,22},{6,24},{8,26},{10,28},{12,30},{14,0},{16,2},{... | collective-permute-start | bytes 36872 | tf_op jit(solution)/shard_map/ppermute | solution.py:541
  31.3 2.9 %collective-permute-start.9 = (bf16[24,256]{1,0:T(8,128)(2,1)S(1)}, bf16[24,256]{1,0:T(8,128)(2,1)S(1)}, u32[]{:S(2)}, u32[]{:S(2)}) collective-permute-start(bf16[24,256]{1,0:T(8,128)(2,1)S(1)} %get-tuple-element.45), channel_id=1, source_target_pairs={{0,20},{2,22},{4,24},{6,26},{8,28},{10,30},{12,0},{14,2},{16,4},{1... | collective-permute-start | bytes 36872 | tf_op jit(solution)/shard_map/ppermute | solution.py:541
  34.2 2.4 %collective-permute-start.11 = (bf16[24,256]{1,0:T(8,128)(2,1)S(1)}, bf16[24,256]{1,0:T(8,128)(2,1)S(1)}, u32[]{:S(2)}, u32[]{:S(2)}) collective-permute-start(bf16[24,256]{1,0:T(8,128)(2,1)S(1)} %get-tuple-element.47), channel_id=1, source_target_pairs={{0,24},{2,26},{4,28},{6,30},{8,0},{10,2},{12,4},{14,6},{16,8},{18,... | collective-permute-start | bytes 36872 | tf_op jit(solution)/shard_map/ppermute | solution.py:541
  37.0 2.3 %collective-permute-start.14 = (bf16[24,256]{1,0:T(8,128)(2,1)S(1)}, bf16[24,256]{1,0:T(8,128)(2,1)S(1)}, u32[]{:S(2)}, u32[]{:S(2)}) collective-permute-start(bf16[24,256]{1,0:T(8,128)(2,1)S(1)} %get-tuple-element.50), channel_id=1, source_target_pairs={{0,30},{2,0},{4,2},{6,4},{8,6},{10,8},{12,10},{14,12},{16,14},{18,... | collective-permute-start | bytes 36872 | tf_op jit(solution)/shard_map/ppermute | solution.py:541
  39.3 2.3 %head_tokens.1 = (f32[2,32,16,128]{3,2,1,0:T(8,128)S(1)}, f32[2,32,16,128]{3,2,1,0:T(8,128)S(1)}) custom-call(s32[32]{0:T(128)S(1)} %copy-done.14, bf16[16,72,256]{2,1,0:T(8,128)(2,1)S(1)} %all-to-all-done.x_ref, f32[3,7,256]{2,1,0:T(8,128)S(1)} %get-tuple-element.52.taps_ref, f32[16,256]{1,0:T(8,128)S(1)} %get-tuple-element.53.rates_ref.refs_18_, ...), custom_call_target="tpu_custom_call" | custom-call | tf_op jit(solution)/shard_map/head_tokens/pallas_call | solution.py:567
  41.6 2.9 %carry_states.1 = bf16[16,48,256]{2,1,0:T(8,128)(2,1)S(1)} custom-call(s32[1]{0:T(128)} %bitcast.refs_0_.me_ref, s32[32]{0:T(128)S(1)} %copy-done.14, bf16[24,256]{1,0:T(8,128)(2,1)S(1)} %get-tuple-element.35.refs_0_, bf16[24,256]{1,0:T(8,128)(2,1)S(1)} %collective-permute-done.refs_1_, bf16[24,256]{1,0:T(8,128)(2,1)S(1)} %collective-permute-done.1.refs_2_, ...), custom_call_target="tpu_custom_call" | custom-call | tf_op jit(solution)/shard_map/carry_states/pallas_call | solution.py:581
  45.3 4.8 %all-to-all-start.1 = ((bf16[16,48,256]{2,1,0:T(8,128)(2,1)}), bf16[16,48,256]{2,1,0:T(8,128)(2,1)S(1)}, u32[]{:S(2)}, u32[]{:S(2)}) async-start(bf16[16,48,256]{2,1,0:T(8,128)(2,1)} %copy-done.7), calls=%async_computation.1 | async-start | bytes 786432 | tf_op jit(solution)/shard_map/all_to_all | solution.py:600
  54.0 4.0 %local_filter.1 = (f32[128,4096]{1,0:T(8,128)S(1)}, f32[128,4096]{1,0:T(8,128)S(1)}) custom-call(bf16[128,4096]{1,0:T(8,128)(2,1)S(1)} %copy-done, bf16[2,128,4096]{2,1,0:T(8,128)(2,1)S(1)} %copy-done.2, f32[3,7,4096]{2,1,0:T(8,128)S(1)} %copy-done.8, f32[16,4096]{1,0:T(8,128)S(1)} %copy-done.9, f32[16,4096]{1,0:T(8,128)S(1)} %copy-done.10, ...), custom_call_target="tpu_custom_call" | custom-call | flops 1000000000 | bytes 20000000 | tf_op jit(solution)/shard_map/local_filter/pallas_call | solution.py:546
  58.0 1.3 %copy-done.3 = f32[128,4096]{1,0:T(8,128)} copy-done((f32[128,4096]{1,0:T(8,128)}, f32[128,4096]{1,0:T(8,128)S(1)}, u32[]{:S(2)}) %copy-start.3) | copy-done | bytes 2097176
  60.7 1.7 %all-to-all-done.1.back_ref = bf16[16,48,256]{2,1,0:T(8,128)(2,1)S(1)} async-done(((bf16[16,48,256]{2,1,0:T(8,128)(2,1)}), bf16[16,48,256]{2,1,0:T(8,128)(2,1)S(1)}, u32[]{:S(2)}, u32[]{:S(2)}) %all-to-all-start.1) | async-done | bytes 393248 | tf_op jit(solution)/shard_map/all_to_all | solution.py:600
  62.4 1.6 %copy-done.4 = f32[128,4096]{1,0:T(8,128)S(1)} copy-done((f32[128,4096]{1,0:T(8,128)S(1)}, f32[128,4096]{1,0:T(8,128)}, u32[]{:S(2)}) %copy-start.4) | copy-done | bytes 2097176
  63.9 1.6 %copy-done.6 = f32[128,4096]{1,0:T(8,128)S(1)} copy-done((f32[128,4096]{1,0:T(8,128)S(1)}, f32[128,4096]{1,0:T(8,128)}, u32[]{:S(2)}) %copy-start.6) | copy-done | bytes 2097176
  66.3 1.5 %join_carry.1 = (f32[128,4096]{1,0:T(8,128)S(1)}, f32[1,128]{1,0:T(1,128)S(1)}) custom-call(bf16[16,48,256]{2,1,0:T(8,128)(2,1)S(1)} %all-to-all-done.1.back_ref, bf16[128,96]{1,0:T(8,128)(2,1)S(1)} %copy-done.12, f32[128,4096]{1,0:T(8,128)S(1)} %copy-done.4, f32[128,4096]{1,0:T(8,128)S(1)} %copy-done.6), custom_call_target="tpu_custom_call" | custom-call | tf_op jit(solution)/shard_map/join_carry/pallas_call | solution.py:605
  67.8 1.6 %collective-permute-start.15 = (f32[1,128]{1,0:T(1,128)S(1)}, f32[1,128]{1,0:T(1,128)S(1)}, u32[]{:S(2)}, u32[]{:S(2)}) collective-permute-start(f32[1,128]{1,0:T(1,128)S(1)} %get-tuple-element.62), channel_id=1, source_target_pairs={{0,1},{1,0},{2,3},{3,2},{4,5},{5,4},{6,7},{7,6},{8,9},{9,8},{10,11... | collective-permute-start | bytes 1544 | tf_op jit(solution)/shard_map/ppermute | solution.py:620
  69.4 2.0 %collective-permute-done.15 = f32[1,128]{1,0:T(1,128)S(1)} collective-permute-done((f32[1,128]{1,0:T(1,128)S(1)}, f32[1,128]{1,0:T(1,128)S(1)}, u32[]{:S(2)}, u32[]{:S(2)}) %collective-permute-start.15) | collective-permute-done | bytes 544 | tf_op jit(solution)/shard_map/ppermute | solution.py:620
  (54 shorter events, 11.0 us)
Async XLA Ops:
  0.0 10.0 %copy-start.15 = (bf16[16,192]{1,0:T(8,128)(2,1)S(1)}, bf16[16,192]{1,0:T(8,128)(2,1)}, u32[]{:S(2)}) copy-start(bf16[16,192]{1,0:T(8,128)(2,1)} %constant.17.clone.refs_4_) | copy-start | bytes 18436
  2.6 36.7 %all-to-all-start = ((bf16[16,72,256]{2,1,0:T(8,128)(2,1)}), bf16[16,72,256]{2,1,0:T(8,128)(2,1)S(1)}, u32[]{:S(2)}, u32[]{:S(2)}) async-start(bf16[16,72,256]{2,1,0:T(8,128)(2,1)} %edge_rows.1), calls=%async_computation | async-start | bytes 1179648 | tf_op jit(solution)/shard_map/all_to_all | solution.py:474
  10.0 29.3 %copy-start.14 = (s32[32]{0:T(128)S(1)}, s32[32]{0:T(128)}, u32[]{:S(2)}) copy-start(s32[32]{0:T(128)} %perm_ref.3) | copy-start | bytes 388
  10.0 40.1 %copy-start.13 = (f32[4096]{0:T(1024)S(1)}, f32[4096]{0:T(1024)}, u32[]{:S(2)}) copy-start(f32[4096]{0:T(1024)} %param.19) | copy-start | bytes 49156
  16.4 33.8 %copy-start = (bf16[128,4096]{1,0:T(8,128)(2,1)S(1)}, bf16[128,4096]{1,0:T(8,128)(2,1)}, u32[]{:S(2)}) copy-start(bf16[128,4096]{1,0:T(8,128)(2,1)} %q_ref.3) | copy-start | bytes 3145732
  16.4 9.0 %collective-permute-start = (bf16[24,256]{1,0:T(8,128)(2,1)S(1)}, bf16[24,256]{1,0:T(8,128)(2,1)S(1)}, u32[]{:S(2)}, u32[]{:S(2)}) collective-permute-start(bf16[24,256]{1,0:T(8,128)(2,1)S(1)} %get-tuple-element.36), channel_id=1, source_target_pairs={{0,2},{2,4},{4,6},{6,8},{8,10},{10,12},{12,14},{14,16},{16,18},{18... | collective-permute-start | bytes 36872 | tf_op jit(solution)/shard_map/ppermute | solution.py:541
  16.8 9.4 %collective-permute-start.1 = (bf16[24,256]{1,0:T(8,128)(2,1)S(1)}, bf16[24,256]{1,0:T(8,128)(2,1)S(1)}, u32[]{:S(2)}, u32[]{:S(2)}) collective-permute-start(bf16[24,256]{1,0:T(8,128)(2,1)S(1)} %get-tuple-element.37), channel_id=1, source_target_pairs={{0,4},{2,6},{4,8},{6,10},{8,12},{10,14},{12,16},{14,18},{16,20},{1... | collective-permute-start | bytes 36872 | tf_op jit(solution)/shard_map/ppermute | solution.py:541
  18.5 9.3 %collective-permute-start.2 = (bf16[24,256]{1,0:T(8,128)(2,1)S(1)}, bf16[24,256]{1,0:T(8,128)(2,1)S(1)}, u32[]{:S(2)}, u32[]{:S(2)}) collective-permute-start(bf16[24,256]{1,0:T(8,128)(2,1)S(1)} %get-tuple-element.38), channel_id=1, source_target_pairs={{0,6},{2,8},{4,10},{6,12},{8,14},{10,16},{12,18},{14,20},{16,22},{... | collective-permute-start | bytes 36872 | tf_op jit(solution)/shard_map/ppermute | solution.py:541
  20.7 8.3 %collective-permute-start.3 = (bf16[24,256]{1,0:T(8,128)(2,1)S(1)}, bf16[24,256]{1,0:T(8,128)(2,1)S(1)}, u32[]{:S(2)}, u32[]{:S(2)}) collective-permute-start(bf16[24,256]{1,0:T(8,128)(2,1)S(1)} %get-tuple-element.39), channel_id=1, source_target_pairs={{0,8},{2,10},{4,12},{6,14},{8,16},{10,18},{12,20},{14,22},{16,24},... | collective-permute-start | bytes 36872 | tf_op jit(solution)/shard_map/ppermute | solution.py:541
  22.1 9.2 %collective-permute-start.4 = (bf16[24,256]{1,0:T(8,128)(2,1)S(1)}, bf16[24,256]{1,0:T(8,128)(2,1)S(1)}, u32[]{:S(2)}, u32[]{:S(2)}) collective-permute-start(bf16[24,256]{1,0:T(8,128)(2,1)S(1)} %get-tuple-element.40), channel_id=1, source_target_pairs={{0,10},{2,12},{4,14},{6,16},{8,18},{10,20},{12,22},{14,24},{16,26}... | collective-permute-start | bytes 36872 | tf_op jit(solution)/shard_map/ppermute | solution.py:541
  25.3 8.9 %collective-permute-start.5 = (bf16[24,256]{1,0:T(8,128)(2,1)S(1)}, bf16[24,256]{1,0:T(8,128)(2,1)S(1)}, u32[]{:S(2)}, u32[]{:S(2)}) collective-permute-start(bf16[24,256]{1,0:T(8,128)(2,1)S(1)} %get-tuple-element.41), channel_id=1, source_target_pairs={{0,12},{2,14},{4,16},{6,18},{8,20},{10,22},{12,24},{14,26},{16,28}... | collective-permute-start | bytes 36872 | tf_op jit(solution)/shard_map/ppermute | solution.py:541
  26.2 8.0 %collective-permute-start.6 = (bf16[24,256]{1,0:T(8,128)(2,1)S(1)}, bf16[24,256]{1,0:T(8,128)(2,1)S(1)}, u32[]{:S(2)}, u32[]{:S(2)}) collective-permute-start(bf16[24,256]{1,0:T(8,128)(2,1)S(1)} %get-tuple-element.42), channel_id=1, source_target_pairs={{0,14},{2,16},{4,18},{6,20},{8,22},{10,24},{12,26},{14,28},{16,30}... | collective-permute-start | bytes 36872 | tf_op jit(solution)/shard_map/ppermute | solution.py:541
  27.8 8.9 %collective-permute-start.7 = (bf16[24,256]{1,0:T(8,128)(2,1)S(1)}, bf16[24,256]{1,0:T(8,128)(2,1)S(1)}, u32[]{:S(2)}, u32[]{:S(2)}) collective-permute-start(bf16[24,256]{1,0:T(8,128)(2,1)S(1)} %get-tuple-element.43), channel_id=1, source_target_pairs={{0,16},{2,18},{4,20},{6,22},{8,24},{10,26},{12,28},{14,30},{16,0},... | collective-permute-start | bytes 36872 | tf_op jit(solution)/shard_map/ppermute | solution.py:541
  29.0 7.7 %collective-permute-start.8 = (bf16[24,256]{1,0:T(8,128)(2,1)S(1)}, bf16[24,256]{1,0:T(8,128)(2,1)S(1)}, u32[]{:S(2)}, u32[]{:S(2)}) collective-permute-start(bf16[24,256]{1,0:T(8,128)(2,1)S(1)} %get-tuple-element.44), channel_id=1, source_target_pairs={{0,18},{2,20},{4,22},{6,24},{8,26},{10,28},{12,30},{14,0},{16,2},{... | collective-permute-start | bytes 36872 | tf_op jit(solution)/shard_map/ppermute | solution.py:541
  31.3 5.7 %collective-permute-start.9 = (bf16[24,256]{1,0:T(8,128)(2,1)S(1)}, bf16[24,256]{1,0:T(8,128)(2,1)S(1)}, u32[]{:S(2)}, u32[]{:S(2)}) collective-permute-start(bf16[24,256]{1,0:T(8,128)(2,1)S(1)} %get-tuple-element.45), channel_id=1, source_target_pairs={{0,20},{2,22},{4,24},{6,26},{8,28},{10,30},{12,0},{14,2},{16,4},{1... | collective-permute-start | bytes 36872 | tf_op jit(solution)/shard_map/ppermute | solution.py:541
  34.2 7.4 %collective-permute-start.10 = (bf16[24,256]{1,0:T(8,128)(2,1)S(1)}, bf16[24,256]{1,0:T(8,128)(2,1)S(1)}, u32[]{:S(2)}, u32[]{:S(2)}) collective-permute-start(bf16[24,256]{1,0:T(8,128)(2,1)S(1)} %get-tuple-element.46), channel_id=1, source_target_pairs={{0,22},{2,24},{4,26},{6,28},{8,30},{10,0},{12,2},{14,4},{16,6},{18... | collective-permute-start | bytes 36872 | tf_op jit(solution)/shard_map/ppermute | solution.py:541
  34.2 7.4 %collective-permute-start.11 = (bf16[24,256]{1,0:T(8,128)(2,1)S(1)}, bf16[24,256]{1,0:T(8,128)(2,1)S(1)}, u32[]{:S(2)}, u32[]{:S(2)}) collective-permute-start(bf16[24,256]{1,0:T(8,128)(2,1)S(1)} %get-tuple-element.47), channel_id=1, source_target_pairs={{0,24},{2,26},{4,28},{6,30},{8,0},{10,2},{12,4},{14,6},{16,8},{18,... | collective-permute-start | bytes 36872 | tf_op jit(solution)/shard_map/ppermute | solution.py:541
  36.6 4.9 %collective-permute-start.12 = (bf16[24,256]{1,0:T(8,128)(2,1)S(1)}, bf16[24,256]{1,0:T(8,128)(2,1)S(1)}, u32[]{:S(2)}, u32[]{:S(2)}) collective-permute-start(bf16[24,256]{1,0:T(8,128)(2,1)S(1)} %get-tuple-element.48), channel_id=1, source_target_pairs={{0,26},{2,28},{4,30},{6,0},{8,2},{10,4},{12,6},{14,8},{16,10},{18,... | collective-permute-start | bytes 36872 | tf_op jit(solution)/shard_map/ppermute | solution.py:541
  36.6 4.9 %collective-permute-start.13 = (bf16[24,256]{1,0:T(8,128)(2,1)S(1)}, bf16[24,256]{1,0:T(8,128)(2,1)S(1)}, u32[]{:S(2)}, u32[]{:S(2)}) collective-permute-start(bf16[24,256]{1,0:T(8,128)(2,1)S(1)} %get-tuple-element.49), channel_id=1, source_target_pairs={{0,28},{2,30},{4,0},{6,2},{8,4},{10,6},{12,8},{14,10},{16,12},{18,... | collective-permute-start | bytes 36872 | tf_op jit(solution)/shard_map/ppermute | solution.py:541
  37.0 4.6 %collective-permute-start.14 = (bf16[24,256]{1,0:T(8,128)(2,1)S(1)}, bf16[24,256]{1,0:T(8,128)(2,1)S(1)}, u32[]{:S(2)}, u32[]{:S(2)}) collective-permute-start(bf16[24,256]{1,0:T(8,128)(2,1)S(1)} %get-tuple-element.50), channel_id=1, source_target_pairs={{0,30},{2,0},{4,2},{6,4},{8,6},{10,8},{12,10},{14,12},{16,14},{18,... | collective-permute-start | bytes 36872 | tf_op jit(solution)/shard_map/ppermute | solution.py:541
  41.5 8.6 %copy-start.2 = (bf16[2,128,4096]{2,1,0:T(8,128)(2,1)S(1)}, bf16[2,128,4096]{2,1,0:T(8,128)(2,1)}, u32[]{:S(2)}) copy-start(bf16[2,128,4096]{2,1,0:T(8,128)(2,1)} %copy-done.1) | copy-start | bytes 6291460
  45.3 17.1 %all-to-all-start.1 = ((bf16[16,48,256]{2,1,0:T(8,128)(2,1)}), bf16[16,48,256]{2,1,0:T(8,128)(2,1)S(1)}, u32[]{:S(2)}, u32[]{:S(2)}) async-start(bf16[16,48,256]{2,1,0:T(8,128)(2,1)} %copy-done.7), calls=%async_computation.1 | async-start | bytes 786432 | tf_op jit(solution)/shard_map/all_to_all | solution.py:600
  66.3 5.2 %copy-start.16 = (f32[4096]{0:T(1024)S(1)}, f32[4096]{0:T(1024)}, u32[]{:S(2)}) copy-start(f32[4096]{0:T(1024)} %param.20) | copy-start | bytes 49156
  67.8 3.6 %collective-permute-start.15 = (f32[1,128]{1,0:T(1,128)S(1)}, f32[1,128]{1,0:T(1,128)S(1)}, u32[]{:S(2)}, u32[]{:S(2)}) collective-permute-start(f32[1,128]{1,0:T(1,128)S(1)} %get-tuple-element.62), channel_id=1, source_target_pairs={{0,1},{1,0},{2,3},{3,2},{4,5},{5,4},{6,7},{7,6},{8,9},{9,8},{10,11... | collective-permute-start | bytes 1544 | tf_op jit(solution)/shard_map/ppermute | solution.py:620
  (11 other events, 12.6 us)

commit v4 on v3

v4 whole, which is shorter than its diff:
```python
import functools
from decimal import Decimal, getcontext

import jax
import jax.numpy as jnp
import ml_dtypes
import numpy as np
from jax import lax
from jax.experimental import pallas as pl
from jax.experimental.pallas import tpu as pltpu
from jax.sharding import PartitionSpec as P

F32, BF16 = jnp.float32, jnp.bfloat16
LANES = 128
SPAN = 256
STRETCH = 64
REACH = 6
INNER = STRETCH - REACH
PIVOTS = (8, 49, 21, 56, 36, 1)
ANCHORS = ("0.0020", "0.0235", "0.0110", "0.0295", "0.0185", "0.0004")
RANK = len(PIVOTS)
FINE = 2
COEFS = RANK + FINE
RAW = 6 * REACH
PIECE = RAW + COEFS
BACK = 2 * REACH + COEFS


def shape_table():
    getcontext().prec = 50
    rest = [[(-Decimal(a) * d).exp() for d in range(INNER)] for a in ANCHORS]
    table = []
    for p in range(RANK):
        shape = [x / rest[p][PIVOTS[p]] for x in rest[p]]
        rest = [[x - row[PIVOTS[p]] * y for x, y in zip(row, shape)] for row in rest]
        table.append([float(x) for x in shape])
    return table


SHAPE = shape_table()


def halves(values):
    high = values.astype(ml_dtypes.bfloat16)
    low = (values - high.astype(np.float32)).astype(ml_dtypes.bfloat16)
    return high, low


def constant_matrices():
    shape = np.array(SHAPE, np.float32)
    ends = np.zeros((16, STRETCH), np.float32)
    local = np.zeros((RANK, STRETCH, STRETCH), np.float32)
    lift = np.zeros((2, 2 * STRETCH, 2 * BACK), np.float32)
    parts = [h.astype(np.float32) for h in halves(shape)]
    for p in range(RANK):
        for s in range(REACH, STRETCH):
            ends[p, s] = shape[p, STRETCH - 1 - s]
            local[p, s:, s] = shape[p, : STRETCH - s]
        for half in range(2):
            rows = slice(half * STRETCH + REACH, (half + 1) * STRETCH)
            at = half * BACK + 2 * REACH
            for k in range(2):
                lift[k, rows, at + p] = parts[k][p]
                if p < FINE:
                    lift[k, rows, at + RANK + p] = parts[k][p]
    for half in range(2):
        for t in range(REACH):
            lift[0, half * STRETCH + t, half * BACK + t] = 1.0
            lift[0, half * STRETCH + t, half * BACK + REACH + t] = 1.0
    local = local.reshape(RANK * STRETCH, STRETCH)

    def triple(m):
        h, l = halves(m)
        return np.concatenate([h, h, l], axis=1)

    return triple(ends), triple(local), lift.astype(ml_dtypes.bfloat16)


def strengths(rate):
    found = []
    for p in range(RANK):
        value = jnp.exp(-rate * float(PIVOTS[p]))
        for q in range(p):
            value = value - found[q] * SHAPE[q][PIVOTS[p]]
        found.append(value)
    return found


def split(values):
    high = values.astype(BF16)
    return high, (values - high.astype(F32)).astype(BF16)


def amplitude(rate, residue):
    x = 2.0 * rate
    series = 1.0 - x * (0.5 - x * (1 / 6 - x * (1 / 24 - x * (1 / 120 - x * (1 / 720)))))
    return residue * jnp.sqrt(x * series)


EDGES = (0, STRETCH - 16, STRETCH, 2 * STRETCH - 16)


def front_kernel(*refs, direct):
    me_ref, q_ref, k_ref, v_ref, taps_ref, ends_ref = refs[:6]
    refs = refs[6:]
    weights, refs = (refs[:4], refs[4:]) if direct else ((), refs)
    pay_ref, u_ref, refs = refs[0], refs[1], refs[2:]
    kept, refs = (refs[:4], refs[4:]) if direct else ((), refs)
    held, edge, taps_vm, xs, qs, pay, packed, u_vm, in_sems, edge_sems, tap_sem, own_sems, out_sems = refs
    blocks = k_ref.shape[1] // SPAN

    def lanes(c):
        return pl.ds(pl.multiple_of(c * SPAN, SPAN), SPAN)

    def loads(c):
        return [
            pltpu.make_async_copy(ref.at[:, lanes(c)], held.at[a, :, lanes(c)], in_sems.at[a, c])
            for a, ref in enumerate((k_ref, v_ref))
        ]

    def edge_loads():
        return [
            pltpu.make_async_copy(q_ref.at[pl.ds(at, 16), :], edge.at[e], edge_sems.at[e])
            for e, at in enumerate(EDGES)
        ]

    def stores(c):
        target = pay_ref.at[c] if direct else pay_ref.at[:, lanes(c)]
        return [
            pltpu.make_async_copy(packed.at[c], target, out_sems.at[0, c]),
            pltpu.make_async_copy(u_vm.at[:, :, lanes(c)], u_ref.at[:, :, lanes(c)], out_sems.at[1, c]),
        ]

    def own_loads():
        share = kept[0].shape[-1]
        cols = pl.ds(pl.multiple_of(me_ref[0] * share, share), share)
        views = (weights[0].at[:, :, cols], weights[1].at[:, cols], weights[2].at[:, cols], weights[3].at[:, cols])
        return [pltpu.make_async_copy(view, ref, own_sems.at[n]) for n, (view, ref) in enumerate(zip(views, kept))]

    tap_copy = pltpu.make_async_copy(taps_ref, taps_vm, tap_sem.at[0])
    tap_copy.start()
    for copy in loads(0) + edge_loads():
        copy.start()

    def begin(c, carry):
        for copy in loads(c):
            copy.start()
        return carry

    lax.fori_loop(1, blocks, begin, 0)
    if direct:
        for copy in own_loads():
            copy.start()
    for parity in range(2):
        for a in range(2):
            for h in range(2):
                for i in range(2):
                    at = i * (STRETCH + 8)
                    xs[parity, a, h, at : at + 8, :] = jnp.zeros((8, LANES), F32)
    tap_copy.wait()

    def features(c):
        for copy in loads(c):
            copy.wait()
        parity = lax.rem(c, 2)
        for h in range(2):
            cols = pl.ds(pl.multiple_of(c * SPAN + h * LANES, LANES), LANES)
            for a in range(2):
                for i in range(2):
                    base = i * (STRETCH + 8) + 8
                    xs[parity, a, h, base : base + STRETCH, :] = held[
                        a, i * STRETCH : (i + 1) * STRETCH, cols
                    ].astype(F32)
            taps = [[taps_vm[a, j : j + 1, cols] for j in range(REACH + 1)] for a in (1, 2)]
            for i in range(2):
                for b in range(STRETCH // 16):
                    base = i * (STRETCH + 8) + 8 + 16 * b
                    both = []
                    for a in range(2):
                        total = taps[a][0] * xs[parity, a, h, base : base + 16, :]
                        for j in range(1, REACH + 1):
                            total = total + taps[a][j] * xs[parity, a, h, base - j : base - j + 16, :]
                        both.append(total)
                    mixed = both[0] * both[1]
                    if b == 0:
                        row = lax.broadcasted_iota(jnp.int32, (16, LANES), 0)
                        mixed = jnp.where(row >= REACH, mixed, 0.0)
                    high, low = split(mixed)
                    rows = slice(i * STRETCH + 16 * b, i * STRETCH + 16 * b + 16)
                    u_vm[0, rows, cols] = high
                    u_vm[1, rows, cols] = low

    def finish(c):
        parity = lax.rem(c, 2)
        for i in range(2):
            rows = slice(i * STRETCH, (i + 1) * STRETCH)
            high, low = u_vm[0, rows, lanes(c)], u_vm[1, rows, lanes(c)]
            moments = jnp.dot(
                ends_ref[...], jnp.concatenate([high, low, high], axis=0), preferred_element_type=F32
            )[:8]
            rest = (moments - moments.astype(BF16).astype(F32))[:FINE]
            at = PIECE * i + RAW
            for h in range(2):
                part = slice(h * LANES, (h + 1) * LANES)
                pay[h, at : at + RANK, :] = moments[:RANK, part]
                pay[h, at + RANK : at + COEFS, :] = rest[:, part]
        for h in range(2):
            cols = pl.ds(pl.multiple_of(c * SPAN + h * LANES, LANES), LANES)
            for i in range(2):
                base = i * (STRETCH + 8) + 8
                qs[h, i, 0:16, :] = edge[2 * i, :, cols].astype(F32)
                qs[h, i, 16:32, :] = edge[2 * i + 1, :, cols].astype(F32)
                at = i * PIECE
                pay[h, at : at + REACH, :] = qs[h, i, 32 - REACH : 32, :]
                pay[h, at + 3 * REACH : at + 4 * REACH, :] = qs[h, i, 0:REACH, :]
                for a in range(2):
                    at = i * PIECE + (1 + a) * REACH
                    pay[h, at : at + REACH, :] = xs[parity, a, h, base + STRETCH - REACH : base + STRETCH, :]
                    at = at + 3 * REACH
                    pay[h, at : at + REACH, :] = xs[parity, a, h, base : base + REACH, :]
            packed[c, :, h * LANES : (h + 1) * LANES] = pay[h].astype(BF16)
        for copy in stores(c):
            copy.start()

    features(0)
    for copy in edge_loads():
        copy.wait()

    def both(c, carry):
        finish(c - 1)
        features(c)
        return carry

    lax.fori_loop(1, blocks, both, 0)
    finish(blocks - 1)

    def end(c, carry):
        for copy in stores(c):
            copy.wait()
        return carry

    lax.fori_loop(0, blocks, end, 0)
    if direct:
        for copy in own_loads():
            copy.wait()


def local_kernel(q_ref, u_ref, taps_ref, rates_ref, res_ref, skip_ref, local_ref, qc_ref, y_ref, xs):
    tile = q_ref.shape[1]
    for g in range(tile // LANES):
        cols = slice(g * LANES, (g + 1) * LANES)
        taps = [taps_ref[0, j : j + 1, cols] for j in range(REACH + 1)]
        for i in range(2):
            base = i * (STRETCH + 8) + 8
            xs[g, base - 8 : base, :] = jnp.zeros((8, LANES), F32)
            xs[g, base : base + STRETCH, :] = q_ref[i * STRETCH : (i + 1) * STRETCH, cols].astype(F32)
            for b in range(STRETCH // 8):
                at = base + 8 * b
                total = taps[0] * xs[g, at : at + 8, :]
                for j in range(1, REACH + 1):
                    total = total + taps[j] * xs[g, at - j : at - j + 8, :]
                if b == 0:
                    row = lax.broadcasted_iota(jnp.int32, (8, LANES), 0)
                    total = jnp.where(row >= REACH, total, 1.0)
                qc_ref[i * STRETCH + 8 * b : i * STRETCH + 8 * b + 8, cols] = total
    span = min(tile, 2 * LANES)
    for c in range(tile // span):
        cols = slice(c * span, (c + 1) * span)
        rate = rates_ref[:, cols]
        amount = amplitude(rate, res_ref[:, cols])
        weights = [jnp.sum(amount * value, axis=0, keepdims=True) for value in strengths(rate)]
        for i in range(2):
            rows = slice(i * STRETCH, (i + 1) * STRETCH)
            high, low = u_ref[0, rows, cols], u_ref[1, rows, cols]
            parts = jnp.dot(
                local_ref[...], jnp.concatenate([high, low, high], axis=0), preferred_element_type=F32
            )
            total = skip_ref[:, cols] * (high.astype(F32) + low.astype(F32))
            for p in range(RANK):
                total = total + weights[p] * parts[p * STRETCH : (p + 1) * STRETCH, :]
            y_ref[rows, cols] = total


def middle_kernel(
    perm_ref, x_ref, taps_ref, rates_ref, res_ref, skip_ref, out_ref,
    raw, ext, moments, past, heads, first, second, states, mids, carried, result, packed, out_sems,
):
    slots = perm_ref.shape[0]
    groups = x_ref.shape[2] // LANES
    ext[:, :, 0, :, :] = jnp.zeros((3, groups, 16, LANES), F32)
    ext[:, :, :, 8:16, :] = jnp.zeros((3, groups, slots + 1, 8, LANES), F32)
    past[:, :, 0:8, :] = jnp.zeros((groups, slots, 8, LANES), F32)

    def unpack(src, carry):
        for g in range(groups):
            raw[g] = x_ref[src, :, g * LANES : (g + 1) * LANES].astype(F32)
        for i in range(2):
            n = perm_ref[2 * src + i]
            for g in range(groups):
                for a in range(3):
                    at = i * PIECE + a * REACH
                    ext[a, g, n + 1, 0:REACH, :] = raw[g, at : at + REACH, :]
                    at = at + 3 * REACH
                    ext[a, g, n, REACH : 2 * REACH, :] = raw[g, at : at + REACH, :]
                at = i * PIECE + RAW
                moments[g, n, 0:RANK, :] = raw[g, at : at + RANK, :]
                moments[g, n, 0:FINE, :] = moments[g, n, 0:FINE, :] + raw[g, at + RANK : at + COEFS, :]
        return carry

    lax.fori_loop(0, slots // 2, unpack, 0)
    row = lax.broadcasted_iota(jnp.int32, (8, LANES), 0)
    rate = [rates_ref[:, g * LANES : (g + 1) * LANES] for g in range(groups)]
    amount = [amplitude(rate[g], res_ref[:, g * LANES : (g + 1) * LANES]) for g in range(groups)]
    basis = [strengths(rate[g]) for g in range(groups)]

    for g in range(groups):
        cols = slice(g * LANES, (g + 1) * LANES)
        enter = [jnp.exp(-rate[g] * float(REACH - 1 - s)) for s in range(REACH)]
        taps = [[taps_ref[a, j : j + 1, cols] for j in range(REACH + 1)] for a in range(3)]
        near = [jnp.sum(amount[g] * jnp.exp(-rate[g] * float(d)), axis=0, keepdims=True) for d in range(REACH)]
        near[0] = near[0] + skip_ref[:, cols]

        def head_pass(n, carry, g=g, taps=taps, enter=enter, near=near):
            feats = []
            for a in range(3):
                total = taps[a][0] * ext[a, g, n, REACH : REACH + 8, :]
                for j in range(1, REACH + 1):
                    total = total + taps[a][j] * ext[a, g, n, REACH - j : REACH - j + 8, :]
                feats.append(jnp.where(row < REACH, total, 0.0))
            mixed = feats[1] * feats[2]
            past[g, n, 8:16, :] = mixed
            total = near[0] * mixed
            for d in range(1, REACH):
                total = total + near[d] * past[g, n, 8 - d : 16 - d, :]
            heads[g, n, 0:8, :] = feats[0]
            heads[g, n, 8:16, :] = total
            value = enter[0] * mixed[0:1, :]
            for s in range(1, REACH):
                value = value + enter[s] * mixed[s : s + 1, :]
            first[g, n] = value
            return carry

        lax.fori_loop(0, slots, head_pass, 0, unroll=2)

        def rest_pass(n, carry, g=g):
            value = basis[g][0] * moments[g, n, 0:1, :]
            for p in range(1, RANK):
                value = value + basis[g][p] * moments[g, n, p : p + 1, :]
            second[g, n] = value
            return carry

        lax.fori_loop(0, slots, rest_pass, 0, unroll=4)

    fade_head = [jnp.exp(-rate[g] * float(REACH)) for g in range(groups)]
    fade_rest = [jnp.exp(-rate[g] * float(INNER)) for g in range(groups)]

    def scan_pass(n, state):
        after = []
        for g in range(groups):
            states[g, n] = state[g]
            mid = fade_head[g] * state[g] + first[g, n]
            mids[g, n] = mid
            after.append(fade_rest[g] * mid + second[g, n])
        return tuple(after)

    lax.fori_loop(0, slots, scan_pass, tuple(jnp.zeros((16, LANES), F32) for _ in range(groups)), unroll=4)

    for g in range(groups):
        lifts = [amount[g] * jnp.exp(-rate[g] * float(t + 1)) for t in range(REACH)]
        next_amount = amount[g] * jnp.exp(-rate[g])
        spread = [next_amount * value for value in basis[g]]

        def out_pass(n, carry, g=g, lifts=lifts, spread=spread):
            state, mid = states[g, n], mids[g, n]
            for t in range(REACH):
                carried[g, n, t : 1 + t, :] = jnp.sum(lifts[t] * state, axis=0, keepdims=True)
                carried[g, n, 8 + t : 9 + t, :] = jnp.sum(spread[t] * mid, axis=0, keepdims=True)
            z = heads[g, n, 0:8, :] * (heads[g, n, 8:16, :] + carried[g, n, 0:8, :])
            high, low = split(z)
            result[g, n, 0:REACH, :] = high.astype(F32)[:REACH]
            result[g, n, REACH : 2 * REACH, :] = low.astype(F32)[:REACH]
            coefs = carried[g, n, 8:16, :]
            result[g, n, 2 * REACH : 2 * REACH + RANK, :] = coefs[:RANK]
            result[g, n, 2 * REACH + RANK : BACK, :] = (coefs - coefs.astype(BF16).astype(F32))[:FINE]
            return carry

        lax.fori_loop(0, slots, out_pass, 0, unroll=2)

    def store(src):
        return pltpu.make_async_copy(packed.at[src], out_ref.at[src], out_sems.at[src])

    def pack(src, carry):
        for g in range(groups):
            for i in range(2):
                raw[g, i * BACK : (i + 1) * BACK, :] = result[g, perm_ref[2 * src + i], 0:BACK, :]
            packed[src, :, g * LANES : (g + 1) * LANES] = raw[g, 0 : 2 * BACK, :].astype(BF16)
        store(src).start()
        return carry

    lax.fori_loop(0, slots // 2, pack, 0)

    def end(src, carry):
        store(src).wait()
        return carry

    lax.fori_loop(0, slots // 2, end, 0)


def join_kernel(back_ref, lift_ref, qc_ref, y_ref, z_ref, sq_ref, total):
    step = pl.program_id(0)
    part = jnp.zeros(total.shape, F32)
    by_dest = len(back_ref.shape) == 3
    span = back_ref.shape[-1] if by_dest else 2 * LANES
    for c in range(qc_ref.shape[1] // span):
        cols = slice(c * span, (c + 1) * span)
        back = back_ref[c] if by_dest else back_ref[:, cols]
        carry = jnp.dot(lift_ref[0], back, preferred_element_type=F32)
        carry = carry + jnp.dot(lift_ref[1], back, preferred_element_type=F32)
        z = qc_ref[:, cols] * (y_ref[:, cols] + carry)
        z_ref[:, cols] = z
        squares = z * z
        for g in range(span // LANES):
            part = part + squares[:, g * LANES : (g + 1) * LANES]

    @pl.when(step == 0)
    def _():
        total[...] = part

    @pl.when(step > 0)
    def _():
        total[...] += part

    @pl.when(step == pl.num_programs(0) - 1)
    def _():
        sq_ref[...] = jnp.sum(total[...].T, axis=0, keepdims=True)


def limit(mib):
    return pltpu.CompilerParams(vmem_limit_bytes=mib * 1024 * 1024)


def on_device(sizes, q_in, k_in, v_in, stretch_of_slot, short_weight, rates, residues, skip, gain):
    n_ctx, n_ch = sizes
    tokens, width = q_in.shape
    slots = stretch_of_slot.shape[0]
    order = rates.shape[0]
    share = width // n_ctx
    direct = share == SPAN
    tile = min(width, 1024)
    steps = width // tile
    groups = tile // LANES
    ends_np, local_np, lift_np = constant_matrices()
    ends, local, lift = jnp.asarray(ends_np), jnp.asarray(local_np), jnp.asarray(lift_np)
    skip, gain = skip.reshape(1, width), gain.reshape(1, width)
    me = lax.axis_index("ctx").astype(jnp.int32).reshape(1)

    def whole(array):
        return pl.BlockSpec(array.shape, lambda c: (0,) * array.ndim)

    def columns(*lead):
        return pl.BlockSpec((*lead, tile), lambda c: (0,) * len(lead) + (c,))

    def payload(rows):
        if direct:
            return (
                jax.ShapeDtypeStruct((n_ctx, rows, share), BF16),
                pl.BlockSpec((tile // share, rows, share), lambda c: (c, 0, 0)),
            )
        return jax.ShapeDtypeStruct((rows, width), BF16), columns(rows)

    def exchange(array):
        if direct:
            return lax.all_to_all(array, "ctx", 0, 0, tiled=True)
        array = array.reshape(array.shape[0], n_ctx, share).transpose(1, 0, 2)
        return widen(lax.all_to_all(array, "ctx", 0, 0, tiled=True))

    lanes = -(-share // LANES) * LANES

    def widen(array, fill=0.0):
        pad = [(0, 0)] * (array.ndim - 1) + [(0, lanes - share)]
        return jnp.pad(array, pad, constant_values=fill)

    def cut(array, fill=0.0):
        return widen(lax.dynamic_slice_in_dim(array, lax.axis_index("ctx") * share, share, array.ndim - 1), fill)

    smem = pl.BlockSpec(memory_space=pltpu.SMEM)
    vmem = pl.BlockSpec(memory_space=pltpu.VMEM)
    hbm = pl.BlockSpec(memory_space=pltpu.HBM)
    f32 = lambda *shape: jax.ShapeDtypeStruct(shape, F32)
    pin = lambda array: pltpu.with_memory_space_constraint(array, pltpu.HBM)

    weights = (short_weight, rates, residues, skip)
    own = [f32(*w.shape[:-1], share) for w in weights] if direct else []
    blocks = width // SPAN
    pay, mixed, *mine = pl.pallas_call(
        functools.partial(front_kernel, direct=direct),
        in_specs=[smem] + [hbm] * 4 + [vmem] + [hbm] * len(own),
        out_specs=[hbm] * 2 + [vmem] * len(own),
        out_shape=[
            pltpu.HBM((n_ctx, 2 * PIECE, share) if direct else (2 * PIECE, width), BF16),
            pltpu.HBM((2, tokens, width), BF16),
        ]
        + own,
        scratch_shapes=[
            pltpu.VMEM((2, tokens, width), BF16),
            pltpu.VMEM((4, 16, width), BF16),
            pltpu.VMEM(short_weight.shape, F32),
            pltpu.VMEM((2, 2, 2, 2 * (STRETCH + 8), LANES), F32),
            pltpu.VMEM((2, 2, 32, LANES), F32),
            pltpu.VMEM((2, 2 * PIECE, LANES), F32),
            pltpu.VMEM((blocks, 2 * PIECE, SPAN), BF16),
            pltpu.VMEM((2, tokens, width), BF16),
            pltpu.SemaphoreType.DMA((2, blocks)),
            pltpu.SemaphoreType.DMA((4,)),
            pltpu.SemaphoreType.DMA((1,)),
            pltpu.SemaphoreType.DMA((4,)),
            pltpu.SemaphoreType.DMA((2, blocks)),
        ],
        compiler_params=limit(24),
        name="front_pieces",
    )(me, *map(pin, (q_in, k_in, v_in, short_weight)), ends, *(map(pin, weights) if direct else ()))
    arrived = exchange(pay)
    if not direct:
        mine = (cut(short_weight), cut(rates, 0.01), cut(residues), cut(skip))

    query, inner = pl.pallas_call(
        local_kernel,
        grid=(steps,),
        in_specs=[
            columns(tokens),
            columns(2, tokens),
            columns(3, REACH + 1),
            columns(order),
            columns(order),
            columns(1),
            whole(local),
        ],
        out_specs=[columns(tokens)] * 2,
        out_shape=[pltpu.HBM((tokens, width), F32)] * 2,
        scratch_shapes=[pltpu.VMEM((groups, 2 * (STRETCH + 8), LANES), F32)],
        compiler_params=limit(24),
        name="local_filter",
        cost_estimate=pl.CostEstimate(flops=10**9, bytes_accessed=20 * 10**6, transcendentals=0),
    )(*map(pin, (q_in, mixed, short_weight, rates, residues)), skip, local)
    arrived, query, inner = lax.optimization_barrier((arrived, query, inner))

    groups = lanes // LANES
    back = pl.pallas_call(
        middle_kernel,
        in_specs=[smem] + [vmem] * 5,
        out_specs=hbm,
        scratch_shapes=[
            pltpu.VMEM((groups, 2 * PIECE, LANES), F32),
            pltpu.VMEM((3, groups, slots + 1, 16, LANES), F32),
            pltpu.VMEM((groups, slots, 8, LANES), F32),
            pltpu.VMEM((groups, slots, 16, LANES), F32),
            pltpu.VMEM((groups, slots, 16, LANES), F32),
            pltpu.VMEM((groups, slots, order, LANES), F32),
            pltpu.VMEM((groups, slots, order, LANES), F32),
            pltpu.VMEM((groups, slots, order, LANES), F32),
            pltpu.VMEM((groups, slots, order, LANES), F32),
            pltpu.VMEM((groups, slots, 16, LANES), F32),
            pltpu.VMEM((groups, slots, 24, LANES), F32),
            pltpu.VMEM((n_ctx, 2 * BACK, lanes), BF16),
            pltpu.SemaphoreType.DMA((n_ctx,)),
        ],
        out_shape=pltpu.HBM((n_ctx, 2 * BACK, lanes), BF16),
        compiler_params=limit(24),
        name="middle_states",
    )(stretch_of_slot, arrived, *mine)
    if not direct:
        back = back[:, :, :share]
    back = lax.all_to_all(back, "ctx", 0, 0, tiled=True)
    if not direct:
        back = back.transpose(1, 0, 2).reshape(2 * BACK, width)

    _, back_spec = payload(2 * BACK)
    zvalues, squares = pl.pallas_call(
        join_kernel,
        grid=(steps,),
        in_specs=[back_spec, whole(lift), columns(tokens), columns(tokens)],
        out_specs=[columns(tokens), pl.BlockSpec((1, tokens), lambda c: (0, 0))],
        out_shape=[
            jax.ShapeDtypeStruct((tokens, width), F32),
            jax.ShapeDtypeStruct((1, tokens), F32),
        ],
        scratch_shapes=[pltpu.VMEM((tokens, LANES), F32)],
        compiler_params=limit(24),
        name="join_carry",
    )(back, lift, pin(query), pin(inner))
    total = squares
    for shift in range(1, n_ch):
        total = total + lax.ppermute(squares, "ch", [(i, (i + shift) % n_ch) for i in range(n_ch)])
    scale = lax.rsqrt(total / (width * n_ch) + 1e-05)
    return (zvalues * scale.reshape(tokens, 1) * gain).astype(BF16)


def solution(mesh):
    sizes = (mesh.shape["ctx"], mesh.shape["ch"])
    in_specs = (
        P("ctx", "ch"),
        P("ctx", "ch"),
        P("ctx", "ch"),
        P(),
        P(None, None, "ch"),
        P(None, "ch"),
        P(None, "ch"),
        P("ch"),
        P("ch"),
    )

    def run(*arrays):
        return on_device(sizes, *arrays)

    return jax.shard_map(run, mesh=mesh, in_specs=in_specs, out_specs=P("ctx", "ch"), check_vma=False)
```

time: 73.4 us -> 64.7 us (0.88)
  starting transfers between devices: 32.7 us -> 8.95 us
  blocking collectives: 0 us -> 16.2 us
  local copies, waits for them, and re-layouts: 12.6 us -> 0.72 us
  waiting for transfers between devices: 7.63 us -> 13.5 us
  Pallas kernels: 18.3 us -> 23.6 us
    ppermute x15 -> x0, starting transfers between devices: 18.9 us -> none  [on_device(): lax.ppermute(outs[1 + shift], 'ctx', [(i, (i + shift) % n_ctx) for i in r...]
    all_to_all x0 -> x1, blocking collectives: none -> 16.2 us  [on_device(): back = lax.all_to_all(back, 'ctx', 0, 0, tiled=True)]
    unnamed x34 -> x12, local copies, waits for them, and re-layouts: 12.6 us -> 0.72 us
    all_to_all x1, waiting for transfers between devices: 0.01 us -> 11.4 us  [exchange(): return lax.all_to_all(array, 'ctx', 0, 0, tiled=True)]
    all_to_all x1 -> x0, starting transfers between devices: 4.85 us -> none  [on_device(): back = lax.all_to_all(back, 'ctx', 0, 0, tiled=True)]
    ppermute x15 -> x0, waiting for transfers between devices: 3.95 us -> none  [on_device(): lax.ppermute(outs[1 + shift], 'ctx', [(i, (i + shift) % n_ctx) for i in r...]
    pallas_call x1, Pallas kernels: 3.98 us -> 6.18 us  [on_device(): pl.pallas_call(local_kernel, grid=(steps,), in_specs=[columns(tokens), co...]
    pallas_call x1, Pallas kernels: 1.53 us -> 3.63 us  [on_device(): pl.pallas_call(join_kernel, grid=(steps,), in_specs=[back_spec, whole(lif...]
  transfers between devices with their start and end apart: 18 -> 2, of which waited for: 4 -> 2; matrix products, arithmetic and copies ran while one was open for 0% -> 0% of each run, Pallas kernels for 15% -> 10%
where the time goes in v4:
time: 64.7 us; the launch traced here: 64.3 us
  Pallas kernels  23.6 us (36%)
  blocking collectives  16.2 us (25%)
  waiting for transfers between devices  13.5 us (21%)
  starting transfers between devices  8.95 us (14%)
  other arithmetic  1.27 us (2%)
  local copies, waits for them, and re-layouts  0.72 us (1%)
    all_to_all x1, blocking collectives, on_device(): back = lax.all_to_all(back, 'ctx', 0, 0, tiled=True)  16.2 us
    all_to_all x1, waiting for transfers between devices, exchange(): return lax.all_to_all(array, 'ctx', 0, 0, tiled=True)  11.4 us
    pallas_call x1, Pallas kernels, on_device(): pl.pallas_call(functools.partial(front_kernel, direct=direct), in_specs=[...  8.19 us
    all_to_all x1, starting transfers between devices, exchange(): return lax.all_to_all(array, 'ctx', 0, 0, tiled=True)  7.37 us
    pallas_call x1, Pallas kernels, on_device(): pl.pallas_call(local_kernel, grid=(steps,), in_specs=[columns(tokens), co...  6.18 us
    pallas_call x1, Pallas kernels, on_device(): pl.pallas_call(middle_kernel, in_specs=[smem] + [vmem] * 5, out_specs=hbm...  5.56 us
    pallas_call x1, Pallas kernels, on_device(): pl.pallas_call(join_kernel, grid=(steps,), in_specs=[back_spec, whole(lif...  3.63 us
    ppermute x1, waiting for transfers between devices, on_device(): lax.ppermute(squares, 'ch', [(i, (i + shift) % n_ch) for i in range(n_ch)])  2.02 us
  transfers between devices with their start and end apart: 2, of which 2 were waited for; matrix products, arithmetic and copies ran while one was open for 0% of the time, Pallas kernels for 10%

profile of v4, /device:TPU:0, one launch (start us, length us, event | category | flops | bytes accessed | tf_op | source)
XLA Modules:
  0.0 64.3 jit_solution(13989740045190048731)
XLA Ops:
  0.0 0.0 copy-start.3
  0.0 0.7 %copy-done.3 = bf16[16,192]{1,0:T(8,128)(2,1)S(1)} copy-done((bf16[16,192]{1,0:T(8,128)(2,1)S(1)}, bf16[16,192]{1,0:T(8,128)(2,1)}, u32[]{:S(2)}) %copy-start.3) | copy-done | bytes 6168
  0.7 0.0 copy-start
  0.7 0.0 copy-start.2
  0.7 8.2 %front_pieces.1 = (bf16[16,88,256]{2,1,0:T(8,128)(2,1)}, bf16[2,128,4096]{2,1,0:T(8,128)(2,1)}, f32[3,7,256]{2,1,0:T(8,128)S(1)}, f32[16,256]{1,0:T(8,128)S(1)},...) custom-call(s32[1]{0:T(128)} %bitcast.refs_0_, bf16[128,4096]{1,0:T(8,128)(2,1)} %q_ref.1, bf16[128,4096]{1,0:T(8,128)(2,1)} %refs_2_.1, ...), custom_call_target="tpu_custom_call" | custom-call | tf_op jit(solution)/shard_map/front_pieces/pallas_call | solution.py:495
  8.9 7.4 %all-to-all-start = ((bf16[16,88,256]{2,1,0:T(8,128)(2,1)}), bf16[16,88,256]{2,1,0:T(8,128)(2,1)S(1)}, u32[]{:S(2)}, u32[]{:S(2)}) async-start(bf16[16,88,256]{2,1,0:T(8,128)(2,1)} %get-tuple-element.18), calls=%async_computation | async-start | bytes 1441792 | tf_op jit(solution)/shard_map/all_to_all | solution.py:473
  16.3 0.0 copy-done
  16.3 0.0 copy-done.2
  16.3 0.0 copy-start.4
  16.3 0.0 copy-start.1
  16.3 6.2 %local_filter.1 = (f32[128,4096]{1,0:T(8,128)}, f32[128,4096]{1,0:T(8,128)}) custom-call(bf16[128,4096]{1,0:T(8,128)(2,1)} %q_ref.1, bf16[2,128,4096]{2,1,0:T(8,128)(2,1)} %get-tuple-element.19.u_ref, f32[3,7,4096]{2,1,0:T(8,128)} %taps_ref.1, f32[16,4096]{1,0:T(8,128)} %rates_ref.1, f32[16,4096]{1,0:T(8,128)} %res_ref.1, f32[1,4096]{1,0:T(1,128)S(1)} %bitcast.5, ...), custom_call_target="tpu_custom_call" | custom-call | flops 1000000000 | bytes 20000000 | tf_op jit(solution)/shard_map/local_filter/pallas_call | solution.py:526
  22.5 11.4 %all-to-all-done.x_ref = bf16[16,88,256]{2,1,0:T(8,128)(2,1)S(1)} async-done(((bf16[16,88,256]{2,1,0:T(8,128)(2,1)}), bf16[16,88,256]{2,1,0:T(8,128)(2,1)S(1)}, u32[]{:S(2)}, u32[]{:S(2)}) %all-to-all-start) | async-done | bytes 720928 | tf_op jit(solution)/shard_map/all_to_all | solution.py:473
  33.9 0.0 copy-done.4
  33.9 5.6 %middle_states.1 = bf16[16,40,256]{2,1,0:T(8,128)(2,1)} custom-call(s32[32]{0:T(128)S(1)} %copy-done.4, bf16[16,88,256]{2,1,0:T(8,128)(2,1)S(1)} %all-to-all-done.x_ref, f32[3,7,256]{2,1,0:T(8,128)S(1)} %get-tuple-element.23.taps_ref, f32[16,256]{1,0:T(8,128)S(1)} %get-tuple-element.24.rates_ref, f32[16,256]{1,0:T(8,128)S(1)} %get-tuple-element.25.res_ref, ...), custom_call_target="tpu_custom_call" | custom-call | tf_op jit(solution)/shard_map/middle_states/pallas_call | solution.py:548
  39.5 16.2 %all_to_all.10.back_ref = bf16[16,40,256]{2,1,0:T(8,128)(2,1)S(1)} all-to-all(bf16[16,40,256]{2,1,0:T(8,128)(2,1)} %middle_states.1), channel_id=1, replica_groups=mesh['ctx'=16,'ch'=2] {'ctx'}, dimensions={0} | all-to-all | bytes 655360 | tf_op jit(solution)/shard_map/all_to_all | solution.py:573
  55.7 0.0 copy-done.1
  55.7 0.0 copy-start.5
  55.7 3.6 %join_carry.1 = (f32[128,4096]{1,0:T(8,128)S(1)}, f32[1,128]{1,0:T(1,128)S(1)}) custom-call(bf16[16,40,256]{2,1,0:T(8,128)(2,1)S(1)} %all_to_all.10.back_ref, bf16[2,128,40]{2,1,0:T(8,128)(2,1)S(1)} %copy-done.1, f32[128,4096]{1,0:T(8,128)} %get-tuple-element.27.qc_ref, f32[128,4096]{1,0:T(8,128)} %get-tuple-element.28.y_ref), custom_call_target="tpu_custom_call" | custom-call | tf_op jit(solution)/shard_map/join_carry/pallas_call | solution.py:578
  59.4 1.6 %collective-permute-start = (f32[1,128]{1,0:T(1,128)S(1)}, f32[1,128]{1,0:T(1,128)S(1)}, u32[]{:S(2)}, u32[]{:S(2)}) collective-permute-start(f32[1,128]{1,0:T(1,128)S(1)} %get-tuple-element.30), channel_id=1, source_target_pairs={{0,1},{1,0},{2,3},{3,2},{4,5},{5,4},{6,7},{7,6},{8,9},{9,8},{10,11... | collective-permute-start | bytes 1544 | tf_op jit(solution)/shard_map/ppermute | solution.py:593
  61.0 2.0 %collective-permute-done = f32[1,128]{1,0:T(1,128)S(1)} collective-permute-done((f32[1,128]{1,0:T(1,128)S(1)}, f32[1,128]{1,0:T(1,128)S(1)}, u32[]{:S(2)}, u32[]{:S(2)}) %collective-permute-start) | collective-permute-done | bytes 544 | tf_op jit(solution)/shard_map/ppermute | solution.py:593
  63.0 0.0 copy-done.5
  63.0 1.3 %multiply_convert_fusion = bf16[128,4096]{1,0:T(8,128)(2,1)} fusion(f32[128,4096]{1,0:T(8,128)S(1)} %get-tuple-element.29, f32[4096]{0:T(1024)S(1)} %copy-done.5, f32[128]{0:T(128)S(1)} %rsqrt_bitcast_fusion), kind=kLoop, calls=%fused_computation | loop fusion | flops 1572864 | bytes 3162624 | tf_op jit(solution)/shard_map/convert_element_type | solution.py:595
  (1 shorter events, 0.0 us)
Async XLA Ops:
  0.0 0.7 %copy-start.3 = (bf16[16,192]{1,0:T(8,128)(2,1)S(1)}, bf16[16,192]{1,0:T(8,128)(2,1)}, u32[]{:S(2)}) copy-start(bf16[16,192]{1,0:T(8,128)(2,1)} %constant.17.clone.refs_5_) | copy-start | bytes 18436
  0.7 15.6 %copy-start = (bf16[384,192]{1,0:T(8,128)(2,1)S(1)}, bf16[384,192]{1,0:T(8,128)(2,1)}, u32[]{:S(2)}) copy-start(bf16[384,192]{1,0:T(8,128)(2,1)} %constant.18.clone.local_ref) | copy-start | bytes 442372
  0.7 15.6 %copy-start.2 = (f32[4096]{0:T(1024)S(1)}, f32[4096]{0:T(1024)}, u32[]{:S(2)}) copy-start(f32[4096]{0:T(1024)} %param.19) | copy-start | bytes 49156
  8.9 25.0 %all-to-all-start = ((bf16[16,88,256]{2,1,0:T(8,128)(2,1)}), bf16[16,88,256]{2,1,0:T(8,128)(2,1)S(1)}, u32[]{:S(2)}, u32[]{:S(2)}) async-start(bf16[16,88,256]{2,1,0:T(8,128)(2,1)} %get-tuple-element.18), calls=%async_computation | async-start | bytes 1441792 | tf_op jit(solution)/shard_map/all_to_all | solution.py:473
  16.3 17.6 %copy-start.4 = (s32[32]{0:T(128)S(1)}, s32[32]{0:T(128)}, u32[]{:S(2)}) copy-start(s32[32]{0:T(128)} %perm_ref.1) | copy-start | bytes 388
  16.3 39.4 %copy-start.1 = (bf16[2,128,40]{2,1,0:T(8,128)(2,1)S(1)}, bf16[2,128,40]{2,1,0:T(8,128)(2,1)}, u32[]{:S(2)}) copy-start(bf16[2,128,40]{2,1,0:T(8,128)(2,1)} %constant.19.clone.lift_ref) | copy-start | bytes 61444
  55.7 7.3 %copy-start.5 = (f32[4096]{0:T(1024)S(1)}, f32[4096]{0:T(1024)}, u32[]{:S(2)}) copy-start(f32[4096]{0:T(1024)} %param.20) | copy-start | bytes 49156
  59.4 3.6 %collective-permute-start = (f32[1,128]{1,0:T(1,128)S(1)}, f32[1,128]{1,0:T(1,128)S(1)}, u32[]{:S(2)}, u32[]{:S(2)}) collective-permute-start(f32[1,128]{1,0:T(1,128)S(1)} %get-tuple-element.30), channel_id=1, source_target_pairs={{0,1},{1,0},{2,3},{3,2},{4,5},{5,4},{6,7},{7,6},{8,9},{9,8},{10,11... | collective-permute-start | bytes 1544 | tf_op jit(solution)/shard_map/ppermute | solution.py:593

commit v5 on v4

--- a/solution.py
+++ b/solution.py
@@ -106,7 +106,7 @@
     weights, refs = (refs[:4], refs[4:]) if direct else ((), refs)
     pay_ref, u_ref, refs = refs[0], refs[1], refs[2:]
     kept, refs = (refs[:4], refs[4:]) if direct else ((), refs)
-    held, edge, taps_vm, xs, qs, pay, packed, u_vm, in_sems, edge_sems, tap_sem, own_sems, out_sems = refs
+    held, edge, taps_vm, ends_vm, xs, qs, pay, packed, u_vm, in_sems, edge_sems, tap_sem, own_sems, out_sems = refs
     blocks = k_ref.shape[1] // SPAN
 
     def lanes(c):
@@ -128,7 +128,7 @@
         target = pay_ref.at[c] if direct else pay_ref.at[:, lanes(c)]
         return [
             pltpu.make_async_copy(packed.at[c], target, out_sems.at[0, c]),
-            pltpu.make_async_copy(u_vm.at[:, :, lanes(c)], u_ref.at[:, :, lanes(c)], out_sems.at[1, c]),
+            pltpu.make_async_copy(u_vm.at[c], u_ref.at[c], out_sems.at[1, c]),
         ]
 
     def own_loads():
@@ -138,7 +138,9 @@
         return [pltpu.make_async_copy(view, ref, own_sems.at[n]) for n, (view, ref) in enumerate(zip(views, kept))]
 
     tap_copy = pltpu.make_async_copy(taps_ref, taps_vm, tap_sem.at[0])
+    ends_copy = pltpu.make_async_copy(ends_ref, ends_vm, tap_sem.at[1])
     tap_copy.start()
+    ends_copy.start()
     for copy in loads(0) + edge_loads():
         copy.start()
 
@@ -158,12 +160,16 @@
                     at = i * (STRETCH + 8)
                     xs[parity, a, h, at : at + 8, :] = jnp.zeros((8, LANES), F32)
     tap_copy.wait()
-
-    def features(c):
+    ends_copy.wait()
+
+    def arrive(c):
         for copy in loads(c):
             copy.wait()
+
+    def features(c):
         parity = lax.rem(c, 2)
         for h in range(2):
+            part = slice(h * LANES, (h + 1) * LANES)
             cols = pl.ds(pl.multiple_of(c * SPAN + h * LANES, LANES), LANES)
             for a in range(2):
                 for i in range(2):
@@ -187,17 +193,22 @@
                         mixed = jnp.where(row >= REACH, mixed, 0.0)
                     high, low = split(mixed)
                     rows = slice(i * STRETCH + 16 * b, i * STRETCH + 16 * b + 16)
-                    u_vm[0, rows, cols] = high
-                    u_vm[1, rows, cols] = low
-
-    def finish(c):
+                    u_vm[c, 0, rows, part] = high
+                    u_vm[c, 1, rows, part] = low
+
+    def products(c):
+        found = []
+        for i in range(2):
+            rows = slice(i * STRETCH, (i + 1) * STRETCH)
+            high, low = u_vm[c, 0, rows, :], u_vm[c, 1, rows, :]
+            stacked = jnp.concatenate([high, low, high], axis=0)
+            found.append(jnp.dot(ends_vm[...], stacked, preferred_element_type=F32)[:8])
+        return found
+
+    def finish(c, found):
         parity = lax.rem(c, 2)
         for i in range(2):
-            rows = slice(i * STRETCH, (i + 1) * STRETCH)
-            high, low = u_vm[0, rows, lanes(c)], u_vm[1, rows, lanes(c)]
-            moments = jnp.dot(
-                ends_ref[...], jnp.concatenate([high, low, high], axis=0), preferred_element_type=F32
-            )[:8]
+            moments = found[i]
             rest = (moments - moments.astype(BF16).astype(F32))[:FINE]
             at = PIECE * i + RAW
             for h in range(2):
@@ -219,20 +230,27 @@
                     at = at + 3 * REACH
                     pay[h, at : at + REACH, :] = xs[parity, a, h, base : base + REACH, :]
             packed[c, :, h * LANES : (h + 1) * LANES] = pay[h].astype(BF16)
+
+    def send(c):
         for copy in stores(c):
             copy.start()
 
-    features(0)
+    arrive(0)
     for copy in edge_loads():
         copy.wait()
+    features(0)
 
     def both(c, carry):
-        finish(c - 1)
+        arrive(c)
+        found = products(c - 1)
         features(c)
+        finish(c - 1, found)
+        send(c - 1)
         return carry
 
     lax.fori_loop(1, blocks, both, 0)
-    finish(blocks - 1)
+    finish(blocks - 1, products(blocks - 1))
+    send(blocks - 1)
 
     def end(c, carry):
         for copy in stores(c):
@@ -247,8 +265,10 @@
 
 def local_kernel(q_ref, u_ref, taps_ref, rates_ref, res_ref, skip_ref, local_ref, qc_ref, y_ref, xs):
     tile = q_ref.shape[1]
+    per = SPAN // LANES
     for g in range(tile // LANES):
         cols = slice(g * LANES, (g + 1) * LANES)
+        part = slice(g % per * LANES, (g % per + 1) * LANES)
         taps = [taps_ref[0, j : j + 1, cols] for j in range(REACH + 1)]
         for i in range(2):
             base = i * (STRETCH + 8) + 8
@@ -262,129 +282,152 @@
                 if b == 0:
                     row = lax.broadcasted_iota(jnp.int32, (8, LANES), 0)
                     total = jnp.where(row >= REACH, total, 1.0)
-                qc_ref[i * STRETCH + 8 * b : i * STRETCH + 8 * b + 8, cols] = total
-    span = min(tile, 2 * LANES)
-    for c in range(tile // span):
-        cols = slice(c * span, (c + 1) * span)
+                qc_ref[g // per, i * STRETCH + 8 * b : i * STRETCH + 8 * b + 8, part] = total
+    for c in range(tile // SPAN):
+        cols = slice(c * SPAN, (c + 1) * SPAN)
         rate = rates_ref[:, cols]
         amount = amplitude(rate, res_ref[:, cols])
         weights = [jnp.sum(amount * value, axis=0, keepdims=True) for value in strengths(rate)]
         for i in range(2):
             rows = slice(i * STRETCH, (i + 1) * STRETCH)
-            high, low = u_ref[0, rows, cols], u_ref[1, rows, cols]
+            high, low = u_ref[c, 0, rows, :], u_ref[c, 1, rows, :]
             parts = jnp.dot(
                 local_ref[...], jnp.concatenate([high, low, high], axis=0), preferred_element_type=F32
             )
             total = skip_ref[:, cols] * (high.astype(F32) + low.astype(F32))
             for p in range(RANK):
                 total = total + weights[p] * parts[p * STRETCH : (p + 1) * STRETCH, :]
-            y_ref[rows, cols] = total
+            y_ref[c, rows, :] = total
 
 
 def middle_kernel(
     perm_ref, x_ref, taps_ref, rates_ref, res_ref, skip_ref, out_ref,
-    raw, ext, moments, past, heads, first, second, states, mids, carried, result, packed, out_sems,
+    raw, ext, moments, past, heads, first, second, states, mids, coefs, result, slab, packed, out_sems,
 ):
     slots = perm_ref.shape[0]
     groups = x_ref.shape[2] // LANES
-    ext[:, :, 0, :, :] = jnp.zeros((3, groups, 16, LANES), F32)
-    ext[:, :, :, 8:16, :] = jnp.zeros((3, groups, slots + 1, 8, LANES), F32)
+    order = rates_ref.shape[0]
+    span = 2 * PIECE
+    row = lax.broadcasted_iota(jnp.int32, (8, LANES), 0)
+    ext[:, :, 0, 0:8, :] = jnp.zeros((3, groups, 8, LANES), F32)
     past[:, :, 0:8, :] = jnp.zeros((groups, slots, 8, LANES), F32)
 
     def unpack(src, carry):
         for g in range(groups):
-            raw[g] = x_ref[src, :, g * LANES : (g + 1) * LANES].astype(F32)
+            raw[src, g, 8 : 8 + span, :] = x_ref[src, :, g * LANES : (g + 1) * LANES].astype(F32)
         for i in range(2):
             n = perm_ref[2 * src + i]
             for g in range(groups):
                 for a in range(3):
-                    at = i * PIECE + a * REACH
-                    ext[a, g, n + 1, 0:REACH, :] = raw[g, at : at + REACH, :]
+                    at = 8 + i * PIECE + a * REACH
+                    ext[a, g, n + 1, 0:8, :] = raw[src, g, at + REACH - 8 : at + REACH, :]
                     at = at + 3 * REACH
-                    ext[a, g, n, REACH : 2 * REACH, :] = raw[g, at : at + REACH, :]
-                at = i * PIECE + RAW
-                moments[g, n, 0:RANK, :] = raw[g, at : at + RANK, :]
-                moments[g, n, 0:FINE, :] = moments[g, n, 0:FINE, :] + raw[g, at + RANK : at + COEFS, :]
-        return carry
-
-    lax.fori_loop(0, slots // 2, unpack, 0)
-    row = lax.broadcasted_iota(jnp.int32, (8, LANES), 0)
-    rate = [rates_ref[:, g * LANES : (g + 1) * LANES] for g in range(groups)]
-    amount = [amplitude(rate[g], res_ref[:, g * LANES : (g + 1) * LANES]) for g in range(groups)]
-    basis = [strengths(rate[g]) for g in range(groups)]
-
+                    ext[a, g, n, 8:16, :] = raw[src, g, at : at + 8, :]
+                at = 8 + i * PIECE + RAW
+                fine = jnp.where(row < FINE, raw[src, g, at + RANK : at + RANK + 8, :], 0.0)
+                moments[g, n] = raw[src, g, at : at + 8, :] + fine
+        return carry
+
+    lax.fori_loop(0, slots // 2, unpack, 0, unroll=2)
+
+    fades = []
     for g in range(groups):
         cols = slice(g * LANES, (g + 1) * LANES)
-        enter = [jnp.exp(-rate[g] * float(REACH - 1 - s)) for s in range(REACH)]
+        rate = rates_ref[:, cols]
+        amount = amplitude(rate, res_ref[:, cols])
+        basis = strengths(rate)
+        powers = [jnp.ones_like(rate), jnp.exp(-rate)]
+        for d in range(2, REACH + 1):
+            powers.append(powers[-1] * powers[1])
+        for t in range(REACH):
+            coefs[g, 0, t * order : (t + 1) * order, :] = amount * powers[t + 1]
+        for p in range(RANK):
+            coefs[g, 1, p * order : (p + 1) * order, :] = amount * powers[1] * basis[p]
+        fade_rest = jnp.exp(-rate * float(INNER))
+        fades.append((powers[REACH], fade_rest, fade_rest * powers[REACH]))
         taps = [[taps_ref[a, j : j + 1, cols] for j in range(REACH + 1)] for a in range(3)]
-        near = [jnp.sum(amount[g] * jnp.exp(-rate[g] * float(d)), axis=0, keepdims=True) for d in range(REACH)]
+        near = [jnp.sum(amount * powers[d], axis=0, keepdims=True) for d in range(REACH)]
         near[0] = near[0] + skip_ref[:, cols]
 
-        def head_pass(n, carry, g=g, taps=taps, enter=enter, near=near):
+        def head_pass(n, carry, g=g, taps=taps, powers=powers, near=near):
             feats = []
             for a in range(3):
-                total = taps[a][0] * ext[a, g, n, REACH : REACH + 8, :]
+                total = taps[a][0] * ext[a, g, n, 8:16, :]
                 for j in range(1, REACH + 1):
-                    total = total + taps[a][j] * ext[a, g, n, REACH - j : REACH - j + 8, :]
+                    total = total + taps[a][j] * ext[a, g, n, 8 - j : 16 - j, :]
                 feats.append(jnp.where(row < REACH, total, 0.0))
             mixed = feats[1] * feats[2]
             past[g, n, 8:16, :] = mixed
             total = near[0] * mixed
             for d in range(1, REACH):
                 total = total + near[d] * past[g, n, 8 - d : 16 - d, :]
-            heads[g, n, 0:8, :] = feats[0]
-            heads[g, n, 8:16, :] = total
-            value = enter[0] * mixed[0:1, :]
+            at = pl.multiple_of(n * 16, 16)
+            heads[g, pl.ds(at, 8), :] = feats[0]
+            heads[g, pl.ds(at + 8, 8), :] = total
+            value = powers[REACH - 1] * past[g, n, 8:9, :]
             for s in range(1, REACH):
-                value = value + enter[s] * mixed[s : s + 1, :]
+                value = value + powers[REACH - 1 - s] * past[g, n, 8 + s : 9 + s, :]
             first[g, n] = value
             return carry
 
-        lax.fori_loop(0, slots, head_pass, 0, unroll=2)
-
-        def rest_pass(n, carry, g=g):
-            value = basis[g][0] * moments[g, n, 0:1, :]
-            for p in range(1, RANK):
-                value = value + basis[g][p] * moments[g, n, p : p + 1, :]
+        lax.fori_loop(0, slots, head_pass, 0, unroll=4)
+
+        def rest_pass(n, carry, g=g, basis=basis, fade_rest=fade_rest):
+            value = fade_rest * first[g, n]
+            for p in range(RANK):
+                value = value + basis[p] * moments[g, n, p : p + 1, :]
             second[g, n] = value
             return carry
 
         lax.fori_loop(0, slots, rest_pass, 0, unroll=4)
 
-    fade_head = [jnp.exp(-rate[g] * float(REACH)) for g in range(groups)]
-    fade_rest = [jnp.exp(-rate[g] * float(INNER)) for g in range(groups)]
-
     def scan_pass(n, state):
         after = []
+        at = pl.multiple_of(n * order, order)
         for g in range(groups):
-            states[g, n] = state[g]
-            mid = fade_head[g] * state[g] + first[g, n]
-            mids[g, n] = mid
-            after.append(fade_rest[g] * mid + second[g, n])
+            states[g, pl.ds(at, order), :] = state[g]
+            mids[g, pl.ds(at, order), :] = fades[g][0] * state[g] + first[g, n]
+            after.append(fades[g][2] * state[g] + second[g, n])
         return tuple(after)
 
-    lax.fori_loop(0, slots, scan_pass, tuple(jnp.zeros((16, LANES), F32) for _ in range(groups)), unroll=4)
-
-    for g in range(groups):
-        lifts = [amount[g] * jnp.exp(-rate[g] * float(t + 1)) for t in range(REACH)]
-        next_amount = amount[g] * jnp.exp(-rate[g])
-        spread = [next_amount * value for value in basis[g]]
-
-        def out_pass(n, carry, g=g, lifts=lifts, spread=spread):
-            state, mid = states[g, n], mids[g, n]
+    lax.fori_loop(0, slots, scan_pass, tuple(jnp.zeros((order, LANES), F32) for _ in range(groups)), unroll=4)
+
+    quad = 4
+
+    def sums(g, kind, held, first_tile):
+        totals = [[None] * quad for _ in range(RANK)]
+        for r in range(order):
+            values = [held[g, pl.ds((first_tile + k) * 8 * order + r, 8, stride=order), :] for k in range(quad)]
+            for p in range(RANK):
+                weight = coefs[g, kind, p * order + r : p * order + r + 1, :]
+                for k in range(quad):
+                    term = weight * values[k]
+                    totals[p][k] = term if r == 0 else totals[p][k] + term
+        return totals
+
+    def out_pass(q, carry):
+        for g in range(groups):
+            totals = sums(g, 0, states, q * quad)
             for t in range(REACH):
-                carried[g, n, t : 1 + t, :] = jnp.sum(lifts[t] * state, axis=0, keepdims=True)
-                carried[g, n, 8 + t : 9 + t, :] = jnp.sum(spread[t] * mid, axis=0, keepdims=True)
-            z = heads[g, n, 0:8, :] * (heads[g, n, 8:16, :] + carried[g, n, 0:8, :])
-            high, low = split(z)
-            result[g, n, 0:REACH, :] = high.astype(F32)[:REACH]
-            result[g, n, REACH : 2 * REACH, :] = low.astype(F32)[:REACH]
-            coefs = carried[g, n, 8:16, :]
-            result[g, n, 2 * REACH : 2 * REACH + RANK, :] = coefs[:RANK]
-            result[g, n, 2 * REACH + RANK : BACK, :] = (coefs - coefs.astype(BF16).astype(F32))[:FINE]
-            return carry
-
-        lax.fori_loop(0, slots, out_pass, 0, unroll=2)
+                for k in range(quad):
+                    tile = q * quad + k
+                    query = heads[g, pl.ds(tile * 128 + t, 8, stride=16), :]
+                    local = heads[g, pl.ds(tile * 128 + 8 + t, 8, stride=16), :]
+                    z = query * (local + totals[t][k])
+                    result[g, pl.ds(tile * 192 + t, 8, stride=24), :] = z
+                    result[g, pl.ds(tile * 192 + REACH + t, 8, stride=24), :] = z - z.astype(BF16).astype(F32)
+            totals = sums(g, 1, mids, q * quad)
+            for p in range(RANK):
+                for k in range(quad):
+                    tile = q * quad + k
+                    value = totals[p][k]
+                    result[g, pl.ds(tile * 192 + 2 * REACH + p, 8, stride=24), :] = value
+                    if p < FINE:
+                        rest = value - value.astype(BF16).astype(F32)
+                        result[g, pl.ds(tile * 192 + 2 * REACH + RANK + p, 8, stride=24), :] = rest
+        return carry
+
+    lax.fori_loop(0, slots // (8 * quad), out_pass, 0)
 
     def store(src):
         return pltpu.make_async_copy(packed.at[src], out_ref.at[src], out_sems.at[src])
@@ -392,47 +435,56 @@
     def pack(src, carry):
         for g in range(groups):
             for i in range(2):
-                raw[g, i * BACK : (i + 1) * BACK, :] = result[g, perm_ref[2 * src + i], 0:BACK, :]
-            packed[src, :, g * LANES : (g + 1) * LANES] = raw[g, 0 : 2 * BACK, :].astype(BF16)
+                at = pl.multiple_of(perm_ref[2 * src + i] * 24, 8)
+                slab[src, g, i * BACK : i * BACK + 24, :] = result[g, pl.ds(at, 24), :]
+            packed[src, :, g * LANES : (g + 1) * LANES] = slab[src, g, 0 : 2 * BACK, :].astype(BF16)
+        return carry
+
+    lax.fori_loop(0, slots // 2, pack, 0, unroll=2)
+
+    def send(src, carry):
         store(src).start()
         return carry
-
-    lax.fori_loop(0, slots // 2, pack, 0)
 
     def end(src, carry):
         store(src).wait()
         return carry
 
+    lax.fori_loop(0, slots // 2, send, 0)
     lax.fori_loop(0, slots // 2, end, 0)
 
 
-def join_kernel(back_ref, lift_ref, qc_ref, y_ref, z_ref, sq_ref, total):
-    step = pl.program_id(0)
-    part = jnp.zeros(total.shape, F32)
+def join_kernel(back_ref, lift_ref, qc_ref, y_ref, z_ref, sq_ref, qc_vm, y_vm, carry, sems):
+    blocks, tokens, _ = qc_vm.shape
     by_dest = len(back_ref.shape) == 3
-    span = back_ref.shape[-1] if by_dest else 2 * LANES
-    for c in range(qc_ref.shape[1] // span):
-        cols = slice(c * span, (c + 1) * span)
-        back = back_ref[c] if by_dest else back_ref[:, cols]
-        carry = jnp.dot(lift_ref[0], back, preferred_element_type=F32)
-        carry = carry + jnp.dot(lift_ref[1], back, preferred_element_type=F32)
-        z = qc_ref[:, cols] * (y_ref[:, cols] + carry)
-        z_ref[:, cols] = z
-        squares = z * z
-        for g in range(span // LANES):
-            part = part + squares[:, g * LANES : (g + 1) * LANES]
-
-    @pl.when(step == 0)
-    def _():
-        total[...] = part
-
-    @pl.when(step > 0)
-    def _():
-        total[...] += part
-
-    @pl.when(step == pl.num_programs(0) - 1)
-    def _():
-        sq_ref[...] = jnp.sum(total[...].T, axis=0, keepdims=True)
+    chunk = 4
+
+    def loads(c):
+        rows = pl.ds(c * chunk, chunk)
+        return [
+            pltpu.make_async_copy(ref.at[rows], held.at[rows], sems.at[n, c])
+            for n, (ref, held) in enumerate(((qc_ref, qc_vm), (y_ref, y_vm)))
+        ]
+
+    for c in range(blocks // chunk):
+        for copy in loads(c):
+            copy.start()
+    for b in range(blocks):
+        back = back_ref[b] if by_dest else back_ref[:, b * SPAN : (b + 1) * SPAN]
+        carry[b] = jnp.dot(lift_ref[0], back, preferred_element_type=F32) + jnp.dot(
+            lift_ref[1], back, preferred_element_type=F32
+        )
+    total = jnp.zeros((tokens, LANES), F32)
+    for c in range(blocks // chunk):
+        for copy in loads(c):
+            copy.wait()
+        for b in range(c * chunk, (c + 1) * chunk):
+            z = qc_vm[b] * (y_vm[b] + carry[b])
+            z_ref[:, b * SPAN : (b + 1) * SPAN] = z
+            squares = z * z
+            for h in range(SPAN // LANES):
+                total = total + squares[:, h * LANES : (h + 1) * LANES]
+    sq_ref[...] = jnp.sum(total.T, axis=0, keepdims=True)
 
 
 def limit(mib):
@@ -460,14 +512,6 @@
     def columns(*lead):
         return pl.BlockSpec((*lead, tile), lambda c: (0,) * len(lead) + (c,))
 
-    def payload(rows):
-        if direct:
-            return (
-                jax.ShapeDtypeStruct((n_ctx, rows, share), BF16),
-                pl.BlockSpec((tile // share, rows, share), lambda c: (c, 0, 0)),
-            )
-        return jax.ShapeDtypeStruct((rows, width), BF16), columns(rows)
-
     def exchange(array):
         if direct:
             return lax.all_to_all(array, "ctx", 0, 0, tiled=True)
@@ -494,31 +538,32 @@
     blocks = width // SPAN
     pay, mixed, *mine = pl.pallas_call(
         functools.partial(front_kernel, direct=direct),
-        in_specs=[smem] + [hbm] * 4 + [vmem] + [hbm] * len(own),
+        in_specs=[smem] + [hbm] * (5 + len(own)),
         out_specs=[hbm] * 2 + [vmem] * len(own),
         out_shape=[
             pltpu.HBM((n_ctx, 2 * PIECE, share) if direct else (2 * PIECE, width), BF16),
-            pltpu.HBM((2, tokens, width), BF16),
+            pltpu.HBM((blocks, 2, tokens, SPAN), BF16),
         ]
         + own,
         scratch_shapes=[
             pltpu.VMEM((2, tokens, width), BF16),
             pltpu.VMEM((4, 16, width), BF16),
             pltpu.VMEM(short_weight.shape, F32),
+            pltpu.VMEM(ends.shape, BF16),
             pltpu.VMEM((2, 2, 2, 2 * (STRETCH + 8), LANES), F32),
             pltpu.VMEM((2, 2, 32, LANES), F32),
             pltpu.VMEM((2, 2 * PIECE, LANES), F32),
             pltpu.VMEM((blocks, 2 * PIECE, SPAN), BF16),
-            pltpu.VMEM((2, tokens, width), BF16),
+            pltpu.VMEM((blocks, 2, tokens, SPAN), BF16),
             pltpu.SemaphoreType.DMA((2, blocks)),
             pltpu.SemaphoreType.DMA((4,)),
-            pltpu.SemaphoreType.DMA((1,)),
+            pltpu.SemaphoreType.DMA((2,)),
             pltpu.SemaphoreType.DMA((4,)),
             pltpu.SemaphoreType.DMA((2, blocks)),
         ],
         compiler_params=limit(24),
         name="front_pieces",
-    )(me, *map(pin, (q_in, k_in, v_in, short_weight)), ends, *(map(pin, weights) if direct else ()))
+    )(me, *map(pin, (q_in, k_in, v_in, short_weight, ends)), *(map(pin, weights) if direct else ()))
     arrived = exchange(pay)
     if not direct:
         mine = (cut(short_weight), cut(rates, 0.01), cut(residues), cut(skip))
@@ -528,15 +573,15 @@
         grid=(steps,),
         in_specs=[
             columns(tokens),
-            columns(2, tokens),
+            pl.BlockSpec((tile // SPAN, 2, tokens, SPAN), lambda c: (c, 0, 0, 0)),
             columns(3, REACH + 1),
             columns(order),
             columns(order),
             columns(1),
             whole(local),
         ],
-        out_specs=[columns(tokens)] * 2,
-        out_shape=[pltpu.HBM((tokens, width), F32)] * 2,
+        out_specs=[pl.BlockSpec((tile // SPAN, tokens, SPAN), lambda c: (c, 0, 0))] * 2,
+        out_shape=[pltpu.HBM((blocks, tokens, SPAN), F32)] * 2,
         scratch_shapes=[pltpu.VMEM((groups, 2 * (STRETCH + 8), LANES), F32)],
         compiler_params=limit(24),
         name="local_filter",
@@ -550,17 +595,18 @@
         in_specs=[smem] + [vmem] * 5,
         out_specs=hbm,
         scratch_shapes=[
-            pltpu.VMEM((groups, 2 * PIECE, LANES), F32),
+            pltpu.VMEM((n_ctx, groups, 8 + 2 * PIECE + 8, LANES), F32),
             pltpu.VMEM((3, groups, slots + 1, 16, LANES), F32),
             pltpu.VMEM((groups, slots, 8, LANES), F32),
             pltpu.VMEM((groups, slots, 16, LANES), F32),
-            pltpu.VMEM((groups, slots, 16, LANES), F32),
+            pltpu.VMEM((groups, slots * 16, LANES), F32),
             pltpu.VMEM((groups, slots, order, LANES), F32),
             pltpu.VMEM((groups, slots, order, LANES), F32),
-            pltpu.VMEM((groups, slots, order, LANES), F32),
-            pltpu.VMEM((groups, slots, order, LANES), F32),
-            pltpu.VMEM((groups, slots, 16, LANES), F32),
-            pltpu.VMEM((groups, slots, 24, LANES), F32),
+            pltpu.VMEM((groups, slots * order, LANES), F32),
+            pltpu.VMEM((groups, slots * order, LANES), F32),
+            pltpu.VMEM((groups, 2, RANK * order, LANES), F32),
+            pltpu.VMEM((groups, slots * 24, LANES), F32),
+            pltpu.VMEM((n_ctx, groups, BACK + 28, LANES), F32),
             pltpu.VMEM((n_ctx, 2 * BACK, lanes), BF16),
             pltpu.SemaphoreType.DMA((n_ctx,)),
         ],
@@ -574,17 +620,12 @@
     if not direct:
         back = back.transpose(1, 0, 2).reshape(2 * BACK, width)
 
-    _, back_spec = payload(2 * BACK)
     zvalues, squares = pl.pallas_call(
         join_kernel,
-        grid=(steps,),
-        in_specs=[back_spec, whole(lift), columns(tokens), columns(tokens)],
-        out_specs=[columns(tokens), pl.BlockSpec((1, tokens), lambda c: (0, 0))],
-        out_shape=[
-            jax.ShapeDtypeStruct((tokens, width), F32),
-            jax.ShapeDtypeStruct((1, tokens), F32),
-        ],
-        scratch_shapes=[pltpu.VMEM((tokens, LANES), F32)],
+        in_specs=[vmem] * 2 + [hbm] * 2,
+        out_specs=[vmem] * 2,
+        out_shape=[f32(tokens, width), f32(1, tokens)],
+        scratch_shapes=[pltpu.VMEM((blocks, tokens, SPAN), F32)] * 3 + [pltpu.SemaphoreType.DMA((2, blocks // 4))],
         compiler_params=limit(24),
         name="join_carry",
     )(back, lift, pin(query), pin(inner))

time: 64.7 us -> 60.3 us (0.932)
  Pallas kernels: 23.6 us -> 19.9 us
  local copies, waits for them, and re-layouts: 0.72 us -> 0.02 us
    pallas_call x1, Pallas kernels: 8.19 us -> 6.5 us  [on_device(): pl.pallas_call(functools.partial(front_kernel, direct=direct), in_specs=[...]
    pallas_call x1, Pallas kernels: 5.56 us -> 4.34 us  [on_device(): pl.pallas_call(middle_kernel, in_specs=[smem] + [vmem] * 5, out_specs=hbm...]
    pallas_call x2, Pallas kernels: 9.81 us -> 9.04 us  [the longest x1 6.12 us: on_device(): pl.pallas_call(local_kernel, grid=(steps,), in_specs=[columns(tokens), pl...]
    unnamed x12 -> x10, local copies, waits for them, and re-layouts: 0.72 us -> 0.02 us
where the time goes in v5:
time: 60.3 us; the launch traced here: 59.9 us
  Pallas kernels  19.9 us (33%)
  blocking collectives  16.2 us (27%)
  waiting for transfers between devices  13.5 us (22%)
  starting transfers between devices  8.95 us (15%)
  other arithmetic  1.27 us (2%)
    all_to_all x1, blocking collectives, on_device(): back = lax.all_to_all(back, 'ctx', 0, 0, tiled=True)  16.2 us
    all_to_all x1, waiting for transfers between devices, exchange(): return lax.all_to_all(array, 'ctx', 0, 0, tiled=True)  11.5 us
    all_to_all x1, starting transfers between devices, exchange(): return lax.all_to_all(array, 'ctx', 0, 0, tiled=True)  7.37 us
    pallas_call x1, Pallas kernels, on_device(): pl.pallas_call(functools.partial(front_kernel, direct=direct), in_specs=[...  6.5 us
    pallas_call x1, Pallas kernels, on_device(): pl.pallas_call(local_kernel, grid=(steps,), in_specs=[columns(tokens), pl...  6.12 us
    pallas_call x1, Pallas kernels, on_device(): pl.pallas_call(middle_kernel, in_specs=[smem] + [vmem] * 5, out_specs=hbm...  4.34 us
    pallas_call x1, Pallas kernels, on_device(): pl.pallas_call(join_kernel, in_specs=[vmem] * 2 + [hbm] * 2, out_specs=[v...  2.92 us
    ppermute x1, waiting for transfers between devices, on_device(): lax.ppermute(squares, 'ch', [(i, (i + shift) % n_ch) for i in range(n_ch)])  2.02 us
  transfers between devices with their start and end apart: 2, of which 2 were waited for; matrix products, arithmetic and copies ran while one was open for 0% of the time, Pallas kernels for 10%

profile of v5, /device:TPU:0, one launch (start us, length us, event | category | flops | bytes accessed | tf_op | source)
XLA Modules:
  0.0 59.9 jit_solution(2926480130349935538)
XLA Ops:
  0.0 0.0 copy-start
  0.0 0.0 copy-start.2
  0.0 6.5 %front_pieces.1 = (bf16[16,88,256]{2,1,0:T(8,128)(2,1)}, bf16[16,2,128,256]{3,2,1,0:T(8,128)(2,1)}, f32[3,7,256]{2,1,0:T(8,128)S(1)}, f32[16,256]{1,0:T(8,128)S(...) custom-call(s32[1]{0:T(128)} %bitcast.refs_0_, bf16[128,4096]{1,0:T(8,128)(2,1)} %q_ref.1, bf16[128,4096]{1,0:T(8,128)(2,1)} %refs_2_.1, ...), custom_call_target="tpu_custom_call" | custom-call | tf_op jit(solution)/shard_map/front_pieces/pallas_call | solution.py:539
  6.5 7.4 %all-to-all-start = ((bf16[16,88,256]{2,1,0:T(8,128)(2,1)}), bf16[16,88,256]{2,1,0:T(8,128)(2,1)S(1)}, u32[]{:S(2)}, u32[]{:S(2)}) async-start(bf16[16,88,256]{2,1,0:T(8,128)(2,1)} %get-tuple-element.18), calls=%async_computation | async-start | bytes 1441792 | tf_op jit(solution)/shard_map/all_to_all | solution.py:517
  13.9 0.0 copy-done
  13.9 0.0 copy-done.2
  13.9 0.0 copy-start.3
  13.9 0.0 copy-start.1
  13.9 6.1 %local_filter.1 = (f32[16,128,256]{2,1,0:T(8,128)}, f32[16,128,256]{2,1,0:T(8,128)}) custom-call(bf16[128,4096]{1,0:T(8,128)(2,1)} %q_ref.1, bf16[16,2,128,256]{3,2,1,0:T(8,128)(2,1)} %get-tuple-element.19.u_ref, f32[3,7,4096]{2,1,0:T(8,128)} %taps_ref.1, f32[16,4096]{1,0:T(8,128)} %rates_ref.1, f32[16,4096]{1,0:T(8,128)} %res_ref.1, f32[1,4096]{1,0:T(1,128)S(1)} %bitcast.5, ...), custom_call_target="tpu_custom_call" | custom-call | flops 1000000000 | bytes 20000000 | tf_op jit(solution)/shard_map/local_filter/pallas_call | solution.py:571
  20.1 11.5 %all-to-all-done.x_ref = bf16[16,88,256]{2,1,0:T(8,128)(2,1)S(1)} async-done(((bf16[16,88,256]{2,1,0:T(8,128)(2,1)}), bf16[16,88,256]{2,1,0:T(8,128)(2,1)S(1)}, u32[]{:S(2)}, u32[]{:S(2)}) %all-to-all-start) | async-done | bytes 720928 | tf_op jit(solution)/shard_map/all_to_all | solution.py:517
  31.5 0.0 copy-done.3
  31.5 4.3 %middle_states.1 = bf16[16,40,256]{2,1,0:T(8,128)(2,1)} custom-call(s32[32]{0:T(128)S(1)} %copy-done.3, bf16[16,88,256]{2,1,0:T(8,128)(2,1)S(1)} %all-to-all-done.x_ref, f32[3,7,256]{2,1,0:T(8,128)S(1)} %get-tuple-element.23.taps_ref, f32[16,256]{1,0:T(8,128)S(1)} %get-tuple-element.24.rates_ref, f32[16,256]{1,0:T(8,128)S(1)} %get-tuple-element.25.res_ref, ...), custom_call_target="tpu_custom_call" | custom-call | tf_op jit(solution)/shard_map/middle_states/pallas_call | solution.py:593
  35.9 16.2 %all_to_all.10.back_ref = bf16[16,40,256]{2,1,0:T(8,128)(2,1)S(1)} all-to-all(bf16[16,40,256]{2,1,0:T(8,128)(2,1)} %middle_states.1), channel_id=1, replica_groups=mesh['ctx'=16,'ch'=2] {'ctx'}, dimensions={0} | all-to-all | bytes 655360 | tf_op jit(solution)/shard_map/all_to_all | solution.py:619
  52.1 0.0 copy-done.1
  52.1 0.0 copy-start.4
  52.1 2.9 %join_carry.1 = (f32[128,4096]{1,0:T(8,128)S(1)}, f32[1,128]{1,0:T(1,128)S(1)}) custom-call(bf16[16,40,256]{2,1,0:T(8,128)(2,1)S(1)} %all_to_all.10.back_ref, bf16[2,128,40]{2,1,0:T(8,128)(2,1)S(1)} %copy-done.1, f32[16,128,256]{2,1,0:T(8,128)} %get-tuple-element.27.qc_ref, f32[16,128,256]{2,1,0:T(8,128)} %get-tuple-element.28.y_ref), custom_call_target="tpu_custom_call" | custom-call | tf_op jit(solution)/shard_map/join_carry/pallas_call | solution.py:623
  55.1 1.6 %collective-permute-start = (f32[1,128]{1,0:T(1,128)S(1)}, f32[1,128]{1,0:T(1,128)S(1)}, u32[]{:S(2)}, u32[]{:S(2)}) collective-permute-start(f32[1,128]{1,0:T(1,128)S(1)} %get-tuple-element.30), channel_id=1, source_target_pairs={{0,1},{1,0},{2,3},{3,2},{4,5},{5,4},{6,7},{7,6},{8,9},{9,8},{10,11... | collective-permute-start | bytes 1544 | tf_op jit(solution)/shard_map/ppermute | solution.py:634
  56.6 2.0 %collective-permute-done = f32[1,128]{1,0:T(1,128)S(1)} collective-permute-done((f32[1,128]{1,0:T(1,128)S(1)}, f32[1,128]{1,0:T(1,128)S(1)}, u32[]{:S(2)}, u32[]{:S(2)}) %collective-permute-start) | collective-permute-done | bytes 544 | tf_op jit(solution)/shard_map/ppermute | solution.py:634
  58.7 0.0 copy-done.4
  58.7 1.3 %multiply_convert_fusion = bf16[128,4096]{1,0:T(8,128)(2,1)} fusion(f32[128,4096]{1,0:T(8,128)S(1)} %get-tuple-element.29, f32[4096]{0:T(1024)S(1)} %copy-done.4, f32[128]{0:T(128)S(1)} %rsqrt_bitcast_fusion), kind=kLoop, calls=%fused_computation | loop fusion | flops 1572864 | bytes 3162624 | tf_op jit(solution)/shard_map/convert_element_type | solution.py:636
  (1 shorter events, 0.0 us)
Async XLA Ops:
  0.0 13.9 %copy-start = (bf16[384,192]{1,0:T(8,128)(2,1)S(1)}, bf16[384,192]{1,0:T(8,128)(2,1)}, u32[]{:S(2)}) copy-start(bf16[384,192]{1,0:T(8,128)(2,1)} %constant.18.clone.local_ref) | copy-start | bytes 442372
  0.0 13.9 %copy-start.2 = (f32[4096]{0:T(1024)S(1)}, f32[4096]{0:T(1024)}, u32[]{:S(2)}) copy-start(f32[4096]{0:T(1024)} %param.19) | copy-start | bytes 49156
  6.5 25.0 %all-to-all-start = ((bf16[16,88,256]{2,1,0:T(8,128)(2,1)}), bf16[16,88,256]{2,1,0:T(8,128)(2,1)S(1)}, u32[]{:S(2)}, u32[]{:S(2)}) async-start(bf16[16,88,256]{2,1,0:T(8,128)(2,1)} %get-tuple-element.18), calls=%async_computation | async-start | bytes 1441792 | tf_op jit(solution)/shard_map/all_to_all | solution.py:517
  13.9 17.6 %copy-start.3 = (s32[32]{0:T(128)S(1)}, s32[32]{0:T(128)}, u32[]{:S(2)}) copy-start(s32[32]{0:T(128)} %perm_ref.1) | copy-start | bytes 388
  13.9 38.2 %copy-start.1 = (bf16[2,128,40]{2,1,0:T(8,128)(2,1)S(1)}, bf16[2,128,40]{2,1,0:T(8,128)(2,1)}, u32[]{:S(2)}) copy-start(bf16[2,128,40]{2,1,0:T(8,128)(2,1)} %constant.19.clone.lift_ref) | copy-start | bytes 61444
  52.1 6.5 %copy-start.4 = (f32[4096]{0:T(1024)S(1)}, f32[4096]{0:T(1024)}, u32[]{:S(2)}) copy-start(f32[4096]{0:T(1024)} %param.20) | copy-start | bytes 49156
  55.1 3.6 %collective-permute-start = (f32[1,128]{1,0:T(1,128)S(1)}, f32[1,128]{1,0:T(1,128)S(1)}, u32[]{:S(2)}, u32[]{:S(2)}) collective-permute-start(f32[1,128]{1,0:T(1,128)S(1)} %get-tuple-element.30), channel_id=1, source_target_pairs={{0,1},{1,0},{2,3},{3,2},{4,5},{5,4},{6,7},{7,6},{8,9},{9,8},{10,11... | collective-permute-start | bytes 1544 | tf_op jit(solution)/shard_map/ppermute | solution.py:634

commit v6 on v5

--- a/solution.py
+++ b/solution.py
@@ -21,6 +21,7 @@
 RANK = len(PIVOTS)
 FINE = 2
 COEFS = RANK + FINE
+ROLLED = 3
 RAW = 6 * REACH
 PIECE = RAW + COEFS
 BACK = 2 * REACH + COEFS
@@ -183,9 +184,14 @@
                     base = i * (STRETCH + 8) + 8 + 16 * b
                     both = []
                     for a in range(2):
-                        total = taps[a][0] * xs[parity, a, h, base : base + 16, :]
+                        near = xs[parity, a, h, base - 8 : base + 16, :]
+                        total = taps[a][0] * near[8:]
                         for j in range(1, REACH + 1):
-                            total = total + taps[a][j] * xs[parity, a, h, base - j : base - j + 16, :]
+                            if j <= ROLLED:
+                                shifted = pltpu.roll(near, j, 0)[8:]
+                            else:
+                                shifted = xs[parity, a, h, base - j : base - j + 16, :]
+                            total = total + taps[a][j] * shifted
                         both.append(total)
                     mixed = both[0] * both[1]
                     if b == 0:
@@ -454,37 +460,43 @@
     lax.fori_loop(0, slots // 2, end, 0)
 
 
-def join_kernel(back_ref, lift_ref, qc_ref, y_ref, z_ref, sq_ref, qc_vm, y_vm, carry, sems):
-    blocks, tokens, _ = qc_vm.shape
+def join_kernel(back_ref, lift_ref, qc_ref, y_ref, z_ref, sq_ref):
+    blocks, tokens, _ = qc_ref.shape
     by_dest = len(back_ref.shape) == 3
-    chunk = 4
-
-    def loads(c):
-        rows = pl.ds(c * chunk, chunk)
-        return [
-            pltpu.make_async_copy(ref.at[rows], held.at[rows], sems.at[n, c])
-            for n, (ref, held) in enumerate(((qc_ref, qc_vm), (y_ref, y_vm)))
-        ]
-
-    for c in range(blocks // chunk):
-        for copy in loads(c):
-            copy.start()
+    total = jnp.zeros((tokens, LANES), F32)
     for b in range(blocks):
         back = back_ref[b] if by_dest else back_ref[:, b * SPAN : (b + 1) * SPAN]
-        carry[b] = jnp.dot(lift_ref[0], back, preferred_element_type=F32) + jnp.dot(
-            lift_ref[1], back, preferred_element_type=F32
-        )
-    total = jnp.zeros((tokens, LANES), F32)
-    for c in range(blocks // chunk):
-        for copy in loads(c):
-            copy.wait()
-        for b in range(c * chunk, (c + 1) * chunk):
-            z = qc_vm[b] * (y_vm[b] + carry[b])
-            z_ref[:, b * SPAN : (b + 1) * SPAN] = z
-            squares = z * z
-            for h in range(SPAN // LANES):
-                total = total + squares[:, h * LANES : (h + 1) * LANES]
+        carry = jnp.dot(lift_ref[0], back, preferred_element_type=F32)
+        carry = carry + jnp.dot(lift_ref[1], back, preferred_element_type=F32)
+        z = qc_ref[b] * (y_ref[b] + carry)
+        z_ref[:, b * SPAN : (b + 1) * SPAN] = z
+        squares = z * z
+        for h in range(SPAN // LANES):
+            total = total + squares[:, h * LANES : (h + 1) * LANES]
     sq_ref[...] = jnp.sum(total.T, axis=0, keepdims=True)
+
+
+def scale_kernel(*refs, channels):
+    z_ref, gain_ref, refs, (out_ref, held, sems) = refs[0], refs[1], refs[2:-3], refs[-3:]
+    tokens, width = z_ref.shape
+    chunks = sems.shape[0]
+    wide = width // chunks
+    total = refs[0][...]
+    for ref in refs[1:]:
+        total = total + ref[...]
+    scale = lax.rsqrt(total / channels + 1e-05)
+    scale = jnp.broadcast_to(scale, (LANES, tokens)).T
+    copies = []
+    for c in range(chunks):
+        for g in range(c * wide // LANES, (c + 1) * wide // LANES):
+            cols = slice(g * LANES, (g + 1) * LANES)
+            held[:, cols] = (z_ref[:, cols] * scale * gain_ref[:, cols]).astype(BF16)
+        cols = pl.ds(c * wide, wide)
+        copy = pltpu.make_async_copy(held.at[:, cols], out_ref.at[:, cols], sems.at[c])
+        copy.start()
+        copies.append(copy)
+    for copy in copies:
+        copy.wait()
 
 
 def limit(mib):
@@ -581,7 +593,7 @@
             whole(local),
         ],
         out_specs=[pl.BlockSpec((tile // SPAN, tokens, SPAN), lambda c: (c, 0, 0))] * 2,
-        out_shape=[pltpu.HBM((blocks, tokens, SPAN), F32)] * 2,
+        out_shape=[pltpu.VMEM((blocks, tokens, SPAN), F32)] * 2,
         scratch_shapes=[pltpu.VMEM((groups, 2 * (STRETCH + 8), LANES), F32)],
         compiler_params=limit(24),
         name="local_filter",
@@ -620,20 +632,27 @@
     if not direct:
         back = back.transpose(1, 0, 2).reshape(2 * BACK, width)
 
+    keep = lambda array: pltpu.with_memory_space_constraint(array, pltpu.VMEM)
     zvalues, squares = pl.pallas_call(
         join_kernel,
-        in_specs=[vmem] * 2 + [hbm] * 2,
+        in_specs=[vmem] * 4,
         out_specs=[vmem] * 2,
         out_shape=[f32(tokens, width), f32(1, tokens)],
-        scratch_shapes=[pltpu.VMEM((blocks, tokens, SPAN), F32)] * 3 + [pltpu.SemaphoreType.DMA((2, blocks // 4))],
         compiler_params=limit(24),
         name="join_carry",
-    )(back, lift, pin(query), pin(inner))
-    total = squares
+    )(back, lift, keep(query), keep(inner))
+    sums = [squares]
     for shift in range(1, n_ch):
-        total = total + lax.ppermute(squares, "ch", [(i, (i + shift) % n_ch) for i in range(n_ch)])
-    scale = lax.rsqrt(total / (width * n_ch) + 1e-05)
-    return (zvalues * scale.reshape(tokens, 1) * gain).astype(BF16)
+        sums.append(lax.ppermute(squares, "ch", [(i, (i + shift) % n_ch) for i in range(n_ch)]))
+    return pl.pallas_call(
+        functools.partial(scale_kernel, channels=width * n_ch),
+        in_specs=[vmem] * (2 + n_ch),
+        out_specs=hbm,
+        out_shape=pltpu.HBM((tokens, width), BF16),
+        scratch_shapes=[pltpu.VMEM((tokens, width), BF16), pltpu.SemaphoreType.DMA((8 if width % 1024 == 0 else 1,))],
+        compiler_params=limit(24),
+        name="scale_rows",
+    )(zvalues, gain, *sums)
 
 
 def solution(mesh):

time: 60.3 us -> 60.5 us (level)
  local copies, waits for them, and re-layouts: 0.02 us -> 2.94 us
  other arithmetic: 1.27 us -> 0 us
  Pallas kernels: 19.9 us -> 18.8 us
    unnamed x10 -> x14, local copies, waits for them, and re-layouts: 0.02 us -> 2.94 us
    convert_element_type x1 -> x0, other arithmetic: 1.26 us -> none  [on_device(): return (zvalues * scale.reshape(tokens, 1) * gain).astype(BF16)]
    pallas_call x1 -> x2, Pallas kernels: 2.92 us -> 1.92 us  [the longest x1 1.14 us: on_device(): pl.pallas_call(functools.partial(scale_kernel, channels=width * n_ch), in...]
    pallas_call x1, Pallas kernels: 6.12 us -> 5.16 us  [on_device(): pl.pallas_call(local_kernel, grid=(steps,), in_specs=[columns(tokens), pl...]
    pallas_call x1, Pallas kernels: 6.5 us -> 7.38 us  [on_device(): pl.pallas_call(functools.partial(front_kernel, direct=direct), in_specs=[...]
  transfers between devices with their start and end apart: 2 -> 2, of which waited for: 2 -> 2; matrix products, arithmetic and copies ran while one was open for 0% -> 0% of each run, Pallas kernels for 10% -> 9%
where the time goes in v6:
time: 60.5 us; the launch traced here: 60.1 us
  Pallas kernels  18.8 us (31%)
  blocking collectives  16.2 us (27%)
  waiting for transfers between devices  13.1 us (22%)
  starting transfers between devices  8.96 us (15%)
  local copies, waits for them, and re-layouts  2.94 us (5%)
    all_to_all x1, blocking collectives, on_device(): back = lax.all_to_all(back, 'ctx', 0, 0, tiled=True)  16.2 us
    all_to_all x1, waiting for transfers between devices, exchange(): return lax.all_to_all(array, 'ctx', 0, 0, tiled=True)  11.1 us
    pallas_call x1, Pallas kernels, on_device(): pl.pallas_call(functools.partial(front_kernel, direct=direct), in_specs=[...  7.38 us
    all_to_all x1, starting transfers between devices, exchange(): return lax.all_to_all(array, 'ctx', 0, 0, tiled=True)  7.37 us
    pallas_call x1, Pallas kernels, on_device(): pl.pallas_call(local_kernel, grid=(steps,), in_specs=[columns(tokens), pl...  5.16 us
    pallas_call x1, Pallas kernels, on_device(): pl.pallas_call(middle_kernel, in_specs=[smem] + [vmem] * 5, out_specs=hbm...  4.34 us
    unnamed x14, local copies, waits for them, and re-layouts  2.94 us
    ppermute x1, waiting for transfers between devices, on_device(): lax.ppermute(squares, 'ch', [(i, (i + shift) % n_ch) for i in range(n_ch)])  2.01 us
  transfers between devices with their start and end apart: 2, of which 2 were waited for; matrix products, arithmetic and copies ran while one was open for 0% of the time, Pallas kernels for 9%

profile of v6, /device:TPU:0, one launch (start us, length us, event | category | flops | bytes accessed | tf_op | source)
XLA Modules:
  0.0 60.1 jit_solution(10405554036137834624)
XLA Ops:
  0.0 0.0 copy-start.2
  0.0 0.0 copy-start.4
  0.0 7.4 %front_pieces.1 = (bf16[16,88,256]{2,1,0:T(8,128)(2,1)}, bf16[16,2,128,256]{3,2,1,0:T(8,128)(2,1)}, f32[3,7,256]{2,1,0:T(8,128)S(1)}, f32[16,256]{1,0:T(8,128)S(...) custom-call(s32[1]{0:T(128)} %bitcast.refs_0_, bf16[128,4096]{1,0:T(8,128)(2,1)} %q_ref.1, bf16[128,4096]{1,0:T(8,128)(2,1)} %refs_2_.1, ...), custom_call_target="tpu_custom_call" | custom-call | tf_op jit(solution)/shard_map/front_pieces/pallas_call | solution.py:551
  7.4 7.4 %all-to-all-start = ((bf16[16,88,256]{2,1,0:T(8,128)(2,1)}), bf16[16,88,256]{2,1,0:T(8,128)(2,1)S(1)}, u32[]{:S(2)}, u32[]{:S(2)}) async-start(bf16[16,88,256]{2,1,0:T(8,128)(2,1)} %get-tuple-element.18), calls=%async_computation | async-start | bytes 1441792 | tf_op jit(solution)/shard_map/all_to_all | solution.py:529
  14.8 0.0 copy-done.2
  14.8 0.0 copy-done.4
  14.8 0.0 copy-start.6
  14.8 0.0 copy-start.3
  14.8 5.2 %local_filter.1 = (f32[16,128,256]{2,1,0:T(8,128)S(1)}, f32[16,128,256]{2,1,0:T(8,128)S(1)}) custom-call(bf16[128,4096]{1,0:T(8,128)(2,1)} %q_ref.1, bf16[16,2,128,256]{3,2,1,0:T(8,128)(2,1)} %get-tuple-element.19.u_ref, f32[3,7,4096]{2,1,0:T(8,128)} %taps_ref.1, f32[16,4096]{1,0:T(8,128)} %rates_ref.1, f32[16,4096]{1,0:T(8,128)} %res_ref.1, ...), custom_call_target="tpu_custom_call" | custom-call | flops 1000000000 | bytes 20000000 | tf_op jit(solution)/shard_map/local_filter/pallas_call | solution.py:583
  20.0 0.0 copy-start
  20.0 1.3 %copy-done = f32[16,128,256]{2,1,0:T(8,128)} copy-done((f32[16,128,256]{2,1,0:T(8,128)}, f32[16,128,256]{2,1,0:T(8,128)S(1)}, u32[]{:S(2)}) %copy-start) | copy-done | bytes 2097176
  21.3 11.1 %all-to-all-done.x_ref = bf16[16,88,256]{2,1,0:T(8,128)(2,1)S(1)} async-done(((bf16[16,88,256]{2,1,0:T(8,128)(2,1)}), bf16[16,88,256]{2,1,0:T(8,128)(2,1)S(1)}, u32[]{:S(2)}, u32[]{:S(2)}) %all-to-all-start) | async-done | bytes 720928 | tf_op jit(solution)/shard_map/all_to_all | solution.py:529
  32.4 0.0 copy-done.6
  32.4 4.3 %middle_states.1 = bf16[16,40,256]{2,1,0:T(8,128)(2,1)} custom-call(s32[32]{0:T(128)S(1)} %copy-done.6, bf16[16,88,256]{2,1,0:T(8,128)(2,1)S(1)} %all-to-all-done.x_ref, f32[3,7,256]{2,1,0:T(8,128)S(1)} %get-tuple-element.23.taps_ref, f32[16,256]{1,0:T(8,128)S(1)} %get-tuple-element.24.rates_ref, f32[16,256]{1,0:T(8,128)S(1)} %get-tuple-element.25.res_ref, ...), custom_call_target="tpu_custom_call" | custom-call | tf_op jit(solution)/shard_map/middle_states/pallas_call | solution.py:605
  36.8 16.2 %all_to_all.10.back_ref = bf16[16,40,256]{2,1,0:T(8,128)(2,1)S(1)} all-to-all(bf16[16,40,256]{2,1,0:T(8,128)(2,1)} %middle_states.1), channel_id=1, replica_groups=mesh['ctx'=16,'ch'=2] {'ctx'}, dimensions={0} | all-to-all | bytes 655360 | tf_op jit(solution)/shard_map/all_to_all | solution.py:631
  53.0 0.0 copy-done.3
  53.0 0.0 copy-start.1
  53.0 1.6 %copy-done.1 = f32[16,128,256]{2,1,0:T(8,128)S(1)} copy-done((f32[16,128,256]{2,1,0:T(8,128)S(1)}, f32[16,128,256]{2,1,0:T(8,128)}, u32[]{:S(2)}) %copy-start.1) | copy-done | bytes 2097176
  54.6 0.0 copy-start.5
  54.6 0.8 %join_carry.1 = (f32[128,4096]{1,0:T(8,128)S(1)}, f32[1,128]{1,0:T(1,128)S(1)}) custom-call(bf16[16,40,256]{2,1,0:T(8,128)(2,1)S(1)} %all_to_all.10.back_ref, bf16[2,128,40]{2,1,0:T(8,128)(2,1)S(1)} %copy-done.3, f32[16,128,256]{2,1,0:T(8,128)S(1)} %get-tuple-element.27.qc_ref, f32[16,128,256]{2,1,0:T(8,128)S(1)} %copy-done.1), custom_call_target="tpu_custom_call" | custom-call | tf_op jit(solution)/shard_map/join_carry/pallas_call | solution.py:636
  55.4 1.6 %collective-permute-start = (f32[1,128]{1,0:T(1,128)S(1)}, f32[1,128]{1,0:T(1,128)S(1)}, u32[]{:S(2)}, u32[]{:S(2)}) collective-permute-start(f32[1,128]{1,0:T(1,128)S(1)} %get-tuple-element.30.refs_2_), channel_id=1, source_target_pairs={{0,1},{1,0},{2,3},{3,2},{4,5},{5,4},{6,7},{7,6},{8,9},{9,8},{10,11... | collective-permute-start | bytes 1544 | tf_op jit(solution)/shard_map/ppermute | solution.py:646
  57.0 2.0 %collective-permute-done.refs_3_ = f32[1,128]{1,0:T(1,128)S(1)} collective-permute-done((f32[1,128]{1,0:T(1,128)S(1)}, f32[1,128]{1,0:T(1,128)S(1)}, u32[]{:S(2)}, u32[]{:S(2)}) %collective-permute-start) | collective-permute-done | bytes 544 | tf_op jit(solution)/shard_map/ppermute | solution.py:646
  59.0 0.0 copy-done.5
  59.0 1.1 %scale_rows.1 = bf16[128,4096]{1,0:T(8,128)(2,1)} custom-call(f32[128,4096]{1,0:T(8,128)S(1)} %get-tuple-element.29.refs_0_, f32[1,4096]{1,0:T(1,128)S(1)} %bitcast.5, f32[1,128]{1,0:T(1,128)S(1)} %get-tuple-element.30.refs_2_, f32[1,128]{1,0:T(1,128)S(1)} %collective-permute-done.refs_3_), custom_call_target="tpu_custom_call" | custom-call | tf_op jit(solution)/shard_map/scale_rows/pallas_call | solution.py:647
Async XLA Ops:
  0.0 14.8 %copy-start.2 = (bf16[384,192]{1,0:T(8,128)(2,1)S(1)}, bf16[384,192]{1,0:T(8,128)(2,1)}, u32[]{:S(2)}) copy-start(bf16[384,192]{1,0:T(8,128)(2,1)} %constant.13.clone.local_ref) | copy-start | bytes 442372
  0.0 14.8 %copy-start.4 = (f32[4096]{0:T(1024)S(1)}, f32[4096]{0:T(1024)}, u32[]{:S(2)}) copy-start(f32[4096]{0:T(1024)} %param.19) | copy-start | bytes 49156
  7.4 25.0 %all-to-all-start = ((bf16[16,88,256]{2,1,0:T(8,128)(2,1)}), bf16[16,88,256]{2,1,0:T(8,128)(2,1)S(1)}, u32[]{:S(2)}, u32[]{:S(2)}) async-start(bf16[16,88,256]{2,1,0:T(8,128)(2,1)} %get-tuple-element.18), calls=%async_computation | async-start | bytes 1441792 | tf_op jit(solution)/shard_map/all_to_all | solution.py:529
  14.8 17.6 %copy-start.6 = (s32[32]{0:T(128)S(1)}, s32[32]{0:T(128)}, u32[]{:S(2)}) copy-start(s32[32]{0:T(128)} %perm_ref.1) | copy-start | bytes 388
  14.8 38.2 %copy-start.3 = (bf16[2,128,40]{2,1,0:T(8,128)(2,1)S(1)}, bf16[2,128,40]{2,1,0:T(8,128)(2,1)}, u32[]{:S(2)}) copy-start(bf16[2,128,40]{2,1,0:T(8,128)(2,1)} %constant.14.clone.lift_ref) | copy-start | bytes 61444
  20.0 1.3 %copy-start = (f32[16,128,256]{2,1,0:T(8,128)}, f32[16,128,256]{2,1,0:T(8,128)S(1)}, u32[]{:S(2)}) copy-start(f32[16,128,256]{2,1,0:T(8,128)S(1)} %get-tuple-element.28.y_ref) | copy-start | bytes 6291460
  53.0 1.6 %copy-start.1 = (f32[16,128,256]{2,1,0:T(8,128)S(1)}, f32[16,128,256]{2,1,0:T(8,128)}, u32[]{:S(2)}) copy-start(f32[16,128,256]{2,1,0:T(8,128)} %copy-done) | copy-start | bytes 6291460
  54.6 4.4 %copy-start.5 = (f32[4096]{0:T(1024)S(1)}, f32[4096]{0:T(1024)}, u32[]{:S(2)}) copy-start(f32[4096]{0:T(1024)} %param.20) | copy-start | bytes 49156
  55.4 3.6 %collective-permute-start = (f32[1,128]{1,0:T(1,128)S(1)}, f32[1,128]{1,0:T(1,128)S(1)}, u32[]{:S(2)}, u32[]{:S(2)}) collective-permute-start(f32[1,128]{1,0:T(1,128)S(1)} %get-tuple-element.30.refs_2_), channel_id=1, source_target_pairs={{0,1},{1,0},{2,3},{3,2},{4,5},{5,4},{6,7},{7,6},{8,9},{9,8},{10,11... | collective-permute-start | bytes 1544 | tf_op jit(solution)/shard_map/ppermute | solution.py:646

commit v7 on v6

--- a/solution.py
+++ b/solution.py
@@ -21,7 +21,6 @@
 RANK = len(PIVOTS)
 FINE = 2
 COEFS = RANK + FINE
-ROLLED = 3
 RAW = 6 * REACH
 PIECE = RAW + COEFS
 BACK = 2 * REACH + COEFS
@@ -105,7 +104,7 @@
     me_ref, q_ref, k_ref, v_ref, taps_ref, ends_ref = refs[:6]
     refs = refs[6:]
     weights, refs = (refs[:4], refs[4:]) if direct else ((), refs)
-    pay_ref, u_ref, refs = refs[0], refs[1], refs[2:]
+    pay_ref, refs = refs[0], refs[1:]
     kept, refs = (refs[:4], refs[4:]) if direct else ((), refs)
     held, edge, taps_vm, ends_vm, xs, qs, pay, packed, u_vm, in_sems, edge_sems, tap_sem, own_sems, out_sems = refs
     blocks = k_ref.shape[1] // SPAN
@@ -117,7 +116,7 @@
         return [
             pltpu.make_async_copy(ref.at[:, lanes(c)], held.at[a, :, lanes(c)], in_sems.at[a, c])
             for a, ref in enumerate((k_ref, v_ref))
-        ]
+        ] + [pltpu.make_async_copy(taps_ref.at[pl.ds(1, 2), :, lanes(c)], taps_vm.at[c], in_sems.at[2, c])]
 
     def edge_loads():
         return [
@@ -127,10 +126,7 @@
 
     def stores(c):
         target = pay_ref.at[c] if direct else pay_ref.at[:, lanes(c)]
-        return [
-            pltpu.make_async_copy(packed.at[c], target, out_sems.at[0, c]),
-            pltpu.make_async_copy(u_vm.at[c], u_ref.at[c], out_sems.at[1, c]),
-        ]
+        return [pltpu.make_async_copy(packed.at[c], target, out_sems.at[c])]
 
     def own_loads():
         share = kept[0].shape[-1]
@@ -138,12 +134,10 @@
         views = (weights[0].at[:, :, cols], weights[1].at[:, cols], weights[2].at[:, cols], weights[3].at[:, cols])
         return [pltpu.make_async_copy(view, ref, own_sems.at[n]) for n, (view, ref) in enumerate(zip(views, kept))]
 
-    tap_copy = pltpu.make_async_copy(taps_ref, taps_vm, tap_sem.at[0])
-    ends_copy = pltpu.make_async_copy(ends_ref, ends_vm, tap_sem.at[1])
-    tap_copy.start()
-    ends_copy.start()
+    ends_copy = pltpu.make_async_copy(ends_ref, ends_vm, tap_sem.at[0])
     for copy in loads(0) + edge_loads():
         copy.start()
+    ends_copy.start()
 
     def begin(c, carry):
         for copy in loads(c):
@@ -160,8 +154,6 @@
                 for i in range(2):
                     at = i * (STRETCH + 8)
                     xs[parity, a, h, at : at + 8, :] = jnp.zeros((8, LANES), F32)
-    tap_copy.wait()
-    ends_copy.wait()
 
     def arrive(c):
         for copy in loads(c):
@@ -178,20 +170,15 @@
                     xs[parity, a, h, base : base + STRETCH, :] = held[
                         a, i * STRETCH : (i + 1) * STRETCH, cols
                     ].astype(F32)
-            taps = [[taps_vm[a, j : j + 1, cols] for j in range(REACH + 1)] for a in (1, 2)]
+            taps = [[taps_vm[c, a, j : j + 1, part] for j in range(REACH + 1)] for a in range(2)]
             for i in range(2):
                 for b in range(STRETCH // 16):
                     base = i * (STRETCH + 8) + 8 + 16 * b
                     both = []
                     for a in range(2):
-                        near = xs[parity, a, h, base - 8 : base + 16, :]
-                        total = taps[a][0] * near[8:]
+                        total = taps[a][0] * xs[parity, a, h, base : base + 16, :]
                         for j in range(1, REACH + 1):
-                            if j <= ROLLED:
-                                shifted = pltpu.roll(near, j, 0)[8:]
-                            else:
-                                shifted = xs[parity, a, h, base - j : base - j + 16, :]
-                            total = total + taps[a][j] * shifted
+                            total = total + taps[a][j] * xs[parity, a, h, base - j : base - j + 16, :]
                         both.append(total)
                     mixed = both[0] * both[1]
                     if b == 0:
@@ -199,14 +186,15 @@
                         mixed = jnp.where(row >= REACH, mixed, 0.0)
                     high, low = split(mixed)
                     rows = slice(i * STRETCH + 16 * b, i * STRETCH + 16 * b + 16)
-                    u_vm[c, 0, rows, part] = high
-                    u_vm[c, 1, rows, part] = low
+                    u_vm[parity, 0, rows, part] = high
+                    u_vm[parity, 1, rows, part] = low
 
     def products(c):
         found = []
+        parity = lax.rem(c, 2)
         for i in range(2):
             rows = slice(i * STRETCH, (i + 1) * STRETCH)
-            high, low = u_vm[c, 0, rows, :], u_vm[c, 1, rows, :]
+            high, low = u_vm[parity, 0, rows, :], u_vm[parity, 1, rows, :]
             stacked = jnp.concatenate([high, low, high], axis=0)
             found.append(jnp.dot(ends_vm[...], stacked, preferred_element_type=F32)[:8])
         return found
@@ -244,6 +232,7 @@
     arrive(0)
     for copy in edge_loads():
         copy.wait()
+    ends_copy.wait()
     features(0)
 
     def both(c, carry):
@@ -269,26 +258,36 @@
             copy.wait()
 
 
-def local_kernel(q_ref, u_ref, taps_ref, rates_ref, res_ref, skip_ref, local_ref, qc_ref, y_ref, xs):
+def local_kernel(
+    q_ref, k_ref, v_ref, taps_ref, rates_ref, res_ref, skip_ref, local_ref, qc_ref, y_ref, xs, u_vm
+):
     tile = q_ref.shape[1]
     per = SPAN // LANES
+    first_row = lax.broadcasted_iota(jnp.int32, (8, LANES), 0)
     for g in range(tile // LANES):
         cols = slice(g * LANES, (g + 1) * LANES)
         part = slice(g % per * LANES, (g % per + 1) * LANES)
-        taps = [taps_ref[0, j : j + 1, cols] for j in range(REACH + 1)]
+        taps = [[taps_ref[a, j : j + 1, cols] for j in range(REACH + 1)] for a in range(3)]
         for i in range(2):
             base = i * (STRETCH + 8) + 8
-            xs[g, base - 8 : base, :] = jnp.zeros((8, LANES), F32)
-            xs[g, base : base + STRETCH, :] = q_ref[i * STRETCH : (i + 1) * STRETCH, cols].astype(F32)
+            for a, ref in enumerate((q_ref, k_ref, v_ref)):
+                xs[a, g, base - 8 : base, :] = jnp.zeros((8, LANES), F32)
+                xs[a, g, base : base + STRETCH, :] = ref[i * STRETCH : (i + 1) * STRETCH, cols].astype(F32)
             for b in range(STRETCH // 8):
                 at = base + 8 * b
-                total = taps[0] * xs[g, at : at + 8, :]
-                for j in range(1, REACH + 1):
-                    total = total + taps[j] * xs[g, at - j : at - j + 8, :]
+                totals = []
+                for a in range(3):
+                    total = taps[a][0] * xs[a, g, at : at + 8, :]
+                    for j in range(1, REACH + 1):
+                        total = total + taps[a][j] * xs[a, g, at - j : at - j + 8, :]
+                    totals.append(total)
+                query, mixed = totals[0], totals[1] * totals[2]
                 if b == 0:
-                    row = lax.broadcasted_iota(jnp.int32, (8, LANES), 0)
-                    total = jnp.where(row >= REACH, total, 1.0)
-                qc_ref[g // per, i * STRETCH + 8 * b : i * STRETCH + 8 * b + 8, part] = total
+                    query = jnp.where(first_row >= REACH, query, 1.0)
+                    mixed = jnp.where(first_row >= REACH, mixed, 0.0)
+                rows = slice(i * STRETCH + 8 * b, i * STRETCH + 8 * b + 8)
+                qc_ref[g // per, rows, part] = query
+                u_vm[g // per, rows, part] = mixed
     for c in range(tile // SPAN):
         cols = slice(c * SPAN, (c + 1) * SPAN)
         rate = rates_ref[:, cols]
@@ -296,11 +295,12 @@
         weights = [jnp.sum(amount * value, axis=0, keepdims=True) for value in strengths(rate)]
         for i in range(2):
             rows = slice(i * STRETCH, (i + 1) * STRETCH)
-            high, low = u_ref[c, 0, rows, :], u_ref[c, 1, rows, :]
+            mixed = u_vm[c, rows, :]
+            high, low = split(mixed)
             parts = jnp.dot(
                 local_ref[...], jnp.concatenate([high, low, high], axis=0), preferred_element_type=F32
             )
-            total = skip_ref[:, cols] * (high.astype(F32) + low.astype(F32))
+            total = skip_ref[:, cols] * mixed
             for p in range(RANK):
                 total = total + weights[p] * parts[p * STRETCH : (p + 1) * STRETCH, :]
             y_ref[c, rows, :] = total
@@ -460,19 +460,28 @@
     lax.fori_loop(0, slots // 2, end, 0)
 
 
-def join_kernel(back_ref, lift_ref, qc_ref, y_ref, z_ref, sq_ref):
-    blocks, tokens, _ = qc_ref.shape
+def join_kernel(back_ref, lift_ref, qc_ref, y_ref, z_ref, sq_ref, qc_vm, carry, sems):
+    blocks, tokens, _ = qc_vm.shape
     by_dest = len(back_ref.shape) == 3
-    total = jnp.zeros((tokens, LANES), F32)
+    chunk = 4
+    copies = []
+    for c in range(blocks // chunk):
+        rows = pl.ds(c * chunk, chunk)
+        copies.append(pltpu.make_async_copy(qc_ref.at[rows], qc_vm.at[rows], sems.at[c]))
+        copies[-1].start()
     for b in range(blocks):
         back = back_ref[b] if by_dest else back_ref[:, b * SPAN : (b + 1) * SPAN]
-        carry = jnp.dot(lift_ref[0], back, preferred_element_type=F32)
-        carry = carry + jnp.dot(lift_ref[1], back, preferred_element_type=F32)
-        z = qc_ref[b] * (y_ref[b] + carry)
-        z_ref[:, b * SPAN : (b + 1) * SPAN] = z
-        squares = z * z
-        for h in range(SPAN // LANES):
-            total = total + squares[:, h * LANES : (h + 1) * LANES]
+        product = jnp.dot(lift_ref[0], back, preferred_element_type=F32)
+        carry[b] = y_ref[b] + product + jnp.dot(lift_ref[1], back, preferred_element_type=F32)
+    total = jnp.zeros((tokens, LANES), F32)
+    for c in range(blocks // chunk):
+        copies[c].wait()
+        for b in range(c * chunk, (c + 1) * chunk):
+            z = qc_vm[b] * carry[b]
+            z_ref[:, b * SPAN : (b + 1) * SPAN] = z
+            squares = z * z
+            for h in range(SPAN // LANES):
+                total = total + squares[:, h * LANES : (h + 1) * LANES]
     sq_ref[...] = jnp.sum(total.T, axis=0, keepdims=True)
 
 
@@ -548,30 +557,29 @@
     weights = (short_weight, rates, residues, skip)
     own = [f32(*w.shape[:-1], share) for w in weights] if direct else []
     blocks = width // SPAN
-    pay, mixed, *mine = pl.pallas_call(
+    pay, *mine = pl.pallas_call(
         functools.partial(front_kernel, direct=direct),
         in_specs=[smem] + [hbm] * (5 + len(own)),
-        out_specs=[hbm] * 2 + [vmem] * len(own),
+        out_specs=[hbm] + [vmem] * len(own),
         out_shape=[
             pltpu.HBM((n_ctx, 2 * PIECE, share) if direct else (2 * PIECE, width), BF16),
-            pltpu.HBM((blocks, 2, tokens, SPAN), BF16),
         ]
         + own,
         scratch_shapes=[
             pltpu.VMEM((2, tokens, width), BF16),
             pltpu.VMEM((4, 16, width), BF16),
-            pltpu.VMEM(short_weight.shape, F32),
+            pltpu.VMEM((blocks, 2, REACH + 1, SPAN), F32),
             pltpu.VMEM(ends.shape, BF16),
             pltpu.VMEM((2, 2, 2, 2 * (STRETCH + 8), LANES), F32),
             pltpu.VMEM((2, 2, 32, LANES), F32),
             pltpu.VMEM((2, 2 * PIECE, LANES), F32),
             pltpu.VMEM((blocks, 2 * PIECE, SPAN), BF16),
-            pltpu.VMEM((blocks, 2, tokens, SPAN), BF16),
-            pltpu.SemaphoreType.DMA((2, blocks)),
+            pltpu.VMEM((2, 2, tokens, SPAN), BF16),
+            pltpu.SemaphoreType.DMA((3, blocks)),
             pltpu.SemaphoreType.DMA((4,)),
-            pltpu.SemaphoreType.DMA((2,)),
+            pltpu.SemaphoreType.DMA((1,)),
             pltpu.SemaphoreType.DMA((4,)),
-            pltpu.SemaphoreType.DMA((2, blocks)),
+            pltpu.SemaphoreType.DMA((blocks,)),
         ],
         compiler_params=limit(24),
         name="front_pieces",
@@ -583,22 +591,18 @@
     query, inner = pl.pallas_call(
         local_kernel,
         grid=(steps,),
-        in_specs=[
-            columns(tokens),
-            pl.BlockSpec((tile // SPAN, 2, tokens, SPAN), lambda c: (c, 0, 0, 0)),
-            columns(3, REACH + 1),
-            columns(order),
-            columns(order),
-            columns(1),
-            whole(local),
+        in_specs=[columns(tokens)] * 3
+        + [columns(3, REACH + 1), columns(order), columns(order), columns(1), whole(local)],
+        out_specs=[pl.BlockSpec((tile // SPAN, tokens, SPAN), lambda c: (c, 0, 0))] * 2,
+        out_shape=[pltpu.HBM((blocks, tokens, SPAN), F32), pltpu.VMEM((blocks, tokens, SPAN), F32)],
+        scratch_shapes=[
+            pltpu.VMEM((3, groups, 2 * (STRETCH + 8), LANES), F32),
+            pltpu.VMEM((tile // SPAN, tokens, SPAN), F32),
         ],
-        out_specs=[pl.BlockSpec((tile // SPAN, tokens, SPAN), lambda c: (c, 0, 0))] * 2,
-        out_shape=[pltpu.VMEM((blocks, tokens, SPAN), F32)] * 2,
-        scratch_shapes=[pltpu.VMEM((groups, 2 * (STRETCH + 8), LANES), F32)],
         compiler_params=limit(24),
         name="local_filter",
         cost_estimate=pl.CostEstimate(flops=10**9, bytes_accessed=20 * 10**6, transcendentals=0),
-    )(*map(pin, (q_in, mixed, short_weight, rates, residues)), skip, local)
+    )(*map(pin, (q_in, k_in, v_in, short_weight, rates, residues)), skip, local)
     arrived, query, inner = lax.optimization_barrier((arrived, query, inner))
 
     groups = lanes // LANES
@@ -635,12 +639,13 @@
     keep = lambda array: pltpu.with_memory_space_constraint(array, pltpu.VMEM)
     zvalues, squares = pl.pallas_call(
         join_kernel,
-        in_specs=[vmem] * 4,
+        in_specs=[vmem] * 2 + [hbm, vmem],
         out_specs=[vmem] * 2,
         out_shape=[f32(tokens, width), f32(1, tokens)],
+        scratch_shapes=[pltpu.VMEM((blocks, tokens, SPAN), F32)] * 2 + [pltpu.SemaphoreType.DMA((blocks // 4,))],
         compiler_params=limit(24),
         name="join_carry",
-    )(back, lift, keep(query), keep(inner))
+    )(back, lift, pin(query), keep(inner))
     sums = [squares]
     for shift in range(1, n_ch):
         sums.append(lax.ppermute(squares, "ch", [(i, (i + shift) % n_ch) for i in range(n_ch)]))

time: 60.5 us -> 59.3 us (0.980)
  Pallas kernels: 18.8 us -> 22.8 us
  local copies, waits for them, and re-layouts: 2.94 us -> 0.02 us
  waiting for transfers between devices: 13.1 us -> 10.9 us
    pallas_call x2, Pallas kernels: 5.94 us -> 10.9 us  [the longest x1 8.72 us: on_device(): pl.pallas_call(local_kernel, grid=(steps,), in_specs=[columns(tokens)] *...]
    unnamed x14 -> x10, local copies, waits for them, and re-layouts: 2.94 us -> 0.02 us
    all_to_all x1, waiting for transfers between devices: 11.1 us -> 8.89 us  [exchange(): return lax.all_to_all(array, 'ctx', 0, 0, tiled=True)]
    pallas_call x1, Pallas kernels: 7.38 us -> 6.38 us  [on_device(): pl.pallas_call(functools.partial(front_kernel, direct=direct), in_specs=[...]
  transfers between devices with their start and end apart: 2 -> 2, of which waited for: 2 -> 2; matrix products, arithmetic and copies ran while one was open for 0% -> 0% of each run, Pallas kernels for 9% -> 15%
where the time goes in v7:
time: 59.3 us; the launch traced here: 59 us
  Pallas kernels  22.8 us (38%)
  blocking collectives  16.2 us (27%)
  waiting for transfers between devices  10.9 us (18%)
  starting transfers between devices  8.95 us (15%)
    all_to_all x1, blocking collectives, on_device(): back = lax.all_to_all(back, 'ctx', 0, 0, tiled=True)  16.2 us
    all_to_all x1, waiting for transfers between devices, exchange(): return lax.all_to_all(array, 'ctx', 0, 0, tiled=True)  8.89 us
    pallas_call x1, Pallas kernels, on_device(): pl.pallas_call(local_kernel, grid=(steps,), in_specs=[columns(tokens)] *...  8.72 us
    all_to_all x1, starting transfers between devices, exchange(): return lax.all_to_all(array, 'ctx', 0, 0, tiled=True)  7.37 us
    pallas_call x1, Pallas kernels, on_device(): pl.pallas_call(functools.partial(front_kernel, direct=direct), in_specs=[...  6.38 us
    pallas_call x1, Pallas kernels, on_device(): pl.pallas_call(middle_kernel, in_specs=[smem] + [vmem] * 5, out_specs=hbm...  4.34 us
    pallas_call x1, Pallas kernels, on_device(): pl.pallas_call(join_kernel, in_specs=[vmem] * 2 + [hbm, vmem], out_specs=...  2.18 us
    ppermute x1, waiting for transfers between devices, on_device(): lax.ppermute(squares, 'ch', [(i, (i + shift) % n_ch) for i in range(n_ch)])  2.02 us
  transfers between devices with their start and end apart: 2, of which 2 were waited for; matrix products, arithmetic and copies ran while one was open for 0% of the time, Pallas kernels for 15%

profile of v7, /device:TPU:0, one launch (start us, length us, event | category | flops | bytes accessed | tf_op | source)
XLA Modules:
  0.0 59.0 jit_solution(9321729671013023228)
XLA Ops:
  0.0 0.0 copy-start
  0.0 0.0 copy-start.2
  0.0 6.4 %front_pieces.1 = (bf16[16,88,256]{2,1,0:T(8,128)(2,1)}, f32[3,7,256]{2,1,0:T(8,128)S(1)}, f32[16,256]{1,0:T(8,128)S(1)}, f32[16,256]{1,0:T(8,128)S(1)}, f32[1,256]{1,0:T(1,128)S(1)}) custom-call(s32[1]{0:T(128)} %bitcast.refs_0_, bf16[128,4096]{1,0:T(8,128)(2,1)} %q_ref.1, bf16[128,4096]{1,0:T(8,128)(2,1)} %k_ref.1, bf16[128,4096]{1,0:T(8,128)(2,1)} %v_ref.1, ...), custom_call_target="tpu_custom_call" | custom-call | tf_op jit(solution)/shard_map/front_pieces/pallas_call | solution.py:560
  6.4 7.4 %all-to-all-start = ((bf16[16,88,256]{2,1,0:T(8,128)(2,1)}), bf16[16,88,256]{2,1,0:T(8,128)(2,1)S(1)}, u32[]{:S(2)}, u32[]{:S(2)}) async-start(bf16[16,88,256]{2,1,0:T(8,128)(2,1)} %get-tuple-element.17), calls=%async_computation | async-start | bytes 1441792 | tf_op jit(solution)/shard_map/all_to_all | solution.py:538
  13.8 0.0 copy-done
  13.8 0.0 copy-done.2
  13.8 0.0 copy-start.4
  13.8 0.0 copy-start.1
  13.8 8.7 %local_filter.1 = (f32[16,128,256]{2,1,0:T(8,128)}, f32[16,128,256]{2,1,0:T(8,128)S(1)}) custom-call(bf16[128,4096]{1,0:T(8,128)(2,1)} %q_ref.1, bf16[128,4096]{1,0:T(8,128)(2,1)} %k_ref.1, bf16[128,4096]{1,0:T(8,128)(2,1)} %v_ref.1, f32[3,7,4096]{2,1,0:T(8,128)} %taps_ref.1, f32[16,4096]{1,0:T(8,128)} %rates_ref.1, f32[16,4096]{1,0:T(8,128)} %res_ref.1, ...), custom_call_target="tpu_custom_call" | custom-call | flops 1000000000 | bytes 20000000 | tf_op jit(solution)/shard_map/local_filter/pallas_call | solution.py:591
  22.5 8.9 %all-to-all-done.x_ref = bf16[16,88,256]{2,1,0:T(8,128)(2,1)S(1)} async-done(((bf16[16,88,256]{2,1,0:T(8,128)(2,1)}), bf16[16,88,256]{2,1,0:T(8,128)(2,1)S(1)}, u32[]{:S(2)}, u32[]{:S(2)}) %all-to-all-start) | async-done | bytes 720928 | tf_op jit(solution)/shard_map/all_to_all | solution.py:538
  31.4 0.0 copy-done.4
  31.4 4.3 %middle_states.1 = bf16[16,40,256]{2,1,0:T(8,128)(2,1)} custom-call(s32[32]{0:T(128)S(1)} %copy-done.4, bf16[16,88,256]{2,1,0:T(8,128)(2,1)S(1)} %all-to-all-done.x_ref, f32[3,7,256]{2,1,0:T(8,128)S(1)} %get-tuple-element.21.taps_ref, f32[16,256]{1,0:T(8,128)S(1)} %get-tuple-element.22.rates_ref, f32[16,256]{1,0:T(8,128)S(1)} %get-tuple-element.23.res_ref, ...), custom_call_target="tpu_custom_call" | custom-call | tf_op jit(solution)/shard_map/middle_states/pallas_call | solution.py:609
  35.8 16.2 %all_to_all.10.back_ref = bf16[16,40,256]{2,1,0:T(8,128)(2,1)S(1)} all-to-all(bf16[16,40,256]{2,1,0:T(8,128)(2,1)} %middle_states.1), channel_id=1, replica_groups=mesh['ctx'=16,'ch'=2] {'ctx'}, dimensions={0} | all-to-all | bytes 655360 | tf_op jit(solution)/shard_map/all_to_all | solution.py:635
  52.0 0.0 copy-done.1
  52.0 0.0 copy-start.3
  52.0 2.2 %join_carry.1 = (f32[128,4096]{1,0:T(8,128)S(1)}, f32[1,128]{1,0:T(1,128)S(1)}) custom-call(bf16[16,40,256]{2,1,0:T(8,128)(2,1)S(1)} %all_to_all.10.back_ref, bf16[2,128,40]{2,1,0:T(8,128)(2,1)S(1)} %copy-done.1, f32[16,128,256]{2,1,0:T(8,128)} %get-tuple-element.25.qc_ref, f32[16,128,256]{2,1,0:T(8,128)S(1)} %get-tuple-element.26.y_ref), custom_call_target="tpu_custom_call" | custom-call | tf_op jit(solution)/shard_map/join_carry/pallas_call | solution.py:640
  54.2 1.6 %collective-permute-start = (f32[1,128]{1,0:T(1,128)S(1)}, f32[1,128]{1,0:T(1,128)S(1)}, u32[]{:S(2)}, u32[]{:S(2)}) collective-permute-start(f32[1,128]{1,0:T(1,128)S(1)} %get-tuple-element.28.refs_2_), channel_id=1, source_target_pairs={{0,1},{1,0},{2,3},{3,2},{4,5},{5,4},{6,7},{7,6},{8,9},{9,8},{10,11... | collective-permute-start | bytes 1544 | tf_op jit(solution)/shard_map/ppermute | solution.py:651
  55.8 2.0 %collective-permute-done.refs_3_ = f32[1,128]{1,0:T(1,128)S(1)} collective-permute-done((f32[1,128]{1,0:T(1,128)S(1)}, f32[1,128]{1,0:T(1,128)S(1)}, u32[]{:S(2)}, u32[]{:S(2)}) %collective-permute-start) | collective-permute-done | bytes 544 | tf_op jit(solution)/shard_map/ppermute | solution.py:651
  57.8 0.0 copy-done.3
  57.8 1.1 %scale_rows.1 = bf16[128,4096]{1,0:T(8,128)(2,1)} custom-call(f32[128,4096]{1,0:T(8,128)S(1)} %get-tuple-element.27.refs_0_, f32[1,4096]{1,0:T(1,128)S(1)} %bitcast.5, f32[1,128]{1,0:T(1,128)S(1)} %get-tuple-element.28.refs_2_, f32[1,128]{1,0:T(1,128)S(1)} %collective-permute-done.refs_3_), custom_call_target="tpu_custom_call" | custom-call | tf_op jit(solution)/shard_map/scale_rows/pallas_call | solution.py:652
Async XLA Ops:
  0.0 13.8 %copy-start = (bf16[384,192]{1,0:T(8,128)(2,1)S(1)}, bf16[384,192]{1,0:T(8,128)(2,1)}, u32[]{:S(2)}) copy-start(bf16[384,192]{1,0:T(8,128)(2,1)} %constant.13.clone.local_ref) | copy-start | bytes 442372
  0.0 13.8 %copy-start.2 = (f32[4096]{0:T(1024)S(1)}, f32[4096]{0:T(1024)}, u32[]{:S(2)}) copy-start(f32[4096]{0:T(1024)} %param.19) | copy-start | bytes 49156
  6.4 25.0 %all-to-all-start = ((bf16[16,88,256]{2,1,0:T(8,128)(2,1)}), bf16[16,88,256]{2,1,0:T(8,128)(2,1)S(1)}, u32[]{:S(2)}, u32[]{:S(2)}) async-start(bf16[16,88,256]{2,1,0:T(8,128)(2,1)} %get-tuple-element.17), calls=%async_computation | async-start | bytes 1441792 | tf_op jit(solution)/shard_map/all_to_all | solution.py:538
  13.8 17.6 %copy-start.4 = (s32[32]{0:T(128)S(1)}, s32[32]{0:T(128)}, u32[]{:S(2)}) copy-start(s32[32]{0:T(128)} %perm_ref.1) | copy-start | bytes 388
  13.8 38.2 %copy-start.1 = (bf16[2,128,40]{2,1,0:T(8,128)(2,1)S(1)}, bf16[2,128,40]{2,1,0:T(8,128)(2,1)}, u32[]{:S(2)}) copy-start(bf16[2,128,40]{2,1,0:T(8,128)(2,1)} %constant.14.clone.lift_ref) | copy-start | bytes 61444
  52.0 5.8 %copy-start.3 = (f32[4096]{0:T(1024)S(1)}, f32[4096]{0:T(1024)}, u32[]{:S(2)}) copy-start(f32[4096]{0:T(1024)} %param.20) | copy-start | bytes 49156
  54.2 3.6 %collective-permute-start = (f32[1,128]{1,0:T(1,128)S(1)}, f32[1,128]{1,0:T(1,128)S(1)}, u32[]{:S(2)}, u32[]{:S(2)}) collective-permute-start(f32[1,128]{1,0:T(1,128)S(1)} %get-tuple-element.28.refs_2_), channel_id=1, source_target_pairs={{0,1},{1,0},{2,3},{3,2},{4,5},{5,4},{6,7},{7,6},{8,9},{9,8},{10,11... | collective-permute-start | bytes 1544 | tf_op jit(solution)/shard_map/ppermute | solution.py:651

commit v8 on v7

--- a/solution.py
+++ b/solution.py
@@ -135,7 +135,7 @@
         return [pltpu.make_async_copy(view, ref, own_sems.at[n]) for n, (view, ref) in enumerate(zip(views, kept))]
 
     ends_copy = pltpu.make_async_copy(ends_ref, ends_vm, tap_sem.at[0])
-    for copy in loads(0) + edge_loads():
+    for copy in edge_loads() + loads(0) + loads(1):
         copy.start()
     ends_copy.start()
 
@@ -144,11 +144,11 @@
             copy.start()
         return carry
 
-    lax.fori_loop(1, blocks, begin, 0)
+    lax.fori_loop(2, blocks, begin, 0)
     if direct:
         for copy in own_loads():
             copy.start()
-    for parity in range(2):
+    for parity in range(4):
         for a in range(2):
             for h in range(2):
                 for i in range(2):
@@ -160,7 +160,7 @@
             copy.wait()
 
     def features(c):
-        parity = lax.rem(c, 2)
+        parity = lax.rem(c, 4)
         for h in range(2):
             part = slice(h * LANES, (h + 1) * LANES)
             cols = pl.ds(pl.multiple_of(c * SPAN + h * LANES, LANES), LANES)
@@ -191,7 +191,7 @@
 
     def products(c):
         found = []
-        parity = lax.rem(c, 2)
+        parity = lax.rem(c, 4)
         for i in range(2):
             rows = slice(i * STRETCH, (i + 1) * STRETCH)
             high, low = u_vm[parity, 0, rows, :], u_vm[parity, 1, rows, :]
@@ -199,52 +199,67 @@
             found.append(jnp.dot(ends_vm[...], stacked, preferred_element_type=F32)[:8])
         return found
 
+    def query_rows(c, carry):
+        for h in range(2):
+            cols = pl.ds(pl.multiple_of(c * SPAN + h * LANES, LANES), LANES)
+            for i in range(2):
+                qs[h, i, 0:16, :] = edge[2 * i, :, cols].astype(F32)
+                qs[h, i, 16:32, :] = edge[2 * i + 1, :, cols].astype(F32)
+                at = i * PIECE
+                pay[c, h, at : at + REACH, :] = qs[h, i, 32 - REACH : 32, :]
+                pay[c, h, at + 3 * REACH : at + 4 * REACH, :] = qs[h, i, 0:REACH, :]
+        return carry
+
     def finish(c, found):
-        parity = lax.rem(c, 2)
+        parity = lax.rem(c, 4)
         for i in range(2):
             moments = found[i]
             rest = (moments - moments.astype(BF16).astype(F32))[:FINE]
             at = PIECE * i + RAW
             for h in range(2):
                 part = slice(h * LANES, (h + 1) * LANES)
-                pay[h, at : at + RANK, :] = moments[:RANK, part]
-                pay[h, at + RANK : at + COEFS, :] = rest[:, part]
+                pay[c, h, at : at + RANK, :] = moments[:RANK, part]
+                pay[c, h, at + RANK : at + COEFS, :] = rest[:, part]
         for h in range(2):
-            cols = pl.ds(pl.multiple_of(c * SPAN + h * LANES, LANES), LANES)
             for i in range(2):
                 base = i * (STRETCH + 8) + 8
-                qs[h, i, 0:16, :] = edge[2 * i, :, cols].astype(F32)
-                qs[h, i, 16:32, :] = edge[2 * i + 1, :, cols].astype(F32)
-                at = i * PIECE
-                pay[h, at : at + REACH, :] = qs[h, i, 32 - REACH : 32, :]
-                pay[h, at + 3 * REACH : at + 4 * REACH, :] = qs[h, i, 0:REACH, :]
                 for a in range(2):
                     at = i * PIECE + (1 + a) * REACH
-                    pay[h, at : at + REACH, :] = xs[parity, a, h, base + STRETCH - REACH : base + STRETCH, :]
+                    pay[c, h, at : at + REACH, :] = xs[parity, a, h, base + STRETCH - REACH : base + STRETCH, :]
                     at = at + 3 * REACH
-                    pay[h, at : at + REACH, :] = xs[parity, a, h, base : base + REACH, :]
-            packed[c, :, h * LANES : (h + 1) * LANES] = pay[h].astype(BF16)
+                    pay[c, h, at : at + REACH, :] = xs[parity, a, h, base : base + REACH, :]
+            packed[c, :, h * LANES : (h + 1) * LANES] = pay[c, h].astype(BF16)
 
     def send(c):
         for copy in stores(c):
             copy.start()
 
-    arrive(0)
     for copy in edge_loads():
         copy.wait()
+    lax.fori_loop(0, blocks, query_rows, 0, unroll=2)
     ends_copy.wait()
+    arrive(0)
+    arrive(1)
     features(0)
-
-    def both(c, carry):
+    features(1)
+
+    def both(step, carry):
+        c = 2 * step
         arrive(c)
-        found = products(c - 1)
+        arrive(c + 1)
+        before = [products(c - 2), products(c - 1)]
         features(c)
-        finish(c - 1, found)
+        finish(c - 2, before[0])
+        features(c + 1)
+        finish(c - 1, before[1])
+        send(c - 2)
         send(c - 1)
         return carry
 
-    lax.fori_loop(1, blocks, both, 0)
-    finish(blocks - 1, products(blocks - 1))
+    lax.fori_loop(1, blocks // 2, both, 0)
+    for c in (blocks - 2, blocks - 1):
+        finish(c, products(c))
+    send(blocks - 2)
     send(blocks - 1)
 
     def end(c, carry):
@@ -570,11 +585,11 @@
             pltpu.VMEM((4, 16, width), BF16),
             pltpu.VMEM((blocks, 2, REACH + 1, SPAN), F32),
             pltpu.VMEM(ends.shape, BF16),
-            pltpu.VMEM((2, 2, 2, 2 * (STRETCH + 8), LANES), F32),
+            pltpu.VMEM((4, 2, 2, 2 * (STRETCH + 8), LANES), F32),
             pltpu.VMEM((2, 2, 32, LANES), F32),
-            pltpu.VMEM((2, 2 * PIECE, LANES), F32),
+            pltpu.VMEM((blocks, 2, 2 * PIECE, LANES), F32),
             pltpu.VMEM((blocks, 2 * PIECE, SPAN), BF16),
-            pltpu.VMEM((2, 2, tokens, SPAN), BF16),
+            pltpu.VMEM((4, 2, tokens, SPAN), BF16),
             pltpu.SemaphoreType.DMA((3, blocks)),
             pltpu.SemaphoreType.DMA((4,)),
             pltpu.SemaphoreType.DMA((1,)),

time: 59.3 us -> 60.2 us (1.015)
  Pallas kernels: 22.8 us -> 23.6 us
    pallas_call x1, Pallas kernels: 6.38 us -> 7.23 us  [on_device(): pl.pallas_call(functools.partial(front_kernel, direct=direct), in_specs=[...]
where the time goes in v8:
time: 60.2 us; the launch traced here: 59.8 us
  Pallas kernels  23.6 us (39%)
  blocking collectives  16.2 us (27%)
  waiting for transfers between devices  10.9 us (18%)
  starting transfers between devices  8.95 us (15%)
    all_to_all x1, blocking collectives, on_device(): back = lax.all_to_all(back, 'ctx', 0, 0, tiled=True)  16.2 us
    all_to_all x1, waiting for transfers between devices, exchange(): return lax.all_to_all(array, 'ctx', 0, 0, tiled=True)  8.89 us
    pallas_call x1, Pallas kernels, on_device(): pl.pallas_call(local_kernel, grid=(steps,), in_specs=[columns(tokens)] *...  8.72 us
    all_to_all x1, starting transfers between devices, exchange(): return lax.all_to_all(array, 'ctx', 0, 0, tiled=True)  7.37 us
    pallas_call x1, Pallas kernels, on_device(): pl.pallas_call(functools.partial(front_kernel, direct=direct), in_specs=[...  7.23 us
    pallas_call x1, Pallas kernels, on_device(): pl.pallas_call(middle_kernel, in_specs=[smem] + [vmem] * 5, out_specs=hbm...  4.34 us
    pallas_call x1, Pallas kernels, on_device(): pl.pallas_call(join_kernel, in_specs=[vmem] * 2 + [hbm, vmem], out_specs=...  2.18 us
    ppermute x1, waiting for transfers between devices, on_device(): lax.ppermute(squares, 'ch', [(i, (i + shift) % n_ch) for i in range(n_ch)])  2.02 us
  transfers between devices with their start and end apart: 2, of which 2 were waited for; matrix products, arithmetic and copies ran while one was open for 0% of the time, Pallas kernels for 15%

profile of v8, /device:TPU:0, one launch (start us, length us, event | category | flops | bytes accessed | tf_op | source)
XLA Modules:
  0.0 59.8 jit_solution(11212900874053265661)
XLA Ops:
  0.0 0.0 copy-start
  0.0 0.0 copy-start.2
  0.0 7.2 %front_pieces.1 = (bf16[16,88,256]{2,1,0:T(8,128)(2,1)}, f32[3,7,256]{2,1,0:T(8,128)S(1)}, f32[16,256]{1,0:T(8,128)S(1)}, f32[16,256]{1,0:T(8,128)S(1)}, f32[1,256]{1,0:T(1,128)S(1)}) custom-call(s32[1]{0:T(128)} %bitcast.refs_0_, bf16[128,4096]{1,0:T(8,128)(2,1)} %q_ref.1, bf16[128,4096]{1,0:T(8,128)(2,1)} %k_ref.1, bf16[128,4096]{1,0:T(8,128)(2,1)} %v_ref.1, ...), custom_call_target="tpu_custom_call" | custom-call | tf_op jit(solution)/shard_map/front_pieces/pallas_call | solution.py:575
  7.2 7.4 %all-to-all-start = ((bf16[16,88,256]{2,1,0:T(8,128)(2,1)}), bf16[16,88,256]{2,1,0:T(8,128)(2,1)S(1)}, u32[]{:S(2)}, u32[]{:S(2)}) async-start(bf16[16,88,256]{2,1,0:T(8,128)(2,1)} %get-tuple-element.17), calls=%async_computation | async-start | bytes 1441792 | tf_op jit(solution)/shard_map/all_to_all | solution.py:553
  14.6 0.0 copy-done
  14.6 0.0 copy-done.2
  14.6 0.0 copy-start.4
  14.7 0.0 copy-start.1
  14.7 8.7 %local_filter.1 = (f32[16,128,256]{2,1,0:T(8,128)}, f32[16,128,256]{2,1,0:T(8,128)S(1)}) custom-call(bf16[128,4096]{1,0:T(8,128)(2,1)} %q_ref.1, bf16[128,4096]{1,0:T(8,128)(2,1)} %k_ref.1, bf16[128,4096]{1,0:T(8,128)(2,1)} %v_ref.1, f32[3,7,4096]{2,1,0:T(8,128)} %taps_ref.1, f32[16,4096]{1,0:T(8,128)} %rates_ref.1, f32[16,4096]{1,0:T(8,128)} %res_ref.1, ...), custom_call_target="tpu_custom_call" | custom-call | flops 1000000000 | bytes 20000000 | tf_op jit(solution)/shard_map/local_filter/pallas_call | solution.py:606
  23.4 8.9 %all-to-all-done.x_ref = bf16[16,88,256]{2,1,0:T(8,128)(2,1)S(1)} async-done(((bf16[16,88,256]{2,1,0:T(8,128)(2,1)}), bf16[16,88,256]{2,1,0:T(8,128)(2,1)S(1)}, u32[]{:S(2)}, u32[]{:S(2)}) %all-to-all-start) | async-done | bytes 720928 | tf_op jit(solution)/shard_map/all_to_all | solution.py:553
  32.3 0.0 copy-done.4
  32.3 4.3 %middle_states.1 = bf16[16,40,256]{2,1,0:T(8,128)(2,1)} custom-call(s32[32]{0:T(128)S(1)} %copy-done.4, bf16[16,88,256]{2,1,0:T(8,128)(2,1)S(1)} %all-to-all-done.x_ref, f32[3,7,256]{2,1,0:T(8,128)S(1)} %get-tuple-element.21.taps_ref, f32[16,256]{1,0:T(8,128)S(1)} %get-tuple-element.22.rates_ref, f32[16,256]{1,0:T(8,128)S(1)} %get-tuple-element.23.res_ref, ...), custom_call_target="tpu_custom_call" | custom-call | tf_op jit(solution)/shard_map/middle_states/pallas_call | solution.py:624
  36.6 16.2 %all_to_all.10.back_ref = bf16[16,40,256]{2,1,0:T(8,128)(2,1)S(1)} all-to-all(bf16[16,40,256]{2,1,0:T(8,128)(2,1)} %middle_states.1), channel_id=1, replica_groups=mesh['ctx'=16,'ch'=2] {'ctx'}, dimensions={0} | all-to-all | bytes 655360 | tf_op jit(solution)/shard_map/all_to_all | solution.py:650
  52.9 0.0 copy-done.1
  52.9 0.0 copy-start.3
  52.9 2.2 %join_carry.1 = (f32[128,4096]{1,0:T(8,128)S(1)}, f32[1,128]{1,0:T(1,128)S(1)}) custom-call(bf16[16,40,256]{2,1,0:T(8,128)(2,1)S(1)} %all_to_all.10.back_ref, bf16[2,128,40]{2,1,0:T(8,128)(2,1)S(1)} %copy-done.1, f32[16,128,256]{2,1,0:T(8,128)} %get-tuple-element.25.qc_ref, f32[16,128,256]{2,1,0:T(8,128)S(1)} %get-tuple-element.26.y_ref), custom_call_target="tpu_custom_call" | custom-call | tf_op jit(solution)/shard_map/join_carry/pallas_call | solution.py:655
  55.1 1.6 %collective-permute-start = (f32[1,128]{1,0:T(1,128)S(1)}, f32[1,128]{1,0:T(1,128)S(1)}, u32[]{:S(2)}, u32[]{:S(2)}) collective-permute-start(f32[1,128]{1,0:T(1,128)S(1)} %get-tuple-element.28.refs_2_), channel_id=1, source_target_pairs={{0,1},{1,0},{2,3},{3,2},{4,5},{5,4},{6,7},{7,6},{8,9},{9,8},{10,11... | collective-permute-start | bytes 1544 | tf_op jit(solution)/shard_map/ppermute | solution.py:666
  56.6 2.0 %collective-permute-done.refs_3_ = f32[1,128]{1,0:T(1,128)S(1)} collective-permute-done((f32[1,128]{1,0:T(1,128)S(1)}, f32[1,128]{1,0:T(1,128)S(1)}, u32[]{:S(2)}, u32[]{:S(2)}) %collective-permute-start) | collective-permute-done | bytes 544 | tf_op jit(solution)/shard_map/ppermute | solution.py:666
  58.7 0.0 copy-done.3
  58.7 1.1 %scale_rows.1 = bf16[128,4096]{1,0:T(8,128)(2,1)} custom-call(f32[128,4096]{1,0:T(8,128)S(1)} %get-tuple-element.27.refs_0_, f32[1,4096]{1,0:T(1,128)S(1)} %bitcast.5, f32[1,128]{1,0:T(1,128)S(1)} %get-tuple-element.28.refs_2_, f32[1,128]{1,0:T(1,128)S(1)} %collective-permute-done.refs_3_), custom_call_target="tpu_custom_call" | custom-call | tf_op jit(solution)/shard_map/scale_rows/pallas_call | solution.py:667
Async XLA Ops:
  0.0 14.6 %copy-start = (bf16[384,192]{1,0:T(8,128)(2,1)S(1)}, bf16[384,192]{1,0:T(8,128)(2,1)}, u32[]{:S(2)}) copy-start(bf16[384,192]{1,0:T(8,128)(2,1)} %constant.13.clone.local_ref) | copy-start | bytes 442372
  0.0 14.6 %copy-start.2 = (f32[4096]{0:T(1024)S(1)}, f32[4096]{0:T(1024)}, u32[]{:S(2)}) copy-start(f32[4096]{0:T(1024)} %param.19) | copy-start | bytes 49156
  7.2 25.0 %all-to-all-start = ((bf16[16,88,256]{2,1,0:T(8,128)(2,1)}), bf16[16,88,256]{2,1,0:T(8,128)(2,1)S(1)}, u32[]{:S(2)}, u32[]{:S(2)}) async-start(bf16[16,88,256]{2,1,0:T(8,128)(2,1)} %get-tuple-element.17), calls=%async_computation | async-start | bytes 1441792 | tf_op jit(solution)/shard_map/all_to_all | solution.py:553
  14.6 17.6 %copy-start.4 = (s32[32]{0:T(128)S(1)}, s32[32]{0:T(128)}, u32[]{:S(2)}) copy-start(s32[32]{0:T(128)} %perm_ref.1) | copy-start | bytes 388
  14.7 38.2 %copy-start.1 = (bf16[2,128,40]{2,1,0:T(8,128)(2,1)S(1)}, bf16[2,128,40]{2,1,0:T(8,128)(2,1)}, u32[]{:S(2)}) copy-start(bf16[2,128,40]{2,1,0:T(8,128)(2,1)} %constant.14.clone.lift_ref) | copy-start | bytes 61444
  52.9 5.8 %copy-start.3 = (f32[4096]{0:T(1024)S(1)}, f32[4096]{0:T(1024)}, u32[]{:S(2)}) copy-start(f32[4096]{0:T(1024)} %param.20) | copy-start | bytes 49156
  55.1 3.6 %collective-permute-start = (f32[1,128]{1,0:T(1,128)S(1)}, f32[1,128]{1,0:T(1,128)S(1)}, u32[]{:S(2)}, u32[]{:S(2)}) collective-permute-start(f32[1,128]{1,0:T(1,128)S(1)} %get-tuple-element.28.refs_2_), channel_id=1, source_target_pairs={{0,1},{1,0},{2,3},{3,2},{4,5},{5,4},{6,7},{7,6},{8,9},{9,8},{10,11... | collective-permute-start | bytes 1544 | tf_op jit(solution)/shard_map/ppermute | solution.py:666

commit v9 on v7

--- a/solution.py
+++ b/solution.py
@@ -150,48 +150,45 @@
             copy.start()
     for parity in range(2):
         for a in range(2):
-            for h in range(2):
-                for i in range(2):
-                    at = i * (STRETCH + 8)
-                    xs[parity, a, h, at : at + 8, :] = jnp.zeros((8, LANES), F32)
-
-    def arrive(c):
-        for copy in loads(c):
-            copy.wait()
-
-    def features(c):
-        parity = lax.rem(c, 2)
-        for h in range(2):
-            part = slice(h * LANES, (h + 1) * LANES)
-            cols = pl.ds(pl.multiple_of(c * SPAN + h * LANES, LANES), LANES)
-            for a in range(2):
-                for i in range(2):
-                    base = i * (STRETCH + 8) + 8
-                    xs[parity, a, h, base : base + STRETCH, :] = held[
-                        a, i * STRETCH : (i + 1) * STRETCH, cols
-                    ].astype(F32)
-            taps = [[taps_vm[c, a, j : j + 1, part] for j in range(REACH + 1)] for a in range(2)]
             for i in range(2):
-                for b in range(STRETCH // 16):
-                    base = i * (STRETCH + 8) + 8 + 16 * b
-                    both = []
-                    for a in range(2):
-                        total = taps[a][0] * xs[parity, a, h, base : base + 16, :]
-                        for j in range(1, REACH + 1):
-                            total = total + taps[a][j] * xs[parity, a, h, base - j : base - j + 16, :]
-                        both.append(total)
-                    mixed = both[0] * both[1]
-                    if b == 0:
-                        row = lax.broadcasted_iota(jnp.int32, (16, LANES), 0)
-                        mixed = jnp.where(row >= REACH, mixed, 0.0)
-                    high, low = split(mixed)
-                    rows = slice(i * STRETCH + 16 * b, i * STRETCH + 16 * b + 16)
-                    u_vm[parity, 0, rows, part] = high
-                    u_vm[parity, 1, rows, part] = low
-
-    def products(c):
+                at = i * (STRETCH + 8)
+                xs[parity, a, at : at + 8, :] = jnp.zeros((8, LANES), F32)
+    for copy in edge_loads():
+        copy.wait()
+    ends_copy.wait()
+    halves_of = SPAN // LANES
+    groups = blocks * halves_of
+
+    def features(g):
+        parity = lax.rem(g, 2)
+        block, part = g // halves_of, pl.ds(pl.multiple_of(lax.rem(g, halves_of) * LANES, LANES), LANES)
+        cols = pl.ds(pl.multiple_of(g * LANES, LANES), LANES)
+        for a in range(2):
+            for i in range(2):
+                base = i * (STRETCH + 8) + 8
+                xs[parity, a, base : base + STRETCH, :] = held[a, i * STRETCH : (i + 1) * STRETCH, cols].astype(F32)
+        taps = [[taps_vm[block, a, j : j + 1, part] for j in range(REACH + 1)] for a in range(2)]
+        for i in range(2):
+            for b in range(STRETCH // 16):
+                base = i * (STRETCH + 8) + 8 + 16 * b
+                both = []
+                for a in range(2):
+                    total = taps[a][0] * xs[parity, a, base : base + 16, :]
+                    for j in range(1, REACH + 1):
+                        total = total + taps[a][j] * xs[parity, a, base - j : base - j + 16, :]
+                    both.append(total)
+                mixed = both[0] * both[1]
+                if b == 0:
+                    row = lax.broadcasted_iota(jnp.int32, (16, LANES), 0)
+                    mixed = jnp.where(row >= REACH, mixed, 0.0)
+                high, low = split(mixed)
+                rows = slice(i * STRETCH + 16 * b, i * STRETCH + 16 * b + 16)
+                u_vm[parity, 0, rows, :] = high
+                u_vm[parity, 1, rows, :] = low
+
+    def products(g):
+        parity = lax.rem(g, 2)
         found = []
-        parity = lax.rem(c, 2)
         for i in range(2):
             rows = slice(i * STRETCH, (i + 1) * STRETCH)
             high, low = u_vm[parity, 0, rows, :], u_vm[parity, 1, rows, :]
@@ -199,53 +196,47 @@
             found.append(jnp.dot(ends_vm[...], stacked, preferred_element_type=F32)[:8])
         return found
 
-    def finish(c, found):
-        parity = lax.rem(c, 2)
+    def finish(g, found):
+        parity = lax.rem(g, 2)
+        block, part = g // halves_of, pl.ds(pl.multiple_of(lax.rem(g, halves_of) * LANES, LANES), LANES)
+        cols = pl.ds(pl.multiple_of(g * LANES, LANES), LANES)
         for i in range(2):
-            moments = found[i]
-            rest = (moments - moments.astype(BF16).astype(F32))[:FINE]
             at = PIECE * i + RAW
-            for h in range(2):
-                part = slice(h * LANES, (h + 1) * LANES)
-                pay[h, at : at + RANK, :] = moments[:RANK, part]
-                pay[h, at + RANK : at + COEFS, :] = rest[:, part]
-        for h in range(2):
-            cols = pl.ds(pl.multiple_of(c * SPAN + h * LANES, LANES), LANES)
-            for i in range(2):
-                base = i * (STRETCH + 8) + 8
-                qs[h, i, 0:16, :] = edge[2 * i, :, cols].astype(F32)
-                qs[h, i, 16:32, :] = edge[2 * i + 1, :, cols].astype(F32)
-                at = i * PIECE
-                pay[h, at : at + REACH, :] = qs[h, i, 32 - REACH : 32, :]
-                pay[h, at + 3 * REACH : at + 4 * REACH, :] = qs[h, i, 0:REACH, :]
-                for a in range(2):
-                    at = i * PIECE + (1 + a) * REACH
-                    pay[h, at : at + REACH, :] = xs[parity, a, h, base + STRETCH - REACH : base + STRETCH, :]
-                    at = at + 3 * REACH
-                    pay[h, at : at + REACH, :] = xs[parity, a, h, base : base + REACH, :]
-            packed[c, :, h * LANES : (h + 1) * LANES] = pay[h].astype(BF16)
-
-    def send(c):
-        for copy in stores(c):
-            copy.start()
-
-    arrive(0)
-    for copy in edge_loads():
-        copy.wait()
-    ends_copy.wait()
-    features(0)
-
-    def both(c, carry):
-        arrive(c)
-        found = products(c - 1)
-        features(c)
-        finish(c - 1, found)
-        send(c - 1)
-        return carry
-
-    lax.fori_loop(1, blocks, both, 0)
-    finish(blocks - 1, products(blocks - 1))
-    send(blocks - 1)
+            pay[parity, at : at + RANK, :] = found[i][:RANK]
+            pay[parity, at + RANK : at + COEFS, :] = (found[i] - found[i].astype(BF16).astype(F32))[:FINE]
+            base = i * (STRETCH + 8) + 8
+            qs[parity, i, 0:16, :] = edge[2 * i, :, cols].astype(F32)
+            qs[parity, i, 16:32, :] = edge[2 * i + 1, :, cols].astype(F32)
+            at = i * PIECE
+            pay[parity, at : at + REACH, :] = qs[parity, i, 32 - REACH : 32, :]
+            pay[parity, at + 3 * REACH : at + 4 * REACH, :] = qs[parity, i, 0:REACH, :]
+            for a in range(2):
+                at = i * PIECE + (1 + a) * REACH
+                pay[parity, at : at + REACH, :] = xs[parity, a, base + STRETCH - REACH : base + STRETCH, :]
+                at = at + 3 * REACH
+                pay[parity, at : at + REACH, :] = xs[parity, a, base : base + REACH, :]
+        packed[block, :, part] = pay[parity].astype(BF16)
+
+    def step(g, carry):
+        now, before = jnp.minimum(g, groups - 1), jnp.maximum(g - 1, 0)
+
+        @pl.when((lax.rem(g, halves_of) == 0) & (g < groups))
+        def _():
+            for copy in loads(g // halves_of):
+                copy.wait()
+
+        found = products(before)
+        features(now)
+        finish(before, found)
+
+        @pl.when((lax.rem(g, halves_of) == 0) & (g > 0))
+        def _():
+            for copy in stores(g // halves_of - 1):
+                copy.start()
+
+        return carry
+
+    lax.fori_loop(0, groups + 1, step, 0)
 
     def end(c, carry):
         for copy in stores(c):
@@ -308,7 +299,7 @@
 
 def middle_kernel(
     perm_ref, x_ref, taps_ref, rates_ref, res_ref, skip_ref, out_ref,
-    raw, ext, moments, past, heads, first, second, states, mids, coefs, result, slab, packed, out_sems,
+    raw, ext, moments, past, heads, first, second, states, mids, coefs, fades, result, slab, packed, out_sems,
 ):
     slots = perm_ref.shape[0]
     groups = x_ref.shape[2] // LANES
@@ -336,9 +327,8 @@
 
     lax.fori_loop(0, slots // 2, unpack, 0, unroll=2)
 
-    fades = []
-    for g in range(groups):
-        cols = slice(g * LANES, (g + 1) * LANES)
+    def group_pass(g, carry):
+        cols = pl.ds(pl.multiple_of(g * LANES, LANES), LANES)
         rate = rates_ref[:, cols]
         amount = amplitude(rate, res_ref[:, cols])
         basis = strengths(rate)
@@ -350,12 +340,13 @@
         for p in range(RANK):
             coefs[g, 1, p * order : (p + 1) * order, :] = amount * powers[1] * basis[p]
         fade_rest = jnp.exp(-rate * float(INNER))
-        fades.append((powers[REACH], fade_rest, fade_rest * powers[REACH]))
+        fades[g, 0] = powers[REACH]
+        fades[g, 1] = fade_rest * powers[REACH]
         taps = [[taps_ref[a, j : j + 1, cols] for j in range(REACH + 1)] for a in range(3)]
         near = [jnp.sum(amount * powers[d], axis=0, keepdims=True) for d in range(REACH)]
         near[0] = near[0] + skip_ref[:, cols]
 
-        def head_pass(n, carry, g=g, taps=taps, powers=powers, near=near):
+        def head_pass(n, carry):
             feats = []
             for a in range(3):
                 total = taps[a][0] * ext[a, g, n, 8:16, :]
@@ -378,7 +369,7 @@
 
         lax.fori_loop(0, slots, head_pass, 0, unroll=4)
 
-        def rest_pass(n, carry, g=g, basis=basis, fade_rest=fade_rest):
+        def rest_pass(n, carry):
             value = fade_rest * first[g, n]
             for p in range(RANK):
                 value = value + basis[p] * moments[g, n, p : p + 1, :]
@@ -386,14 +377,17 @@
             return carry
 
         lax.fori_loop(0, slots, rest_pass, 0, unroll=4)
+        return carry
+
+    lax.fori_loop(0, groups, group_pass, 0)
 
     def scan_pass(n, state):
         after = []
         at = pl.multiple_of(n * order, order)
         for g in range(groups):
             states[g, pl.ds(at, order), :] = state[g]
-            mids[g, pl.ds(at, order), :] = fades[g][0] * state[g] + first[g, n]
-            after.append(fades[g][2] * state[g] + second[g, n])
+            mids[g, pl.ds(at, order), :] = fades[g, 0] * state[g] + first[g, n]
+            after.append(fades[g, 1] * state[g] + second[g, n])
         return tuple(after)
 
     lax.fori_loop(0, slots, scan_pass, tuple(jnp.zeros((order, LANES), F32) for _ in range(groups)), unroll=4)
@@ -411,29 +405,31 @@
                     totals[p][k] = term if r == 0 else totals[p][k] + term
         return totals
 
-    def out_pass(q, carry):
-        for g in range(groups):
-            totals = sums(g, 0, states, q * quad)
-            for t in range(REACH):
-                for k in range(quad):
-                    tile = q * quad + k
-                    query = heads[g, pl.ds(tile * 128 + t, 8, stride=16), :]
-                    local = heads[g, pl.ds(tile * 128 + 8 + t, 8, stride=16), :]
-                    z = query * (local + totals[t][k])
-                    result[g, pl.ds(tile * 192 + t, 8, stride=24), :] = z
-                    result[g, pl.ds(tile * 192 + REACH + t, 8, stride=24), :] = z - z.astype(BF16).astype(F32)
-            totals = sums(g, 1, mids, q * quad)
-            for p in range(RANK):
-                for k in range(quad):
-                    tile = q * quad + k
-                    value = totals[p][k]
-                    result[g, pl.ds(tile * 192 + 2 * REACH + p, 8, stride=24), :] = value
-                    if p < FINE:
-                        rest = value - value.astype(BF16).astype(F32)
-                        result[g, pl.ds(tile * 192 + 2 * REACH + RANK + p, 8, stride=24), :] = rest
-        return carry
-
-    lax.fori_loop(0, slots // (8 * quad), out_pass, 0)
+    quads = slots // (8 * quad)
+
+    def out_pass(step, carry):
+        g, q = step // quads, lax.rem(step, quads)
+        totals = sums(g, 0, states, q * quad)
+        for t in range(REACH):
+            for k in range(quad):
+                tile = q * quad + k
+                query = heads[g, pl.ds(tile * 128 + t, 8, stride=16), :]
+                local = heads[g, pl.ds(tile * 128 + 8 + t, 8, stride=16), :]
+                z = query * (local + totals[t][k])
+                result[g, pl.ds(tile * 192 + t, 8, stride=24), :] = z
+                result[g, pl.ds(tile * 192 + REACH + t, 8, stride=24), :] = z - z.astype(BF16).astype(F32)
+        totals = sums(g, 1, mids, q * quad)
+        for p in range(RANK):
+            for k in range(quad):
+                tile = q * quad + k
+                value = totals[p][k]
+                result[g, pl.ds(tile * 192 + 2 * REACH + p, 8, stride=24), :] = value
+                if p < FINE:
+                    rest = value - value.astype(BF16).astype(F32)
+                    result[g, pl.ds(tile * 192 + 2 * REACH + RANK + p, 8, stride=24), :] = rest
+        return carry
+
+    lax.fori_loop(0, groups * quads, out_pass, 0)
 
     def store(src):
         return pltpu.make_async_copy(packed.at[src], out_ref.at[src], out_sems.at[src])
@@ -460,29 +456,47 @@
     lax.fori_loop(0, slots // 2, end, 0)
 
 
-def join_kernel(back_ref, lift_ref, qc_ref, y_ref, z_ref, sq_ref, qc_vm, carry, sems):
+def join_kernel(back_ref, lift_ref, qc_ref, y_ref, z_ref, sq_ref, qc_vm, carry, total, sems):
     blocks, tokens, _ = qc_vm.shape
     by_dest = len(back_ref.shape) == 3
     chunk = 4
-    copies = []
+
+    def load(c):
+        rows = pl.ds(c * chunk, chunk)
+        return pltpu.make_async_copy(qc_ref.at[rows], qc_vm.at[rows], sems.at[c])
+
+    def lanes(b):
+        return pl.ds(pl.multiple_of(b * SPAN, SPAN), SPAN)
+
     for c in range(blocks // chunk):
-        rows = pl.ds(c * chunk, chunk)
-        copies.append(pltpu.make_async_copy(qc_ref.at[rows], qc_vm.at[rows], sems.at[c]))
-        copies[-1].start()
-    for b in range(blocks):
-        back = back_ref[b] if by_dest else back_ref[:, b * SPAN : (b + 1) * SPAN]
-        product = jnp.dot(lift_ref[0], back, preferred_element_type=F32)
-        carry[b] = y_ref[b] + product + jnp.dot(lift_ref[1], back, preferred_element_type=F32)
-    total = jnp.zeros((tokens, LANES), F32)
-    for c in range(blocks // chunk):
-        copies[c].wait()
-        for b in range(c * chunk, (c + 1) * chunk):
+        load(c).start()
+
+    def products(c, unused):
+        for k in range(chunk):
+            b = c * chunk + k
+            back = back_ref[b] if by_dest else back_ref[:, lanes(b)]
+            product = jnp.dot(lift_ref[0], back, preferred_element_type=F32)
+            carry[b] = y_ref[b] + product + jnp.dot(lift_ref[1], back, preferred_element_type=F32)
+        return unused
+
+    lax.fori_loop(0, blocks // chunk, products, 0)
+    total[...] = jnp.zeros((tokens, LANES), F32)
+
+    def square(c, unused):
+        load(c).wait()
+        part = total[...]
+        for k in range(chunk):
+            b = c * chunk + k
             z = qc_vm[b] * carry[b]
-            z_ref[:, b * SPAN : (b + 1) * SPAN] = z
+            z_ref[:, lanes(b)] = z
             squares = z * z
             for h in range(SPAN // LANES):
-                total = total + squares[:, h * LANES : (h + 1) * LANES]
-    sq_ref[...] = jnp.sum(total.T, axis=0, keepdims=True)
+                part = part + squares[:, h * LANES : (h + 1) * LANES]
+        total[...] = part
+        return unused
+
+    lax.fori_loop(0, blocks // chunk, square, 0)
+    sq_ref[...] = jnp.sum(total[...].T, axis=0, keepdims=True)
 
 
 def scale_kernel(*refs, channels):
@@ -495,17 +509,24 @@
         total = total + ref[...]
     scale = lax.rsqrt(total / channels + 1e-05)
     scale = jnp.broadcast_to(scale, (LANES, tokens)).T
-    copies = []
-    for c in range(chunks):
-        for g in range(c * wide // LANES, (c + 1) * wide // LANES):
-            cols = slice(g * LANES, (g + 1) * LANES)
+
+    def store(c):
+        cols = pl.ds(pl.multiple_of(c * wide, LANES), wide)
+        return pltpu.make_async_copy(held.at[:, cols], out_ref.at[:, cols], sems.at[c])
+
+    def run(c, unused):
+        for g in range(wide // LANES):
+            cols = pl.ds(pl.multiple_of(c * wide + g * LANES, LANES), LANES)
             held[:, cols] = (z_ref[:, cols] * scale * gain_ref[:, cols]).astype(BF16)
-        cols = pl.ds(c * wide, wide)
-        copy = pltpu.make_async_copy(held.at[:, cols], out_ref.at[:, cols], sems.at[c])
-        copy.start()
-        copies.append(copy)
-    for copy in copies:
-        copy.wait()
+        store(c).start()
+        return unused
+
+    def end(c, unused):
+        store(c).wait()
+        return unused
+
+    lax.fori_loop(0, chunks, run, 0)
+    lax.fori_loop(0, chunks, end, 0)
 
 
 def limit(mib):
@@ -570,11 +591,11 @@
             pltpu.VMEM((4, 16, width), BF16),
             pltpu.VMEM((blocks, 2, REACH + 1, SPAN), F32),
             pltpu.VMEM(ends.shape, BF16),
-            pltpu.VMEM((2, 2, 2, 2 * (STRETCH + 8), LANES), F32),
+            pltpu.VMEM((2, 2, 2 * (STRETCH + 8), LANES), F32),
             pltpu.VMEM((2, 2, 32, LANES), F32),
             pltpu.VMEM((2, 2 * PIECE, LANES), F32),
             pltpu.VMEM((blocks, 2 * PIECE, SPAN), BF16),
-            pltpu.VMEM((2, 2, tokens, SPAN), BF16),
+            pltpu.VMEM((2, 2, tokens, LANES), BF16),
             pltpu.SemaphoreType.DMA((3, blocks)),
             pltpu.SemaphoreType.DMA((4,)),
             pltpu.SemaphoreType.DMA((1,)),
@@ -621,6 +642,7 @@
             pltpu.VMEM((groups, slots * order, LANES), F32),
             pltpu.VMEM((groups, slots * order, LANES), F32),
             pltpu.VMEM((groups, 2, RANK * order, LANES), F32),
+            pltpu.VMEM((groups, 2, order, LANES), F32),
             pltpu.VMEM((groups, slots * 24, LANES), F32),
             pltpu.VMEM((n_ctx, groups, BACK + 28, LANES), F32),
             pltpu.VMEM((n_ctx, 2 * BACK, lanes), BF16),
@@ -642,7 +664,8 @@
         in_specs=[vmem] * 2 + [hbm, vmem],
         out_specs=[vmem] * 2,
         out_shape=[f32(tokens, width), f32(1, tokens)],
-        scratch_shapes=[pltpu.VMEM((blocks, tokens, SPAN), F32)] * 2 + [pltpu.SemaphoreType.DMA((blocks // 4,))],
+        scratch_shapes=[pltpu.VMEM((blocks, tokens, SPAN), F32)] * 2
+        + [pltpu.VMEM((tokens, LANES), F32), pltpu.SemaphoreType.DMA((blocks // 4,))],
         compiler_params=limit(24),
         name="join_carry",
     )(back, lift, pin(query), keep(inner))

time: 59.3 us -> 61.4 us (1.035)
  Pallas kernels: 22.8 us -> 24.9 us
    pallas_call x1, Pallas kernels: 6.38 us -> 8.77 us  [on_device(): pl.pallas_call(functools.partial(front_kernel, direct=direct), in_specs=[...]
  transfers between devices with their start and end apart: 2 -> 2, of which waited for: 2 -> 2; matrix products, arithmetic and copies ran while one was open for 0% -> 0% of each run, Pallas kernels for 15% -> 14%
where the time goes in v9:
time: 61.4 us; the launch traced here: 61.1 us
  Pallas kernels  24.9 us (41%)
  blocking collectives  16.2 us (26%)
  waiting for transfers between devices  10.9 us (18%)
  starting transfers between devices  8.95 us (15%)
    all_to_all x1, blocking collectives, on_device(): back = lax.all_to_all(back, 'ctx', 0, 0, tiled=True)  16.2 us
    all_to_all x1, waiting for transfers between devices, exchange(): return lax.all_to_all(array, 'ctx', 0, 0, tiled=True)  8.9 us
    pallas_call x1, Pallas kernels, on_device(): pl.pallas_call(functools.partial(front_kernel, direct=direct), in_specs=[...  8.77 us
    pallas_call x1, Pallas kernels, on_device(): pl.pallas_call(local_kernel, grid=(steps,), in_specs=[columns(tokens)] *...  8.71 us
    all_to_all x1, starting transfers between devices, exchange(): return lax.all_to_all(array, 'ctx', 0, 0, tiled=True)  7.37 us
    pallas_call x1, Pallas kernels, on_device(): pl.pallas_call(middle_kernel, in_specs=[smem] + [vmem] * 5, out_specs=hbm...  4.3 us
    ppermute x1, waiting for transfers between devices, on_device(): lax.ppermute(squares, 'ch', [(i, (i + shift) % n_ch) for i in range(n_ch)])  2.02 us
    pallas_call x1, Pallas kernels, on_device(): pl.pallas_call(join_kernel, in_specs=[vmem] * 2 + [hbm, vmem], out_specs=...  1.75 us
  transfers between devices with their start and end apart: 2, of which 2 were waited for; matrix products, arithmetic and copies ran while one was open for 0% of the time, Pallas kernels for 14%

profile of v9, /device:TPU:0, one launch (start us, length us, event | category | flops | bytes accessed | tf_op | source)
XLA Modules:
  0.0 61.1 jit_solution(14312429477499928063)
XLA Ops:
  0.0 0.0 copy-start
  0.0 0.0 copy-start.2
  0.0 8.8 %front_pieces.1 = (bf16[16,88,256]{2,1,0:T(8,128)(2,1)}, f32[3,7,256]{2,1,0:T(8,128)S(1)}, f32[16,256]{1,0:T(8,128)S(1)}, f32[16,256]{1,0:T(8,128)S(1)}, f32[1,256]{1,0:T(1,128)S(1)}) custom-call(s32[1]{0:T(128)} %bitcast.refs_0_, bf16[128,4096]{1,0:T(8,128)(2,1)} %q_ref.1, bf16[128,4096]{1,0:T(8,128)(2,1)} %k_ref.1, bf16[128,4096]{1,0:T(8,128)(2,1)} %v_ref.1, ...), custom_call_target="tpu_custom_call" | custom-call | tf_op jit(solution)/shard_map/front_pieces/pallas_call | solution.py:581
  8.8 7.4 %all-to-all-start = ((bf16[16,88,256]{2,1,0:T(8,128)(2,1)}), bf16[16,88,256]{2,1,0:T(8,128)(2,1)S(1)}, u32[]{:S(2)}, u32[]{:S(2)}) async-start(bf16[16,88,256]{2,1,0:T(8,128)(2,1)} %get-tuple-element.17), calls=%async_computation | async-start | bytes 1441792 | tf_op jit(solution)/shard_map/all_to_all | solution.py:559
  16.2 0.0 copy-done
  16.2 0.0 copy-done.2
  16.2 0.0 copy-start.4
  16.2 0.0 copy-start.1
  16.2 8.7 %local_filter.1 = (f32[16,128,256]{2,1,0:T(8,128)}, f32[16,128,256]{2,1,0:T(8,128)S(1)}) custom-call(bf16[128,4096]{1,0:T(8,128)(2,1)} %q_ref.1, bf16[128,4096]{1,0:T(8,128)(2,1)} %k_ref.1, bf16[128,4096]{1,0:T(8,128)(2,1)} %v_ref.1, f32[3,7,4096]{2,1,0:T(8,128)} %taps_ref.1, f32[16,4096]{1,0:T(8,128)} %rates_ref.1, f32[16,4096]{1,0:T(8,128)} %res_ref.1, ...), custom_call_target="tpu_custom_call" | custom-call | flops 1000000000 | bytes 20000000 | tf_op jit(solution)/shard_map/local_filter/pallas_call | solution.py:612
  24.9 8.9 %all-to-all-done.x_ref = bf16[16,88,256]{2,1,0:T(8,128)(2,1)S(1)} async-done(((bf16[16,88,256]{2,1,0:T(8,128)(2,1)}), bf16[16,88,256]{2,1,0:T(8,128)(2,1)S(1)}, u32[]{:S(2)}, u32[]{:S(2)}) %all-to-all-start) | async-done | bytes 720928 | tf_op jit(solution)/shard_map/all_to_all | solution.py:559
  33.8 0.0 copy-done.4
  33.8 4.3 %middle_states.1 = bf16[16,40,256]{2,1,0:T(8,128)(2,1)} custom-call(s32[32]{0:T(128)S(1)} %copy-done.4, bf16[16,88,256]{2,1,0:T(8,128)(2,1)S(1)} %all-to-all-done.x_ref, f32[3,7,256]{2,1,0:T(8,128)S(1)} %get-tuple-element.21.taps_ref, f32[16,256]{1,0:T(8,128)S(1)} %get-tuple-element.22.rates_ref, f32[16,256]{1,0:T(8,128)S(1)} %get-tuple-element.23.res_ref, ...), custom_call_target="tpu_custom_call" | custom-call | tf_op jit(solution)/shard_map/middle_states/pallas_call | solution.py:630
  38.1 16.2 %all_to_all.10.back_ref = bf16[16,40,256]{2,1,0:T(8,128)(2,1)S(1)} all-to-all(bf16[16,40,256]{2,1,0:T(8,128)(2,1)} %middle_states.1), channel_id=1, replica_groups=mesh['ctx'=16,'ch'=2] {'ctx'}, dimensions={0} | all-to-all | bytes 655360 | tf_op jit(solution)/shard_map/all_to_all | solution.py:657
  54.4 0.0 copy-done.1
  54.4 0.0 copy-start.3
  54.4 1.7 %join_carry.1 = (f32[128,4096]{1,0:T(8,128)S(1)}, f32[1,128]{1,0:T(1,128)S(1)}) custom-call(bf16[16,40,256]{2,1,0:T(8,128)(2,1)S(1)} %all_to_all.10.back_ref, bf16[2,128,40]{2,1,0:T(8,128)(2,1)S(1)} %copy-done.1, f32[16,128,256]{2,1,0:T(8,128)} %get-tuple-element.25.qc_ref, f32[16,128,256]{2,1,0:T(8,128)S(1)} %get-tuple-element.26.y_ref), custom_call_target="tpu_custom_call" | custom-call | tf_op jit(solution)/shard_map/join_carry/pallas_call | solution.py:662
  56.1 1.6 %collective-permute-start = (f32[1,128]{1,0:T(1,128)S(1)}, f32[1,128]{1,0:T(1,128)S(1)}, u32[]{:S(2)}, u32[]{:S(2)}) collective-permute-start(f32[1,128]{1,0:T(1,128)S(1)} %get-tuple-element.28.refs_2_), channel_id=1, source_target_pairs={{0,1},{1,0},{2,3},{3,2},{4,5},{5,4},{6,7},{7,6},{8,9},{9,8},{10,11... | collective-permute-start | bytes 1544 | tf_op jit(solution)/shard_map/ppermute | solution.py:674
  57.7 2.0 %collective-permute-done.refs_3_ = f32[1,128]{1,0:T(1,128)S(1)} collective-permute-done((f32[1,128]{1,0:T(1,128)S(1)}, f32[1,128]{1,0:T(1,128)S(1)}, u32[]{:S(2)}, u32[]{:S(2)}) %collective-permute-start) | collective-permute-done | bytes 544 | tf_op jit(solution)/shard_map/ppermute | solution.py:674
  59.7 0.0 copy-done.3
  59.7 1.4 %scale_rows.1 = bf16[128,4096]{1,0:T(8,128)(2,1)} custom-call(f32[128,4096]{1,0:T(8,128)S(1)} %get-tuple-element.27.refs_0_, f32[1,4096]{1,0:T(1,128)S(1)} %bitcast.5, f32[1,128]{1,0:T(1,128)S(1)} %get-tuple-element.28.refs_2_, f32[1,128]{1,0:T(1,128)S(1)} %collective-permute-done.refs_3_), custom_call_target="tpu_custom_call" | custom-call | tf_op jit(solution)/shard_map/scale_rows/pallas_call | solution.py:675
Async XLA Ops:
  0.0 16.2 %copy-start = (bf16[384,192]{1,0:T(8,128)(2,1)S(1)}, bf16[384,192]{1,0:T(8,128)(2,1)}, u32[]{:S(2)}) copy-start(bf16[384,192]{1,0:T(8,128)(2,1)} %constant.13.clone.local_ref) | copy-start | bytes 442372
  0.0 16.2 %copy-start.2 = (f32[4096]{0:T(1024)S(1)}, f32[4096]{0:T(1024)}, u32[]{:S(2)}) copy-start(f32[4096]{0:T(1024)} %param.19) | copy-start | bytes 49156
  8.8 25.0 %all-to-all-start = ((bf16[16,88,256]{2,1,0:T(8,128)(2,1)}), bf16[16,88,256]{2,1,0:T(8,128)(2,1)S(1)}, u32[]{:S(2)}, u32[]{:S(2)}) async-start(bf16[16,88,256]{2,1,0:T(8,128)(2,1)} %get-tuple-element.17), calls=%async_computation | async-start | bytes 1441792 | tf_op jit(solution)/shard_map/all_to_all | solution.py:559
  16.2 17.6 %copy-start.4 = (s32[32]{0:T(128)S(1)}, s32[32]{0:T(128)}, u32[]{:S(2)}) copy-start(s32[32]{0:T(128)} %perm_ref.1) | copy-start | bytes 388
  16.2 38.2 %copy-start.1 = (bf16[2,128,40]{2,1,0:T(8,128)(2,1)S(1)}, bf16[2,128,40]{2,1,0:T(8,128)(2,1)}, u32[]{:S(2)}) copy-start(bf16[2,128,40]{2,1,0:T(8,128)(2,1)} %constant.14.clone.lift_ref) | copy-start | bytes 61444
  54.4 5.4 %copy-start.3 = (f32[4096]{0:T(1024)S(1)}, f32[4096]{0:T(1024)}, u32[]{:S(2)}) copy-start(f32[4096]{0:T(1024)} %param.20) | copy-start | bytes 49156
  56.1 3.6 %collective-permute-start = (f32[1,128]{1,0:T(1,128)S(1)}, f32[1,128]{1,0:T(1,128)S(1)}, u32[]{:S(2)}, u32[]{:S(2)}) collective-permute-start(f32[1,128]{1,0:T(1,128)S(1)} %get-tuple-element.28.refs_2_), channel_id=1, source_target_pairs={{0,1},{1,0},{2,3},{3,2},{4,5},{5,4},{6,7},{7,6},{8,9},{9,8},{10,11... | collective-permute-start | bytes 1544 | tf_op jit(solution)/shard_map/ppermute | solution.py:674

commit v10 on v9

--- a/solution.py
+++ b/solution.py
@@ -150,93 +150,81 @@
             copy.start()
     for parity in range(2):
         for a in range(2):
-            for i in range(2):
-                at = i * (STRETCH + 8)
-                xs[parity, a, at : at + 8, :] = jnp.zeros((8, LANES), F32)
+            for h in range(2):
+                for i in range(2):
+                    at = i * (STRETCH + 8)
+                    xs[parity, a, h, at : at + 8, :] = jnp.zeros((8, LANES), F32)
     for copy in edge_loads():
         copy.wait()
     ends_copy.wait()
-    halves_of = SPAN // LANES
-    groups = blocks * halves_of
-
-    def features(g):
-        parity = lax.rem(g, 2)
-        block, part = g // halves_of, pl.ds(pl.multiple_of(lax.rem(g, halves_of) * LANES, LANES), LANES)
-        cols = pl.ds(pl.multiple_of(g * LANES, LANES), LANES)
-        for a in range(2):
+
+    def features(c, carry):
+        for copy in loads(c):
+            copy.wait()
+        parity = lax.rem(c, 2)
+        for h in range(2):
+            part = slice(h * LANES, (h + 1) * LANES)
+            cols = pl.ds(pl.multiple_of(c * SPAN + h * LANES, LANES), LANES)
             for i in range(2):
                 base = i * (STRETCH + 8) + 8
-                xs[parity, a, base : base + STRETCH, :] = held[a, i * STRETCH : (i + 1) * STRETCH, cols].astype(F32)
-        taps = [[taps_vm[block, a, j : j + 1, part] for j in range(REACH + 1)] for a in range(2)]
-        for i in range(2):
-            for b in range(STRETCH // 16):
-                base = i * (STRETCH + 8) + 8 + 16 * b
-                both = []
                 for a in range(2):
-                    total = taps[a][0] * xs[parity, a, base : base + 16, :]
-                    for j in range(1, REACH + 1):
-                        total = total + taps[a][j] * xs[parity, a, base - j : base - j + 16, :]
-                    both.append(total)
-                mixed = both[0] * both[1]
-                if b == 0:
-                    row = lax.broadcasted_iota(jnp.int32, (16, LANES), 0)
-                    mixed = jnp.where(row >= REACH, mixed, 0.0)
-                high, low = split(mixed)
-                rows = slice(i * STRETCH + 16 * b, i * STRETCH + 16 * b + 16)
-                u_vm[parity, 0, rows, :] = high
-                u_vm[parity, 1, rows, :] = low
-
-    def products(g):
-        parity = lax.rem(g, 2)
-        found = []
-        for i in range(2):
-            rows = slice(i * STRETCH, (i + 1) * STRETCH)
-            high, low = u_vm[parity, 0, rows, :], u_vm[parity, 1, rows, :]
-            stacked = jnp.concatenate([high, low, high], axis=0)
-            found.append(jnp.dot(ends_vm[...], stacked, preferred_element_type=F32)[:8])
-        return found
-
-    def finish(g, found):
-        parity = lax.rem(g, 2)
-        block, part = g // halves_of, pl.ds(pl.multiple_of(lax.rem(g, halves_of) * LANES, LANES), LANES)
-        cols = pl.ds(pl.multiple_of(g * LANES, LANES), LANES)
-        for i in range(2):
-            at = PIECE * i + RAW
-            pay[parity, at : at + RANK, :] = found[i][:RANK]
-            pay[parity, at + RANK : at + COEFS, :] = (found[i] - found[i].astype(BF16).astype(F32))[:FINE]
-            base = i * (STRETCH + 8) + 8
-            qs[parity, i, 0:16, :] = edge[2 * i, :, cols].astype(F32)
-            qs[parity, i, 16:32, :] = edge[2 * i + 1, :, cols].astype(F32)
-            at = i * PIECE
-            pay[parity, at : at + REACH, :] = qs[parity, i, 32 - REACH : 32, :]
-            pay[parity, at + 3 * REACH : at + 4 * REACH, :] = qs[parity, i, 0:REACH, :]
-            for a in range(2):
-                at = i * PIECE + (1 + a) * REACH
-                pay[parity, at : at + REACH, :] = xs[parity, a, base + STRETCH - REACH : base + STRETCH, :]
-                at = at + 3 * REACH
-                pay[parity, at : at + REACH, :] = xs[parity, a, base : base + REACH, :]
-        packed[block, :, part] = pay[parity].astype(BF16)
-
-    def step(g, carry):
-        now, before = jnp.minimum(g, groups - 1), jnp.maximum(g - 1, 0)
-
-        @pl.when((lax.rem(g, halves_of) == 0) & (g < groups))
-        def _():
-            for copy in loads(g // halves_of):
-                copy.wait()
-
-        found = products(before)
-        features(now)
-        finish(before, found)
-
-        @pl.when((lax.rem(g, halves_of) == 0) & (g > 0))
-        def _():
-            for copy in stores(g // halves_of - 1):
+                    xs[parity, a, h, base : base + STRETCH, :] = held[
+                        a, i * STRETCH : (i + 1) * STRETCH, cols
+                    ].astype(F32)
+                    at = i * PIECE + (1 + a) * REACH
+                    pay[c, h, at : at + REACH, :] = xs[parity, a, h, base + STRETCH - REACH : base + STRETCH, :]
+                    at = at + 3 * REACH
+                    pay[c, h, at : at + REACH, :] = xs[parity, a, h, base : base + REACH, :]
+                qs[parity, h, i, 0:16, :] = edge[2 * i, :, cols].astype(F32)
+                qs[parity, h, i, 16:32, :] = edge[2 * i + 1, :, cols].astype(F32)
+                at = i * PIECE
+                pay[c, h, at : at + REACH, :] = qs[parity, h, i, 32 - REACH : 32, :]
+                pay[c, h, at + 3 * REACH : at + 4 * REACH, :] = qs[parity, h, i, 0:REACH, :]
+            taps = [[taps_vm[c, a, j : j + 1, part] for j in range(REACH + 1)] for a in range(2)]
+            for i in range(2):
+                for b in range(STRETCH // 16):
+                    base = i * (STRETCH + 8) + 8 + 16 * b
+                    both = []
+                    for a in range(2):
+                        total = taps[a][0] * xs[parity, a, h, base : base + 16, :]
+                        for j in range(1, REACH + 1):
+                            total = total + taps[a][j] * xs[parity, a, h, base - j : base - j + 16, :]
+                        both.append(total)
+                    mixed = both[0] * both[1]
+                    if b == 0:
+                        row = lax.broadcasted_iota(jnp.int32, (16, LANES), 0)
+                        mixed = jnp.where(row >= REACH, mixed, 0.0)
+                    high, low = split(mixed)
+                    rows = slice(i * STRETCH + 16 * b, i * STRETCH + 16 * b + 16)
+                    u_vm[c, 0, rows, part] = high
+                    u_vm[c, 1, rows, part] = low
+        return carry
+
+    lax.fori_loop(0, blocks, features, 0)
+    chunk = 4
+
+    def finish(step, carry):
+        for k in range(chunk):
+            c = step * chunk + k
+            for i in range(2):
+                rows = slice(i * STRETCH, (i + 1) * STRETCH)
+                high, low = u_vm[c, 0, rows, :], u_vm[c, 1, rows, :]
+                stacked = jnp.concatenate([high, low, high], axis=0)
+                moments = jnp.dot(ends_vm[...], stacked, preferred_element_type=F32)[:8]
+                rest = (moments - moments.astype(BF16).astype(F32))[:FINE]
+                at = PIECE * i + RAW
+                for h in range(2):
+                    part = slice(h * LANES, (h + 1) * LANES)
+                    pay[c, h, at : at + RANK, :] = moments[:RANK, part]
+                    pay[c, h, at + RANK : at + COEFS, :] = rest[:, part]
+            for h in range(2):
+                packed[c, :, h * LANES : (h + 1) * LANES] = pay[c, h].astype(BF16)
+        for k in range(chunk):
+            for copy in stores(step * chunk + k):
                 copy.start()
-
-        return carry
-
-    lax.fori_loop(0, groups + 1, step, 0)
+        return carry
+
+    lax.fori_loop(0, blocks // chunk, finish, 0)
 
     def end(c, carry):
         for copy in stores(c):
@@ -509,24 +497,17 @@
         total = total + ref[...]
     scale = lax.rsqrt(total / channels + 1e-05)
     scale = jnp.broadcast_to(scale, (LANES, tokens)).T
-
-    def store(c):
-        cols = pl.ds(pl.multiple_of(c * wide, LANES), wide)
-        return pltpu.make_async_copy(held.at[:, cols], out_ref.at[:, cols], sems.at[c])
-
-    def run(c, unused):
-        for g in range(wide // LANES):
-            cols = pl.ds(pl.multiple_of(c * wide + g * LANES, LANES), LANES)
+    copies = []
+    for c in range(chunks):
+        for g in range(c * wide // LANES, (c + 1) * wide // LANES):
+            cols = slice(g * LANES, (g + 1) * LANES)
             held[:, cols] = (z_ref[:, cols] * scale * gain_ref[:, cols]).astype(BF16)
-        store(c).start()
-        return unused
-
-    def end(c, unused):
-        store(c).wait()
-        return unused
-
-    lax.fori_loop(0, chunks, run, 0)
-    lax.fori_loop(0, chunks, end, 0)
+        cols = pl.ds(c * wide, wide)
+        copy = pltpu.make_async_copy(held.at[:, cols], out_ref.at[:, cols], sems.at[c])
+        copy.start()
+        copies.append(copy)
+    for copy in copies:
+        copy.wait()
 
 
 def limit(mib):
@@ -591,11 +572,11 @@
             pltpu.VMEM((4, 16, width), BF16),
             pltpu.VMEM((blocks, 2, REACH + 1, SPAN), F32),
             pltpu.VMEM(ends.shape, BF16),
-            pltpu.VMEM((2, 2, 2 * (STRETCH + 8), LANES), F32),
-            pltpu.VMEM((2, 2, 32, LANES), F32),
-            pltpu.VMEM((2, 2 * PIECE, LANES), F32),
+            pltpu.VMEM((2, 2, 2, 2 * (STRETCH + 8), LANES), F32),
+            pltpu.VMEM((2, 2, 2, 32, LANES), F32),
+            pltpu.VMEM((blocks, 2, 2 * PIECE, LANES), F32),
             pltpu.VMEM((blocks, 2 * PIECE, SPAN), BF16),
-            pltpu.VMEM((2, 2, tokens, LANES), BF16),
+            pltpu.VMEM((blocks, 2, tokens, SPAN), BF16),
             pltpu.SemaphoreType.DMA((3, blocks)),
             pltpu.SemaphoreType.DMA((4,)),
             pltpu.SemaphoreType.DMA((1,)),

time: 61.4 us -> 59.1 us (0.963)
  Pallas kernels: 24.9 us -> 22.5 us
    pallas_call x1, Pallas kernels: 8.77 us -> 6.6 us  [on_device(): pl.pallas_call(functools.partial(front_kernel, direct=direct), in_specs=[...]
  transfers between devices with their start and end apart: 2 -> 2, of which waited for: 2 -> 2; matrix products, arithmetic and copies ran while one was open for 0% -> 0% of each run, Pallas kernels for 14% -> 15%
where the time goes in v10:
time: 59.1 us; the launch traced here: 58.7 us
  Pallas kernels  22.5 us (38%)
  blocking collectives  16.2 us (27%)
  waiting for transfers between devices  10.9 us (18%)
  starting transfers between devices  8.95 us (15%)
    all_to_all x1, blocking collectives, on_device(): back = lax.all_to_all(back, 'ctx', 0, 0, tiled=True)  16.2 us
    all_to_all x1, waiting for transfers between devices, exchange(): return lax.all_to_all(array, 'ctx', 0, 0, tiled=True)  8.89 us
    pallas_call x1, Pallas kernels, on_device(): pl.pallas_call(local_kernel, grid=(steps,), in_specs=[columns(tokens)] *...  8.72 us
    all_to_all x1, starting transfers between devices, exchange(): return lax.all_to_all(array, 'ctx', 0, 0, tiled=True)  7.37 us
    pallas_call x1, Pallas kernels, on_device(): pl.pallas_call(functools.partial(front_kernel, direct=direct), in_specs=[...  6.6 us
    pallas_call x1, Pallas kernels, on_device(): pl.pallas_call(middle_kernel, in_specs=[smem] + [vmem] * 5, out_specs=hbm...  4.31 us
    ppermute x1, waiting for transfers between devices, on_device(): lax.ppermute(squares, 'ch', [(i, (i + shift) % n_ch) for i in range(n_ch)])  2.02 us
    pallas_call x1, Pallas kernels, on_device(): pl.pallas_call(join_kernel, in_specs=[vmem] * 2 + [hbm, vmem], out_specs=...  1.75 us
  transfers between devices with their start and end apart: 2, of which 2 were waited for; matrix products, arithmetic and copies ran while one was open for 0% of the time, Pallas kernels for 15%

profile of v10, /device:TPU:0, one launch (start us, length us, event | category | flops | bytes accessed | tf_op | source)
XLA Modules:
  0.0 58.7 jit_solution(16534017618160116138)
XLA Ops:
  0.0 0.0 copy-start
  0.0 0.0 copy-start.2
  0.0 6.6 %front_pieces.1 = (bf16[16,88,256]{2,1,0:T(8,128)(2,1)}, f32[3,7,256]{2,1,0:T(8,128)S(1)}, f32[16,256]{1,0:T(8,128)S(1)}, f32[16,256]{1,0:T(8,128)S(1)}, f32[1,256]{1,0:T(1,128)S(1)}) custom-call(s32[1]{0:T(128)} %bitcast.refs_0_, bf16[128,4096]{1,0:T(8,128)(2,1)} %q_ref.1, bf16[128,4096]{1,0:T(8,128)(2,1)} %k_ref.1, bf16[128,4096]{1,0:T(8,128)(2,1)} %v_ref.1, ...), custom_call_target="tpu_custom_call" | custom-call | tf_op jit(solution)/shard_map/front_pieces/pallas_call | solution.py:562
  6.6 7.4 %all-to-all-start = ((bf16[16,88,256]{2,1,0:T(8,128)(2,1)}), bf16[16,88,256]{2,1,0:T(8,128)(2,1)S(1)}, u32[]{:S(2)}, u32[]{:S(2)}) async-start(bf16[16,88,256]{2,1,0:T(8,128)(2,1)} %get-tuple-element.17), calls=%async_computation | async-start | bytes 1441792 | tf_op jit(solution)/shard_map/all_to_all | solution.py:540
  14.0 0.0 copy-done
  14.0 0.0 copy-done.2
  14.0 0.0 copy-start.4
  14.0 0.0 copy-start.1
  14.0 8.7 %local_filter.1 = (f32[16,128,256]{2,1,0:T(8,128)}, f32[16,128,256]{2,1,0:T(8,128)S(1)}) custom-call(bf16[128,4096]{1,0:T(8,128)(2,1)} %q_ref.1, bf16[128,4096]{1,0:T(8,128)(2,1)} %k_ref.1, bf16[128,4096]{1,0:T(8,128)(2,1)} %v_ref.1, f32[3,7,4096]{2,1,0:T(8,128)} %taps_ref.1, f32[16,4096]{1,0:T(8,128)} %rates_ref.1, f32[16,4096]{1,0:T(8,128)} %res_ref.1, ...), custom_call_target="tpu_custom_call" | custom-call | flops 1000000000 | bytes 20000000 | tf_op jit(solution)/shard_map/local_filter/pallas_call | solution.py:593
  22.7 8.9 %all-to-all-done.x_ref = bf16[16,88,256]{2,1,0:T(8,128)(2,1)S(1)} async-done(((bf16[16,88,256]{2,1,0:T(8,128)(2,1)}), bf16[16,88,256]{2,1,0:T(8,128)(2,1)S(1)}, u32[]{:S(2)}, u32[]{:S(2)}) %all-to-all-start) | async-done | bytes 720928 | tf_op jit(solution)/shard_map/all_to_all | solution.py:540
  31.6 0.0 copy-done.4
  31.6 4.3 %middle_states.1 = bf16[16,40,256]{2,1,0:T(8,128)(2,1)} custom-call(s32[32]{0:T(128)S(1)} %copy-done.4, bf16[16,88,256]{2,1,0:T(8,128)(2,1)S(1)} %all-to-all-done.x_ref, f32[3,7,256]{2,1,0:T(8,128)S(1)} %get-tuple-element.21.taps_ref, f32[16,256]{1,0:T(8,128)S(1)} %get-tuple-element.22.rates_ref, f32[16,256]{1,0:T(8,128)S(1)} %get-tuple-element.23.res_ref, ...), custom_call_target="tpu_custom_call" | custom-call | tf_op jit(solution)/shard_map/middle_states/pallas_call | solution.py:611
  36.0 16.2 %all_to_all.10.back_ref = bf16[16,40,256]{2,1,0:T(8,128)(2,1)S(1)} all-to-all(bf16[16,40,256]{2,1,0:T(8,128)(2,1)} %middle_states.1), channel_id=1, replica_groups=mesh['ctx'=16,'ch'=2] {'ctx'}, dimensions={0} | all-to-all | bytes 655360 | tf_op jit(solution)/shard_map/all_to_all | solution.py:638
  52.2 0.0 copy-done.1
  52.2 0.0 copy-start.3
  52.2 1.7 %join_carry.1 = (f32[128,4096]{1,0:T(8,128)S(1)}, f32[1,128]{1,0:T(1,128)S(1)}) custom-call(bf16[16,40,256]{2,1,0:T(8,128)(2,1)S(1)} %all_to_all.10.back_ref, bf16[2,128,40]{2,1,0:T(8,128)(2,1)S(1)} %copy-done.1, f32[16,128,256]{2,1,0:T(8,128)} %get-tuple-element.25.qc_ref, f32[16,128,256]{2,1,0:T(8,128)S(1)} %get-tuple-element.26.y_ref), custom_call_target="tpu_custom_call" | custom-call | tf_op jit(solution)/shard_map/join_carry/pallas_call | solution.py:643
  54.0 1.6 %collective-permute-start = (f32[1,128]{1,0:T(1,128)S(1)}, f32[1,128]{1,0:T(1,128)S(1)}, u32[]{:S(2)}, u32[]{:S(2)}) collective-permute-start(f32[1,128]{1,0:T(1,128)S(1)} %get-tuple-element.28.refs_2_), channel_id=1, source_target_pairs={{0,1},{1,0},{2,3},{3,2},{4,5},{5,4},{6,7},{7,6},{8,9},{9,8},{10,11... | collective-permute-start | bytes 1544 | tf_op jit(solution)/shard_map/ppermute | solution.py:655
  55.5 2.0 %collective-permute-done.refs_3_ = f32[1,128]{1,0:T(1,128)S(1)} collective-permute-done((f32[1,128]{1,0:T(1,128)S(1)}, f32[1,128]{1,0:T(1,128)S(1)}, u32[]{:S(2)}, u32[]{:S(2)}) %collective-permute-start) | collective-permute-done | bytes 544 | tf_op jit(solution)/shard_map/ppermute | solution.py:655
  57.6 0.0 copy-done.3
  57.6 1.1 %scale_rows.1 = bf16[128,4096]{1,0:T(8,128)(2,1)} custom-call(f32[128,4096]{1,0:T(8,128)S(1)} %get-tuple-element.27.refs_0_, f32[1,4096]{1,0:T(1,128)S(1)} %bitcast.5, f32[1,128]{1,0:T(1,128)S(1)} %get-tuple-element.28.refs_2_, f32[1,128]{1,0:T(1,128)S(1)} %collective-permute-done.refs_3_), custom_call_target="tpu_custom_call" | custom-call | tf_op jit(solution)/shard_map/scale_rows/pallas_call | solution.py:656
Async XLA Ops:
  0.0 14.0 %copy-start = (bf16[384,192]{1,0:T(8,128)(2,1)S(1)}, bf16[384,192]{1,0:T(8,128)(2,1)}, u32[]{:S(2)}) copy-start(bf16[384,192]{1,0:T(8,128)(2,1)} %constant.13.clone.local_ref) | copy-start | bytes 442372
  0.0 14.0 %copy-start.2 = (f32[4096]{0:T(1024)S(1)}, f32[4096]{0:T(1024)}, u32[]{:S(2)}) copy-start(f32[4096]{0:T(1024)} %param.19) | copy-start | bytes 49156
  6.6 25.0 %all-to-all-start = ((bf16[16,88,256]{2,1,0:T(8,128)(2,1)}), bf16[16,88,256]{2,1,0:T(8,128)(2,1)S(1)}, u32[]{:S(2)}, u32[]{:S(2)}) async-start(bf16[16,88,256]{2,1,0:T(8,128)(2,1)} %get-tuple-element.17), calls=%async_computation | async-start | bytes 1441792 | tf_op jit(solution)/shard_map/all_to_all | solution.py:540
  14.0 17.6 %copy-start.4 = (s32[32]{0:T(128)S(1)}, s32[32]{0:T(128)}, u32[]{:S(2)}) copy-start(s32[32]{0:T(128)} %perm_ref.1) | copy-start | bytes 388
  14.0 38.2 %copy-start.1 = (bf16[2,128,40]{2,1,0:T(8,128)(2,1)S(1)}, bf16[2,128,40]{2,1,0:T(8,128)(2,1)}, u32[]{:S(2)}) copy-start(bf16[2,128,40]{2,1,0:T(8,128)(2,1)} %constant.14.clone.lift_ref) | copy-start | bytes 61444
  52.2 5.4 %copy-start.3 = (f32[4096]{0:T(1024)S(1)}, f32[4096]{0:T(1024)}, u32[]{:S(2)}) copy-start(f32[4096]{0:T(1024)} %param.20) | copy-start | bytes 49156
  54.0 3.6 %collective-permute-start = (f32[1,128]{1,0:T(1,128)S(1)}, f32[1,128]{1,0:T(1,128)S(1)}, u32[]{:S(2)}, u32[]{:S(2)}) collective-permute-start(f32[1,128]{1,0:T(1,128)S(1)} %get-tuple-element.28.refs_2_), channel_id=1, source_target_pairs={{0,1},{1,0},{2,3},{3,2},{4,5},{5,4},{6,7},{7,6},{8,9},{9,8},{10,11... | collective-permute-start | bytes 1544 | tf_op jit(solution)/shard_map/ppermute | solution.py:655

commit v11 on v10

--- a/solution.py
+++ b/solution.py
@@ -13,6 +13,7 @@
 F32, BF16 = jnp.float32, jnp.bfloat16
 LANES = 128
 SPAN = 256
+WIDE = 4
 STRETCH = 64
 REACH = 6
 INNER = STRETCH - REACH
@@ -112,11 +113,12 @@
     def lanes(c):
         return pl.ds(pl.multiple_of(c * SPAN, SPAN), SPAN)
 
-    def loads(c):
+    def loads(w):
+        cols = pl.ds(pl.multiple_of(w * WIDE * SPAN, SPAN), WIDE * SPAN)
         return [
-            pltpu.make_async_copy(ref.at[:, lanes(c)], held.at[a, :, lanes(c)], in_sems.at[a, c])
+            pltpu.make_async_copy(ref.at[:, cols], held.at[a, :, cols], in_sems.at[a, w])
             for a, ref in enumerate((k_ref, v_ref))
-        ] + [pltpu.make_async_copy(taps_ref.at[pl.ds(1, 2), :, lanes(c)], taps_vm.at[c], in_sems.at[2, c])]
+        ] + [pltpu.make_async_copy(taps_ref.at[pl.ds(1, 2), :, cols], taps_vm.at[:, :, cols], in_sems.at[2, w])]
 
     def edge_loads():
         return [
@@ -138,13 +140,14 @@
     for copy in loads(0) + edge_loads():
         copy.start()
     ends_copy.start()
+    waves = blocks // WIDE
 
     def begin(c, carry):
         for copy in loads(c):
             copy.start()
         return carry
 
-    lax.fori_loop(1, blocks, begin, 0)
+    lax.fori_loop(1, waves, begin, 0)
     if direct:
         for copy in own_loads():
             copy.start()
@@ -159,8 +162,11 @@
     ends_copy.wait()
 
     def features(c, carry):
-        for copy in loads(c):
-            copy.wait()
+        @pl.when(lax.rem(c, WIDE) == 0)
+        def _():
+            for copy in loads(c // WIDE):
+                copy.wait()
+
         parity = lax.rem(c, 2)
         for h in range(2):
             part = slice(h * LANES, (h + 1) * LANES)
@@ -180,7 +186,7 @@
                 at = i * PIECE
                 pay[c, h, at : at + REACH, :] = qs[parity, h, i, 32 - REACH : 32, :]
                 pay[c, h, at + 3 * REACH : at + 4 * REACH, :] = qs[parity, h, i, 0:REACH, :]
-            taps = [[taps_vm[c, a, j : j + 1, part] for j in range(REACH + 1)] for a in range(2)]
+            taps = [[taps_vm[a, j : j + 1, cols] for j in range(REACH + 1)] for a in range(2)]
             for i in range(2):
                 for b in range(STRETCH // 16):
                     base = i * (STRETCH + 8) + 8 + 16 * b
@@ -570,14 +576,14 @@
         scratch_shapes=[
             pltpu.VMEM((2, tokens, width), BF16),
             pltpu.VMEM((4, 16, width), BF16),
-            pltpu.VMEM((blocks, 2, REACH + 1, SPAN), F32),
+            pltpu.VMEM((2, REACH + 1, width), F32),
             pltpu.VMEM(ends.shape, BF16),
             pltpu.VMEM((2, 2, 2, 2 * (STRETCH + 8), LANES), F32),
             pltpu.VMEM((2, 2, 2, 32, LANES), F32),
             pltpu.VMEM((blocks, 2, 2 * PIECE, LANES), F32),
             pltpu.VMEM((blocks, 2 * PIECE, SPAN), BF16),
             pltpu.VMEM((blocks, 2, tokens, SPAN), BF16),
-            pltpu.SemaphoreType.DMA((3, blocks)),
+            pltpu.SemaphoreType.DMA((3, blocks // WIDE)),
             pltpu.SemaphoreType.DMA((4,)),
             pltpu.SemaphoreType.DMA((1,)),
             pltpu.SemaphoreType.DMA((4,)),

time: 59.1 us -> 58.9 us (level)
  no operation moved by 1% of the time
where the time goes in v11:
time: 58.9 us; the launch traced here: 58.6 us
  Pallas kernels  22.4 us (38%)
  blocking collectives  16.2 us (28%)
  waiting for transfers between devices  10.9 us (19%)
  starting transfers between devices  8.95 us (15%)
    all_to_all x1, blocking collectives, on_device(): back = lax.all_to_all(back, 'ctx', 0, 0, tiled=True)  16.2 us
    all_to_all x1, waiting for transfers between devices, exchange(): return lax.all_to_all(array, 'ctx', 0, 0, tiled=True)  8.9 us
    pallas_call x1, Pallas kernels, on_device(): pl.pallas_call(local_kernel, grid=(steps,), in_specs=[columns(tokens)] *...  8.71 us
    all_to_all x1, starting transfers between devices, exchange(): return lax.all_to_all(array, 'ctx', 0, 0, tiled=True)  7.37 us
    pallas_call x1, Pallas kernels, on_device(): pl.pallas_call(functools.partial(front_kernel, direct=direct), in_specs=[...  6.46 us
    pallas_call x1, Pallas kernels, on_device(): pl.pallas_call(middle_kernel, in_specs=[smem] + [vmem] * 5, out_specs=hbm...  4.3 us
    ppermute x1, waiting for transfers between devices, on_device(): lax.ppermute(squares, 'ch', [(i, (i + shift) % n_ch) for i in range(n_ch)])  2.02 us
    pallas_call x1, Pallas kernels, on_device(): pl.pallas_call(join_kernel, in_specs=[vmem] * 2 + [hbm, vmem], out_specs=...  1.75 us
  transfers between devices with their start and end apart: 2, of which 2 were waited for; matrix products, arithmetic and copies ran while one was open for 0% of the time, Pallas kernels for 15%

profile of v11, /device:TPU:0, one launch (start us, length us, event | category | flops | bytes accessed | tf_op | source)
XLA Modules:
  0.0 58.6 jit_solution(8018008789447550673)
XLA Ops:
  0.0 0.0 copy-start
  0.0 0.0 copy-start.2
  0.0 6.5 %front_pieces.1 = (bf16[16,88,256]{2,1,0:T(8,128)(2,1)}, f32[3,7,256]{2,1,0:T(8,128)S(1)}, f32[16,256]{1,0:T(8,128)S(1)}, f32[16,256]{1,0:T(8,128)S(1)}, f32[1,256]{1,0:T(1,128)S(1)}) custom-call(s32[1]{0:T(128)} %bitcast.refs_0_, bf16[128,4096]{1,0:T(8,128)(2,1)} %q_ref.1, bf16[128,4096]{1,0:T(8,128)(2,1)} %k_ref.1, bf16[128,4096]{1,0:T(8,128)(2,1)} %v_ref.1, ...), custom_call_target="tpu_custom_call" | custom-call | tf_op jit(solution)/shard_map/front_pieces/pallas_call | solution.py:568
  6.5 7.4 %all-to-all-start = ((bf16[16,88,256]{2,1,0:T(8,128)(2,1)}), bf16[16,88,256]{2,1,0:T(8,128)(2,1)S(1)}, u32[]{:S(2)}, u32[]{:S(2)}) async-start(bf16[16,88,256]{2,1,0:T(8,128)(2,1)} %get-tuple-element.17), calls=%async_computation | async-start | bytes 1441792 | tf_op jit(solution)/shard_map/all_to_all | solution.py:546
  13.8 0.0 copy-done
  13.9 0.0 copy-done.2
  13.9 0.0 copy-start.4
  13.9 0.0 copy-start.1
  13.9 8.7 %local_filter.1 = (f32[16,128,256]{2,1,0:T(8,128)}, f32[16,128,256]{2,1,0:T(8,128)S(1)}) custom-call(bf16[128,4096]{1,0:T(8,128)(2,1)} %q_ref.1, bf16[128,4096]{1,0:T(8,128)(2,1)} %k_ref.1, bf16[128,4096]{1,0:T(8,128)(2,1)} %v_ref.1, f32[3,7,4096]{2,1,0:T(8,128)} %taps_ref.1, f32[16,4096]{1,0:T(8,128)} %rates_ref.1, f32[16,4096]{1,0:T(8,128)} %res_ref.1, ...), custom_call_target="tpu_custom_call" | custom-call | flops 1000000000 | bytes 20000000 | tf_op jit(solution)/shard_map/local_filter/pallas_call | solution.py:599
  22.6 8.9 %all-to-all-done.x_ref = bf16[16,88,256]{2,1,0:T(8,128)(2,1)S(1)} async-done(((bf16[16,88,256]{2,1,0:T(8,128)(2,1)}), bf16[16,88,256]{2,1,0:T(8,128)(2,1)S(1)}, u32[]{:S(2)}, u32[]{:S(2)}) %all-to-all-start) | async-done | bytes 720928 | tf_op jit(solution)/shard_map/all_to_all | solution.py:546
  31.5 0.0 copy-done.4
  31.5 4.3 %middle_states.1 = bf16[16,40,256]{2,1,0:T(8,128)(2,1)} custom-call(s32[32]{0:T(128)S(1)} %copy-done.4, bf16[16,88,256]{2,1,0:T(8,128)(2,1)S(1)} %all-to-all-done.x_ref, f32[3,7,256]{2,1,0:T(8,128)S(1)} %get-tuple-element.21.taps_ref, f32[16,256]{1,0:T(8,128)S(1)} %get-tuple-element.22.rates_ref, f32[16,256]{1,0:T(8,128)S(1)} %get-tuple-element.23.res_ref, ...), custom_call_target="tpu_custom_call" | custom-call | tf_op jit(solution)/shard_map/middle_states/pallas_call | solution.py:617
  35.8 16.2 %all_to_all.10.back_ref = bf16[16,40,256]{2,1,0:T(8,128)(2,1)S(1)} all-to-all(bf16[16,40,256]{2,1,0:T(8,128)(2,1)} %middle_states.1), channel_id=1, replica_groups=mesh['ctx'=16,'ch'=2] {'ctx'}, dimensions={0} | all-to-all | bytes 655360 | tf_op jit(solution)/shard_map/all_to_all | solution.py:644
  52.0 0.0 copy-done.1
  52.0 0.0 copy-start.3
  52.1 1.7 %join_carry.1 = (f32[128,4096]{1,0:T(8,128)S(1)}, f32[1,128]{1,0:T(1,128)S(1)}) custom-call(bf16[16,40,256]{2,1,0:T(8,128)(2,1)S(1)} %all_to_all.10.back_ref, bf16[2,128,40]{2,1,0:T(8,128)(2,1)S(1)} %copy-done.1, f32[16,128,256]{2,1,0:T(8,128)} %get-tuple-element.25.qc_ref, f32[16,128,256]{2,1,0:T(8,128)S(1)} %get-tuple-element.26.y_ref), custom_call_target="tpu_custom_call" | custom-call | tf_op jit(solution)/shard_map/join_carry/pallas_call | solution.py:649
  53.8 1.6 %collective-permute-start = (f32[1,128]{1,0:T(1,128)S(1)}, f32[1,128]{1,0:T(1,128)S(1)}, u32[]{:S(2)}, u32[]{:S(2)}) collective-permute-start(f32[1,128]{1,0:T(1,128)S(1)} %get-tuple-element.28.refs_2_), channel_id=1, source_target_pairs={{0,1},{1,0},{2,3},{3,2},{4,5},{5,4},{6,7},{7,6},{8,9},{9,8},{10,11... | collective-permute-start | bytes 1544 | tf_op jit(solution)/shard_map/ppermute | solution.py:661
  55.4 2.0 %collective-permute-done.refs_3_ = f32[1,128]{1,0:T(1,128)S(1)} collective-permute-done((f32[1,128]{1,0:T(1,128)S(1)}, f32[1,128]{1,0:T(1,128)S(1)}, u32[]{:S(2)}, u32[]{:S(2)}) %collective-permute-start) | collective-permute-done | bytes 544 | tf_op jit(solution)/shard_map/ppermute | solution.py:661
  57.4 0.0 copy-done.3
  57.4 1.1 %scale_rows.1 = bf16[128,4096]{1,0:T(8,128)(2,1)} custom-call(f32[128,4096]{1,0:T(8,128)S(1)} %get-tuple-element.27.refs_0_, f32[1,4096]{1,0:T(1,128)S(1)} %bitcast.5, f32[1,128]{1,0:T(1,128)S(1)} %get-tuple-element.28.refs_2_, f32[1,128]{1,0:T(1,128)S(1)} %collective-permute-done.refs_3_), custom_call_target="tpu_custom_call" | custom-call | tf_op jit(solution)/shard_map/scale_rows/pallas_call | solution.py:662
Async XLA Ops:
  0.0 13.8 %copy-start = (bf16[384,192]{1,0:T(8,128)(2,1)S(1)}, bf16[384,192]{1,0:T(8,128)(2,1)}, u32[]{:S(2)}) copy-start(bf16[384,192]{1,0:T(8,128)(2,1)} %constant.13.clone.local_ref) | copy-start | bytes 442372
  0.0 13.9 %copy-start.2 = (f32[4096]{0:T(1024)S(1)}, f32[4096]{0:T(1024)}, u32[]{:S(2)}) copy-start(f32[4096]{0:T(1024)} %param.19) | copy-start | bytes 49156
  6.5 25.0 %all-to-all-start = ((bf16[16,88,256]{2,1,0:T(8,128)(2,1)}), bf16[16,88,256]{2,1,0:T(8,128)(2,1)S(1)}, u32[]{:S(2)}, u32[]{:S(2)}) async-start(bf16[16,88,256]{2,1,0:T(8,128)(2,1)} %get-tuple-element.17), calls=%async_computation | async-start | bytes 1441792 | tf_op jit(solution)/shard_map/all_to_all | solution.py:546
  13.9 17.6 %copy-start.4 = (s32[32]{0:T(128)S(1)}, s32[32]{0:T(128)}, u32[]{:S(2)}) copy-start(s32[32]{0:T(128)} %perm_ref.1) | copy-start | bytes 388
  13.9 38.2 %copy-start.1 = (bf16[2,128,40]{2,1,0:T(8,128)(2,1)S(1)}, bf16[2,128,40]{2,1,0:T(8,128)(2,1)}, u32[]{:S(2)}) copy-start(bf16[2,128,40]{2,1,0:T(8,128)(2,1)} %constant.14.clone.lift_ref) | copy-start | bytes 61444
  52.0 5.4 %copy-start.3 = (f32[4096]{0:T(1024)S(1)}, f32[4096]{0:T(1024)}, u32[]{:S(2)}) copy-start(f32[4096]{0:T(1024)} %param.20) | copy-start | bytes 49156
  53.8 3.6 %collective-permute-start = (f32[1,128]{1,0:T(1,128)S(1)}, f32[1,128]{1,0:T(1,128)S(1)}, u32[]{:S(2)}, u32[]{:S(2)}) collective-permute-start(f32[1,128]{1,0:T(1,128)S(1)} %get-tuple-element.28.refs_2_), channel_id=1, source_target_pairs={{0,1},{1,0},{2,3},{3,2},{4,5},{5,4},{6,7},{7,6},{8,9},{9,8},{10,11... | collective-permute-start | bytes 1544 | tf_op jit(solution)/shard_map/ppermute | solution.py:661

commit v12 on v11

--- a/solution.py
+++ b/solution.py
@@ -69,6 +69,7 @@
             lift[0, half * STRETCH + t, half * BACK + t] = 1.0
             lift[0, half * STRETCH + t, half * BACK + REACH + t] = 1.0
     local = local.reshape(RANK * STRETCH, STRETCH)
+    ends = ends.reshape(16, 8, STRETCH // 8).transpose(0, 2, 1).reshape(16, STRETCH)
 
     def triple(m):
         h, l = halves(m)
@@ -188,20 +189,23 @@
                 pay[c, h, at + 3 * REACH : at + 4 * REACH, :] = qs[parity, h, i, 0:REACH, :]
             taps = [[taps_vm[a, j : j + 1, cols] for j in range(REACH + 1)] for a in range(2)]
             for i in range(2):
-                for b in range(STRETCH // 16):
-                    base = i * (STRETCH + 8) + 8 + 16 * b
-                    both = []
-                    for a in range(2):
-                        total = taps[a][0] * xs[parity, a, h, base : base + 16, :]
+                base = i * (STRETCH + 8) + 8
+                both = []
+                for a in range(2):
+                    strided = {
+                        m: xs[parity, a, h, pl.ds(base + m, 8, stride=8), :] for m in range(-REACH, STRETCH // 8)
+                    }
+                    found = []
+                    for m in range(STRETCH // 8):
+                        total = taps[a][0] * strided[m]
                         for j in range(1, REACH + 1):
-                            total = total + taps[a][j] * xs[parity, a, h, base - j : base - j + 16, :]
-                        both.append(total)
-                    mixed = both[0] * both[1]
-                    if b == 0:
-                        row = lax.broadcasted_iota(jnp.int32, (16, LANES), 0)
-                        mixed = jnp.where(row >= REACH, mixed, 0.0)
-                    high, low = split(mixed)
-                    rows = slice(i * STRETCH + 16 * b, i * STRETCH + 16 * b + 16)
+                            total = total + taps[a][j] * strided[m - j]
+                        found.append(total)
+                    both.append(found)
+                mixed = [k * v for k, v in zip(*both)]
+                for m in range(0, STRETCH // 8, 2):
+                    high, low = split(jnp.concatenate(mixed[m : m + 2], axis=0))
+                    rows = slice(i * STRETCH + 8 * m, i * STRETCH + 8 * m + 16)
                     u_vm[c, 0, rows, part] = high
                     u_vm[c, 1, rows, part] = low
         return carry

time: 58.9 us -> 59 us (level)
  no operation moved by 1% of the time
where the time goes in v12:
time: 59 us; the launch traced here: 58.7 us
  Pallas kernels  22.5 us (38%)
  blocking collectives  16.2 us (27%)
  waiting for transfers between devices  10.9 us (18%)
  starting transfers between devices  8.95 us (15%)
    all_to_all x1, blocking collectives, on_device(): back = lax.all_to_all(back, 'ctx', 0, 0, tiled=True)  16.2 us
    all_to_all x1, waiting for transfers between devices, exchange(): return lax.all_to_all(array, 'ctx', 0, 0, tiled=True)  8.9 us
    pallas_call x1, Pallas kernels, on_device(): pl.pallas_call(local_kernel, grid=(steps,), in_specs=[columns(tokens)] *...  8.71 us
    all_to_all x1, starting transfers between devices, exchange(): return lax.all_to_all(array, 'ctx', 0, 0, tiled=True)  7.37 us
    pallas_call x1, Pallas kernels, on_device(): pl.pallas_call(functools.partial(front_kernel, direct=direct), in_specs=[...  6.59 us
    pallas_call x1, Pallas kernels, on_device(): pl.pallas_call(middle_kernel, in_specs=[smem] + [vmem] * 5, out_specs=hbm...  4.3 us
    ppermute x1, waiting for transfers between devices, on_device(): lax.ppermute(squares, 'ch', [(i, (i + shift) % n_ch) for i in range(n_ch)])  2.02 us
    pallas_call x1, Pallas kernels, on_device(): pl.pallas_call(join_kernel, in_specs=[vmem] * 2 + [hbm, vmem], out_specs=...  1.75 us
  transfers between devices with their start and end apart: 2, of which 2 were waited for; matrix products, arithmetic and copies ran while one was open for 0% of the time, Pallas kernels for 15%

profile of v12, /device:TPU:0, one launch (start us, length us, event | category | flops | bytes accessed | tf_op | source)
XLA Modules:
  0.0 58.7 jit_solution(16036595078788281014)
XLA Ops:
  0.0 0.0 copy-start
  0.0 0.0 copy-start.2
  0.0 6.6 %front_pieces.1 = (bf16[16,88,256]{2,1,0:T(8,128)(2,1)}, f32[3,7,256]{2,1,0:T(8,128)S(1)}, f32[16,256]{1,0:T(8,128)S(1)}, f32[16,256]{1,0:T(8,128)S(1)}, f32[1,256]{1,0:T(1,128)S(1)}) custom-call(s32[1]{0:T(128)} %bitcast.refs_0_, bf16[128,4096]{1,0:T(8,128)(2,1)} %q_ref.1, bf16[128,4096]{1,0:T(8,128)(2,1)} %k_ref.1, bf16[128,4096]{1,0:T(8,128)(2,1)} %v_ref.1, ...), custom_call_target="tpu_custom_call" | custom-call | tf_op jit(solution)/shard_map/front_pieces/pallas_call | solution.py:572
  6.6 7.4 %all-to-all-start = ((bf16[16,88,256]{2,1,0:T(8,128)(2,1)}), bf16[16,88,256]{2,1,0:T(8,128)(2,1)S(1)}, u32[]{:S(2)}, u32[]{:S(2)}) async-start(bf16[16,88,256]{2,1,0:T(8,128)(2,1)} %get-tuple-element.17), calls=%async_computation | async-start | bytes 1441792 | tf_op jit(solution)/shard_map/all_to_all | solution.py:550
  14.0 0.0 copy-done
  14.0 0.0 copy-done.2
  14.0 0.0 copy-start.4
  14.0 0.0 copy-start.1
  14.0 8.7 %local_filter.1 = (f32[16,128,256]{2,1,0:T(8,128)}, f32[16,128,256]{2,1,0:T(8,128)S(1)}) custom-call(bf16[128,4096]{1,0:T(8,128)(2,1)} %q_ref.1, bf16[128,4096]{1,0:T(8,128)(2,1)} %k_ref.1, bf16[128,4096]{1,0:T(8,128)(2,1)} %v_ref.1, f32[3,7,4096]{2,1,0:T(8,128)} %taps_ref.1, f32[16,4096]{1,0:T(8,128)} %rates_ref.1, f32[16,4096]{1,0:T(8,128)} %res_ref.1, ...), custom_call_target="tpu_custom_call" | custom-call | flops 1000000000 | bytes 20000000 | tf_op jit(solution)/shard_map/local_filter/pallas_call | solution.py:603
  22.7 8.9 %all-to-all-done.x_ref = bf16[16,88,256]{2,1,0:T(8,128)(2,1)S(1)} async-done(((bf16[16,88,256]{2,1,0:T(8,128)(2,1)}), bf16[16,88,256]{2,1,0:T(8,128)(2,1)S(1)}, u32[]{:S(2)}, u32[]{:S(2)}) %all-to-all-start) | async-done | bytes 720928 | tf_op jit(solution)/shard_map/all_to_all | solution.py:550
  31.6 0.0 copy-done.4
  31.6 4.3 %middle_states.1 = bf16[16,40,256]{2,1,0:T(8,128)(2,1)} custom-call(s32[32]{0:T(128)S(1)} %copy-done.4, bf16[16,88,256]{2,1,0:T(8,128)(2,1)S(1)} %all-to-all-done.x_ref, f32[3,7,256]{2,1,0:T(8,128)S(1)} %get-tuple-element.21.taps_ref, f32[16,256]{1,0:T(8,128)S(1)} %get-tuple-element.22.rates_ref, f32[16,256]{1,0:T(8,128)S(1)} %get-tuple-element.23.res_ref, ...), custom_call_target="tpu_custom_call" | custom-call | tf_op jit(solution)/shard_map/middle_states/pallas_call | solution.py:621
  35.9 16.2 %all_to_all.10.back_ref = bf16[16,40,256]{2,1,0:T(8,128)(2,1)S(1)} all-to-all(bf16[16,40,256]{2,1,0:T(8,128)(2,1)} %middle_states.1), channel_id=1, replica_groups=mesh['ctx'=16,'ch'=2] {'ctx'}, dimensions={0} | all-to-all | bytes 655360 | tf_op jit(solution)/shard_map/all_to_all | solution.py:648
  52.2 0.0 copy-done.1
  52.2 0.0 copy-start.3
  52.2 1.7 %join_carry.1 = (f32[128,4096]{1,0:T(8,128)S(1)}, f32[1,128]{1,0:T(1,128)S(1)}) custom-call(bf16[16,40,256]{2,1,0:T(8,128)(2,1)S(1)} %all_to_all.10.back_ref, bf16[2,128,40]{2,1,0:T(8,128)(2,1)S(1)} %copy-done.1, f32[16,128,256]{2,1,0:T(8,128)} %get-tuple-element.25.qc_ref, f32[16,128,256]{2,1,0:T(8,128)S(1)} %get-tuple-element.26.y_ref), custom_call_target="tpu_custom_call" | custom-call | tf_op jit(solution)/shard_map/join_carry/pallas_call | solution.py:653
  53.9 1.6 %collective-permute-start = (f32[1,128]{1,0:T(1,128)S(1)}, f32[1,128]{1,0:T(1,128)S(1)}, u32[]{:S(2)}, u32[]{:S(2)}) collective-permute-start(f32[1,128]{1,0:T(1,128)S(1)} %get-tuple-element.28.refs_2_), channel_id=1, source_target_pairs={{0,1},{1,0},{2,3},{3,2},{4,5},{5,4},{6,7},{7,6},{8,9},{9,8},{10,11... | collective-permute-start | bytes 1544 | tf_op jit(solution)/shard_map/ppermute | solution.py:665
  55.5 2.0 %collective-permute-done.refs_3_ = f32[1,128]{1,0:T(1,128)S(1)} collective-permute-done((f32[1,128]{1,0:T(1,128)S(1)}, f32[1,128]{1,0:T(1,128)S(1)}, u32[]{:S(2)}, u32[]{:S(2)}) %collective-permute-start) | collective-permute-done | bytes 544 | tf_op jit(solution)/shard_map/ppermute | solution.py:665
  57.5 0.0 copy-done.3
  57.6 1.1 %scale_rows.1 = bf16[128,4096]{1,0:T(8,128)(2,1)} custom-call(f32[128,4096]{1,0:T(8,128)S(1)} %get-tuple-element.27.refs_0_, f32[1,4096]{1,0:T(1,128)S(1)} %bitcast.5, f32[1,128]{1,0:T(1,128)S(1)} %get-tuple-element.28.refs_2_, f32[1,128]{1,0:T(1,128)S(1)} %collective-permute-done.refs_3_), custom_call_target="tpu_custom_call" | custom-call | tf_op jit(solution)/shard_map/scale_rows/pallas_call | solution.py:666
Async XLA Ops:
  0.0 14.0 %copy-start = (bf16[384,192]{1,0:T(8,128)(2,1)S(1)}, bf16[384,192]{1,0:T(8,128)(2,1)}, u32[]{:S(2)}) copy-start(bf16[384,192]{1,0:T(8,128)(2,1)} %constant.13.clone.local_ref) | copy-start | bytes 442372
  0.0 14.0 %copy-start.2 = (f32[4096]{0:T(1024)S(1)}, f32[4096]{0:T(1024)}, u32[]{:S(2)}) copy-start(f32[4096]{0:T(1024)} %param.19) | copy-start | bytes 49156
  6.6 25.0 %all-to-all-start = ((bf16[16,88,256]{2,1,0:T(8,128)(2,1)}), bf16[16,88,256]{2,1,0:T(8,128)(2,1)S(1)}, u32[]{:S(2)}, u32[]{:S(2)}) async-start(bf16[16,88,256]{2,1,0:T(8,128)(2,1)} %get-tuple-element.17), calls=%async_computation | async-start | bytes 1441792 | tf_op jit(solution)/shard_map/all_to_all | solution.py:550
  14.0 17.6 %copy-start.4 = (s32[32]{0:T(128)S(1)}, s32[32]{0:T(128)}, u32[]{:S(2)}) copy-start(s32[32]{0:T(128)} %perm_ref.1) | copy-start | bytes 388
  14.0 38.2 %copy-start.1 = (bf16[2,128,40]{2,1,0:T(8,128)(2,1)S(1)}, bf16[2,128,40]{2,1,0:T(8,128)(2,1)}, u32[]{:S(2)}) copy-start(bf16[2,128,40]{2,1,0:T(8,128)(2,1)} %constant.14.clone.lift_ref) | copy-start | bytes 61444
  52.2 5.4 %copy-start.3 = (f32[4096]{0:T(1024)S(1)}, f32[4096]{0:T(1024)}, u32[]{:S(2)}) copy-start(f32[4096]{0:T(1024)} %param.20) | copy-start | bytes 49156
  53.9 3.6 %collective-permute-start = (f32[1,128]{1,0:T(1,128)S(1)}, f32[1,128]{1,0:T(1,128)S(1)}, u32[]{:S(2)}, u32[]{:S(2)}) collective-permute-start(f32[1,128]{1,0:T(1,128)S(1)} %get-tuple-element.28.refs_2_), channel_id=1, source_target_pairs={{0,1},{1,0},{2,3},{3,2},{4,5},{5,4},{6,7},{7,6},{8,9},{9,8},{10,11... | collective-permute-start | bytes 1544 | tf_op jit(solution)/shard_map/ppermute | solution.py:665

commit v13 on v12

--- a/solution.py
+++ b/solution.py
@@ -13,7 +13,7 @@
 F32, BF16 = jnp.float32, jnp.bfloat16
 LANES = 128
 SPAN = 256
-WIDE = 4
+WIDE = 2
 STRETCH = 64
 REACH = 6
 INNER = STRETCH - REACH
@@ -162,12 +162,7 @@
         copy.wait()
     ends_copy.wait()
 
-    def features(c, carry):
-        @pl.when(lax.rem(c, WIDE) == 0)
-        def _():
-            for copy in loads(c // WIDE):
-                copy.wait()
-
+    def features(c):
         parity = lax.rem(c, 2)
         for h in range(2):
             part = slice(h * LANES, (h + 1) * LANES)
@@ -208,33 +203,50 @@
                     rows = slice(i * STRETCH + 8 * m, i * STRETCH + 8 * m + 16)
                     u_vm[c, 0, rows, part] = high
                     u_vm[c, 1, rows, part] = low
-        return carry
-
-    lax.fori_loop(0, blocks, features, 0)
-    chunk = 4
-
-    def finish(step, carry):
-        for k in range(chunk):
-            c = step * chunk + k
-            for i in range(2):
-                rows = slice(i * STRETCH, (i + 1) * STRETCH)
-                high, low = u_vm[c, 0, rows, :], u_vm[c, 1, rows, :]
-                stacked = jnp.concatenate([high, low, high], axis=0)
-                moments = jnp.dot(ends_vm[...], stacked, preferred_element_type=F32)[:8]
-                rest = (moments - moments.astype(BF16).astype(F32))[:FINE]
-                at = PIECE * i + RAW
-                for h in range(2):
-                    part = slice(h * LANES, (h + 1) * LANES)
-                    pay[c, h, at : at + RANK, :] = moments[:RANK, part]
-                    pay[c, h, at + RANK : at + COEFS, :] = rest[:, part]
+
+    def products(c):
+        found = []
+        for i in range(2):
+            rows = slice(i * STRETCH, (i + 1) * STRETCH)
+            high, low = u_vm[c, 0, rows, :], u_vm[c, 1, rows, :]
+            stacked = jnp.concatenate([high, low, high], axis=0)
+            found.append(jnp.dot(ends_vm[...], stacked, preferred_element_type=F32)[:8])
+        return found
+
+    def finish(c, found):
+        for i in range(2):
+            moments = found[i]
+            rest = (moments - moments.astype(BF16).astype(F32))[:FINE]
+            at = PIECE * i + RAW
             for h in range(2):
-                packed[c, :, h * LANES : (h + 1) * LANES] = pay[c, h].astype(BF16)
-        for k in range(chunk):
-            for copy in stores(step * chunk + k):
+                part = slice(h * LANES, (h + 1) * LANES)
+                pay[c, h, at : at + RANK, :] = moments[:RANK, part]
+                pay[c, h, at + RANK : at + COEFS, :] = rest[:, part]
+        for h in range(2):
+            packed[c, :, h * LANES : (h + 1) * LANES] = pay[c, h].astype(BF16)
+
+    def step(c, carry):
+        @pl.when(lax.rem(c, WIDE) == 0)
+        def _():
+            for copy in loads(c // WIDE):
+                copy.wait()
+
+        before = jnp.maximum(c - 1, 0)
+        found = products(before)
+        features(c)
+
+        @pl.when(c > 0)
+        def _():
+            finish(before, found)
+            for copy in stores(before):
                 copy.start()
-        return carry
-
-    lax.fori_loop(0, blocks // chunk, finish, 0)
+
+        return carry
+
+    lax.fori_loop(0, blocks, step, 0)
+    finish(blocks - 1, products(blocks - 1))
+    for copy in stores(blocks - 1):
+        copy.start()
 
     def end(c, carry):
         for copy in stores(c):

time: 59 us -> 59.1 us (level)
  no operation moved by 1% of the time
where the time goes in v13:
time: 59.1 us; the launch traced here: 58.7 us
  Pallas kernels  22.5 us (38%)
  blocking collectives  16.2 us (27%)
  waiting for transfers between devices  10.9 us (18%)
  starting transfers between devices  8.95 us (15%)
    all_to_all x1, blocking collectives, on_device(): back = lax.all_to_all(back, 'ctx', 0, 0, tiled=True)  16.2 us
    all_to_all x1, waiting for transfers between devices, exchange(): return lax.all_to_all(array, 'ctx', 0, 0, tiled=True)  8.9 us
    pallas_call x1, Pallas kernels, on_device(): pl.pallas_call(local_kernel, grid=(steps,), in_specs=[columns(tokens)] *...  8.71 us
    all_to_all x1, starting transfers between devices, exchange(): return lax.all_to_all(array, 'ctx', 0, 0, tiled=True)  7.37 us
    pallas_call x1, Pallas kernels, on_device(): pl.pallas_call(functools.partial(front_kernel, direct=direct), in_specs=[...  6.64 us
    pallas_call x1, Pallas kernels, on_device(): pl.pallas_call(middle_kernel, in_specs=[smem] + [vmem] * 5, out_specs=hbm...  4.3 us
    ppermute x1, waiting for transfers between devices, on_device(): lax.ppermute(squares, 'ch', [(i, (i + shift) % n_ch) for i in range(n_ch)])  2.02 us
    pallas_call x1, Pallas kernels, on_device(): pl.pallas_call(join_kernel, in_specs=[vmem] * 2 + [hbm, vmem], out_specs=...  1.75 us
  transfers between devices with their start and end apart: 2, of which 2 were waited for; matrix products, arithmetic and copies ran while one was open for 0% of the time, Pallas kernels for 15%

profile of v13, /device:TPU:0, one launch (start us, length us, event | category | flops | bytes accessed | tf_op | source)
XLA Modules:
  0.0 58.7 jit_solution(2926604621155038790)
XLA Ops:
  0.0 0.0 copy-start
  0.0 0.0 copy-start.2
  0.0 6.6 %front_pieces.1 = (bf16[16,88,256]{2,1,0:T(8,128)(2,1)}, f32[3,7,256]{2,1,0:T(8,128)S(1)}, f32[16,256]{1,0:T(8,128)S(1)}, f32[16,256]{1,0:T(8,128)S(1)}, f32[1,256]{1,0:T(1,128)S(1)}) custom-call(s32[1]{0:T(128)} %bitcast.refs_0_, bf16[128,4096]{1,0:T(8,128)(2,1)} %q_ref.1, bf16[128,4096]{1,0:T(8,128)(2,1)} %k_ref.1, bf16[128,4096]{1,0:T(8,128)(2,1)} %v_ref.1, ...), custom_call_target="tpu_custom_call" | custom-call | tf_op jit(solution)/shard_map/front_pieces/pallas_call | solution.py:584
  6.7 7.4 %all-to-all-start = ((bf16[16,88,256]{2,1,0:T(8,128)(2,1)}), bf16[16,88,256]{2,1,0:T(8,128)(2,1)S(1)}, u32[]{:S(2)}, u32[]{:S(2)}) async-start(bf16[16,88,256]{2,1,0:T(8,128)(2,1)} %get-tuple-element.17), calls=%async_computation | async-start | bytes 1441792 | tf_op jit(solution)/shard_map/all_to_all | solution.py:562
  14.0 0.0 copy-done
  14.0 0.0 copy-done.2
  14.0 0.0 copy-start.4
  14.1 0.0 copy-start.1
  14.1 8.7 %local_filter.1 = (f32[16,128,256]{2,1,0:T(8,128)}, f32[16,128,256]{2,1,0:T(8,128)S(1)}) custom-call(bf16[128,4096]{1,0:T(8,128)(2,1)} %q_ref.1, bf16[128,4096]{1,0:T(8,128)(2,1)} %k_ref.1, bf16[128,4096]{1,0:T(8,128)(2,1)} %v_ref.1, f32[3,7,4096]{2,1,0:T(8,128)} %taps_ref.1, f32[16,4096]{1,0:T(8,128)} %rates_ref.1, f32[16,4096]{1,0:T(8,128)} %res_ref.1, ...), custom_call_target="tpu_custom_call" | custom-call | flops 1000000000 | bytes 20000000 | tf_op jit(solution)/shard_map/local_filter/pallas_call | solution.py:615
  22.8 8.9 %all-to-all-done.x_ref = bf16[16,88,256]{2,1,0:T(8,128)(2,1)S(1)} async-done(((bf16[16,88,256]{2,1,0:T(8,128)(2,1)}), bf16[16,88,256]{2,1,0:T(8,128)(2,1)S(1)}, u32[]{:S(2)}, u32[]{:S(2)}) %all-to-all-start) | async-done | bytes 720928 | tf_op jit(solution)/shard_map/all_to_all | solution.py:562
  31.7 0.0 copy-done.4
  31.7 4.3 %middle_states.1 = bf16[16,40,256]{2,1,0:T(8,128)(2,1)} custom-call(s32[32]{0:T(128)S(1)} %copy-done.4, bf16[16,88,256]{2,1,0:T(8,128)(2,1)S(1)} %all-to-all-done.x_ref, f32[3,7,256]{2,1,0:T(8,128)S(1)} %get-tuple-element.21.taps_ref, f32[16,256]{1,0:T(8,128)S(1)} %get-tuple-element.22.rates_ref, f32[16,256]{1,0:T(8,128)S(1)} %get-tuple-element.23.res_ref, ...), custom_call_target="tpu_custom_call" | custom-call | tf_op jit(solution)/shard_map/middle_states/pallas_call | solution.py:633
  36.0 16.2 %all_to_all.10.back_ref = bf16[16,40,256]{2,1,0:T(8,128)(2,1)S(1)} all-to-all(bf16[16,40,256]{2,1,0:T(8,128)(2,1)} %middle_states.1), channel_id=1, replica_groups=mesh['ctx'=16,'ch'=2] {'ctx'}, dimensions={0} | all-to-all | bytes 655360 | tf_op jit(solution)/shard_map/all_to_all | solution.py:660
  52.2 0.0 copy-done.1
  52.2 0.0 copy-start.3
  52.2 1.7 %join_carry.1 = (f32[128,4096]{1,0:T(8,128)S(1)}, f32[1,128]{1,0:T(1,128)S(1)}) custom-call(bf16[16,40,256]{2,1,0:T(8,128)(2,1)S(1)} %all_to_all.10.back_ref, bf16[2,128,40]{2,1,0:T(8,128)(2,1)S(1)} %copy-done.1, f32[16,128,256]{2,1,0:T(8,128)} %get-tuple-element.25.qc_ref, f32[16,128,256]{2,1,0:T(8,128)S(1)} %get-tuple-element.26.y_ref), custom_call_target="tpu_custom_call" | custom-call | tf_op jit(solution)/shard_map/join_carry/pallas_call | solution.py:665
  54.0 1.6 %collective-permute-start = (f32[1,128]{1,0:T(1,128)S(1)}, f32[1,128]{1,0:T(1,128)S(1)}, u32[]{:S(2)}, u32[]{:S(2)}) collective-permute-start(f32[1,128]{1,0:T(1,128)S(1)} %get-tuple-element.28.refs_2_), channel_id=1, source_target_pairs={{0,1},{1,0},{2,3},{3,2},{4,5},{5,4},{6,7},{7,6},{8,9},{9,8},{10,11... | collective-permute-start | bytes 1544 | tf_op jit(solution)/shard_map/ppermute | solution.py:677
  55.6 2.0 %collective-permute-done.refs_3_ = f32[1,128]{1,0:T(1,128)S(1)} collective-permute-done((f32[1,128]{1,0:T(1,128)S(1)}, f32[1,128]{1,0:T(1,128)S(1)}, u32[]{:S(2)}, u32[]{:S(2)}) %collective-permute-start) | collective-permute-done | bytes 544 | tf_op jit(solution)/shard_map/ppermute | solution.py:677
  57.6 0.0 copy-done.3
  57.6 1.1 %scale_rows.1 = bf16[128,4096]{1,0:T(8,128)(2,1)} custom-call(f32[128,4096]{1,0:T(8,128)S(1)} %get-tuple-element.27.refs_0_, f32[1,4096]{1,0:T(1,128)S(1)} %bitcast.5, f32[1,128]{1,0:T(1,128)S(1)} %get-tuple-element.28.refs_2_, f32[1,128]{1,0:T(1,128)S(1)} %collective-permute-done.refs_3_), custom_call_target="tpu_custom_call" | custom-call | tf_op jit(solution)/shard_map/scale_rows/pallas_call | solution.py:678
Async XLA Ops:
  0.0 14.0 %copy-start = (bf16[384,192]{1,0:T(8,128)(2,1)S(1)}, bf16[384,192]{1,0:T(8,128)(2,1)}, u32[]{:S(2)}) copy-start(bf16[384,192]{1,0:T(8,128)(2,1)} %constant.13.clone.local_ref) | copy-start | bytes 442372
  0.0 14.0 %copy-start.2 = (f32[4096]{0:T(1024)S(1)}, f32[4096]{0:T(1024)}, u32[]{:S(2)}) copy-start(f32[4096]{0:T(1024)} %param.19) | copy-start | bytes 49156
  6.7 25.0 %all-to-all-start = ((bf16[16,88,256]{2,1,0:T(8,128)(2,1)}), bf16[16,88,256]{2,1,0:T(8,128)(2,1)S(1)}, u32[]{:S(2)}, u32[]{:S(2)}) async-start(bf16[16,88,256]{2,1,0:T(8,128)(2,1)} %get-tuple-element.17), calls=%async_computation | async-start | bytes 1441792 | tf_op jit(solution)/shard_map/all_to_all | solution.py:562
  14.0 17.6 %copy-start.4 = (s32[32]{0:T(128)S(1)}, s32[32]{0:T(128)}, u32[]{:S(2)}) copy-start(s32[32]{0:T(128)} %perm_ref.1) | copy-start | bytes 388
  14.1 38.2 %copy-start.1 = (bf16[2,128,40]{2,1,0:T(8,128)(2,1)S(1)}, bf16[2,128,40]{2,1,0:T(8,128)(2,1)}, u32[]{:S(2)}) copy-start(bf16[2,128,40]{2,1,0:T(8,128)(2,1)} %constant.14.clone.lift_ref) | copy-start | bytes 61444
  52.2 5.4 %copy-start.3 = (f32[4096]{0:T(1024)S(1)}, f32[4096]{0:T(1024)}, u32[]{:S(2)}) copy-start(f32[4096]{0:T(1024)} %param.20) | copy-start | bytes 49156
  54.0 3.6 %collective-permute-start = (f32[1,128]{1,0:T(1,128)S(1)}, f32[1,128]{1,0:T(1,128)S(1)}, u32[]{:S(2)}, u32[]{:S(2)}) collective-permute-start(f32[1,128]{1,0:T(1,128)S(1)} %get-tuple-element.28.refs_2_), channel_id=1, source_target_pairs={{0,1},{1,0},{2,3},{3,2},{4,5},{5,4},{6,7},{7,6},{8,9},{9,8},{10,11... | collective-permute-start | bytes 1544 | tf_op jit(solution)/shard_map/ppermute | solution.py:677

commit v14 on v13

--- a/solution.py
+++ b/solution.py
@@ -259,9 +259,8 @@
             copy.wait()
 
 
-def local_kernel(
-    q_ref, k_ref, v_ref, taps_ref, rates_ref, res_ref, skip_ref, local_ref, qc_ref, y_ref, xs, u_vm
-):
+def local_kernel(q_ref, k_ref, v_ref, taps_ref, rates_ref, res_ref, skip_ref, local_ref, *refs):
+    *kept, rest_ref, y_ref, xs, u_vm, qc_ref = refs
     tile = q_ref.shape[1]
     per = SPAN // LANES
     first_row = lax.broadcasted_iota(jnp.int32, (8, LANES), 0)
@@ -305,6 +304,18 @@
             for p in range(RANK):
                 total = total + weights[p] * parts[p * STRETCH : (p + 1) * STRETCH, :]
             y_ref[c, rows, :] = total
+    if not kept:
+        rest_ref[...] = qc_ref[...]
+        return
+    half = pl.num_programs(0) // 2
+
+    @pl.when(pl.program_id(0) < half)
+    def _():
+        kept[0][...] = qc_ref[...]
+
+    @pl.when(pl.program_id(0) >= half)
+    def _():
+        rest_ref[...] = qc_ref[...]
 
 
 def middle_kernel(
@@ -466,19 +477,21 @@
     lax.fori_loop(0, slots // 2, end, 0)
 
 
-def join_kernel(back_ref, lift_ref, qc_ref, y_ref, z_ref, sq_ref, qc_vm, carry, total, sems):
-    blocks, tokens, _ = qc_vm.shape
+def join_kernel(back_ref, lift_ref, *refs):
+    *kept, rest_ref, y_ref, z_ref, sq_ref, rest_vm, carry, total, sems = refs
+    blocks, tokens, _ = y_ref.shape
     by_dest = len(back_ref.shape) == 3
     chunk = 4
+    first = blocks - rest_vm.shape[0]
 
     def load(c):
         rows = pl.ds(c * chunk, chunk)
-        return pltpu.make_async_copy(qc_ref.at[rows], qc_vm.at[rows], sems.at[c])
+        return pltpu.make_async_copy(rest_ref.at[rows], rest_vm.at[rows], sems.at[c])
 
     def lanes(b):
         return pl.ds(pl.multiple_of(b * SPAN, SPAN), SPAN)
 
-    for c in range(blocks // chunk):
+    for c in range((blocks - first) // chunk):
         load(c).start()
 
     def products(c, unused):
@@ -492,20 +505,29 @@
     lax.fori_loop(0, blocks // chunk, products, 0)
     total[...] = jnp.zeros((tokens, LANES), F32)
 
-    def square(c, unused):
-        load(c).wait()
+    def square(held, offset, c):
         part = total[...]
         for k in range(chunk):
             b = c * chunk + k
-            z = qc_vm[b] * carry[b]
-            z_ref[:, lanes(b)] = z
+            z = held[b] * carry[offset + b]
+            z_ref[:, lanes(offset + b)] = z
             squares = z * z
             for h in range(SPAN // LANES):
                 part = part + squares[:, h * LANES : (h + 1) * LANES]
         total[...] = part
+
+    def from_kept(c, unused):
+        square(kept[0], 0, c)
         return unused
 
-    lax.fori_loop(0, blocks // chunk, square, 0)
+    def from_rest(c, unused):
+        load(c).wait()
+        square(rest_vm, first, c)
+        return unused
+
+    if kept:
+        lax.fori_loop(0, first // chunk, from_kept, 0)
+    lax.fori_loop(0, (blocks - first) // chunk, from_rest, 0)
     sq_ref[...] = jnp.sum(total[...].T, axis=0, keepdims=True)
 
 
@@ -612,15 +634,21 @@
     if not direct:
         mine = (cut(short_weight), cut(rates, 0.01), cut(residues), cut(skip))
 
-    query, inner = pl.pallas_call(
+    half = steps // 2 if steps % 2 == 0 else 0
+    kept = half * (tile // SPAN)
+    places = [lambda c: (jnp.minimum(c, half - 1), 0, 0)] * (kept > 0)
+    places += [lambda c: (jnp.maximum(c - half, 0), 0, 0), lambda c: (c, 0, 0)]
+    *query, inner = pl.pallas_call(
         local_kernel,
         grid=(steps,),
         in_specs=[columns(tokens)] * 3
         + [columns(3, REACH + 1), columns(order), columns(order), columns(1), whole(local)],
-        out_specs=[pl.BlockSpec((tile // SPAN, tokens, SPAN), lambda c: (c, 0, 0))] * 2,
-        out_shape=[pltpu.HBM((blocks, tokens, SPAN), F32), pltpu.VMEM((blocks, tokens, SPAN), F32)],
+        out_specs=[pl.BlockSpec((tile // SPAN, tokens, SPAN), at) for at in places],
+        out_shape=[pltpu.VMEM((kept, tokens, SPAN), F32)] * (kept > 0)
+        + [pltpu.HBM((blocks - kept, tokens, SPAN), F32), pltpu.VMEM((blocks, tokens, SPAN), F32)],
         scratch_shapes=[
             pltpu.VMEM((3, groups, 2 * (STRETCH + 8), LANES), F32),
+            pltpu.VMEM((tile // SPAN, tokens, SPAN), F32),
             pltpu.VMEM((tile // SPAN, tokens, SPAN), F32),
         ],
         compiler_params=limit(24),
@@ -664,14 +692,18 @@
     keep = lambda array: pltpu.with_memory_space_constraint(array, pltpu.VMEM)
     zvalues, squares = pl.pallas_call(
         join_kernel,
-        in_specs=[vmem] * 2 + [hbm, vmem],
+        in_specs=[vmem] * (1 + len(query)) + [hbm, vmem],
         out_specs=[vmem] * 2,
         out_shape=[f32(tokens, width), f32(1, tokens)],
-        scratch_shapes=[pltpu.VMEM((blocks, tokens, SPAN), F32)] * 2
-        + [pltpu.VMEM((tokens, LANES), F32), pltpu.SemaphoreType.DMA((blocks // 4,))],
+        scratch_shapes=[
+            pltpu.VMEM((blocks - kept, tokens, SPAN), F32),
+            pltpu.VMEM((blocks, tokens, SPAN), F32),
+            pltpu.VMEM((tokens, LANES), F32),
+            pltpu.SemaphoreType.DMA(((blocks - kept) // 4,)),
+        ],
         compiler_params=limit(24),
         name="join_carry",
-    )(back, lift, pin(query), keep(inner))
+    )(back, lift, *map(keep, query[:-1]), pin(query[-1]), keep(inner))
     sums = [squares]
     for shift in range(1, n_ch):
         sums.append(lax.ppermute(squares, "ch", [(i, (i + shift) % n_ch) for i in range(n_ch)]))

time: 59.1 us -> 58.9 us (level)
  waiting for transfers between devices: 10.9 us -> 9.82 us
  local copies, waits for them, and re-layouts: 0.02 us -> 1 us
    all_to_all x1, waiting for transfers between devices: 8.9 us -> 7.79 us  [exchange(): return lax.all_to_all(array, 'ctx', 0, 0, tiled=True)]
    unnamed x10 -> x14, local copies, waits for them, and re-layouts: 0.02 us -> 1 us
where the time goes in v14:
time: 58.9 us; the launch traced here: 58.6 us
  Pallas kernels  22.5 us (38%)
  blocking collectives  16.2 us (28%)
  waiting for transfers between devices  9.82 us (17%)
  starting transfers between devices  8.95 us (15%)
  local copies, waits for them, and re-layouts  1 us (2%)
    all_to_all x1, blocking collectives, on_device(): back = lax.all_to_all(back, 'ctx', 0, 0, tiled=True)  16.2 us
    pallas_call x1, Pallas kernels, on_device(): pl.pallas_call(local_kernel, grid=(steps,), in_specs=[columns(tokens)] *...  8.84 us
    all_to_all x1, waiting for transfers between devices, exchange(): return lax.all_to_all(array, 'ctx', 0, 0, tiled=True)  7.79 us
    all_to_all x1, starting transfers between devices, exchange(): return lax.all_to_all(array, 'ctx', 0, 0, tiled=True)  7.37 us
    pallas_call x1, Pallas kernels, on_device(): pl.pallas_call(functools.partial(front_kernel, direct=direct), in_specs=[...  6.63 us
    pallas_call x1, Pallas kernels, on_device(): pl.pallas_call(middle_kernel, in_specs=[smem] + [vmem] * 5, out_specs=hbm...  4.35 us
    ppermute x1, waiting for transfers between devices, on_device(): lax.ppermute(squares, 'ch', [(i, (i + shift) % n_ch) for i in range(n_ch)])  2.02 us
    ppermute x1, starting transfers between devices, on_device(): lax.ppermute(squares, 'ch', [(i, (i + shift) % n_ch) for i in range(n_ch)])  1.58 us
  transfers between devices with their start and end apart: 2, of which 2 were waited for; matrix products, arithmetic and copies ran while one was open for 0% of the time, Pallas kernels for 15%

profile of v14, /device:TPU:0, one launch (start us, length us, event | category | flops | bytes accessed | tf_op | source)
XLA Modules:
  0.0 58.6 jit_solution(8573579160633647239)
XLA Ops:
  0.0 0.0 copy-start.2
  0.0 0.0 copy-start.4
  0.0 6.6 %front_pieces.1 = (bf16[16,88,256]{2,1,0:T(8,128)(2,1)}, f32[3,7,256]{2,1,0:T(8,128)S(1)}, f32[16,256]{1,0:T(8,128)S(1)}, f32[16,256]{1,0:T(8,128)S(1)}, f32[1,256]{1,0:T(1,128)S(1)}) custom-call(s32[1]{0:T(128)} %bitcast.refs_0_, bf16[128,4096]{1,0:T(8,128)(2,1)} %q_ref.1, bf16[128,4096]{1,0:T(8,128)(2,1)} %k_ref.1, bf16[128,4096]{1,0:T(8,128)(2,1)} %v_ref.1, ...), custom_call_target="tpu_custom_call" | custom-call | tf_op jit(solution)/shard_map/front_pieces/pallas_call | solution.py:606
  6.6 7.4 %all-to-all-start = ((bf16[16,88,256]{2,1,0:T(8,128)(2,1)}), bf16[16,88,256]{2,1,0:T(8,128)(2,1)S(1)}, u32[]{:S(2)}, u32[]{:S(2)}) async-start(bf16[16,88,256]{2,1,0:T(8,128)(2,1)} %get-tuple-element.19), calls=%async_computation | async-start | bytes 1441792 | tf_op jit(solution)/shard_map/all_to_all | solution.py:584
  14.0 0.0 copy-done.2
  14.0 0.0 copy-done.4
  14.0 0.0 copy-start.6
  14.1 0.0 copy-start.3
  14.1 8.8 %local_filter.1 = (f32[8,128,256]{2,1,0:T(8,128)S(1)}, f32[8,128,256]{2,1,0:T(8,128)}, f32[16,128,256]{2,1,0:T(8,128)S(1)}) custom-call(bf16[128,4096]{1,0:T(8,128)(2,1)} %q_ref.1, bf16[128,4096]{1,0:T(8,128)(2,1)} %k_ref.1, bf16[128,4096]{1,0:T(8,128)(2,1)} %v_ref.1, f32[3,7,4096]{2,1,0:T(8,128)} %taps_ref.1, f32[16,4096]{1,0:T(8,128)} %rates_ref.1, ...), custom_call_target="tpu_custom_call" | custom-call | flops 1000000000 | bytes 20000000 | tf_op jit(solution)/shard_map/local_filter/pallas_call | solution.py:641
  22.9 0.0 copy-start
  22.9 1.0 %copy-done = f32[8,128,256]{2,1,0:T(8,128)} copy-done((f32[8,128,256]{2,1,0:T(8,128)}, f32[8,128,256]{2,1,0:T(8,128)S(1)}, u32[]{:S(2)}) %copy-start) | copy-done | bytes 1048600
  23.9 7.8 %all-to-all-done.x_ref = bf16[16,88,256]{2,1,0:T(8,128)(2,1)S(1)} async-done(((bf16[16,88,256]{2,1,0:T(8,128)(2,1)}), bf16[16,88,256]{2,1,0:T(8,128)(2,1)S(1)}, u32[]{:S(2)}, u32[]{:S(2)}) %all-to-all-start) | async-done | bytes 720928 | tf_op jit(solution)/shard_map/all_to_all | solution.py:584
  31.7 0.0 copy-start.1
  31.7 0.0 copy-done.6
  31.7 4.4 %middle_states.1 = bf16[16,40,256]{2,1,0:T(8,128)(2,1)} custom-call(s32[32]{0:T(128)S(1)} %copy-done.6, bf16[16,88,256]{2,1,0:T(8,128)(2,1)S(1)} %all-to-all-done.x_ref, f32[3,7,256]{2,1,0:T(8,128)S(1)} %get-tuple-element.24.taps_ref, f32[16,256]{1,0:T(8,128)S(1)} %get-tuple-element.25.rates_ref, f32[16,256]{1,0:T(8,128)S(1)} %get-tuple-element.26.res_ref, ...), custom_call_target="tpu_custom_call" | custom-call | tf_op jit(solution)/shard_map/middle_states/pallas_call | solution.py:661
  36.0 16.2 %all_to_all.10.back_ref = bf16[16,40,256]{2,1,0:T(8,128)(2,1)S(1)} all-to-all(bf16[16,40,256]{2,1,0:T(8,128)(2,1)} %middle_states.1), channel_id=1, replica_groups=mesh['ctx'=16,'ch'=2] {'ctx'}, dimensions={0} | all-to-all | bytes 655360 | tf_op jit(solution)/shard_map/all_to_all | solution.py:688
  52.3 0.0 copy-done.3
  52.3 0.0 copy-done.1
  52.3 0.0 copy-start.5
  52.3 1.5 %join_carry.1 = (f32[128,4096]{1,0:T(8,128)S(1)}, f32[1,128]{1,0:T(1,128)S(1)}) custom-call(bf16[16,40,256]{2,1,0:T(8,128)(2,1)S(1)} %all_to_all.10.back_ref, bf16[2,128,40]{2,1,0:T(8,128)(2,1)S(1)} %copy-done.3, f32[8,128,256]{2,1,0:T(8,128)S(1)} %copy-done.1, f32[8,128,256]{2,1,0:T(8,128)} %get-tuple-element.29.refs_1_, ...), custom_call_target="tpu_custom_call" | custom-call | tf_op jit(solution)/shard_map/join_carry/pallas_call | solution.py:693
  53.8 1.6 %collective-permute-start = (f32[1,128]{1,0:T(1,128)S(1)}, f32[1,128]{1,0:T(1,128)S(1)}, u32[]{:S(2)}, u32[]{:S(2)}) collective-permute-start(f32[1,128]{1,0:T(1,128)S(1)} %get-tuple-element.32.refs_2_), channel_id=1, source_target_pairs={{0,1},{1,0},{2,3},{3,2},{4,5},{5,4},{6,7},{7,6},{8,9},{9,8},{10,11... | collective-permute-start | bytes 1544 | tf_op jit(solution)/shard_map/ppermute | solution.py:709
  55.4 2.0 %collective-permute-done.refs_3_ = f32[1,128]{1,0:T(1,128)S(1)} collective-permute-done((f32[1,128]{1,0:T(1,128)S(1)}, f32[1,128]{1,0:T(1,128)S(1)}, u32[]{:S(2)}, u32[]{:S(2)}) %collective-permute-start) | collective-permute-done | bytes 544 | tf_op jit(solution)/shard_map/ppermute | solution.py:709
  57.4 0.0 copy-done.5
  57.4 1.1 %scale_rows.1 = bf16[128,4096]{1,0:T(8,128)(2,1)} custom-call(f32[128,4096]{1,0:T(8,128)S(1)} %get-tuple-element.31.refs_0_, f32[1,4096]{1,0:T(1,128)S(1)} %bitcast.5, f32[1,128]{1,0:T(1,128)S(1)} %get-tuple-element.32.refs_2_, f32[1,128]{1,0:T(1,128)S(1)} %collective-permute-done.refs_3_), custom_call_target="tpu_custom_call" | custom-call | tf_op jit(solution)/shard_map/scale_rows/pallas_call | solution.py:710
Async XLA Ops:
  0.0 14.0 %copy-start.2 = (bf16[384,192]{1,0:T(8,128)(2,1)S(1)}, bf16[384,192]{1,0:T(8,128)(2,1)}, u32[]{:S(2)}) copy-start(bf16[384,192]{1,0:T(8,128)(2,1)} %constant.13.clone.local_ref) | copy-start | bytes 442372
  0.0 14.0 %copy-start.4 = (f32[4096]{0:T(1024)S(1)}, f32[4096]{0:T(1024)}, u32[]{:S(2)}) copy-start(f32[4096]{0:T(1024)} %param.19) | copy-start | bytes 49156
  6.6 25.0 %all-to-all-start = ((bf16[16,88,256]{2,1,0:T(8,128)(2,1)}), bf16[16,88,256]{2,1,0:T(8,128)(2,1)S(1)}, u32[]{:S(2)}, u32[]{:S(2)}) async-start(bf16[16,88,256]{2,1,0:T(8,128)(2,1)} %get-tuple-element.19), calls=%async_computation | async-start | bytes 1441792 | tf_op jit(solution)/shard_map/all_to_all | solution.py:584
  14.0 17.6 %copy-start.6 = (s32[32]{0:T(128)S(1)}, s32[32]{0:T(128)}, u32[]{:S(2)}) copy-start(s32[32]{0:T(128)} %perm_ref.1) | copy-start | bytes 388
  14.1 38.2 %copy-start.3 = (bf16[2,128,40]{2,1,0:T(8,128)(2,1)S(1)}, bf16[2,128,40]{2,1,0:T(8,128)(2,1)}, u32[]{:S(2)}) copy-start(bf16[2,128,40]{2,1,0:T(8,128)(2,1)} %constant.14.clone.lift_ref) | copy-start | bytes 61444
  22.9 1.0 %copy-start = (f32[8,128,256]{2,1,0:T(8,128)}, f32[8,128,256]{2,1,0:T(8,128)S(1)}, u32[]{:S(2)}) copy-start(f32[8,128,256]{2,1,0:T(8,128)S(1)} %get-tuple-element.28.refs_0_) | copy-start | bytes 3145732
  31.7 20.6 %copy-start.1 = (f32[8,128,256]{2,1,0:T(8,128)S(1)}, f32[8,128,256]{2,1,0:T(8,128)}, u32[]{:S(2)}) copy-start(f32[8,128,256]{2,1,0:T(8,128)} %copy-done) | copy-start | bytes 3145732
  52.3 5.2 %copy-start.5 = (f32[4096]{0:T(1024)S(1)}, f32[4096]{0:T(1024)}, u32[]{:S(2)}) copy-start(f32[4096]{0:T(1024)} %param.20) | copy-start | bytes 49156
  53.8 3.6 %collective-permute-start = (f32[1,128]{1,0:T(1,128)S(1)}, f32[1,128]{1,0:T(1,128)S(1)}, u32[]{:S(2)}, u32[]{:S(2)}) collective-permute-start(f32[1,128]{1,0:T(1,128)S(1)} %get-tuple-element.32.refs_2_), channel_id=1, source_target_pairs={{0,1},{1,0},{2,3},{3,2},{4,5},{5,4},{6,7},{7,6},{8,9},{9,8},{10,11... | collective-permute-start | bytes 1544 | tf_op jit(solution)/shard_map/ppermute | solution.py:709

commit v15 on v14

--- a/solution.py
+++ b/solution.py
@@ -463,8 +463,6 @@
             packed[src, :, g * LANES : (g + 1) * LANES] = slab[src, g, 0 : 2 * BACK, :].astype(BF16)
         return carry
 
-    lax.fori_loop(0, slots // 2, pack, 0, unroll=2)
-
     def send(src, carry):
         store(src).start()
         return carry
@@ -473,7 +471,10 @@
         store(src).wait()
         return carry
 
-    lax.fori_loop(0, slots // 2, send, 0)
+    middle = slots // 4
+    for low, high in ((0, middle), (middle, slots // 2)):
+        lax.fori_loop(low, high, pack, 0, unroll=4)
+        lax.fori_loop(low, high, send, 0)
     lax.fori_loop(0, slots // 2, end, 0)
 
 

time: 58.9 us -> 58.9 us (level)
  no operation moved by 1% of the time
where the time goes in v15:
time: 58.9 us; the launch traced here: 58.5 us
  Pallas kernels  22.5 us (38%)
  blocking collectives  16.2 us (28%)
  waiting for transfers between devices  9.8 us (17%)
  starting transfers between devices  8.97 us (15%)
  local copies, waits for them, and re-layouts  1 us (2%)
    all_to_all x1, blocking collectives, on_device(): back = lax.all_to_all(back, 'ctx', 0, 0, tiled=True)  16.2 us
    pallas_call x1, Pallas kernels, on_device(): pl.pallas_call(local_kernel, grid=(steps,), in_specs=[columns(tokens)] *...  8.84 us
    all_to_all x1, waiting for transfers between devices, exchange(): return lax.all_to_all(array, 'ctx', 0, 0, tiled=True)  7.79 us
    all_to_all x1, starting transfers between devices, exchange(): return lax.all_to_all(array, 'ctx', 0, 0, tiled=True)  7.37 us
    pallas_call x1, Pallas kernels, on_device(): pl.pallas_call(functools.partial(front_kernel, direct=direct), in_specs=[...  6.63 us
    pallas_call x1, Pallas kernels, on_device(): pl.pallas_call(middle_kernel, in_specs=[smem] + [vmem] * 5, out_specs=hbm...  4.32 us
    ppermute x1, waiting for transfers between devices, on_device(): lax.ppermute(squares, 'ch', [(i, (i + shift) % n_ch) for i in range(n_ch)])  2.01 us
    ppermute x1, starting transfers between devices, on_device(): lax.ppermute(squares, 'ch', [(i, (i + shift) % n_ch) for i in range(n_ch)])  1.6 us
  transfers between devices with their start and end apart: 2, of which 2 were waited for; matrix products, arithmetic and copies ran while one was open for 0% of the time, Pallas kernels for 15%

profile of v15, /device:TPU:0, one launch (start us, length us, event | category | flops | bytes accessed | tf_op | source)
XLA Modules:
  0.0 58.5 jit_solution(12653993232069255814)
XLA Ops:
  0.0 0.0 copy-start.2
  0.0 0.0 copy-start.4
  0.0 6.6 %front_pieces.1 = (bf16[16,88,256]{2,1,0:T(8,128)(2,1)}, f32[3,7,256]{2,1,0:T(8,128)S(1)}, f32[16,256]{1,0:T(8,128)S(1)}, f32[16,256]{1,0:T(8,128)S(1)}, f32[1,256]{1,0:T(1,128)S(1)}) custom-call(s32[1]{0:T(128)} %bitcast.refs_0_, bf16[128,4096]{1,0:T(8,128)(2,1)} %q_ref.1, bf16[128,4096]{1,0:T(8,128)(2,1)} %k_ref.1, bf16[128,4096]{1,0:T(8,128)(2,1)} %v_ref.1, ...), custom_call_target="tpu_custom_call" | custom-call | tf_op jit(solution)/shard_map/front_pieces/pallas_call | solution.py:607
  6.6 7.4 %all-to-all-start = ((bf16[16,88,256]{2,1,0:T(8,128)(2,1)}), bf16[16,88,256]{2,1,0:T(8,128)(2,1)S(1)}, u32[]{:S(2)}, u32[]{:S(2)}) async-start(bf16[16,88,256]{2,1,0:T(8,128)(2,1)} %get-tuple-element.19), calls=%async_computation | async-start | bytes 1441792 | tf_op jit(solution)/shard_map/all_to_all | solution.py:585
  14.0 0.0 copy-done.2
  14.0 0.0 copy-done.4
  14.0 0.0 copy-start.6
  14.1 0.0 copy-start.3
  14.1 8.8 %local_filter.1 = (f32[8,128,256]{2,1,0:T(8,128)S(1)}, f32[8,128,256]{2,1,0:T(8,128)}, f32[16,128,256]{2,1,0:T(8,128)S(1)}) custom-call(bf16[128,4096]{1,0:T(8,128)(2,1)} %q_ref.1, bf16[128,4096]{1,0:T(8,128)(2,1)} %k_ref.1, bf16[128,4096]{1,0:T(8,128)(2,1)} %v_ref.1, f32[3,7,4096]{2,1,0:T(8,128)} %taps_ref.1, f32[16,4096]{1,0:T(8,128)} %rates_ref.1, ...), custom_call_target="tpu_custom_call" | custom-call | flops 1000000000 | bytes 20000000 | tf_op jit(solution)/shard_map/local_filter/pallas_call | solution.py:642
  22.9 0.0 copy-start
  22.9 1.0 %copy-done = f32[8,128,256]{2,1,0:T(8,128)} copy-done((f32[8,128,256]{2,1,0:T(8,128)}, f32[8,128,256]{2,1,0:T(8,128)S(1)}, u32[]{:S(2)}) %copy-start) | copy-done | bytes 1048600
  23.9 7.8 %all-to-all-done.x_ref = bf16[16,88,256]{2,1,0:T(8,128)(2,1)S(1)} async-done(((bf16[16,88,256]{2,1,0:T(8,128)(2,1)}), bf16[16,88,256]{2,1,0:T(8,128)(2,1)S(1)}, u32[]{:S(2)}, u32[]{:S(2)}) %all-to-all-start) | async-done | bytes 720928 | tf_op jit(solution)/shard_map/all_to_all | solution.py:585
  31.7 0.0 copy-start.1
  31.7 0.0 copy-done.6
  31.7 4.3 %middle_states.1 = bf16[16,40,256]{2,1,0:T(8,128)(2,1)} custom-call(s32[32]{0:T(128)S(1)} %copy-done.6, bf16[16,88,256]{2,1,0:T(8,128)(2,1)S(1)} %all-to-all-done.x_ref, f32[3,7,256]{2,1,0:T(8,128)S(1)} %get-tuple-element.24.taps_ref, f32[16,256]{1,0:T(8,128)S(1)} %get-tuple-element.25.rates_ref, f32[16,256]{1,0:T(8,128)S(1)} %get-tuple-element.26.res_ref, ...), custom_call_target="tpu_custom_call" | custom-call | tf_op jit(solution)/shard_map/middle_states/pallas_call | solution.py:662
  36.0 16.2 %all_to_all.10.back_ref = bf16[16,40,256]{2,1,0:T(8,128)(2,1)S(1)} all-to-all(bf16[16,40,256]{2,1,0:T(8,128)(2,1)} %middle_states.1), channel_id=1, replica_groups=mesh['ctx'=16,'ch'=2] {'ctx'}, dimensions={0} | all-to-all | bytes 655360 | tf_op jit(solution)/shard_map/all_to_all | solution.py:689
  52.2 0.0 copy-done.3
  52.2 0.0 copy-done.1
  52.2 0.0 copy-start.5
  52.3 1.5 %join_carry.1 = (f32[128,4096]{1,0:T(8,128)S(1)}, f32[1,128]{1,0:T(1,128)S(1)}) custom-call(bf16[16,40,256]{2,1,0:T(8,128)(2,1)S(1)} %all_to_all.10.back_ref, bf16[2,128,40]{2,1,0:T(8,128)(2,1)S(1)} %copy-done.3, f32[8,128,256]{2,1,0:T(8,128)S(1)} %copy-done.1, f32[8,128,256]{2,1,0:T(8,128)} %get-tuple-element.29.refs_1_, ...), custom_call_target="tpu_custom_call" | custom-call | tf_op jit(solution)/shard_map/join_carry/pallas_call | solution.py:694
  53.8 1.6 %collective-permute-start = (f32[1,128]{1,0:T(1,128)S(1)}, f32[1,128]{1,0:T(1,128)S(1)}, u32[]{:S(2)}, u32[]{:S(2)}) collective-permute-start(f32[1,128]{1,0:T(1,128)S(1)} %get-tuple-element.32.refs_2_), channel_id=1, source_target_pairs={{0,1},{1,0},{2,3},{3,2},{4,5},{5,4},{6,7},{7,6},{8,9},{9,8},{10,11... | collective-permute-start | bytes 1544 | tf_op jit(solution)/shard_map/ppermute | solution.py:710
  55.4 2.0 %collective-permute-done.refs_3_ = f32[1,128]{1,0:T(1,128)S(1)} collective-permute-done((f32[1,128]{1,0:T(1,128)S(1)}, f32[1,128]{1,0:T(1,128)S(1)}, u32[]{:S(2)}, u32[]{:S(2)}) %collective-permute-start) | collective-permute-done | bytes 544 | tf_op jit(solution)/shard_map/ppermute | solution.py:710
  57.4 0.0 copy-done.5
  57.4 1.1 %scale_rows.1 = bf16[128,4096]{1,0:T(8,128)(2,1)} custom-call(f32[128,4096]{1,0:T(8,128)S(1)} %get-tuple-element.31.refs_0_, f32[1,4096]{1,0:T(1,128)S(1)} %bitcast.5, f32[1,128]{1,0:T(1,128)S(1)} %get-tuple-element.32.refs_2_, f32[1,128]{1,0:T(1,128)S(1)} %collective-permute-done.refs_3_), custom_call_target="tpu_custom_call" | custom-call | tf_op jit(solution)/shard_map/scale_rows/pallas_call | solution.py:711
Async XLA Ops:
  0.0 14.0 %copy-start.2 = (bf16[384,192]{1,0:T(8,128)(2,1)S(1)}, bf16[384,192]{1,0:T(8,128)(2,1)}, u32[]{:S(2)}) copy-start(bf16[384,192]{1,0:T(8,128)(2,1)} %constant.13.clone.local_ref) | copy-start | bytes 442372
  0.0 14.0 %copy-start.4 = (f32[4096]{0:T(1024)S(1)}, f32[4096]{0:T(1024)}, u32[]{:S(2)}) copy-start(f32[4096]{0:T(1024)} %param.19) | copy-start | bytes 49156
  6.6 25.0 %all-to-all-start = ((bf16[16,88,256]{2,1,0:T(8,128)(2,1)}), bf16[16,88,256]{2,1,0:T(8,128)(2,1)S(1)}, u32[]{:S(2)}, u32[]{:S(2)}) async-start(bf16[16,88,256]{2,1,0:T(8,128)(2,1)} %get-tuple-element.19), calls=%async_computation | async-start | bytes 1441792 | tf_op jit(solution)/shard_map/all_to_all | solution.py:585
  14.0 17.6 %copy-start.6 = (s32[32]{0:T(128)S(1)}, s32[32]{0:T(128)}, u32[]{:S(2)}) copy-start(s32[32]{0:T(128)} %perm_ref.1) | copy-start | bytes 388
  14.1 38.2 %copy-start.3 = (bf16[2,128,40]{2,1,0:T(8,128)(2,1)S(1)}, bf16[2,128,40]{2,1,0:T(8,128)(2,1)}, u32[]{:S(2)}) copy-start(bf16[2,128,40]{2,1,0:T(8,128)(2,1)} %constant.14.clone.lift_ref) | copy-start | bytes 61444
  22.9 1.0 %copy-start = (f32[8,128,256]{2,1,0:T(8,128)}, f32[8,128,256]{2,1,0:T(8,128)S(1)}, u32[]{:S(2)}) copy-start(f32[8,128,256]{2,1,0:T(8,128)S(1)} %get-tuple-element.28.refs_0_) | copy-start | bytes 3145732
  31.7 20.6 %copy-start.1 = (f32[8,128,256]{2,1,0:T(8,128)S(1)}, f32[8,128,256]{2,1,0:T(8,128)}, u32[]{:S(2)}) copy-start(f32[8,128,256]{2,1,0:T(8,128)} %copy-done) | copy-start | bytes 3145732
  52.2 5.1 %copy-start.5 = (f32[4096]{0:T(1024)S(1)}, f32[4096]{0:T(1024)}, u32[]{:S(2)}) copy-start(f32[4096]{0:T(1024)} %param.20) | copy-start | bytes 49156
  53.8 3.6 %collective-permute-start = (f32[1,128]{1,0:T(1,128)S(1)}, f32[1,128]{1,0:T(1,128)S(1)}, u32[]{:S(2)}, u32[]{:S(2)}) collective-permute-start(f32[1,128]{1,0:T(1,128)S(1)} %get-tuple-element.32.refs_2_), channel_id=1, source_target_pairs={{0,1},{1,0},{2,3},{3,2},{4,5},{5,4},{6,7},{7,6},{8,9},{9,8},{10,11... | collective-permute-start | bytes 1544 | tf_op jit(solution)/shard_map/ppermute | solution.py:710
